TPU v7x, 32 devices: a whole 2x2x4 slice. The times are simulated.
32 devices in a mesh: seq: 4 (over y, x), ctx: 8 (over z, core).
Axes of the slice: x: 2, y: 2, z: 4, core: 2. Of those that a mesh axis runs over, the one named last changes fastest.
Arguments:
- tokens: bfloat16 [4096, 2048], P(('seq', 'ctx')), may hold values from -6 to 6
- cotangent: bfloat16 [4096, 2048], P(('seq', 'ctx')), may hold values from -6 to 6
- norm_gain: bfloat16 [2048], P(('seq', 'ctx')), may hold values from 0.5 to 1.5
- gating_weight: bfloat16 [2048, 3072], P(('seq', 'ctx')), may hold values from -0.125 to 0.125
- inner_weight: bfloat16 [2048, 3072], P(('seq', 'ctx')), may hold values from -0.125 to 0.125
- state_weight: bfloat16 [2048, 512], P(('seq', 'ctx')), may hold values from -0.125 to 0.125
- step_weight: bfloat16 [2048, 48], P(('seq', 'ctx')), may hold values from -0.125 to 0.125
- conv_weight: bfloat16 [4, 3584], P(None, ('seq', 'ctx')), may hold values from -3 to 3
- conv_bias: bfloat16 [3584], P(('seq', 'ctx')), may hold values from -1.5 to 1.5
- mixer_gain: bfloat16 [3072], P(('seq', 'ctx')), may hold values from 0.5 to 1.5
- mixer_out: bfloat16 [3072, 2048], P(None, ('seq', 'ctx')), may hold values from -0.109375 to 0.109375
- query_weight: bfloat16 [2048, 1024], P(('seq', 'ctx')), may hold values from -0.125 to 0.125
- key_weight: bfloat16 [2048, 256], P(('seq', 'ctx')), may hold values from -0.125 to 0.125
- value_weight: bfloat16 [2048, 256], P(('seq', 'ctx')), may hold values from -0.125 to 0.125
- output_weight: bfloat16 [1024, 2048], P(None, ('seq', 'ctx')), may hold values from -0.75 to 0.75
- feed_gain: bfloat16 [2048], P(('seq', 'ctx')), may hold values from 0.5 to 1.5
- gate_matrix: bfloat16 [2048, 4096], P(('seq', 'ctx')), may hold values from -0.125 to 0.125
- lift_matrix: bfloat16 [2048, 4096], P(('seq', 'ctx')), may hold values from -0.125 to 0.125
- drop_matrix: bfloat16 [4096, 2048], P(None, ('seq', 'ctx')), may hold values from -0.09375 to 0.09375
- step_bias: float32 [48], replicated, may hold values from -4 to 0
- decay_log: float32 [48], replicated, may hold values from -10 to -1
- skip_scale: float32 [48], replicated, may hold values from 0.5 to 2
Outputs:
- layer_output: bfloat16 [4096, 2048], P(('seq', 'ctx'))
- tokens_grad: float32 [4096, 2048], P(('seq', 'ctx'))
- norm_gain_grad: float32 [2048], P(('seq', 'ctx'))
- gating_weight_grad: float32 [2048, 3072], P(('seq', 'ctx'))
- inner_weight_grad: float32 [2048, 3072], P(('seq', 'ctx'))
- state_weight_grad: float32 [2048, 512], P(('seq', 'ctx'))
- step_weight_grad: float32 [2048, 48], P(('seq', 'ctx'))
- conv_weight_grad: float32 [4, 3584], P(None, ('seq', 'ctx'))
- conv_bias_grad: float32 [3584], P(('seq', 'ctx'))
- mixer_gain_grad: float32 [3072], P(('seq', 'ctx'))
- mixer_out_grad: float32 [3072, 2048], P(None, ('seq', 'ctx'))
- query_weight_grad: float32 [2048, 1024], P(('seq', 'ctx'))
- key_weight_grad: float32 [2048, 256], P(('seq', 'ctx'))
- value_weight_grad: float32 [2048, 256], P(('seq', 'ctx'))
- output_weight_grad: float32 [1024, 2048], P(None, ('seq', 'ctx'))
- feed_gain_grad: float32 [2048], P(('seq', 'ctx'))
- gate_matrix_grad: float32 [2048, 4096], P(('seq', 'ctx'))
- lift_matrix_grad: float32 [2048, 4096], P(('seq', 'ctx'))
- drop_matrix_grad: float32 [4096, 2048], P(None, ('seq', 'ctx'))
- step_bias_grad: float32 [48], replicated
- decay_log_grad: float32 [48], replicated
- skip_scale_grad: float32 [48], replicated
All inputs are finite; a program needn't handle non-finite values.
Results may differ from a plain program's by a relative error of at most 0.013.
Values may be sent and summed in bfloat16 or wider, within the bound.
No kernel may reach another device: no remote copies, remote signals or barrier semaphores. Data moves between devices by JAX's collectives and lax.ppermute only.
A program may use at most 320 MiB of HBM per device.

v0:
```python
import jax
import jax.numpy as jnp
from jax import lax
from jax.sharding import PartitionSpec as P

DI = 3072
HM = 48
PM = 64
NS = 256
KC = 4
HA = 8
HK = 2
HD = 128


epsilon = 1e-06
highest = lax.Precision.HIGHEST
negative = -1e30


def from_behind(value, axis, steps):
    count = lax.axis_size(axis)
    leading, last = (max(0, -steps), min(count, count - steps))
    return lax.ppermute(value, axis, [(source, source + steps) for source in range(leading, last)])


def entering(part, axis, combine, identity, reverse):
    count = lax.axis_size(axis)
    place = lax.axis_index(axis)
    ahead = count - 1 - place if reverse else place
    gathered = jax.tree.map(lambda a: lax.all_gather(a, axis), part)
    state = jax.tree.map(lambda a, e: jnp.zeros_like(a) + jnp.asarray(e, a.dtype), part, identity)

    def one(step, state):
        source = count - 1 - step if reverse else step
        return combine(
            state, jax.tree.map(lambda a: lax.dynamic_index_in_dim(a, source, 0, False), gathered)
        )

    return lax.fori_loop(0, ahead, one, state)


def shortened(shard):
    return jax.tree.map(lambda a: a.astype(jnp.bfloat16) if a.dtype == jnp.float32 else a, shard)


def normalize(values):
    return values * lax.rsqrt(jnp.mean(values * values, axis=-1, keepdims=True) + epsilon)


def norm_back(values, upstream):
    scaled = lax.rsqrt(jnp.mean(values * values, axis=-1, keepdims=True) + epsilon)
    normed = values * scaled
    return scaled * (upstream - normed * jnp.mean(upstream * normed, axis=-1, keepdims=True))


def silu_value(values):
    return values * jax.nn.sigmoid(values)


def silu_slope(values):
    sigmoid_part = jax.nn.sigmoid(values)
    return sigmoid_part * (1.0 + values * (1.0 - sigmoid_part))


def softplus(values):
    return jnp.maximum(values, 0.0) + jnp.log1p(jnp.exp(-jnp.abs(values)))


def plain_dot(operand, against):
    return jnp.dot(operand, against, preferred_element_type=jnp.float32)


def tail_dot(operand, against):
    return lax.dot_general(
        operand, against, (((1,), (1,)), ((), ())), preferred_element_type=jnp.float32
    )


def lead_dot(operand, against):
    return lax.dot_general(
        operand, against, (((0,), (0,)), ((), ())), preferred_element_type=jnp.float32
    )


def chain_step(earlier, later_part):
    return (earlier[0] * later_part[0], later_part[0][:, None, None] * earlier[1] + later_part[1])


def block_split():
    return 512


def score_block(queries, key_block, start_row, query_place):
    key_heads = key_block.reshape(key_block.shape[0], HK, HD)
    scores = jnp.einsum(
        "tkgd,nkd->kgtn", queries, key_heads, preferred_element_type=jnp.float32
    ) * HD ** (-0.5)
    key_place = start_row + jnp.arange(key_block.shape[0], dtype=jnp.int32)
    visible = query_place[:, None] >= key_place[None, :]
    return (jnp.where(visible, scores, negative), visible)


def attend_rows(run_state, key_block, value_block, start_row, queries, query_place):
    run_max, run_total, run_acc = run_state
    scores, visible = score_block(queries, key_block, start_row, query_place)
    new_max = jnp.maximum(run_max, jnp.max(scores, axis=-1))
    weights = jnp.where(visible, jnp.exp(scores - new_max[..., None]), 0.0)
    factor = jnp.exp(run_max - new_max)
    value_heads = value_block.reshape(value_block.shape[0], HK, HD).astype(jnp.float32)
    run_acc = run_acc * factor[..., None] + jnp.einsum(
        "kgtn,nkd->kgtd", weights, value_heads, precision=highest
    )
    return (new_max, run_total * factor + jnp.sum(weights, axis=-1), run_acc)


def back_rows(
    query_sum,
    key_block,
    value_block,
    start_row,
    queries,
    grad_heads,
    grad_float,
    log_total,
    delta_rows,
    query_place,
):
    scores, visible = score_block(queries, key_block, start_row, query_place)
    probability = jnp.where(visible, jnp.exp(scores - log_total[..., None]), 0.0)
    key_heads = key_block.reshape(key_block.shape[0], HK, HD)
    value_heads = value_block.reshape(value_block.shape[0], HK, HD)
    prob_grad = jnp.einsum(
        "tkgd,nkd->kgtn", grad_heads, value_heads, preferred_element_type=jnp.float32
    )
    score_grad = (probability * (prob_grad - delta_rows[..., None])).astype(jnp.bfloat16)
    query_sum = query_sum + jnp.einsum(
        "kgtn,nkd->tkgd", score_grad, key_heads, preferred_element_type=jnp.float32
    ) * HD ** (-0.5)
    key_part = jnp.einsum(
        "kgtn,tkgd->nkd", score_grad, queries, preferred_element_type=jnp.float32
    ) * HD ** (-0.5)
    value_part = jnp.einsum("kgtn,tkgd->nkd", probability, grad_float, precision=highest)
    key_count = key_block.shape[0]
    return (
        query_sum,
        jnp.concatenate(
            [key_part.reshape(key_count, HK * HD), value_part.reshape(key_count, HK * HD)], 1
        ),
    )


def local(
    tokens,
    cotangent,
    norm_gain,
    gating_weight,
    inner_weight,
    state_weight,
    step_weight,
    conv_weight,
    conv_bias,
    mixer_gain,
    mixer_out,
    query_weight,
    key_weight,
    value_weight,
    output_weight,
    feed_gain,
    gate_matrix,
    lift_matrix,
    drop_matrix,
    step_bias,
    decay_log,
    skip_scale,
):
    row_count = tokens.shape[0]
    groups = HA // HK
    length = row_count * lax.axis_size("ctx")
    query_place = lax.axis_index("ctx") * row_count + jnp.arange(row_count, dtype=jnp.int32)
    conv_width = DI + 2 * NS
    mixer_full = (
        lax.all_gather(norm_gain, ("seq", "ctx"), axis=0, tiled=True),
        lax.all_gather(gating_weight, ("seq", "ctx"), axis=0, tiled=True),
        lax.all_gather(inner_weight, ("seq", "ctx"), axis=0, tiled=True),
        lax.all_gather(state_weight, ("seq", "ctx"), axis=0, tiled=True),
        lax.all_gather(step_weight, ("seq", "ctx"), axis=0, tiled=True),
        lax.all_gather(conv_weight, ("seq", "ctx"), axis=1, tiled=True),
        lax.all_gather(conv_bias, ("seq", "ctx"), axis=0, tiled=True),
        lax.all_gather(mixer_gain, ("seq", "ctx"), axis=0, tiled=True),
        lax.all_gather(mixer_out, ("seq", "ctx"), axis=1, tiled=True),
        lax.all_gather(query_weight, ("seq", "ctx"), axis=0, tiled=True),
        lax.all_gather(key_weight, ("seq", "ctx"), axis=0, tiled=True),
        lax.all_gather(value_weight, ("seq", "ctx"), axis=0, tiled=True),
        lax.all_gather(output_weight, ("seq", "ctx"), axis=1, tiled=True),
    )
    (
        wide_norm,
        wide_gating,
        wide_inner,
        wide_state,
        wide_step,
        wide_conv,
        wide_bias,
        wide_gain,
        wide_mixer,
        wide_query,
        wide_key,
        wide_value,
        wide_output,
    ) = mixer_full
    inputs = tokens.astype(jnp.float32)
    normed = normalize(inputs)
    hidden = (normed * wide_norm.astype(jnp.float32)).astype(jnp.bfloat16)
    gating = plain_dot(hidden, wide_gating)
    pre_conv = jnp.concatenate([plain_dot(hidden, wide_inner), plain_dot(hidden, wide_state)], 1)
    step_pre = plain_dot(hidden, wide_step)
    edge_rows = from_behind(pre_conv[row_count - (KC - 1) :], "ctx", 1)
    padded = jnp.concatenate([edge_rows, pre_conv], 0)
    conv_taps = wide_conv.astype(jnp.float32)
    conv_sum = wide_bias.astype(jnp.float32)[None, :]
    for offset in range(KC):
        conv_sum = conv_sum + conv_taps[offset][None, :] * padded[offset : offset + row_count]
    mixed_in = silu_value(conv_sum)
    inner_heads = mixed_in[:, :DI].reshape(row_count, HM, PM)
    in_state = mixed_in[:, DI : DI + NS]
    out_state = mixed_in[:, DI + NS :]
    step_arg = step_pre + step_bias[None, :]
    step_size = softplus(step_arg)
    decay_rates = -jnp.exp(decay_log)
    cumulative = jnp.cumsum(step_size * decay_rates[None, :], axis=0)
    causal_mask = jnp.arange(row_count)[:, None] >= jnp.arange(row_count)[None, :]
    span_logs = cumulative.T[:, :, None] - cumulative.T[:, None, :]
    fading = jnp.where(
        causal_mask[None], jnp.exp(jnp.where(causal_mask[None], span_logs, 0.0)), 0.0
    )
    pairing = jnp.dot(out_state, in_state.T, precision=highest)
    mixing = fading * pairing[None] * step_size.T[:, None, :]
    within = jnp.einsum("hts,shp->thp", mixing, inner_heads, precision=highest)
    to_end = jnp.exp(cumulative[-1][None, :] - cumulative)
    feeding = to_end * step_size
    local_state = jnp.einsum("th,thp,tn->hpn", feeding, inner_heads, in_state, precision=highest)
    total_decay = jnp.exp(cumulative[-1])
    carried = entering(
        (total_decay, local_state),
        "ctx",
        chain_step,
        (jnp.ones_like(total_decay), jnp.zeros_like(local_state)),
        False,
    )[1]
    growth = jnp.exp(cumulative)
    readout = jnp.einsum("tn,hpn->thp", out_state, carried, precision=highest)
    ssm_heads = within + growth[:, :, None] * readout + skip_scale[None, :, None] * inner_heads
    ssm_flat = ssm_heads.reshape(row_count, DI)
    gate_act = silu_value(gating)
    gated_rows = ssm_flat * gate_act
    gated_norm = normalize(gated_rows)
    mixer_rows = (gated_norm * wide_gain.astype(jnp.float32)).astype(jnp.bfloat16)
    mamba_branch = plain_dot(mixer_rows, wide_mixer)
    query_rows = plain_dot(hidden, wide_query).astype(jnp.bfloat16)
    key_rows = plain_dot(hidden, wide_key).astype(jnp.bfloat16)
    value_rows = plain_dot(hidden, wide_value).astype(jnp.bfloat16)
    queries = query_rows.reshape(row_count, HK, groups, HD)
    start_state = (
        jnp.full((HK, groups, row_count), negative, jnp.float32),
        jnp.zeros((HK, groups, row_count), jnp.float32),
        jnp.zeros((HK, groups, row_count, HD), jnp.float32),
    )
    run_state = start_state
    key_part = lax.all_gather(key_rows, "ctx", axis=0, tiled=True)
    value_part = lax.all_gather(value_rows, "ctx", axis=0, tiled=True)
    key_count = key_part.shape[0]
    block_width = block_split()

    def one_block(carry_state, scan_item):
        return (
            attend_rows(
                carry_state, scan_item[0], scan_item[1], scan_item[2], queries, query_place
            ),
            None,
        )

    offsets = jnp.arange(key_count // block_width, dtype=jnp.int32) * block_width
    run_state, unused = lax.scan(
        one_block,
        run_state,
        (
            key_part.reshape(key_count // block_width, block_width, HK * HD),
            value_part.reshape(key_count // block_width, block_width, HK * HD),
            offsets,
        ),
    )
    run_max, run_total, run_acc = run_state
    attended = (run_acc / run_total[..., None]).transpose(2, 0, 1, 3)
    log_total = run_max + jnp.log(run_total)
    attn_rows = attended.reshape(row_count, HA * HD).astype(jnp.bfloat16)
    attn_branch = plain_dot(attn_rows, wide_output)
    residual = inputs + mamba_branch + attn_branch
    feed_full = (
        lax.all_gather(feed_gain, ("seq", "ctx"), axis=0, tiled=True),
        lax.all_gather(gate_matrix, ("seq", "ctx"), axis=0, tiled=True),
        lax.all_gather(lift_matrix, ("seq", "ctx"), axis=0, tiled=True),
        lax.all_gather(drop_matrix, ("seq", "ctx"), axis=1, tiled=True),
    )
    wide_feed, wide_gate, wide_lift, wide_drop = feed_full
    second = normalize(residual)
    feed_rows = (second * wide_feed.astype(jnp.float32)).astype(jnp.bfloat16)
    gate_pre = plain_dot(feed_rows, wide_gate)
    lift_pre = plain_dot(feed_rows, wide_lift)
    swish_gate = silu_value(gate_pre)
    active = (swish_gate * lift_pre).astype(jnp.bfloat16)
    layer_output = (residual + plain_dot(active, wide_drop)).astype(jnp.bfloat16)
    back_feed, back_gate, back_lift, back_drop = (
        lax.all_gather(feed_gain, ("seq", "ctx"), axis=0, tiled=True),
        lax.all_gather(gate_matrix, ("seq", "ctx"), axis=0, tiled=True),
        lax.all_gather(lift_matrix, ("seq", "ctx"), axis=0, tiled=True),
        lax.all_gather(drop_matrix, ("seq", "ctx"), axis=1, tiled=True),
    )
    drop_grad = lead_dot(active, cotangent)
    active_grad = tail_dot(cotangent, back_drop)
    gate_rows_grad = (active_grad * lift_pre * silu_slope(gate_pre)).astype(jnp.bfloat16)
    lift_rows_grad = (active_grad * swish_gate).astype(jnp.bfloat16)
    gate_grad = lead_dot(feed_rows, gate_rows_grad)
    lift_grad = lead_dot(feed_rows, lift_rows_grad)
    second_grad = tail_dot(gate_rows_grad, back_gate) + tail_dot(lift_rows_grad, back_lift)
    feed_gain_grad = jnp.sum(second_grad * second, axis=0)
    residual_grad = cotangent.astype(jnp.float32) + norm_back(
        residual, second_grad * back_feed.astype(jnp.float32)
    )
    feed_gain_out, gate_out, lift_out, drop_out = (
        lax.psum_scatter(feed_gain_grad, ("seq", "ctx"), scatter_dimension=0, tiled=True),
        lax.psum_scatter(gate_grad, ("seq", "ctx"), scatter_dimension=0, tiled=True),
        lax.psum_scatter(lift_grad, ("seq", "ctx"), scatter_dimension=0, tiled=True),
        lax.psum_scatter(drop_grad, ("seq", "ctx"), scatter_dimension=1, tiled=True),
    )
    mixer_back = (
        lax.all_gather(norm_gain, ("seq", "ctx"), axis=0, tiled=True),
        lax.all_gather(gating_weight, ("seq", "ctx"), axis=0, tiled=True),
        lax.all_gather(inner_weight, ("seq", "ctx"), axis=0, tiled=True),
        lax.all_gather(state_weight, ("seq", "ctx"), axis=0, tiled=True),
        lax.all_gather(step_weight, ("seq", "ctx"), axis=0, tiled=True),
        lax.all_gather(conv_weight, ("seq", "ctx"), axis=1, tiled=True),
        lax.all_gather(conv_bias, ("seq", "ctx"), axis=0, tiled=True),
        lax.all_gather(mixer_gain, ("seq", "ctx"), axis=0, tiled=True),
        lax.all_gather(mixer_out, ("seq", "ctx"), axis=1, tiled=True),
        lax.all_gather(query_weight, ("seq", "ctx"), axis=0, tiled=True),
        lax.all_gather(key_weight, ("seq", "ctx"), axis=0, tiled=True),
        lax.all_gather(value_weight, ("seq", "ctx"), axis=0, tiled=True),
        lax.all_gather(output_weight, ("seq", "ctx"), axis=1, tiled=True),
    )
    (
        back_norm,
        back_gating,
        back_inner,
        back_state,
        back_step,
        back_conv,
        back_bias,
        back_gain,
        back_mixer,
        back_query,
        back_key,
        back_value,
        back_output,
    ) = mixer_back
    branch_grad = residual_grad.astype(jnp.bfloat16)
    output_grad = lead_dot(attn_rows, branch_grad)
    mixer_out_grad = lead_dot(mixer_rows, branch_grad)
    attn_grad = tail_dot(branch_grad, back_output).astype(jnp.bfloat16)
    mixer_rows_grad = tail_dot(branch_grad, back_mixer)
    grad_heads = attn_grad.reshape(row_count, HK, groups, HD)
    grad_float = grad_heads.astype(jnp.float32)
    delta_rows = jnp.sum(grad_float * attended, axis=-1).transpose(1, 2, 0)
    all_keys, all_values = (
        lax.all_gather(key_rows, "ctx", axis=0, tiled=True),
        lax.all_gather(value_rows, "ctx", axis=0, tiled=True),
    )
    block_width = block_split()
    blocks = length // block_width

    def attend_block(query_sum, scan_item):
        return back_rows(
            query_sum,
            scan_item[0],
            scan_item[1],
            scan_item[2],
            queries,
            grad_heads,
            grad_float,
            log_total,
            delta_rows,
            query_place,
        )

    query_sum, key_value_terms = lax.scan(
        attend_block,
        jnp.zeros((row_count, HK, groups, HD), jnp.float32),
        (
            all_keys.reshape(blocks, block_width, HK * HD),
            all_values.reshape(blocks, block_width, HK * HD),
            jnp.arange(blocks, dtype=jnp.int32) * block_width,
        ),
    )
    key_value_sum = lax.psum_scatter(
        key_value_terms.reshape(length, 2 * HK * HD), "ctx", scatter_dimension=0, tiled=True
    )
    query_grad_rows = query_sum.reshape(row_count, HA * HD).astype(jnp.bfloat16)
    key_grad_rows = key_value_sum[:, : HK * HD].astype(jnp.bfloat16)
    value_grad_rows = key_value_sum[:, HK * HD :].astype(jnp.bfloat16)
    query_grad = lead_dot(hidden, query_grad_rows)
    key_grad = lead_dot(hidden, key_grad_rows)
    value_grad = lead_dot(hidden, value_grad_rows)
    hidden_grad = (
        tail_dot(query_grad_rows, back_query)
        + tail_dot(key_grad_rows, back_key)
        + tail_dot(value_grad_rows, back_value)
    )
    mixer_gain_grad = jnp.sum(mixer_rows_grad * gated_norm, axis=0)
    gated_grad = norm_back(gated_rows, mixer_rows_grad * back_gain.astype(jnp.float32))
    ssm_grad = (gated_grad * gate_act).reshape(row_count, HM, PM)
    gating_rows_grad = (gated_grad * ssm_flat * silu_slope(gating)).astype(jnp.bfloat16)
    skip_grad = jnp.sum(ssm_grad * inner_heads, axis=(0, 2))
    mixing_grad = jnp.where(
        causal_mask[None], jnp.einsum("thp,shp->hts", ssm_grad, inner_heads, precision=highest), 0.0
    )
    inner_grad = (
        jnp.einsum("hts,thp->shp", mixing, ssm_grad, precision=highest)
        + skip_scale[None, :, None] * ssm_grad
    )
    pairing_grad = jnp.sum(mixing_grad * fading * step_size.T[:, None, :], axis=0)
    step_grad = jnp.sum(mixing_grad * fading * pairing[None], axis=1).T
    fading_flow = mixing_grad * pairing[None] * step_size.T[:, None, :] * fading
    cumulative_grad = jnp.sum(fading_flow, axis=2).T - jnp.sum(fading_flow, axis=1).T
    out_state_grad = jnp.dot(pairing_grad, in_state, precision=highest)
    in_state_grad = jnp.dot(pairing_grad.T, out_state, precision=highest)
    cumulative_grad = cumulative_grad + jnp.sum(ssm_grad * readout, axis=2) * growth
    readout_grad = ssm_grad * growth[:, :, None]
    out_state_grad = out_state_grad + jnp.einsum(
        "thp,hpn->tn", readout_grad, carried, precision=highest
    )
    carried_grad = jnp.einsum("thp,tn->hpn", readout_grad, out_state, precision=highest)
    later_grad = entering(
        (total_decay, carried_grad),
        "ctx",
        chain_step,
        (jnp.ones_like(total_decay), jnp.zeros_like(carried_grad)),
        True,
    )[1]
    decay_grad = jnp.sum(later_grad * carried, axis=(1, 2))
    spread = jnp.einsum("hpn,sn->shp", later_grad, in_state, precision=highest)
    feeding_grad = jnp.sum(spread * inner_heads, axis=2)
    inner_grad = inner_grad + feeding[:, :, None] * spread
    in_state_grad = in_state_grad + jnp.einsum(
        "sh,shp,hpn->sn", feeding, inner_heads, later_grad, precision=highest
    )
    step_grad = step_grad + feeding_grad * to_end
    last_grad = jnp.sum(feeding_grad * feeding, axis=0) + decay_grad * total_decay
    cumulative_grad = cumulative_grad - feeding_grad * feeding
    cumulative_grad = cumulative_grad + jnp.where(
        jnp.arange(row_count)[:, None] == row_count - 1, last_grad[None, :], 0.0
    )
    rate_step_grad = jnp.cumsum(cumulative_grad[::-1], axis=0)[::-1]
    step_grad = step_grad + rate_step_grad * decay_rates[None, :]
    decay_log_grad = jnp.sum(rate_step_grad * step_size, axis=0) * decay_rates
    arg_grad = step_grad * jax.nn.sigmoid(step_arg)
    step_bias_grad = jnp.sum(arg_grad, axis=0)
    step_rows_grad = arg_grad.astype(jnp.bfloat16)
    mixed_grad = jnp.concatenate(
        [inner_grad.reshape(row_count, DI), in_state_grad, out_state_grad], 1
    )
    conv_grad_rows = mixed_grad * silu_slope(conv_sum)
    conv_bias_grad = jnp.sum(conv_grad_rows, axis=0)
    conv_weight_grad = jnp.stack(
        [
            jnp.sum(conv_grad_rows * padded[offset : offset + row_count], axis=0)
            for offset in range(KC)
        ],
        0,
    )
    back_taps = back_conv.astype(jnp.float32)
    padded_grad = jnp.zeros((row_count + KC - 1, conv_width), jnp.float32)
    for offset in range(KC):
        padded_grad = padded_grad + jnp.pad(
            back_taps[offset][None, :] * conv_grad_rows, ((offset, KC - 1 - offset), (0, 0))
        )
    returned = from_behind(shortened(padded_grad[: KC - 1]), "ctx", -1)
    pre_grad = padded_grad[KC - 1 :] + jnp.pad(returned, ((row_count - (KC - 1), 0), (0, 0)))
    pre_grad_rows = pre_grad.astype(jnp.bfloat16)
    inner_rows_grad = pre_grad_rows[:, :DI]
    state_rows_grad = pre_grad_rows[:, DI:]
    gating_grad = lead_dot(hidden, gating_rows_grad)
    inner_weight_grad = lead_dot(hidden, inner_rows_grad)
    state_weight_grad = lead_dot(hidden, state_rows_grad)
    step_weight_grad = lead_dot(hidden, step_rows_grad)
    hidden_grad = (
        hidden_grad
        + tail_dot(gating_rows_grad, back_gating)
        + tail_dot(inner_rows_grad, back_inner)
        + tail_dot(state_rows_grad, back_state)
        + tail_dot(step_rows_grad, back_step)
    )
    norm_gain_grad = jnp.sum(hidden_grad * normed, axis=0)
    tokens_grad = residual_grad + norm_back(inputs, hidden_grad * back_norm.astype(jnp.float32))
    (
        norm_out,
        gating_out,
        inner_out,
        state_out,
        step_out,
        conv_weight_out,
        conv_bias_out,
        mixer_gain_out,
        mixer_out_out,
        query_out,
        key_out,
        value_out,
        output_out,
    ) = (
        lax.psum_scatter(norm_gain_grad, ("seq", "ctx"), scatter_dimension=0, tiled=True),
        lax.psum_scatter(gating_grad, ("seq", "ctx"), scatter_dimension=0, tiled=True),
        lax.psum_scatter(inner_weight_grad, ("seq", "ctx"), scatter_dimension=0, tiled=True),
        lax.psum_scatter(state_weight_grad, ("seq", "ctx"), scatter_dimension=0, tiled=True),
        lax.psum_scatter(step_weight_grad, ("seq", "ctx"), scatter_dimension=0, tiled=True),
        lax.psum_scatter(conv_weight_grad, ("seq", "ctx"), scatter_dimension=1, tiled=True),
        lax.psum_scatter(conv_bias_grad, ("seq", "ctx"), scatter_dimension=0, tiled=True),
        lax.psum_scatter(mixer_gain_grad, ("seq", "ctx"), scatter_dimension=0, tiled=True),
        lax.psum_scatter(mixer_out_grad, ("seq", "ctx"), scatter_dimension=1, tiled=True),
        lax.psum_scatter(query_grad, ("seq", "ctx"), scatter_dimension=0, tiled=True),
        lax.psum_scatter(key_grad, ("seq", "ctx"), scatter_dimension=0, tiled=True),
        lax.psum_scatter(value_grad, ("seq", "ctx"), scatter_dimension=0, tiled=True),
        lax.psum_scatter(output_grad, ("seq", "ctx"), scatter_dimension=1, tiled=True),
    )
    bias_total, decay_total_grad, skip_total = lax.psum(
        (step_bias_grad, decay_log_grad, skip_grad), ("seq", "ctx")
    )
    return (
        layer_output,
        tokens_grad,
        norm_out,
        gating_out,
        inner_out,
        state_out,
        step_out,
        conv_weight_out,
        conv_bias_out,
        mixer_gain_out,
        mixer_out_out,
        query_out,
        key_out,
        value_out,
        output_out,
        feed_gain_out,
        gate_out,
        lift_out,
        drop_out,
        bias_total,
        decay_total_grad,
        skip_total,
    )


def solution(mesh):
    in_specs = (
        P(("seq", "ctx"), None),
        P(("seq", "ctx"), None),
        P(("seq", "ctx")),
        P(("seq", "ctx"), None),
        P(("seq", "ctx"), None),
        P(("seq", "ctx"), None),
        P(("seq", "ctx"), None),
        P(None, ("seq", "ctx")),
        P(("seq", "ctx")),
        P(("seq", "ctx")),
        P(None, ("seq", "ctx")),
        P(("seq", "ctx"), None),
        P(("seq", "ctx"), None),
        P(("seq", "ctx"), None),
        P(None, ("seq", "ctx")),
        P(("seq", "ctx")),
        P(("seq", "ctx"), None),
        P(("seq", "ctx"), None),
        P(None, ("seq", "ctx")),
        P(),
        P(),
        P(),
    )
    out_specs = (
        P(("seq", "ctx"), None),
        P(("seq", "ctx"), None),
        P(("seq", "ctx")),
        P(("seq", "ctx"), None),
        P(("seq", "ctx"), None),
        P(("seq", "ctx"), None),
        P(("seq", "ctx"), None),
        P(None, ("seq", "ctx")),
        P(("seq", "ctx")),
        P(("seq", "ctx")),
        P(None, ("seq", "ctx")),
        P(("seq", "ctx"), None),
        P(("seq", "ctx"), None),
        P(("seq", "ctx"), None),
        P(None, ("seq", "ctx")),
        P(("seq", "ctx")),
        P(("seq", "ctx"), None),
        P(("seq", "ctx"), None),
        P(None, ("seq", "ctx")),
        P(),
        P(),
        P(),
    )
    return jax.shard_map(local, mesh=mesh, in_specs=in_specs, out_specs=out_specs, check_vma=False)
```

profile of v0, /device:TPU:0, one launch (start us, length us, event | category | flops | bytes accessed | tf_op | source)
XLA Modules:
  0.0 4347.7 jit_solution(956829497874343571)
XLA Ops:
  14.1 42.3 all-reduce.14
  56.4 40.8 all-gather.2
  97.3 40.5 all-gather.3
  142.1 27.7 all-gather.19.cloned.1.call-done
  209.7 15.5 all-gather.27.cloned.1.call-done
  226.7 15.3 all_gather.106
  242.2 38.6 all-gather.31.cloned.1.call-done
  282.4 15.5 all_gather.109
  298.1 46.6 %all-gather.29.cloned.1.call-done = bf16[2048,1024]{1,0:T(8,128)(2,1)} async-done(((bf16[64,1024]{1,0:T(8,128)(2,1)}), bf16[2048,1024]{1,0:T(8,128)(2,1)}) %all-gather.29.cloned.1.call-update) | async-done | bytes 4194320 | tf_op jit(solution)/shard_map/all_gather | solution.py:192
  365.6 199.1 %all-gather.41.cloned.1.call-done = f32[384,64,256]{2,1,0:T(8,128)} async-done(((f32[48,64,256]{2,1,0:T(8,128)}), f32[384,64,256]{2,1,0:T(8,128)}) %all-gather.41.cloned.1.call-update) | async-done | bytes 25165840 | tf_op jit(solution)/shard_map/all_gather | solution.py:31
  579.9 82.2 %all-gather.23.cloned.1.call-done = bf16[2048,3072]{1,0:T(8,128)(2,1)} async-done(((bf16[64,3072]{1,0:T(8,128)(2,1)}), bf16[2048,3072]{1,0:T(8,128)(2,1)}) %all-gather.23.cloned.1.call-update) | async-done | bytes 12582928 | tf_op jit(solution)/shard_map/all_gather | solution.py:184
  671.0 88.3 %all-gather.25.cloned.1.call-done = bf16[3072,2048]{0,1:T(8,128)(2,1)} async-done(((bf16[3072,64]{0,1:T(8,128)(2,1)}), bf16[3072,2048]{0,1:T(8,128)(2,1)}) %all-gather.25.cloned.1.call-update) | async-done | bytes 12582928 | tf_op jit(solution)/shard_map/all_gather | solution.py:191
  769.9 52.9 %all-gather.33.cloned.1.call-done = bf16[1024,2048]{0,1:T(8,128)(2,1)} async-done(((bf16[1024,64]{0,1:T(8,128)(2,1)}), bf16[1024,2048]{0,1:T(8,128)(2,1)}) %all-gather.33.cloned.1.call-update) | async-done | bytes 4194320 | tf_op jit(solution)/shard_map/all_gather | solution.py:195
  828.8 110.3 %all-gather.35.cloned.1.call-done = bf16[2048,4096]{1,0:T(8,128)(2,1)} async-done(((bf16[64,4096]{1,0:T(8,128)(2,1)}), bf16[2048,4096]{1,0:T(8,128)(2,1)}) %all-gather.35.cloned.1.call-update) | async-done | bytes 16777232 | tf_op jit(solution)/shard_map/all_gather | solution.py:301
  948.7 106.5 %all-gather.37.cloned.1.call-done = bf16[2048,4096]{1,0:T(8,128)(2,1)} async-done(((bf16[64,4096]{1,0:T(8,128)(2,1)}), bf16[2048,4096]{1,0:T(8,128)(2,1)}) %all-gather.37.cloned.1.call-update) | async-done | bytes 16777232 | tf_op jit(solution)/shard_map/all_gather | solution.py:302
  1064.9 106.4 %all-gather.39.cloned.1.call-done = bf16[4096,2048]{0,1:T(8,128)(2,1)} async-done(((bf16[4096,64]{0,1:T(8,128)(2,1)}), bf16[4096,2048]{0,1:T(8,128)(2,1)}) %all-gather.39.cloned.1.call-update) | async-done | bytes 16777232 | tf_op jit(solution)/shard_map/all_gather | solution.py:303
  1259.0 32.6 while.57
  1291.7 159.2 %all-gather.43.cloned.1.call-done = f32[384,64,256]{2,1,0:T(8,128)} async-done(((f32[48,64,256]{2,1,0:T(8,128)}), f32[384,64,256]{2,1,0:T(8,128)}) %all-gather.43.cloned.1.call-update) | async-done | bytes 25165840 | tf_op jit(solution)/shard_map/all_gather | solution.py:31
  1452.9 34.7 while.55
  1663.4 39.2 all-reduce.13
  1709.2 77.0 %reduce-scatter.43.cloned.1.call-done = f32[64,48]{1,0:T(8,128)} async-done(((f32[2048,48]{1,0:T(8,128)}), f32[64,48]{1,0:T(8,128)}) %reduce-scatter.43.cloned.1.call-update) | async-done | bytes 12304
  1787.7 134.0 %reduce-scatter.31.cloned.1.call-done = f32[64,256]{1,0:T(8,128)} async-done(((f32[2048,256]{1,0:T(8,128)}), f32[64,256]{1,0:T(8,128)}) %reduce-scatter.31.cloned.1.call-update) | async-done | bytes 65552 | tf_op jit(solution)/shard_map/reduce_scatter | solution.py:529
  1921.7 136.1 %reduce-scatter.33.cloned.1.call-done = f32[64,256]{1,0:T(8,128)} async-done(((f32[2048,256]{1,0:T(8,128)}), f32[64,256]{1,0:T(8,128)}) %reduce-scatter.33.cloned.1.call-update) | async-done | bytes 65552 | tf_op jit(solution)/shard_map/reduce_scatter | solution.py:530
  2057.7 150.9 %reduce-scatter.29.cloned.1.call-done = f32[64,1024]{1,0:T(8,128)} async-done(((f32[2048,1024]{1,0:T(8,128)}), f32[64,1024]{1,0:T(8,128)}) %reduce-scatter.29.cloned.1.call-update) | async-done | bytes 262160 | tf_op jit(solution)/shard_map/reduce_scatter | solution.py:528
  2208.6 152.0 %reduce-scatter.35.cloned.1.call-done = f32[1024,64]{0,1:T(8,128)} async-done(((f32[1024,2048]{0,1:T(8,128)}), f32[1024,64]{0,1:T(8,128)}) %reduce-scatter.35.cloned.1.call-update) | async-done | bytes 262160 | tf_op jit(solution)/shard_map/reduce_scatter | solution.py:531
  2360.6 250.8 %reduce-scatter.27.cloned.1.call-done = f32[3072,64]{0,1:T(8,128)} async-done(((f32[3072,2048]{0,1:T(8,128)}), f32[3072,64]{0,1:T(8,128)}) %reduce-scatter.27.cloned.1.call-update) | async-done | bytes 786448 | tf_op jit(solution)/shard_map/reduce_scatter | solution.py:527
  2611.4 253.2 %reduce-scatter.21.cloned.1.call-done = f32[64,3072]{1,0:T(8,128)} async-done(((f32[2048,3072]{1,0:T(8,128)}), f32[64,3072]{1,0:T(8,128)}) %reduce-scatter.21.cloned.1.call-update) | async-done | bytes 786448 | tf_op jit(solution)/shard_map/reduce_scatter | solution.py:520
  2864.6 145.0 %reduce-scatter.25.cloned.1.call-done = f32[64,512]{1,0:T(8,128)} async-done(((f32[2048,512]{1,0:T(8,128)}), f32[64,512]{1,0:T(8,128)}) %reduce-scatter.25.cloned.1.call-update) | async-done | bytes 131088 | tf_op jit(solution)/shard_map/reduce_scatter | solution.py:522
  3009.6 361.2 %reduce-scatter.37.cloned.1.call-done = f32[64,4096]{1,0:T(8,128)} async-done(((f32[2048,4096]{1,0:T(8,128)}), f32[64,4096]{1,0:T(8,128)}) %reduce-scatter.37.cloned.1.call-update) | async-done | bytes 1048592 | tf_op jit(solution)/shard_map/reduce_scatter | solution.py:332
  3370.9 360.5 %reduce-scatter.39.cloned.1.call-done = f32[64,4096]{1,0:T(8,128)} async-done(((f32[2048,4096]{1,0:T(8,128)}), f32[64,4096]{1,0:T(8,128)}) %reduce-scatter.39.cloned.1.call-update) | async-done | bytes 1048592 | tf_op jit(solution)/shard_map/reduce_scatter | solution.py:333
  3731.4 360.4 %reduce-scatter.41.cloned.1.call-done = f32[4096,64]{0,1:T(8,128)} async-done(((f32[4096,2048]{0,1:T(8,128)}), f32[4096,64]{0,1:T(8,128)}) %reduce-scatter.41.cloned.1.call-update) | async-done | bytes 1048592 | tf_op jit(solution)/shard_map/reduce_scatter | solution.py:334
  4091.7 248.9 %reduce-scatter.23.cloned.1.call-done = f32[64,3072]{1,0:T(8,128)} async-done(((f32[2048,3072]{1,0:T(8,128)}), f32[64,3072]{1,0:T(8,128)}) %reduce-scatter.23.cloned.1.call-update) | async-done | bytes 786448 | tf_op jit(solution)/shard_map/reduce_scatter | solution.py:521
  (505 shorter events, 488.1 us)
Async XLA Ops:
  7.2 132.8 %all-gather.21.cloned.1.call-start = ((), (), s32[]{:S(2)}) async-start(), calls=%async_computation.15 | async-start | bytes 2162688 | tf_op jit(solution)/shard_map/all_gather | solution.py:186
  8.0 161.9 %all-gather.19.cloned.1.call-start = ((), (), s32[]{:S(2)}) async-start(), calls=%async_computation.14 | async-start | bytes 12976128 | tf_op jit(solution)/shard_map/all_gather | solution.py:185
  8.7 216.4 %all-gather.27.cloned.1.call-start = ((), (), s32[]{:S(2)}) async-start(), calls=%async_computation.18 | async-start | bytes 1081344 | tf_op jit(solution)/shard_map/all_gather | solution.py:193
  9.4 271.4 %all-gather.31.cloned.1.call-start = ((), (), s32[]{:S(2)}) async-start(), calls=%async_computation.20 | async-start | bytes 1081344 | tf_op jit(solution)/shard_map/all_gather | solution.py:194
  10.0 334.8 %all-gather.29.cloned.1.call-start = ((), (), s32[]{:S(2)}) async-start(), calls=%async_computation.19 | async-start | bytes 4325376 | tf_op jit(solution)/shard_map/all_gather | solution.py:192
  10.6 554.1 %all-gather.41.cloned.1.call-start = ((), (), s32[]{:S(2)}) async-start(), calls=%async_computation.37 | async-start | bytes 28311552 | tf_op jit(solution)/shard_map/all_gather | solution.py:31
  176.4 3.0 collective-permute-start
  191.8 470.2 %all-gather.23.cloned.1.call-start = ((), (), s32[]{:S(2)}) async-start(), calls=%async_computation.16 | async-start | bytes 12976128 | tf_op jit(solution)/shard_map/all_gather | solution.py:184
  192.6 566.8 %all-gather.25.cloned.1.call-start = ((), (), s32[]{:S(2)}) async-start(), calls=%async_computation.17 | async-start | bytes 12976128 | tf_op jit(solution)/shard_map/all_gather | solution.py:191
  193.3 629.5 %all-gather.33.cloned.1.call-start = ((), (), s32[]{:S(2)}) async-start(), calls=%async_computation.21 | async-start | bytes 4325376 | tf_op jit(solution)/shard_map/all_gather | solution.py:195
  194.1 745.1 %all-gather.35.cloned.1.call-start = ((), (), s32[]{:S(2)}) async-start(), calls=%async_computation.22 | async-start | bytes 17301504 | tf_op jit(solution)/shard_map/all_gather | solution.py:301
  194.6 860.6 %all-gather.37.cloned.1.call-start = ((), (), s32[]{:S(2)}) async-start(), calls=%async_computation.23 | async-start | bytes 17301504 | tf_op jit(solution)/shard_map/all_gather | solution.py:302
  195.4 975.9 %all-gather.39.cloned.1.call-start = ((), (), s32[]{:S(2)}) async-start(), calls=%async_computation.24 | async-start | bytes 17301504 | tf_op jit(solution)/shard_map/all_gather | solution.py:303
  195.9 1254.9 %all-gather.43.cloned.1.call-start = ((), (), s32[]{:S(2)}) async-start(), calls=%async_computation.38 | async-start | bytes 28311552 | tf_op jit(solution)/shard_map/all_gather | solution.py:31
  196.7 1013.9 %copy-start.61 = (f32[2048]{0:T(1024)}, f32[2048]{0:T(1024)S(1)}, u32[]{:S(2)}) copy-start(f32[2048]{0:T(1024)S(1)} %convert_element_type.117) | copy-start | bytes 24580
  364.2 458.6 %copy-start.41 = (bf16[128,2,4,128]{0,3,2,1:T(8,128)(2,1)}, bf16[128,2,4,128]{0,3,2,1:T(8,128)(2,1)S(1)}, u32[]{:S(2)}) copy-start(bf16[128,2,4,128]{0,3,2,1:T(8,128)(2,1)S(1)} %bitcast_convert_fusion) | copy-start | bytes 786436
  365.6 883.4 %copy-start.77 = (f32[128,128]{1,0:T(8,128)}, f32[128,128]{1,0:T(8,128)S(1)}, u32[]{:S(2)}) copy-start(f32[128,128]{1,0:T(8,128)S(1)} %fusion.100) | copy-start | bytes 196612
  1232.7 287.9 %reduce-scatter.19.cloned.1.call-start = ((), (), s32[]{:S(2)}) async-start(), calls=%async_computation.25 | async-start | bytes 2359296 | tf_op jit(solution)/shard_map/reduce_scatter | solution.py:404
  1291.7 416.1 %reduce-scatter.45.cloned.1.call-start = ((), (), s32[]{:S(2)}) async-start(), calls=%async_computation.40 | async-start | bytes 1892352
  1517.9 268.4 %reduce-scatter.43.cloned.1.call-start = ((), (), s32[]{:S(2)}) async-start(), calls=%async_computation.39 | async-start | bytes 1081344
  1520.5 401.2 %reduce-scatter.31.cloned.1.call-start = ((), (), s32[]{:S(2)}) async-start(), calls=%async_computation.31 | async-start | bytes 2162688 | tf_op jit(solution)/shard_map/reduce_scatter | solution.py:529
  1523.5 534.2 %reduce-scatter.33.cloned.1.call-start = ((), (), s32[]{:S(2)}) async-start(), calls=%async_computation.32 | async-start | bytes 2162688 | tf_op jit(solution)/shard_map/reduce_scatter | solution.py:530
  1525.4 683.2 %reduce-scatter.29.cloned.1.call-start = ((), (), s32[]{:S(2)}) async-start(), calls=%async_computation.30 | async-start | bytes 8650752 | tf_op jit(solution)/shard_map/reduce_scatter | solution.py:528
  1530.3 830.3 %reduce-scatter.35.cloned.1.call-start = ((), (), s32[]{:S(2)}) async-start(), calls=%async_computation.33 | async-start | bytes 8650752 | tf_op jit(solution)/shard_map/reduce_scatter | solution.py:531
  1536.1 1075.4 %reduce-scatter.27.cloned.1.call-start = ((), (), s32[]{:S(2)}) async-start(), calls=%async_computation.29 | async-start | bytes 25952256 | tf_op jit(solution)/shard_map/reduce_scatter | solution.py:527
  1547.7 1316.9 %reduce-scatter.21.cloned.1.call-start = ((), (), s32[]{:S(2)}) async-start(), calls=%async_computation.26 | async-start | bytes 25952256 | tf_op jit(solution)/shard_map/reduce_scatter | solution.py:520
  1559.1 1450.5 %reduce-scatter.25.cloned.1.call-start = ((), (), s32[]{:S(2)}) async-start(), calls=%async_computation.28 | async-start | bytes 4325376 | tf_op jit(solution)/shard_map/reduce_scatter | solution.py:522
  1562.2 3.1 collective-permute-start.1
  1568.4 1802.5 %reduce-scatter.37.cloned.1.call-start = ((), (), s32[]{:S(2)}) async-start(), calls=%async_computation.34 | async-start | bytes 34603008 | tf_op jit(solution)/shard_map/reduce_scatter | solution.py:332
  1583.8 2147.5 %reduce-scatter.39.cloned.1.call-start = ((), (), s32[]{:S(2)}) async-start(), calls=%async_computation.35 | async-start | bytes 34603008 | tf_op jit(solution)/shard_map/reduce_scatter | solution.py:333
  1598.3 2493.4 %reduce-scatter.41.cloned.1.call-start = ((), (), s32[]{:S(2)}) async-start(), calls=%async_computation.36 | async-start | bytes 34603008 | tf_op jit(solution)/shard_map/reduce_scatter | solution.py:334
  1613.8 2726.7 %reduce-scatter.23.cloned.1.call-start = ((), (), s32[]{:S(2)}) async-start(), calls=%async_computation.27 | async-start | bytes 25952256 | tf_op jit(solution)/shard_map/reduce_scatter | solution.py:521
  (113 other events, 2330.8 us)
Sparse Core Ops, SparseCore 0:
  11.0 59.1 all-gather.20
  73.3 96.5 all-gather.18
  172.8 52.2 all-gather.26
  228.0 52.7 all-gather.30
  283.7 61.0 all-gather.28
  346.3 218.4 all-gather.40
  567.7 94.2 all-gather.22
  665.0 94.3 all-gather.24
  762.4 60.3 all-gather.32
  825.6 113.4 all-gather.34
  942.1 113.0 all-gather.36
  1058.1 113.0 all-gather.38
  1232.8 218.0 all-gather.42
  1453.0 34.0 reduce-scatter.18
  1518.0 134.3 reduce-scatter.44
  1654.6 131.5 reduce-scatter.42
  1788.9 132.7 reduce-scatter.30
  1924.5 133.2 reduce-scatter.32
  2060.6 147.9 reduce-scatter.28
  2211.3 149.2 reduce-scatter.34
  2367.6 243.7 reduce-scatter.26
  2619.5 245.0 reduce-scatter.20
  2867.5 142.0 reduce-scatter.24
  3012.3 358.4 reduce-scatter.36
  3373.7 357.5 reduce-scatter.38
  3734.1 357.5 reduce-scatter.40
  4098.6 241.9 reduce-scatter.22
where the time goes:
time: 4360 us; the launch traced here: 4350 us
  waiting for transfers between devices  3670 us (84%)
  matrix products  311 us (7%)
  blocking collectives  206 us (5%)
  other arithmetic  70.4 us (2%)
  local copies, waits for them, and re-layouts  65.8 us (2%)
    reduce_scatter x1, waiting for transfers between devices, local(): lax.psum_scatter(gate_grad, ('seq', 'ctx'), scatter_dimension=0, tiled=True)  361 us
    reduce_scatter x1, waiting for transfers between devices, local(): lax.psum_scatter(lift_grad, ('seq', 'ctx'), scatter_dimension=0, tiled=True)  360 us
    reduce_scatter x1, waiting for transfers between devices, local(): lax.psum_scatter(drop_grad, ('seq', 'ctx'), scatter_dimension=1, tiled=True)  360 us
    all_gather x2, waiting for transfers between devices, entering(): gathered = jax.tree.map(lambda a: lax.all_gather(a, axis), part)  358 us
    reduce_scatter x1, waiting for transfers between devices, local(): lax.psum_scatter(gating_grad, ('seq', 'ctx'), scatter_dimension=0, tiled=...  253 us
    reduce_scatter x1, waiting for transfers between devices, local(): lax.psum_scatter(mixer_out_grad, ('seq', 'ctx'), scatter_dimension=1, til...  251 us
    reduce_scatter x1, waiting for transfers between devices, local(): lax.psum_scatter(inner_weight_grad, ('seq', 'ctx'), scatter_dimension=0,...  249 us
    reduce_scatter x1, waiting for transfers between devices, local(): lax.psum_scatter(output_grad, ('seq', 'ctx'), scatter_dimension=1, tiled=...  152 us
  transfers between devices with their start and end apart: 29, of which 26 were waited for; matrix products, arithmetic and copies ran while one was open for 9% of the time, Pallas kernels for 0%

commit v1 on v0

v1 whole, which is shorter than its diff:
```python
import jax
import jax.numpy as jnp
from jax import lax
from jax.sharding import Mesh
from jax.sharding import PartitionSpec as P

DI = 3072
HM = 48
PM = 64
NS = 256
KC = 4
HA = 8
HK = 2
HD = 128
FF = 4096
BLOCK = 128

epsilon = 1e-06
negative = -1e30
BF = jnp.bfloat16
F32 = jnp.float32

TEAM = ("sl", "zl", "core")
PEERS = ("sh", "ch")
WORLD = ("sh", "sl", "ch", "zl", "core")
RANKS = 8


def swap(value, axis):
    return lax.ppermute(value, axis, [(0, 1), (1, 0)])


def paired(mine, theirs, axis_name, dim):
    bit = lax.axis_index(axis_name)
    return jnp.where(bit == 0, jnp.stack([mine, theirs], dim), jnp.stack([theirs, mine], dim))


def kept(value, axis_name, dim):
    return lax.dynamic_index_in_dim(value, lax.axis_index(axis_name), dim, False)


def given(value, axis_name, dim):
    return lax.dynamic_index_in_dim(value, 1 - lax.axis_index(axis_name), dim, False)


def added(mine, theirs):
    return mine.astype(F32) + theirs.astype(F32)


def team_gather(rows):
    count, width = rows.shape
    half = count // 2
    first, second = rows[:half], rows[half:]
    first_x = swap(first, "sl")
    second_z = swap(second, "zl")
    first = paired(first, first_x, "sl", 0)
    second = paired(second, second_z, "zl", 0)
    first_z = swap(first, "zl")
    second_x = swap(second, "sl")
    first = paired(first, first_z, "zl", 1)
    second = paired(second, second_x, "sl", 0)
    both = jnp.concatenate([first, second], 2)
    return paired(both, swap(both, "core"), "core", 2).reshape(RANKS * count, width)


def team_scatter(rows):
    total, width = rows.shape
    count = total // RANKS
    half = count // 2
    rows = rows.reshape(2, 2, 2, count, width)
    rows = added(kept(rows, "core", 2), swap(given(rows, "core", 2).astype(BF), "core"))
    first, second = rows[:, :, :half], rows[:, :, half:]
    first_z = swap(given(first, "zl", 1).astype(BF), "zl")
    second_x = swap(given(second, "sl", 0).astype(BF), "sl")
    first = added(kept(first, "zl", 1), first_z)
    second = added(kept(second, "sl", 0), second_x)
    first_x = swap(given(first, "sl", 0).astype(BF), "sl")
    second_z = swap(given(second, "zl", 0).astype(BF), "zl")
    first = added(kept(first, "sl", 0), first_x)
    second = added(kept(second, "zl", 0), second_z)
    return jnp.concatenate([first, second], 0)


def team_sum(value):
    for axis in TEAM[::-1]:
        value = value + swap(value, axis)
    return value


def columns_gather(part, axes):
    out = part[:, None, :]
    for axis in axes[::-1]:
        out = paired(out, swap(out, axis), axis, 1).reshape(out.shape[0], -1, out.shape[2])
    return out.reshape(part.shape[0], -1)


def columns_scatter(value, axes):
    rows, width = value.shape
    pieces = 2 ** len(axes)
    out = value.reshape(rows, pieces, width // pieces)
    for axis in axes:
        pieces //= 2
        out = out.reshape(rows, 2, pieces, -1)
        out = added(kept(out, axis, 1), swap(given(out, axis, 1).astype(BF), axis))
    return out.reshape(rows, -1)


def peers_gather(part):
    if lax.axis_size("ch") == 2:
        part = paired(part, swap(part, "ch"), "ch", 0).reshape(-1, part.shape[1])
    elif lax.axis_size("ch") > 2:
        part = lax.all_gather(part, "ch", axis=0, tiled=True)
    if lax.axis_size("sh") == 2:
        part = paired(part, swap(part, "sh"), "sh", 0).reshape(-1, part.shape[1])
    elif lax.axis_size("sh") > 2:
        part = lax.all_gather(part, "sh", axis=0, tiled=True)
    return part


def peers_scatter(value):
    for axis in PEERS:
        size = lax.axis_size(axis)
        if size == 2:
            value = value.reshape(2, -1, value.shape[-1])
            value = added(kept(value, axis, 0), swap(given(value, axis, 0).astype(BF), axis))
        elif size > 2:
            value = lax.psum_scatter(value.astype(BF), axis, scatter_dimension=0, tiled=True)
    return value


def weight_gather(pack):
    mixed = lax.all_to_all(pack, TEAM, split_axis=0, concat_axis=0, tiled=True)
    return peers_gather(mixed.reshape(-1, pack.shape[2]))


def weight_scatter(grad, rows):
    part = peers_scatter(grad).astype(BF).reshape(RANKS, rows, grad.shape[1])
    return lax.all_to_all(part, TEAM, split_axis=0, concat_axis=0, tiled=True).astype(F32)


def by_rank(weight):
    rows = weight.shape[0]
    return weight.reshape(rows, RANKS, -1).transpose(1, 0, 2)


def to_columns(pieces):
    return pieces.transpose(1, 0, 2).reshape(pieces.shape[1], -1)


def shuffled(rows, sh, sl, ch):
    count, width = rows.shape
    return rows.reshape(count, sh, sl, ch, -1).swapaxes(2, 3).reshape(count, width)


def unshuffled(rows, sh, sl, ch):
    count, width = rows.shape
    return rows.reshape(count, sh, ch, sl, -1).swapaxes(2, 3).reshape(count, width)


def shifted(value, steps):
    count = lax.axis_size("ch")
    if count == 1:
        return jnp.zeros_like(value)
    leading, last = max(0, -steps), min(count, count - steps)
    return lax.ppermute(value, "ch", [(at, at + steps) for at in range(leading, last)])


def entering(decay, state, reverse):
    count = lax.axis_size("ch")
    if count == 1:
        return jnp.zeros_like(state)
    if count == 2:
        return shifted(state.astype(BF), -1 if reverse else 1).astype(F32)
    place = lax.axis_index("ch")
    ahead = count - 1 - place if reverse else place
    decays = lax.all_gather(decay, "ch")
    states = lax.all_gather(state.astype(BF), "ch")

    def one(step, run):
        source = count - 1 - step if reverse else step
        factor = lax.dynamic_index_in_dim(decays, source, 0, False)
        return factor[..., None, None] * run + lax.dynamic_index_in_dim(
            states, source, 0, False
        ).astype(F32)

    return lax.fori_loop(0, ahead, one, jnp.zeros_like(state))


def inverse_root(values):
    return lax.rsqrt(jnp.mean(values * values, axis=-1, keepdims=True) + epsilon)


def norm_back(values, scaled, upstream):
    normed = values * scaled
    return scaled * (upstream - normed * jnp.mean(upstream * normed, axis=-1, keepdims=True))


def silu_value(values):
    return values * jax.nn.sigmoid(values)


def silu_slope(values):
    sigmoid_part = jax.nn.sigmoid(values)
    return sigmoid_part * (1.0 + values * (1.0 - sigmoid_part))


def softplus(values):
    return jnp.maximum(values, 0.0) + jnp.log1p(jnp.exp(-jnp.abs(values)))


def plain_dot(operand, against):
    return jnp.dot(operand, against, preferred_element_type=F32)


def tail_dot(operand, against):
    return lax.dot_general(
        operand, against, (((1,), (1,)), ((), ())), preferred_element_type=F32
    )


def lead_dot(operand, against):
    return lax.dot_general(
        operand, against, (((0,), (0,)), ((), ())), preferred_element_type=F32
    )


def dots(spec, *operands):
    return jnp.einsum(
        spec, *[o.astype(BF) for o in operands], preferred_element_type=F32
    )


def local(
    tokens,
    cotangent,
    norm_gain,
    gating_weight,
    inner_weight,
    state_weight,
    step_weight,
    conv_weight,
    conv_bias,
    mixer_gain,
    mixer_out,
    query_weight,
    key_weight,
    value_weight,
    output_weight,
    feed_gain,
    gate_matrix,
    lift_matrix,
    drop_matrix,
    step_bias,
    decay_log,
    skip_scale,
):
    sh, sl, ch = lax.axis_size("sh"), lax.axis_size("sl"), lax.axis_size("ch")
    world = sh * sl * ch * 4
    rows, width = tokens.shape
    drows = norm_gain.shape[0]
    rank = (lax.axis_index("sl") * 2 + lax.axis_index("zl")) * 2 + lax.axis_index("core")
    total = RANKS * rows
    count = 4 * rows
    heads = HM // RANKS
    inner_cols = DI // RANKS
    bc_cols = 2 * NS // RANKS
    kv_cols = 2 * HD // 4
    conv_cols = inner_cols + bc_cols

    conv_own = conv_weight.shape[1]
    gain_own = mixer_gain.shape[0]
    step_scaled = (step_weight.astype(F32) * norm_gain.astype(F32)[:, None]).astype(BF)
    small = lax.all_gather(
        jnp.concatenate(
            [conv_weight.reshape(-1), conv_bias, mixer_gain, step_scaled.reshape(-1)]
        ),
        WORLD,
        axis=0,
        tiled=False,
    )
    at = 0
    wide_conv = small[:, at : at + KC * conv_own].reshape(world, KC, conv_own)
    wide_conv = wide_conv.transpose(1, 0, 2).reshape(KC, -1).astype(F32)
    at += KC * conv_own
    wide_bias = small[:, at : at + conv_own].reshape(1, -1).astype(F32)
    at += conv_own
    wide_gain = small[:, at : at + gain_own].reshape(1, -1).astype(F32)
    at += gain_own
    wide_step = small[:, at:].reshape(sh, sl, ch, 4 * drows, HM).swapaxes(1, 2)
    wide_step = wide_step.reshape(width, HM)
    own_step = lax.dynamic_slice_in_dim(wide_step, rank * heads, heads, 1)
    taps = jnp.concatenate(
        [
            lax.dynamic_slice_in_dim(wide_conv, rank * inner_cols, inner_cols, 1),
            lax.dynamic_slice_in_dim(wide_conv, DI + rank * bc_cols, bc_cols, 1),
        ],
        1,
    )
    bias = jnp.concatenate(
        [
            lax.dynamic_slice_in_dim(wide_bias, rank * inner_cols, inner_cols, 1),
            lax.dynamic_slice_in_dim(wide_bias, DI + rank * bc_cols, bc_cols, 1),
        ],
        1,
    )
    own_gain = lax.dynamic_slice_in_dim(wide_gain, rank * inner_cols, inner_cols, 1)
    own_bias = lax.dynamic_slice_in_dim(step_bias, rank * heads, heads)
    rates = -jnp.exp(lax.dynamic_slice_in_dim(decay_log, rank * heads, heads))
    skip = lax.dynamic_slice_in_dim(skip_scale, rank * heads, heads)

    def scaled(weight, gain):
        return (weight.astype(F32) * gain.astype(F32)[:, None]).astype(BF)

    key_value = jnp.stack(
        [key_weight.reshape(drows, HK, 2, kv_cols), value_weight.reshape(drows, HK, 2, kv_cols)], 2
    ).reshape(drows, RANKS * kv_cols)
    pack_inner = jnp.concatenate(
        [by_rank(scaled(w, norm_gain)) for w in (inner_weight, state_weight, key_value)], 2
    )
    pack_gating = jnp.concatenate(
        [by_rank(scaled(w, norm_gain)) for w in (gating_weight, query_weight)], 2
    )
    pack_out = jnp.concatenate([by_rank(mixer_out.T), by_rank(output_weight.T)], 2)
    pack_gate = by_rank(scaled(gate_matrix, feed_gain))
    pack_lift = by_rank(scaled(lift_matrix, feed_gain))
    pack_drop = by_rank(drop_matrix.T)
    own_tokens = shuffled(tokens, sh, sl, ch)
    own_cotangent = shuffled(cotangent, sh, sl, ch)

    team_tokens = team_gather(own_tokens)
    w_inner = weight_gather(pack_inner)
    w_gating = weight_gather(pack_gating)
    w_out = weight_gather(pack_out)
    team_cotangent = team_gather(own_cotangent)
    w_gate = weight_gather(pack_gate)
    w_lift = weight_gather(pack_lift)
    w_drop = weight_gather(pack_drop)

    root = inverse_root(team_tokens.astype(F32))
    pre_inner = plain_dot(team_tokens, w_inner) * root
    pre_gating = plain_dot(team_tokens, w_gating) * root
    step_pre = plain_dot(team_tokens, own_step) * root
    key_value_rows = columns_gather(pre_inner[:, conv_cols:].astype(BF), ("zl", "core"))
    gating = pre_gating[:, :inner_cols]
    queries = pre_gating[:, inner_cols:].astype(BF).reshape(sl, count, HD)
    pre_conv = pre_inner[:, :conv_cols].reshape(sl, count, conv_cols)
    edge = shifted(pre_conv[:, count - (KC - 1) :], 1)
    padded = jnp.concatenate([edge, pre_conv], 1)
    conv_sum = bias
    for offset in range(KC):
        conv_sum = conv_sum + taps[offset] * padded[:, offset : offset + count]
    mixed_in = silu_value(conv_sum)
    state_io = columns_gather(mixed_in[:, :, inner_cols:].reshape(total, -1).astype(BF), TEAM)
    blocks = count // BLOCK
    in_state = state_io[:, :NS].reshape(sl, blocks, BLOCK, NS)
    out_state = state_io[:, NS:].reshape(sl, blocks, BLOCK, NS)
    inner = mixed_in[:, :, :inner_cols].reshape(sl, blocks, BLOCK, heads, PM)
    step_arg = step_pre + own_bias
    step_size = softplus(step_arg).reshape(sl, blocks, BLOCK, heads)
    cumulative = jnp.cumsum(step_size * rates, axis=2)
    causal = jnp.arange(BLOCK)[:, None] >= jnp.arange(BLOCK)[None, :]
    cum_t = cumulative.swapaxes(2, 3)
    step_t = step_size.swapaxes(2, 3)
    span = cum_t[..., :, None] - cum_t[..., None, :]
    fading = jnp.where(causal, jnp.exp(jnp.where(causal, span, 0.0)), 0.0)
    pairing = dots("nctk,ncsk->ncts", out_state, in_state)[:, :, None]
    mixing = fading * pairing * step_t[..., None, :]
    within = dots("nchts,ncshp->ncthp", mixing, inner)
    to_end = jnp.exp(cumulative[:, :, -1:] - cumulative)
    feeding = to_end * step_size
    fresh = dots("ncthp,nctk->nchpk", feeding[..., None] * inner, in_state)
    decay = jnp.exp(cumulative[:, :, -1])
    run = jnp.zeros_like(fresh[:, 0])
    for c in range(blocks):
        run = decay[:, c, :, None, None] * run + fresh[:, c]
    piece_decay = jnp.exp(jnp.sum(cumulative[:, :, -1], axis=1))
    run = entering(piece_decay, run, False)
    starts = []
    for c in range(blocks):
        starts.append(run)
        run = decay[:, c, :, None, None] * run + fresh[:, c]
    carried = jnp.stack(starts, 1)
    growth = jnp.exp(cumulative)
    readout = dots("nctk,nchpk->ncthp", out_state, carried)
    ssm = within + growth[..., None] * readout + skip[:, None] * inner
    ssm_flat = ssm.reshape(total, inner_cols)
    gate_act = silu_value(gating)
    gated = ssm_flat * gate_act
    square = team_sum(jnp.sum(gated * gated, axis=-1, keepdims=True))
    mixer_root = lax.rsqrt(square / DI + epsilon)

    whole = ch * count
    key_value_all = key_value_rows.reshape(sl, count, 2 * HD)
    if ch > 1:
        key_value_all = lax.all_gather(key_value_all, "ch", axis=1, tiled=True)
    keys, values = key_value_all[..., :HD], key_value_all[..., HD:]
    place = lax.axis_index("ch") * count + jnp.arange(count)
    visible = place[:, None] >= jnp.arange(whole)[None, :]
    scores = dots("ntd,nsd->nts", queries, keys) * HD**-0.5
    scores = jnp.where(visible, scores, negative)
    top = jnp.max(scores, axis=-1, keepdims=True)
    log_total = top + jnp.log(jnp.sum(jnp.exp(scores - top), axis=-1, keepdims=True))
    probs = jnp.exp(scores - log_total)
    attended = dots("nts,nsd->ntd", probs, values).reshape(total, HD)

    branch_rows = jnp.concatenate(
        [(gated * mixer_root * own_gain).astype(BF), attended.astype(BF)], 1
    )
    branch = team_scatter(tail_dot(branch_rows, w_out))

    residual = own_tokens.astype(F32) + branch
    feed_root = inverse_root(residual)
    feed_rows = team_gather((residual * feed_root).astype(BF))
    gate_pre = plain_dot(feed_rows, w_gate)
    lift_pre = plain_dot(feed_rows, w_lift)
    swish = silu_value(gate_pre)
    active = (swish * lift_pre).astype(BF)
    active_grad = plain_dot(team_cotangent, w_drop)
    gate_rows_grad = (active_grad * lift_pre * silu_slope(gate_pre)).astype(BF)
    lift_rows_grad = (active_grad * swish).astype(BF)
    feed_grad = team_scatter(tail_dot(gate_rows_grad, w_gate) + tail_dot(lift_rows_grad, w_lift))
    layer_output = (residual + team_scatter(tail_dot(active, w_drop))).astype(BF)
    residual_grad = own_cotangent.astype(F32) + norm_back(residual, feed_root, feed_grad)
    branch_grad = team_gather(residual_grad.astype(BF))
    drop_back = weight_scatter(lead_dot(team_cotangent, active), drows)
    gate_back = weight_scatter(lead_dot(feed_rows, gate_rows_grad), drows)
    lift_back = weight_scatter(lead_dot(feed_rows, lift_rows_grad), drows)

    rows_grad = plain_dot(branch_grad, w_out)
    out_back = weight_scatter(lead_dot(branch_grad, branch_rows), drows)
    mixer_rows_grad = rows_grad[:, :inner_cols]
    attn_grad = rows_grad[:, inner_cols:].astype(BF)

    mixer_norm = gated * mixer_root
    gain_part = jnp.sum(mixer_rows_grad * mixer_norm, axis=0)
    upstream = mixer_rows_grad * own_gain
    along = team_sum(jnp.sum(upstream * mixer_norm, axis=-1, keepdims=True)) / DI
    gated_grad = mixer_root * (upstream - mixer_norm * along)
    ssm_grad = (gated_grad * gate_act).reshape(sl, blocks, BLOCK, heads, PM)
    gating_grad = gated_grad * ssm_flat * silu_slope(gating)

    delta = jnp.sum(attn_grad.astype(F32) * attended, axis=-1).reshape(sl, count, 1)
    attn_rows_grad = attn_grad.reshape(sl, count, HD)
    probs_grad = dots("ntd,nsd->nts", attn_rows_grad, values)
    scores_grad = (probs * (probs_grad - delta)).astype(BF)
    query_grad = dots("nts,nsd->ntd", scores_grad, keys).reshape(total, HD) * HD**-0.5
    key_part = dots("nts,ntd->nsd", scores_grad, queries) * HD**-0.5
    value_part = dots("nts,ntd->nsd", probs, attn_rows_grad)
    key_value_part = jnp.concatenate([key_part, value_part], 2).reshape(sl * whole, 2 * HD)
    key_value_part = columns_scatter(key_value_part, ("zl", "core")).reshape(sl, whole, kv_cols)
    if ch == 1:
        key_value_grad = key_value_part
    else:
        key_value_grad = lax.psum_scatter(
            key_value_part.astype(BF), "ch", scatter_dimension=1, tiled=True
        ).astype(F32)
    key_value_grad = key_value_grad.reshape(total, kv_cols)

    skip_part = jnp.sum(ssm_grad * inner, axis=(0, 1, 2, 4))
    grown = growth[..., None] * ssm_grad
    carried_grad = dots("ncthp,nctk->nchpk", grown, out_state)
    run = jnp.zeros_like(carried_grad[:, 0])
    for c in range(blocks)[::-1]:
        run = carried_grad[:, c] + decay[:, c, :, None, None] * run
    run = entering(piece_decay, run, True)
    ends = [None] * blocks
    for c in range(blocks)[::-1]:
        ends[c] = run
        run = carried_grad[:, c] + decay[:, c, :, None, None] * run
    later = jnp.stack(ends, 1)
    mixing_grad = jnp.where(causal, dots("ncthp,ncshp->nchts", ssm_grad, inner), 0.0)
    faded = mixing_grad * fading
    pairing_grad = jnp.sum(faded * step_t[..., None, :], axis=2)
    stepwise = faded * pairing
    step_grad = jnp.sum(stepwise, axis=3).swapaxes(2, 3)
    flow = stepwise * step_t[..., None, :]
    cum_grad = (jnp.sum(flow, axis=4) - jnp.sum(flow, axis=3)).swapaxes(2, 3)
    spread = dots("nchpk,ncsk->ncshp", later, in_state)
    inner_grad = (
        dots("nchts,ncthp->ncshp", mixing, ssm_grad)
        + skip[:, None] * ssm_grad
        + feeding[..., None] * spread
    )
    out_state_grad = dots("ncts,ncsk->nctk", pairing_grad, in_state) + dots(
        "ncthp,nchpk->nctk", grown, carried
    )
    in_state_grad = dots("ncts,nctk->ncsk", pairing_grad, out_state) + dots(
        "ncshp,nchpk->ncsk", feeding[..., None] * inner, later
    )
    cum_grad = cum_grad + jnp.sum(ssm_grad * readout, axis=4) * growth
    feeding_grad = jnp.sum(spread * inner, axis=4)
    step_grad = step_grad + feeding_grad * to_end
    fed = feeding_grad * feeding
    last_grad = jnp.sum(fed, axis=2) + jnp.sum(later * carried, axis=(3, 4)) * decay
    increment_grad = lax.cumsum(cum_grad - fed, axis=2, reverse=True) + last_grad[:, :, None]
    step_grad = step_grad + increment_grad * rates
    decay_part = jnp.sum(increment_grad * step_size, axis=(0, 1, 2)) * rates
    arg_grad = step_grad.reshape(total, heads) * jax.nn.sigmoid(step_arg)
    bias_part = jnp.sum(arg_grad, axis=0)

    state_grad = columns_scatter(
        jnp.concatenate([in_state_grad, out_state_grad], 3).reshape(total, 2 * NS), TEAM
    )
    mixed_grad = jnp.concatenate([inner_grad.reshape(total, inner_cols), state_grad], 1)
    conv_grad = mixed_grad.reshape(sl, count, conv_cols) * silu_slope(conv_sum)
    conv_bias_part = jnp.sum(conv_grad, axis=(0, 1))
    conv_part = jnp.stack(
        [
            jnp.sum(conv_grad * padded[:, offset : offset + count], axis=(0, 1))
            for offset in range(KC)
        ],
        0,
    )
    follow = shifted(conv_grad[:, : KC - 1].astype(BF), -1).astype(F32)
    extended = jnp.concatenate([conv_grad, follow], 1)
    pre_grad = jnp.zeros_like(conv_grad)
    for offset in range(KC):
        pre_grad = pre_grad + taps[offset] * extended[:, KC - 1 - offset : KC - 1 - offset + count]
    inner_rows_grad = jnp.concatenate([pre_grad.reshape(total, conv_cols), key_value_grad], 1)
    gating_rows_grad = jnp.concatenate([gating_grad, query_grad], 1)
    inner_rows_grad = (inner_rows_grad * root).astype(BF)
    gating_rows_grad = (gating_rows_grad * root).astype(BF)
    step_rows_grad = (arg_grad * root).astype(BF)
    hidden_grad = team_scatter(
        (
            tail_dot(inner_rows_grad, w_inner)
            + tail_dot(gating_rows_grad, w_gating)
            + tail_dot(step_rows_grad, own_step)
        )
        / root
    )
    gating_back = weight_scatter(lead_dot(team_tokens, gating_rows_grad), drows)
    inner_back = weight_scatter(lead_dot(team_tokens, inner_rows_grad), drows)
    step_back = lead_dot(team_tokens, step_rows_grad)
    token_values = own_tokens.astype(F32)
    tokens_grad = residual_grad + norm_back(token_values, inverse_root(token_values), hidden_grad)

    def placed(part, extent, at):
        base = jnp.zeros(part.shape[:-1] + (extent,), F32)
        return lax.dynamic_update_slice_in_dim(base, part, at, part.ndim - 1)

    conv_all = jnp.concatenate(
        [
            placed(conv_part[:, :inner_cols], DI, rank * inner_cols),
            placed(conv_part[:, inner_cols:], 2 * NS, rank * bc_cols),
        ],
        1,
    )
    conv_bias_all = jnp.concatenate(
        [
            placed(conv_bias_part[:inner_cols], DI, rank * inner_cols),
            placed(conv_bias_part[inner_cols:], 2 * NS, rank * bc_cols),
        ],
        0,
    )
    gain_all = placed(gain_part, DI, rank * inner_cols)
    step_all = placed(step_back, HM, rank * heads)
    step_all = step_all.reshape(sh, ch, sl, 4, drows * HM).swapaxes(1, 2)
    per_head = jnp.concatenate(
        [placed(v, HM, rank * heads) for v in (bias_part, decay_part, skip_part)]
    )
    sent = jnp.concatenate(
        [
            conv_all.reshape(KC, world, conv_own).swapaxes(0, 1).reshape(world, -1),
            conv_bias_all.reshape(world, -1),
            gain_all.reshape(world, -1),
            step_all.reshape(world, -1),
            jnp.broadcast_to(per_head[None], (world, 3 * HM)),
        ],
        1,
    )
    got = jnp.sum(
        lax.all_to_all(sent, WORLD, split_axis=0, concat_axis=0, tiled=True), axis=0
    )
    at = 0
    conv_out = got[at : at + KC * conv_own].reshape(KC, conv_own)
    at += KC * conv_own
    conv_bias_out = got[at : at + conv_own]
    at += conv_own
    gain_out = got[at : at + gain_own]
    at += gain_own
    step_core = got[at : at + drows * HM].reshape(drows, HM)
    at += drows * HM
    bias_out, decay_out, skip_out = (got[at + i * HM : at + (i + 1) * HM] for i in range(3))

    def against(weight, grad):
        return jnp.sum(weight.astype(F32) * grad, axis=1)

    inner_core = to_columns(inner_back[:, :, :inner_cols])
    state_core = to_columns(inner_back[:, :, inner_cols:conv_cols])
    key_value_core = to_columns(inner_back[:, :, conv_cols:]).reshape(drows, HK, 2, 2 * kv_cols)
    key_core = key_value_core[:, :, 0].reshape(drows, HK * HD)
    value_core = key_value_core[:, :, 1].reshape(drows, HK * HD)
    gating_core = to_columns(gating_back[:, :, :inner_cols])
    query_core = to_columns(gating_back[:, :, inner_cols:])
    gate_core, lift_core = to_columns(gate_back), to_columns(lift_back)
    norm_out = (
        against(gating_weight, gating_core)
        + against(inner_weight, inner_core)
        + against(state_weight, state_core)
        + against(step_weight, step_core)
        + against(query_weight, query_core)
        + against(key_weight, key_core)
        + against(value_weight, value_core)
    )
    feed_out = against(gate_matrix, gate_core) + against(lift_matrix, lift_core)
    norm_scale = norm_gain.astype(F32)[:, None]
    feed_scale = feed_gain.astype(F32)[:, None]
    mixer_out_out = out_back[:, :, :inner_cols].transpose(0, 2, 1).reshape(DI, drows)
    output_out = out_back[:, :, inner_cols:].transpose(0, 2, 1).reshape(HA * HD, drows)
    drop_out = drop_back.transpose(0, 2, 1).reshape(-1, drows)
    return (
        unshuffled(layer_output, sh, sl, ch),
        unshuffled(tokens_grad, sh, sl, ch),
        norm_out,
        gating_core * norm_scale,
        inner_core * norm_scale,
        state_core * norm_scale,
        step_core * norm_scale,
        conv_out,
        conv_bias_out,
        gain_out,
        mixer_out_out,
        query_core * norm_scale,
        key_core * norm_scale,
        value_core * norm_scale,
        output_out,
        feed_out,
        gate_core * feed_scale,
        lift_core * feed_scale,
        drop_out,
        bias_out,
        decay_out,
        skip_out,
    )


def solution(mesh):
    seq, ctx = mesh.shape["seq"], mesh.shape["ctx"]
    fine = Mesh(mesh.devices.reshape(seq // 2, 2, ctx // 4, 2, 2), WORLD)
    lead, vector, tail = P(WORLD, None), P(WORLD), P(None, WORLD)
    in_specs = (
        lead,
        lead,
        vector,
        lead,
        lead,
        lead,
        lead,
        tail,
        vector,
        vector,
        tail,
        lead,
        lead,
        lead,
        tail,
        vector,
        lead,
        lead,
        tail,
        P(),
        P(),
        P(),
    )
    out_specs = (
        lead,
        lead,
        vector,
        lead,
        lead,
        lead,
        lead,
        tail,
        vector,
        vector,
        tail,
        lead,
        lead,
        lead,
        tail,
        vector,
        lead,
        lead,
        tail,
        P(),
        P(),
        P(),
    )
    return jax.shard_map(local, mesh=fine, in_specs=in_specs, out_specs=out_specs, check_vma=False)
```

time: 4360 us -> 1220 us (0.28)
  waiting for transfers between devices: 3670 us -> 402 us
  local copies, waits for them, and re-layouts: 65.8 us -> 324 us
  matrix products: 311 us -> 97.9 us
  blocking collectives: 206 us -> 0 us
  starting transfers between devices: 5.12 us -> 150 us
  other arithmetic: 70.4 us -> 215 us
    reduce_scatter x12 -> x0, waiting for transfers between devices: 2550 us -> none  [the longest x1 361 us: local(): lax.psum_scatter(gate_grad, ('seq', 'ctx'), scatter_dimension=0, tiled=True)]
    all_gather x13 -> x1, waiting for transfers between devices: 1030 us -> 7.23 us  [local(): key_value_all = lax.all_gather(key_value_all, 'ch', axis=1, tiled=True)]
    ppermute x2 -> x84, waiting for transfers between devices: 2.46 us -> 252 us  [the longest x80 235 us: swap(): return lax.ppermute(value, axis, [(0, 1), (1, 0)])]
    all_gather x5 -> x0, blocking collectives: 124 us -> none  [the longest x1 40.8 us: local(): lax.all_gather(conv_weight, ('seq', 'ctx'), axis=1, tiled=True)]
    unnamed x225 -> x529, local copies, waits for them, and re-layouts: 25.8 us -> 129 us
    dot_general x38 -> x25, matrix products: 144 us -> 51.2 us  [the longest x18 30.9 us: dots(): jnp.einsum(spec, *[o.astype(BF) for o in operands], preferred_element_typ...]
    ppermute x2 -> x84, starting transfers between devices: 3.46 us -> 95.9 us  [the longest x80 82.9 us: swap(): return lax.ppermute(value, axis, [(0, 1), (1, 0)])]
    unnamed x2 -> x0, blocking collectives: 81.5 us -> none
  transfers between devices with their start and end apart: 29 -> 100, of which waited for: 26 -> 43; matrix products, arithmetic and copies ran while one was open for 9% -> 46% of each run, Pallas kernels for 0% -> 0%
where the time goes in v1:
time: 1220 us; the launch traced here: 1210 us
  waiting for transfers between devices  402 us (33%)
  local copies, waits for them, and re-layouts  324 us (27%)
  other arithmetic  215 us (18%)
  starting transfers between devices  150 us (12%)
  matrix products  97.9 us (8%)
  between operations  18.2 us (1%)
    ppermute x80, waiting for transfers between devices, swap(): return lax.ppermute(value, axis, [(0, 1), (1, 0)])  235 us
    unnamed x529, local copies, waits for them, and re-layouts  129 us
    unnamed x5, waiting for transfers between devices  126 us
    ppermute x80, starting transfers between devices, swap(): return lax.ppermute(value, axis, [(0, 1), (1, 0)])  82.9 us
    select_n x43, other arithmetic, paired(): jnp.where(bit == 0, jnp.stack([mine, theirs], dim), jnp.stack([theirs, mi...  64.3 us
    add x30, other arithmetic, added(): return mine.astype(F32) + theirs.astype(F32)  47.4 us
    dot_general x18, matrix products, dots(): jnp.einsum(spec, *[o.astype(BF) for o in operands], preferred_element_typ...  30.9 us
    dot_general x7, matrix products, tail_dot(): lax.dot_general(operand, against, (((1,), (1,)), ((), ())), preferred_ele...  26.5 us
  transfers between devices with their start and end apart: 100, of which 43 were waited for; matrix products, arithmetic and copies ran while one was open for 46% of the time, Pallas kernels for 0%

profile of v1, /device:TPU:0, one launch (start us, length us, event | category | flops | bytes accessed | tf_op | source)
XLA Modules:
  0.0 1207.3 jit_solution(12350652844356239918)
XLA Ops:
  43.3 8.1 collective-permute-done.3
  69.9 106.5 %all-reduce.3.cloned.1.call-done = bf16[119296]{0:T(1024)(128)(2,1)} async-done(((bf16[119296]{0:T(1024)(128)(2,1)}), bf16[119296]{0:T(1024)(128)(2,1)}) %all-reduce.3.cloned.1.call-update) | async-done | bytes 238608
  194.1 22.1 %collective-permute-done.19 = bf16[512,512]{1,0:T(8,128)(2,1)S(1)} collective-permute-done((bf16[512,512]{1,0:T(8,128)(2,1)}, bf16[512,512]{1,0:T(8,128)(2,1)S(1)}, u32[]{:S(2)}, u32[]{:S(2)}) %collective-permute-start.19) | collective-permute-done | bytes 524320 | tf_op jit(solution)/shard_map/ppermute | solution.py:30
  221.9 7.0 collective-permute-done.13
  260.7 9.8 collective-permute-start.9
  343.1 7.2 all-gather.3.cloned.1.call-done
  438.5 10.9 collective-permute-done.22
  452.8 10.6 collective-permute-done.24
  472.4 11.1 collective-permute-done.25
  506.0 8.8 collective-permute-done.27
  529.8 12.2 %collective-permute-done.36 = bf16[1024,512]{1,0:T(8,128)(2,1)} collective-permute-done((bf16[1024,512]{1,0:T(8,128)(2,1)}, bf16[1024,512]{1,0:T(8,128)(2,1)}, u32[]{:S(2)}, u32[]{:S(2)}) %collective-permute-start.36) | collective-permute-done | bytes 1048608 | tf_op jit(solution)/shard_map/ppermute | solution.py:30
  551.2 6.5 copy.1179
  557.7 6.4 copy.1182
  589.3 6.7 copy.1183
  623.0 13.7 %collective-permute-done.78 = bf16[1024,512]{1,0:T(8,128)(2,1)} collective-permute-done((bf16[1024,512]{1,0:T(8,128)(2,1)}, bf16[1024,512]{1,0:T(8,128)(2,1)}, u32[]{:S(2)}, u32[]{:S(2)}) %collective-permute-start.78) | collective-permute-done | bytes 1048608 | tf_op jit(solution)/shard_map/ppermute | solution.py:30
  638.7 18.3 %collective-permute-done.80 = bf16[1024,512]{1,0:T(8,128)(2,1)} collective-permute-done((bf16[1024,512]{1,0:T(8,128)(2,1)}, bf16[1024,512]{1,0:T(8,128)(2,1)}, u32[]{:S(2)}, u32[]{:S(2)}) %collective-permute-start.80) | collective-permute-done | bytes 1048608 | tf_op jit(solution)/shard_map/ppermute | solution.py:30
  662.7 18.0 %collective-permute-done.79 = bf16[512,512]{1,0:T(8,128)(2,1)S(1)} collective-permute-done((bf16[512,512]{1,0:T(8,128)(2,1)S(1)}, bf16[512,512]{1,0:T(8,128)(2,1)S(1)}, u32[]{:S(2)}, u32[]{:S(2)}) %collective-permute-start.79) | collective-permute-done | bytes 524320 | tf_op jit(solution)/shard_map/ppermute | solution.py:30
  735.4 7.2 collective-permute-done.49
  767.2 10.0 collective-permute-done.55
  784.6 6.1 collective-permute-done.39
  805.4 6.6 copy.1177
  879.3 13.1 %collective-permute-done.60 = bf16[2,6,64,256]{3,2,1,0:T(8,128)(2,1)S(1)} collective-permute-done((bf16[2,6,64,256]{3,2,1,0:T(8,128)(2,1)}, bf16[2,6,64,256]{3,2,1,0:T(8,128)(2,1)S(1)}, u32[]{:S(2)}, u32[]{:S(2)}) %collective-permute-start.60) | collective-permute-done | bytes 393248 | tf_op jit(solution)/shard_map/ppermute | solution.py:165
  904.6 8.8 reduce_window_sum.22
  940.1 26.4 %copy.1180 = bf16[2,1024,64]{0,2,1:T(8,128)(2,1)} copy(bf16[2,1024,64]{1,0,2:T(2,128)(2,1)S(1)} %convert_element_type.752) | data formatting | bytes 524288
  966.5 25.5 %reshape.1640 = bf16[1024,128]{1,0:T(8,128)(2,1)} reshape(bf16[1024,64,2]{2,1,0:T(8,128)(2,1)} %bitcast.736) | data formatting | bytes 524288
  996.8 7.9 collective-permute-done.62
  1009.8 19.7 %reduce-scatter.4.cloned.1.call-done = bf16[512,128]{1,0:T(8,128)(2,1)} async-done(((bf16[1024,128]{1,0:T(8,128)(2,1)}), bf16[512,128]{1,0:T(8,128)(2,1)}) %reduce-scatter.4.cloned.1.call-update) | async-done | bytes 131088
  1029.5 19.8 %reshape.1641 = bf16[512,64,2]{2,1,0:T(8,128)(2,1)} reshape(bf16[512,128]{1,0:T(8,128)(2,1)} %reduce-scatter.4.cloned.1.call-done) | data formatting | bytes 262144
  1049.3 9.1 copy.1181
  1075.1 6.8 all-to-all-start.8
  1132.9 17.0 %collective-permute-done.75 = bf16[512,512]{1,0:T(8,128)(2,1)} collective-permute-done((bf16[512,512]{1,0:T(8,128)(2,1)}, bf16[512,512]{1,0:T(8,128)(2,1)}, u32[]{:S(2)}, u32[]{:S(2)}) %collective-permute-start.75) | collective-permute-done | bytes 524320 | tf_op jit(solution)/shard_map/ppermute | solution.py:30
  1182.8 5.9 collective-permute-done.71
  (1135 shorter events, 715.0 us)
Async XLA Ops:
  22.9 153.5 %all-reduce.3.cloned.1.call-start = ((), (), s32[]{:S(2)}) async-start(), calls=%async_computation.15 | async-start | bytes 479232
  28.6 352.9 %collective-permute-start.44 = (bf16[64,2048]{1,0:T(8,128)(2,1)}, bf16[64,2048]{1,0:T(8,128)(2,1)}, u32[]{:S(2)}, u32[]{:S(2)}) collective-permute-start(bf16[64,2048]{1,0:T(8,128)(2,1)} %slice.316), channel_id=1, source_target_pairs={{0,2},{2,0},{1,3},{3,1},{4,6},{6,4},{5,7},{7,5},{8,10},{10,8},{9,1... | collective-permute-start | bytes 786440 | tf_op jit(solution)/shard_map/ppermute | solution.py:30
  55.7 122.1 %collective-permute-start.5 = (bf16[512,512]{1,0:T(8,128)(2,1)S(1)}, bf16[512,512]{1,0:T(8,128)(2,1)S(1)}, u32[]{:S(2)}, u32[]{:S(2)}) collective-permute-start(bf16[512,512]{1,0:T(8,128)(2,1)S(1)} %bitcast.795), channel_id=1, source_target_pairs={{0,4},{4,0},{1,5},{5,1},{2,6},{6,2},{3,7},{7,3},{8,12},{12,8},{9,1... | collective-permute-start | bytes 1572872 | tf_op jit(solution)/shard_map/ppermute | solution.py:30
  60.2 172.7 %collective-permute-start.4 = (bf16[2,2,128,2048]{3,2,1,0:T(8,128)(2,1)}, bf16[2,2,128,2048]{3,2,1,0:T(8,128)(2,1)}, u32[]{:S(2)}, u32[]{:S(2)}) collective-permute-start(bf16[2,2,128,2048]{3,2,1,0:T(8,128)(2,1)} %get-tuple-element.279), channel_id=1, source_target_pairs={{0,1},{1,0},{2,3},{3,2},{4,5},{5,4},{6,7},{7,6},{8,9},{9,8},{10,11... | collective-permute-start | bytes 6291464 | tf_op jit(solution)/shard_map/ppermute | solution.py:30
  63.1 127.6 %all-to-all-start.2 = ((bf16[8,64,512]{2,1,0:T(8,128)(2,1)}), bf16[8,64,512]{2,1,0:T(8,128)(2,1)}, u32[]{:S(2)}, u32[]{:S(2)}) async-start(bf16[8,64,512]{2,1,0:T(8,128)(2,1)} %copy.1068), calls=%async_computation.2 | async-start | bytes 1048576 | tf_op jit(solution)/shard_map/all_to_all | solution.py:132
  67.2 283.1 %all-gather.3.cloned.1.call-start = ((), (), s32[]{:S(2)}) async-start(), calls=%async_computation.14 | async-start | bytes 1572864 | tf_op jit(solution)/shard_map/all_gather | solution.py:395
  67.5 114.4 %collective-permute-start.12 = (bf16[512,512]{1,0:T(8,128)(2,1)}, bf16[512,512]{1,0:T(8,128)(2,1)}, u32[]{:S(2)}, u32[]{:S(2)}) collective-permute-start(bf16[512,512]{1,0:T(8,128)(2,1)} %bitcast.63), channel_id=1, source_target_pairs={{0,4},{4,0},{1,5},{5,1},{2,6},{6,2},{3,7},{7,3},{8,12},{12,8},{9,1... | collective-permute-start | bytes 1572872 | tf_op jit(solution)/shard_map/ppermute | solution.py:30
  180.3 39.7 %collective-permute-start.6 = (bf16[1024,512]{1,0:T(8,128)(2,1)S(1)}, bf16[1024,512]{1,0:T(8,128)(2,1)}, u32[]{:S(2)}, u32[]{:S(2)}) collective-permute-start(bf16[1024,512]{1,0:T(8,128)(2,1)S(1)} %bitcast.780), channel_id=1, source_target_pairs={{0,16},{16,0},{1,17},{17,1},{2,18},{18,2},{3,19},{19,3},{4,20},{20... | collective-permute-start | bytes 3145736 | tf_op jit(solution)/shard_map/ppermute | solution.py:30
  184.5 44.4 %collective-permute-start.13 = (bf16[1024,512]{1,0:T(8,128)(2,1)}, bf16[1024,512]{1,0:T(8,128)(2,1)}, u32[]{:S(2)}, u32[]{:S(2)}) collective-permute-start(bf16[1024,512]{1,0:T(8,128)(2,1)} %bitcast.66), channel_id=1, source_target_pairs={{0,16},{16,0},{1,17},{17,1},{2,18},{18,2},{3,19},{19,3},{4,20},{20... | collective-permute-start | bytes 3145736 | tf_op jit(solution)/shard_map/ppermute | solution.py:30
  218.6 118.6 %collective-permute-start.20 = (bf16[1024,512]{1,0:T(8,128)(2,1)}, bf16[1024,512]{1,0:T(8,128)(2,1)}, u32[]{:S(2)}, u32[]{:S(2)}) collective-permute-start(bf16[1024,512]{1,0:T(8,128)(2,1)} %bitcast.85), channel_id=1, source_target_pairs={{0,16},{16,0},{1,17},{17,1},{2,18},{18,2},{3,19},{19,3},{4,20},{20... | collective-permute-start | bytes 3145736 | tf_op jit(solution)/shard_map/ppermute | solution.py:30
  428.7 117.4 %collective-permute-start.46 = (bf16[2,2,128,2048]{3,2,1,0:T(8,128)(2,1)}, bf16[2,2,128,2048]{3,2,1,0:T(8,128)(2,1)}, u32[]{:S(2)}, u32[]{:S(2)}) collective-permute-start(bf16[2,2,128,2048]{3,2,1,0:T(8,128)(2,1)} %get-tuple-element.274), channel_id=1, source_target_pairs={{0,1},{1,0},{2,3},{3,2},{4,5},{5,4},{6,7},{7,6},{8,9},{9,8},{10,11... | collective-permute-start | bytes 6291464 | tf_op jit(solution)/shard_map/ppermute | solution.py:30
  428.7 63.1 %collective-permute-start.31 = (bf16[512,512]{1,0:T(8,128)(2,1)}, bf16[512,512]{1,0:T(8,128)(2,1)}, u32[]{:S(2)}, u32[]{:S(2)}) collective-permute-start(bf16[512,512]{1,0:T(8,128)(2,1)} %bitcast.116), channel_id=1, source_target_pairs={{0,4},{4,0},{1,5},{5,1},{2,6},{6,2},{3,7},{7,3},{8,12},{12,8},{9,1... | collective-permute-start | bytes 1572872 | tf_op jit(solution)/shard_map/ppermute | solution.py:30
  433.2 62.7 %collective-permute-start.35 = (bf16[512,512]{1,0:T(8,128)(2,1)}, bf16[512,512]{1,0:T(8,128)(2,1)}, u32[]{:S(2)}, u32[]{:S(2)}) collective-permute-start(bf16[512,512]{1,0:T(8,128)(2,1)} %bitcast.134), channel_id=1, source_target_pairs={{0,4},{4,0},{1,5},{5,1},{2,6},{6,2},{3,7},{7,3},{8,12},{12,8},{9,1... | collective-permute-start | bytes 1572872 | tf_op jit(solution)/shard_map/ppermute | solution.py:30
  435.6 86.5 %collective-permute-start.34 = (bf16[1024,512]{1,0:T(8,128)(2,1)}, bf16[1024,512]{1,0:T(8,128)(2,1)}, u32[]{:S(2)}, u32[]{:S(2)}) collective-permute-start(bf16[1024,512]{1,0:T(8,128)(2,1)} %bitcast.127), channel_id=1, source_target_pairs={{0,16},{16,0},{1,17},{17,1},{2,18},{18,2},{3,19},{19,3},{4,20},{20... | collective-permute-start | bytes 3145736 | tf_op jit(solution)/shard_map/ppermute | solution.py:30
  519.0 49.1 %collective-permute-start.30 = (bf16[2,2,128,2048]{3,2,1,0:T(8,128)(2,1)}, bf16[2,2,128,2048]{3,2,1,0:T(8,128)(2,1)}, u32[]{:S(2)}, u32[]{:S(2)}) collective-permute-start(bf16[2,2,128,2048]{3,2,1,0:T(8,128)(2,1)} %get-tuple-element.276), channel_id=1, source_target_pairs={{0,1},{1,0},{2,3},{3,2},{4,5},{5,4},{6,7},{7,6},{8,9},{9,8},{10,11... | collective-permute-start | bytes 6291464 | tf_op jit(solution)/shard_map/ppermute | solution.py:30
  608.6 48.4 %collective-permute-start.80 = (bf16[1024,512]{1,0:T(8,128)(2,1)}, bf16[1024,512]{1,0:T(8,128)(2,1)}, u32[]{:S(2)}, u32[]{:S(2)}) collective-permute-start(bf16[1024,512]{1,0:T(8,128)(2,1)} %fusion.55), channel_id=1, source_target_pairs={{0,16},{16,0},{1,17},{17,1},{2,18},{18,2},{3,19},{19,3},{4,20},{20... | collective-permute-start | bytes 3145736 | tf_op jit(solution)/shard_map/ppermute | solution.py:30
  613.4 80.6 %collective-permute-start.47 = (bf16[2,2,128,2048]{3,2,1,0:T(8,128)(2,1)}, bf16[2,2,128,2048]{3,2,1,0:T(8,128)(2,1)}, u32[]{:S(2)}, u32[]{:S(2)}) collective-permute-start(bf16[2,2,128,2048]{3,2,1,0:T(8,128)(2,1)} %fusion.5), channel_id=1, source_target_pairs={{0,1},{1,0},{2,3},{3,2},{4,5},{5,4},{6,7},{7,6},{8,9},{9,8},{10,11... | collective-permute-start | bytes 6291464 | tf_op jit(solution)/shard_map/ppermute | solution.py:30
  622.7 62.9 %collective-permute-start.83 = (bf16[512,512]{1,0:T(8,128)(2,1)}, bf16[512,512]{1,0:T(8,128)(2,1)}, u32[]{:S(2)}, u32[]{:S(2)}) collective-permute-start(bf16[512,512]{1,0:T(8,128)(2,1)} %fusion.107), channel_id=1, source_target_pairs={{0,4},{4,0},{1,5},{5,1},{2,6},{6,2},{3,7},{7,3},{8,12},{12,8},{9,1... | collective-permute-start | bytes 1572872 | tf_op jit(solution)/shard_map/ppermute | solution.py:30
  638.3 42.3 %collective-permute-start.79 = (bf16[512,512]{1,0:T(8,128)(2,1)S(1)}, bf16[512,512]{1,0:T(8,128)(2,1)S(1)}, u32[]{:S(2)}, u32[]{:S(2)}) collective-permute-start(bf16[512,512]{1,0:T(8,128)(2,1)S(1)} %fusion.105), channel_id=1, source_target_pairs={{0,4},{4,0},{1,5},{5,1},{2,6},{6,2},{3,7},{7,3},{8,12},{12,8},{9,1... | collective-permute-start | bytes 1572872 | tf_op jit(solution)/shard_map/ppermute | solution.py:30
  662.7 38.3 %collective-permute-start.37 = (bf16[2,2,128,2048]{3,2,1,0:T(8,128)(2,1)}, bf16[2,2,128,2048]{3,2,1,0:T(8,128)(2,1)}, u32[]{:S(2)}, u32[]{:S(2)}) collective-permute-start(bf16[2,2,128,2048]{3,2,1,0:T(8,128)(2,1)} %fusion.3), channel_id=1, source_target_pairs={{0,1},{1,0},{2,3},{3,2},{4,5},{5,4},{6,7},{7,6},{8,9},{9,8},{10,11... | collective-permute-start | bytes 6291464 | tf_op jit(solution)/shard_map/ppermute | solution.py:30
  713.7 66.9 %collective-permute-start.38 = (bf16[2,64,2048]{2,1,0:T(8,128)(2,1)}, bf16[2,64,2048]{2,1,0:T(8,128)(2,1)}, u32[]{:S(2)}, u32[]{:S(2)}) collective-permute-start(bf16[2,64,2048]{2,1,0:T(8,128)(2,1)} %fusion.94), channel_id=1, source_target_pairs={{0,2},{2,0},{1,3},{3,1},{4,6},{6,4},{5,7},{7,5},{8,10},{10,8},{9,1... | collective-permute-start | bytes 1572872 | tf_op jit(solution)/shard_map/ppermute | solution.py:30
  716.5 66.0 %collective-permute-start.40 = (bf16[2,64,2048]{2,1,0:T(8,128)(2,1)}, bf16[2,64,2048]{2,1,0:T(8,128)(2,1)}, u32[]{:S(2)}, u32[]{:S(2)}) collective-permute-start(bf16[2,64,2048]{2,1,0:T(8,128)(2,1)} %fusion.95), channel_id=1, source_target_pairs={{0,8},{8,0},{1,9},{9,1},{2,10},{10,2},{3,11},{11,3},{4,12},{12,4},... | collective-permute-start | bytes 1572872 | tf_op jit(solution)/shard_map/ppermute | solution.py:30
  720.5 37.1 %all-to-all-start.12 = ((bf16[8,64,512]{2,1,0:T(8,128)(2,1)}), bf16[8,64,512]{2,1,0:T(8,128)(2,1)}, u32[]{:S(2)}, u32[]{:S(2)}) async-start(bf16[8,64,512]{2,1,0:T(8,128)(2,1)} %bitcast.295), calls=%async_computation.12 | async-start | bytes 1048576 | tf_op jit(solution)/shard_map/all_to_all | solution.py:138
  724.6 304.9 %reduce-scatter.4.cloned.1.call-start = ((), (), s32[]{:S(2)}) async-start(), calls=%async_computation.16 | async-start | bytes 393216
  819.8 173.6 %collective-permute-start.76 = (bf16[1024,512]{1,0:T(8,128)(2,1)}, bf16[1024,512]{1,0:T(8,128)(2,1)}, u32[]{:S(2)}, u32[]{:S(2)}) collective-permute-start(bf16[1024,512]{1,0:T(8,128)(2,1)} %fusion.53), channel_id=1, source_target_pairs={{0,16},{16,0},{1,17},{17,1},{2,18},{18,2},{3,19},{19,3},{4,20},{20... | collective-permute-start | bytes 3145736 | tf_op jit(solution)/shard_map/ppermute | solution.py:30
  841.3 78.4 %collective-permute-start.65 = (bf16[2048,2,64]{0,2,1:T(8,128)(2,1)}, bf16[2048,2,64]{0,2,1:T(8,128)(2,1)}, u32[]{:S(2)}, u32[]{:S(2)}) collective-permute-start(bf16[2048,2,64]{0,2,1:T(8,128)(2,1)} %fusion.99), channel_id=1, source_target_pairs={{0,2},{2,0},{1,3},{3,1},{4,6},{6,4},{5,7},{7,5},{8,10},{10,8},{9,1... | collective-permute-start | bytes 1572872 | tf_op jit(solution)/shard_map/ppermute | solution.py:30
  873.0 133.1 %collective-permute-start.72 = (bf16[1024,512]{1,0:T(8,128)(2,1)}, bf16[1024,512]{1,0:T(8,128)(2,1)}, u32[]{:S(2)}, u32[]{:S(2)}) collective-permute-start(bf16[1024,512]{1,0:T(8,128)(2,1)} %fusion.51), channel_id=1, source_target_pairs={{0,16},{16,0},{1,17},{17,1},{2,18},{18,2},{3,19},{19,3},{4,20},{20... | collective-permute-start | bytes 3145736 | tf_op jit(solution)/shard_map/ppermute | solution.py:30
  902.8 89.3 %collective-permute-start.61 = (bf16[1024,4,64]{0,2,1:T(8,128)(2,1)}, bf16[1024,4,64]{0,2,1:T(8,128)(2,1)}, u32[]{:S(2)}, u32[]{:S(2)}) collective-permute-start(bf16[1024,4,64]{0,2,1:T(8,128)(2,1)} %fusion.98), channel_id=1, source_target_pairs={{0,8},{8,0},{1,9},{9,1},{2,10},{10,2},{3,11},{11,3},{4,12},{12,4},... | collective-permute-start | bytes 1572872 | tf_op jit(solution)/shard_map/ppermute | solution.py:30
  996.8 103.6 %collective-permute-start.77 = (bf16[512,512]{1,0:T(8,128)(2,1)}, bf16[512,512]{1,0:T(8,128)(2,1)}, u32[]{:S(2)}, u32[]{:S(2)}) collective-permute-start(bf16[512,512]{1,0:T(8,128)(2,1)} %fusion.104), channel_id=1, source_target_pairs={{0,4},{4,0},{1,5},{5,1},{2,6},{6,2},{3,7},{7,3},{8,12},{12,8},{9,1... | collective-permute-start | bytes 1572872 | tf_op jit(solution)/shard_map/ppermute | solution.py:30
  1005.5 53.8 %collective-permute-start.63 = (bf16[1024,1,64]{0,2,1:T(8,128)(2,1)}, bf16[1024,1,64]{0,2,1:T(8,128)(2,1)}, u32[]{:S(2)}, u32[]{:S(2)}) collective-permute-start(bf16[1024,1,64]{0,2,1:T(8,128)(2,1)} %dynamic-slice_convert_fusion.34), channel_id=1, source_target_pairs={{0,1},{1,0},{2,3},{3,2},{4,5},{5,4},{6,7},{7,6},{8,9},{9,8},{10,11... | collective-permute-start | bytes 393224 | tf_op jit(solution)/shard_map/ppermute | solution.py:30
  1009.8 100.6 %collective-permute-start.73 = (bf16[512,512]{1,0:T(8,128)(2,1)}, bf16[512,512]{1,0:T(8,128)(2,1)}, u32[]{:S(2)}, u32[]{:S(2)}) collective-permute-start(bf16[512,512]{1,0:T(8,128)(2,1)} %fusion.102), channel_id=1, source_target_pairs={{0,4},{4,0},{1,5},{5,1},{2,6},{6,2},{3,7},{7,3},{8,12},{12,8},{9,1... | collective-permute-start | bytes 1572872 | tf_op jit(solution)/shard_map/ppermute | solution.py:30
  1110.0 45.6 %collective-permute-start.67 = (bf16[2,2,128,2048]{3,2,1,0:T(8,128)(2,1)}, bf16[2,2,128,2048]{3,2,1,0:T(8,128)(2,1)}, u32[]{:S(2)}, u32[]{:S(2)}) collective-permute-start(bf16[2,2,128,2048]{3,2,1,0:T(8,128)(2,1)} %fusion.4), channel_id=1, source_target_pairs={{0,1},{1,0},{2,3},{3,2},{4,5},{5,4},{6,7},{7,6},{8,9},{9,8},{10,11... | collective-permute-start | bytes 6291464 | tf_op jit(solution)/shard_map/ppermute | solution.py:30
  (320 other events, 3707.5 us)
Sparse Core Ops, SparseCore 0:
  29.3 147.1 all-reduce.2
  318.1 32.1 all-gather.2
  992.2 37.2 reduce-scatter.3

commit v2 on v1

v2 whole, which is shorter than its diff:
```python
import jax
import jax.numpy as jnp
from jax import lax
from jax.experimental import pallas as pl
from jax.experimental.pallas import tpu as pltpu
from jax.sharding import Mesh
from jax.sharding import PartitionSpec as P

DI = 3072
HM = 48
PM = 64
NS = 256
KC = 4
HA = 8
HK = 2
HD = 128
FF = 4096
BLOCK = 128

epsilon = 1e-06
negative = -1e30
BF = jnp.bfloat16
F32 = jnp.float32

TEAM = ("sl", "zl", "core")
PEERS = ("sh", "ch")
WORLD = ("sh", "sl", "ch", "zl", "core")
RANKS = 8


def swap(value, axis):
    return lax.ppermute(value, axis, [(0, 1), (1, 0)])


def paired(mine, theirs, axis_name, dim):
    bit = lax.axis_index(axis_name)
    return jnp.where(bit == 0, jnp.stack([mine, theirs], dim), jnp.stack([theirs, mine], dim))


def kept(value, axis_name, dim):
    return lax.dynamic_index_in_dim(value, lax.axis_index(axis_name), dim, False)


def given(value, axis_name, dim):
    return lax.dynamic_index_in_dim(value, 1 - lax.axis_index(axis_name), dim, False)


def added(mine, theirs):
    return mine.astype(F32) + theirs.astype(F32)


def team_order():
    s, z, c = (lax.axis_index(axis) for axis in TEAM)
    blocks = [
        ((s ^ sl) * 2 + (z ^ zl)) * 2 + (c ^ core)
        for core in (0, 1)
        for zl in (0, 1)
        for sl in (0, 1)
    ]
    return jnp.stack(blocks).astype(jnp.int32)


def team_gather(rows):
    half = rows.shape[1] // 2
    left, right = rows[:, :half], rows[:, half:]
    left = jnp.stack([left, swap(left, "sl")])
    right = jnp.stack([right, swap(right, "zl")])
    left_z = swap(left, "zl")
    right_x = swap(right, "sl")
    left = jnp.concatenate([left, left_z], 0)
    right = jnp.stack([right[0], right_x[0], right[1], right_x[1]])
    return left, right, swap(left, "core"), swap(right, "core")


def team_scatter(parts):
    left, right, left_given, right_given = parts
    left_got, right_got = swap(left_given, "core"), swap(right_given, "core")
    left_z = swap(added(left[2:], left_got[2:]).astype(BF), "zl")
    right_x = swap(added(right[1::2], right_got[1::2]).astype(BF), "sl")
    left = added(left[:2], left_got[:2]) + left_z.astype(F32)
    right = added(right[0::2], right_got[0::2]) + right_x.astype(F32)
    left_x = swap(left[1].astype(BF), "sl")
    right_z = swap(right[1].astype(BF), "zl")
    return jnp.concatenate([added(left[0], left_x), added(right[0], right_z)], 1)


def team_sum(value):
    for axis in TEAM[::-1]:
        value = value + swap(value, axis)
    return value


def relative(value, axis_name, dim):
    if lax.axis_size(axis_name) != 2:
        return value
    return jnp.where(lax.axis_index(axis_name) == 0, value, jnp.flip(value, dim))


def peers_gather(part):
    size = lax.axis_size("ch")
    if size == 2:
        part = jnp.concatenate([part, swap(part, "ch")], 0)
    elif size > 2:
        part = lax.all_gather(part, "ch", axis=0, tiled=True)
    return part, swap(part, "sh")


def ranks_exchange(pack):
    mixed = lax.all_to_all(pack, TEAM, split_axis=0, concat_axis=0, tiled=True)
    return mixed.reshape(-1, pack.shape[2])


def peers_sum(mine, theirs):
    part = added(mine, theirs)
    if lax.axis_size("ch") == 2:
        half = part.shape[0] // 2
        part = added(part[:half], swap(part[half:].astype(BF), "ch"))
    elif lax.axis_size("ch") > 2:
        part = lax.psum_scatter(part.astype(BF), "ch", scatter_dimension=0, tiled=True)
    return part.astype(BF)


def ranks_return(parts, rows):
    pack = jnp.concatenate([p.reshape(RANKS, rows, -1) for p in parts], 2)
    return lax.all_to_all(pack, TEAM, split_axis=0, concat_axis=0, tiled=True)


def by_rank(weight):
    rows = weight.shape[0]
    return weight.reshape(rows, RANKS, -1).transpose(1, 0, 2)


def to_columns(pieces):
    return pieces.transpose(1, 0, 2).reshape(pieces.shape[1], -1)


def shuffled(rows, sh, sl, ch):
    count, width = rows.shape
    rows = rows.reshape(count, sh, sl, ch, -1).swapaxes(2, 3)
    return relative(relative(rows, "sh", 1), "ch", 2).reshape(count, width)


def unshuffled(rows, sh, sl, ch):
    count, width = rows.shape
    rows = relative(relative(rows.reshape(count, sh, ch, sl, -1), "sh", 1), "ch", 2)
    return rows.swapaxes(2, 3).reshape(count, width)


def shifted(value, steps):
    count = lax.axis_size("ch")
    if count == 1:
        return jnp.zeros_like(value)
    leading, last = max(0, -steps), min(count, count - steps)
    return lax.ppermute(value, "ch", [(at, at + steps) for at in range(leading, last)])


def entering(decay, state, reverse):
    count = lax.axis_size("ch")
    if count == 1:
        return jnp.zeros_like(state)
    if count == 2:
        return shifted(state, -1 if reverse else 1)
    place = lax.axis_index("ch")
    ahead = count - 1 - place if reverse else place
    decays = lax.all_gather(decay, "ch")
    states = lax.all_gather(state, "ch")

    def one(step, run):
        source = count - 1 - step if reverse else step
        factor = lax.dynamic_index_in_dim(decays, source, 0, False)
        return factor[:, None] * run + lax.dynamic_index_in_dim(states, source, 0, False).astype(
            F32
        )

    return lax.fori_loop(0, ahead, one, jnp.zeros(state.shape, F32)).astype(state.dtype)


def inverse_root(values):
    return lax.rsqrt(jnp.mean(values * values, axis=-1, keepdims=True) + epsilon)


def norm_back(values, scaled, upstream):
    normed = values * scaled
    return scaled * (upstream - normed * jnp.mean(upstream * normed, axis=-1, keepdims=True))


def silu_value(values):
    return values * jax.nn.sigmoid(values)


def silu_slope(values):
    sigmoid_part = jax.nn.sigmoid(values)
    return sigmoid_part * (1.0 + values * (1.0 - sigmoid_part))


def dot(operand, against, at, precision=None):
    return lax.dot_general(
        operand, against, (((at[0],), (at[1],)), ((), ())), precision=precision, preferred_element_type=F32
    )


def exact(operand, against, at):
    return dot(operand, against, at, lax.Precision.HIGHEST)


TILE = 2 * BLOCK
EDGE = 16
LANES = 512
INNER = DI // RANKS
HEADS = HM // RANKS
SIDE = 2 * NS // RANKS
CONV = INNER + SIDE


def call(kernel, grid, in_specs, out_specs, out_shape, scratch=(), scalars=0):
    return pl.pallas_call(
        kernel,
        grid_spec=pltpu.PrefetchScalarGridSpec(
            num_scalar_prefetch=scalars,
            grid=grid,
            in_specs=in_specs,
            out_specs=out_specs,
            scratch_shapes=list(scratch),
        ),
        out_shape=out_shape,
        compiler_params=pltpu.CompilerParams(vmem_limit_bytes=48 * 1024 * 1024),
        cost_estimate=pl.CostEstimate(flops=10**9, bytes_accessed=10**6, transcendentals=0),
    )


def shape(dims, dtype=F32):
    return jax.ShapeDtypeStruct(dims, dtype)


def full(array):
    return pl.BlockSpec(array.shape, lambda *at: (0,) * array.ndim)


def tiled(width, rows=TILE):
    return pl.BlockSpec((rows, width), lambda i, *at: (i, 0))


def place_rows(scalars, gathered, rows):
    left, right, left_other, right_other = gathered
    half = left.shape[2]
    own = pl.multiple_of(scalars[0] * BLOCK, BLOCK)
    other = pl.multiple_of((1 - scalars[0]) * BLOCK, BLOCK)
    rows[pl.ds(own, BLOCK), :half] = left[0]
    rows[pl.ds(own, BLOCK), half:] = right[0]
    rows[pl.ds(other, BLOCK), :half] = left_other[0]
    rows[pl.ds(other, BLOCK), half:] = right_other[0]


def gathered_specs(gathered):
    spec = pl.BlockSpec((1,) + gathered[0].shape[1:], lambda i, s: (s[1 + i], 0, 0))
    return [spec] * 4


def halves_product(rows, mine, theirs):
    half = mine.shape[0]
    return dot(rows[:, :half], mine[...], (1, 0)) + dot(rows[:, half:], theirs[...], (1, 0))


def row_root(rows):
    values = rows.astype(F32)
    return lax.rsqrt(jnp.mean(values * values, axis=-1, keepdims=True) + epsilon)


def project_inner_kernel(tiles, scalars, l, r, lo, ro, mine, theirs, halo, taps, steps, pre_ref, conv_ref, side_ref, step_ref, root_ref, edge_ref, rows, line):
    i = pl.program_id(0)
    place_rows(scalars, (l, r, lo, ro), rows)
    values = rows[...]
    root = row_root(values)
    root_ref[...] = root
    pre = halves_product(values, mine, theirs) * root
    pre_ref[...] = pre
    step_ref[...] = dot(values, steps[...], (1, 1)) * root

    @pl.when(i % tiles == 0)
    def _():
        before = halo[0]
        edge = halves_product(before, mine, theirs) * row_root(before)
        edge_ref[0] = edge
        line[:EDGE] = edge

    @pl.when(i % tiles != 0)
    def _():
        line[:EDGE] = line[TILE:]

    line[EDGE:] = pre
    conv = taps[KC : KC + 1, :]
    for k in range(KC):
        conv = conv + taps[k : k + 1, :] * line[EDGE - (KC - 1) + k : EDGE - (KC - 1) + k + TILE, :]
    conv_ref[...] = conv
    last = conv[:, INNER:]
    lane = lax.broadcasted_iota(jnp.int32, last.shape, 1)
    side_ref[...] = jnp.where(lane < SIDE, silu_value(last), last).astype(BF)


def project_inner(scalars, gathered, weight, halo, taps, steps):
    seqs = halo.shape[0]
    total = 2 * 4 * gathered[0].shape[1]
    tiles = total // TILE // seqs
    width = 2 * gathered[0].shape[2]
    return call(
        lambda *refs: project_inner_kernel(tiles, *refs),
        (total // TILE,),
        gathered_specs(gathered)
        + [full(weight[0]), full(weight[1])]
        + [pl.BlockSpec((1, EDGE, width), lambda i, s: (i // tiles, 0, 0)), full(taps), full(steps)],
        [
            tiled(LANES),
            tiled(LANES),
            tiled(2 * SIDE),
            tiled(8),
            tiled(1),
            pl.BlockSpec((1, EDGE, LANES), lambda i, s: (i // tiles, 0, 0)),
        ],
        [
            shape((total, LANES)),
            shape((total, LANES)),
            shape((total, 2 * SIDE), BF),
            shape((total, 8)),
            shape((total, 1)),
            shape((seqs, EDGE, LANES)),
        ],
        [pltpu.VMEM((TILE, width), BF), pltpu.VMEM((EDGE + TILE, LANES), F32)],
        1,
    )(scalars, *gathered, *weight, halo, taps, steps)


def project_gating_kernel(scalars, l, r, lo, ro, mine, theirs, root, gating_ref, query_ref, rows):
    place_rows(scalars, (l, r, lo, ro), rows)
    product = halves_product(rows[...], mine, theirs) * root[...]
    gating_ref[...] = product[:, :INNER]
    query_ref[...] = product[:, INNER:].astype(BF)


def project_gating(scalars, gathered, weight, root):
    total, width = root.shape[0], 2 * gathered[0].shape[2]
    return call(
        project_gating_kernel,
        (total // TILE,),
        gathered_specs(gathered) + [full(weight[0]), full(weight[1]), tiled(1)],
        [tiled(INNER), tiled(HD)],
        [shape((total, INNER)), shape((total, HD), BF)],
        [pltpu.VMEM((TILE, width), BF)],
        1,
    )(scalars, *gathered, *weight, root)


def rows_back_kernel(scalars, l, r, lo, ro, mine, theirs, ssm, gating, root, gain, mixer_ref, attn_ref, along_ref, gain_ref, rows):
    place_rows(scalars, (l, r, lo, ro), rows)
    product = halves_product(rows[...], mine, theirs)
    mixer = product[:, :INNER]
    mixer_ref[...] = mixer
    attn_ref[...] = product[:, INNER:].astype(BF)
    norm = ssm[...] * silu_value(gating[...]) * root[...]
    together = mixer * norm
    along_ref[0] = exact(jnp.ones((8, INNER), F32), together * gain[...], (1, 1))

    @pl.when(pl.program_id(0) == 0)
    def _():
        gain_ref[...] = jnp.zeros_like(gain_ref)

    gain_ref[...] += jnp.sum(together, axis=0, keepdims=True)


def rows_back(scalars, gathered, weight, ssm, gating, root, gain):
    total, width = root.shape[0], 2 * gathered[0].shape[2]
    tiles = total // TILE
    return call(
        rows_back_kernel,
        (tiles,),
        gathered_specs(gathered)
        + [full(weight[0]), full(weight[1]), tiled(INNER), tiled(INNER), tiled(1), full(gain)],
        [
            tiled(INNER),
            tiled(HD),
            pl.BlockSpec((1, 8, TILE), lambda i, s: (i, 0, 0)),
            pl.BlockSpec((1, INNER), lambda i, s: (0, 0)),
        ],
        [
            shape((total, INNER)),
            shape((total, HD), BF),
            shape((tiles, 8, TILE)),
            shape((1, INNER)),
        ],
        [pltpu.VMEM((TILE, width), BF)],
        1,
    )(scalars, *gathered, *weight, ssm, gating, root, gain)


def back_dot_kernel(terms, halves, scalars, *refs):
    ins, outs = refs[: terms * 4], refs[terms * 4 :]
    i = pl.program_id(0)
    for half in range(2):
        product = None
        for t in range(terms):
            first, second = ins[4 * t], ins[4 * t + 1]
            weight = ins[4 * t + 2 + half]
            rows = jnp.concatenate([first[...], second[...]], 0)
            at = (1, 1) if weight.shape[1] == rows.shape[1] else (1, 0)
            one = dot(rows, weight[...], at)
            product = one if product is None else product + one
        product = product.reshape(outs[half].shape)

        @pl.when(i < halves)
        def _():
            outs[2 + half][...] = product.astype(BF)

        @pl.when(i >= halves)
        def _():
            outs[half][...] = product


def back_dot(order, terms):
    total = terms[0][0].shape[0]
    half = terms[0][1][0].shape[0]
    halves = total // TILE // 2
    specs, arrays = [], []
    for rows, weights in terms:
        width = rows.shape[1]
        specs += [
            pl.BlockSpec((BLOCK, width), lambda i, s: (s[(2 * i + 4) % 8], 0)),
            pl.BlockSpec((BLOCK, width), lambda i, s: (s[(2 * i + 5) % 8], 0)),
            full(weights[0]),
            full(weights[1]),
        ]
        arrays += [rows, rows, *weights]
    kept_spec = pl.BlockSpec((2, BLOCK, half), lambda i, s: (jnp.maximum(i - halves, 0), 0, 0))
    given_spec = pl.BlockSpec((2, BLOCK, half), lambda i, s: (jnp.minimum(i, halves - 1), 0, 0))
    blocks = total // BLOCK // 2
    return call(
        lambda *refs: back_dot_kernel(len(terms), halves, *refs),
        (2 * halves,),
        specs,
        [kept_spec, kept_spec, given_spec, given_spec],
        [shape((blocks, BLOCK, half))] * 2 + [shape((blocks, BLOCK, half), BF)] * 2,
        (),
        1,
    )(order, *arrays)


def grad_dot_kernel(scalars, own, other, against, *refs):
    out, ordered = refs[-2], refs[-1]

    @pl.when(pl.program_id(0) == 0)
    def _():
        for k in range(8):
            start = pl.multiple_of(scalars[k] * BLOCK, BLOCK)
            ordered[k * BLOCK : (k + 1) * BLOCK] = against[pl.ds(start, BLOCK), :]

    tile = own.shape[2]
    rows = own.shape[0] * own.shape[1]
    product = dot(own[...].reshape(rows, tile), ordered[:rows], (0, 0))
    product = product + dot(other[...].reshape(rows, tile), ordered[rows:], (0, 0))
    out[...] = product.astype(out.dtype)


def grad_dot(order, own, other, against, dtype):
    half = own.shape[2]
    total, width = against.shape
    tile = 512
    spec = pl.BlockSpec((own.shape[0], own.shape[1], tile), lambda i, s: (0, 0, i))
    return call(
        grad_dot_kernel,
        (half // tile,),
        [spec, spec, full(against)],
        pl.BlockSpec((tile, width), lambda i, s: (i, 0)),
        shape((half, width), dtype),
        [pltpu.VMEM((total, width), BF)],
        1,
    )(order, own, other, against)


def peers_half(order, gathered, against):
    left, right, left_other, right_other = gathered
    theirs = swap(grad_dot(order, right, right_other, against, BF), "sh")
    return grad_dot(order, left, left_other, against, F32), theirs


def feed_kernel(parts, l, r, lo, ro, cl, cr, clo, cro, gm, gt, lm, lt, dm, dt, active_ref, gate_ref, lift_ref):
    i = pl.program_id(0)

    def run(left, right, cleft, cright):
        half = left.shape[2]

        def product(a, b, mine, theirs):
            return dot(a[...].reshape(TILE, half), mine[...], (1, 0)) + dot(
                b[...].reshape(TILE, half), theirs[...], (1, 0)
            )

        gate = product(left, right, gm, gt)
        lift = product(left, right, lm, lt)
        grad = product(cleft, cright, dm, dt)
        sigmoid_part = jax.nn.sigmoid(gate)
        swish = gate * sigmoid_part
        active_ref[...] = (swish * lift).astype(BF)
        gate_ref[...] = (
            grad * lift * sigmoid_part * (1.0 + gate * (1.0 - sigmoid_part))
        ).astype(BF)
        lift_ref[...] = (grad * swish).astype(BF)

    @pl.when(i < parts)
    def _():
        run(l, r, cl, cr)

    @pl.when(i >= parts)
    def _():
        run(lo, ro, clo, cro)


def feed_block(rows, cotangent, gate, lift, drop):
    blocks, count, half = rows[0].shape
    total = 2 * blocks * count
    parts = total // TILE // 2
    own = pl.BlockSpec((2, count, half), lambda i: (jnp.minimum(i, parts - 1), 0, 0))
    other = pl.BlockSpec((2, count, half), lambda i: (jnp.maximum(i - parts, 0), 0, 0))
    weights = [*gate, *lift, *drop]
    return call(
        lambda *refs: feed_kernel(parts, *refs),
        (2 * parts,),
        [own, own, other, other] * 2 + [full(w) for w in weights],
        [tiled(LANES)] * 3,
        [shape((total, LANES), BF)] * 3,
    )(*rows, *cotangent, *weights)


def scores_of(place, queries, keys):
    count, whole = queries.shape[0], keys.shape[0]
    scores = dot(queries, keys, (1, 1)) * HD**-0.5
    row = place + pl.program_id(1) * count + lax.broadcasted_iota(jnp.int32, (count, whole), 0)
    column = lax.broadcasted_iota(jnp.int32, (count, whole), 1)
    return scores, row >= column


def attend_kernel(place, queries, key_value, out_ref, log_ref):
    keys, values = key_value[0, :, :HD], key_value[0, :, HD:]
    scores, visible = scores_of(place[0], queries[...], keys)
    scores = jnp.where(visible, scores, negative)
    top = jnp.max(scores, axis=-1, keepdims=True)
    weights = jnp.exp(scores - top)
    total = jnp.sum(weights, axis=-1, keepdims=True)
    log_ref[...] = top + jnp.log(total)
    out_ref[...] = dot(weights.astype(BF), values, (1, 0)) / total


def attend_specs(seqs, total):
    tiles = total // TILE // seqs
    rows = lambda width: pl.BlockSpec((TILE, width), lambda n, i, s: (n * tiles + i, 0))
    return (seqs, tiles), rows


def attend(place, queries, key_value):
    seqs, whole, width = key_value.shape
    total = queries.shape[0]
    grid, rows = attend_specs(seqs, total)
    return call(
        attend_kernel,
        grid,
        [rows(HD), pl.BlockSpec((1, whole, width), lambda n, i, s: (n, 0, 0))],
        [rows(HD), rows(1)],
        [shape((total, HD)), shape((total, 1))],
        (),
        1,
    )(place, queries, key_value)


def attend_back_kernel(place, queries, grads, attended, logs, root, key_value, query_ref, sum_ref):
    keys, values = key_value[0, :, :HD], key_value[0, :, HD:]
    scores, visible = scores_of(place[0], queries[...], keys)
    probs = jnp.where(visible, jnp.exp(scores - logs[...]), 0.0)
    grad = grads[...]
    delta = jnp.sum(grad.astype(F32) * attended[...], axis=-1, keepdims=True)
    scores_grad = (probs * (dot(grad, values, (1, 1)) - delta)).astype(BF)
    query_ref[...] = (dot(scores_grad, keys, (1, 0)) * (HD**-0.5 * root[...])).astype(BF)

    @pl.when(pl.program_id(1) == 0)
    def _():
        sum_ref[...] = jnp.zeros_like(sum_ref)

    sum_ref[0, :, :HD] += dot(scores_grad, queries[...], (0, 0)) * HD**-0.5
    sum_ref[0, :, HD:] += dot(probs.astype(BF), grad, (0, 0))


def attend_back(place, queries, grads, attended, logs, root, key_value):
    seqs, whole, width = key_value.shape
    total = queries.shape[0]
    grid, rows = attend_specs(seqs, total)
    sums = pl.BlockSpec((1, whole, width), lambda n, i, s: (n, 0, 0))
    return call(
        attend_back_kernel,
        grid,
        [rows(HD), rows(HD), rows(HD), rows(1), rows(1), sums],
        [rows(HD), sums],
        [shape((total, HD), BF), shape((seqs, whole, width))],
        (),
        1,
    )(place, queries, grads, attended, logs, root, key_value)


def over_heads(values):
    rows = values.shape[0]
    return jnp.concatenate(
        [jnp.broadcast_to(values[:, h : h + 1], (rows, PM)) for h in range(HEADS)], 1
    )


def head_sums(values):
    channel = lax.broadcasted_iota(jnp.int32, (INNER, 8), 0)
    head = lax.broadcasted_iota(jnp.int32, (INNER, 8), 1)
    return exact(values, jnp.where(channel // PM == head, 1.0, 0.0), (1, 0))


def triangle():
    row = lax.broadcasted_iota(jnp.int32, (BLOCK, BLOCK), 0)
    column = lax.broadcasted_iota(jnp.int32, (BLOCK, BLOCK), 1)
    return row, column


def block_steps(step_pre, head):
    arg = step_pre[...] + head[0:1, :]
    size = jnp.maximum(arg, 0.0) + jnp.log1p(jnp.exp(-jnp.abs(arg)))
    row, column = triangle()
    cum = exact(jnp.where(row >= column, 1.0, 0.0), size * head[1:2, :], (1, 0))
    return arg, size, cum


def as_rows(values):
    row, column = triangle()
    return exact(values, jnp.where(row == column, 1.0, 0.0), (0, 0))


def as_columns(values):
    row, column = triangle()
    return exact(jnp.where(row == column, 1.0, 0.0), values, (1, 1))


def states_kernel(blocks, step_pre, head, conv, io, out_ref, decay_ref, run):
    i = pl.program_id(0)
    _, size, cum = block_steps(step_pre, head)
    last = cum[BLOCK - 1 :, :]
    feeding = jnp.exp(last - cum) * size
    inner = silu_value(conv[:, :INNER])
    fresh = dot(io[:, :NS], (over_heads(feeding) * inner).astype(BF), (0, 0))
    decay = over_heads(jnp.exp(last))

    @pl.when(i % blocks == 0)
    def _():
        run[...] = fresh
        decay_ref[0] = decay

    @pl.when(i % blocks != 0)
    def _():
        run[...] = decay * run[...] + fresh
        decay_ref[0] = decay_ref[0] * decay

    @pl.when(i % blocks == blocks - 1)
    def _():
        out_ref[0] = run[...].astype(BF)


def states(seqs, step_pre, head, conv, io):
    total = conv.shape[0]
    blocks = total // BLOCK // seqs
    return call(
        lambda *refs: states_kernel(blocks, *refs),
        (total // BLOCK,),
        [tiled(8, BLOCK), full(head), tiled(LANES, BLOCK), tiled(2 * NS, BLOCK)],
        [
            pl.BlockSpec((1, NS, INNER), lambda i: (i // blocks, 0, 0)),
            pl.BlockSpec((1, 1, INNER), lambda i: (i // blocks, 0, 0)),
        ],
        [shape((seqs, NS, INNER), BF), shape((seqs, 1, INNER))],
        [pltpu.VMEM((NS, INNER), F32)],
    )(step_pre, head, conv, io)


def fading_of(cum, cum_rows, h):
    row, column = triangle()
    span = cum[:, h : h + 1] - cum_rows[h : h + 1, :]
    return jnp.where(row >= column, jnp.exp(jnp.minimum(span, 0.0)), 0.0)


def ssm_kernel(blocks, step_pre, head, conv, io, gating, entry, ssm_ref, carried_ref, square_ref, run):
    i = pl.program_id(0)

    @pl.when(i % blocks == 0)
    def _():
        run[...] = entry[0].astype(F32)

    _, size, cum = block_steps(step_pre, head)
    size_rows, cum_rows = as_rows(size), as_rows(cum)
    last = cum[BLOCK - 1 :, :]
    inner = silu_value(conv[:, :INNER])
    inner_low = inner.astype(BF)
    in_state, out_state = io[:, :NS], io[:, NS:]
    carried = run[...].astype(BF)
    carried_ref[0] = carried
    pairing = dot(out_state, in_state, (1, 1))
    within = []
    for h in range(HEADS):
        mixing = fading_of(cum, cum_rows, h) * pairing * size_rows[h : h + 1, :]
        within.append(dot(mixing.astype(BF), inner_low[:, h * PM : (h + 1) * PM], (1, 0)))
    readout = dot(out_state, carried, (1, 0))
    ssm = (
        jnp.concatenate(within, 1)
        + over_heads(jnp.exp(cum)) * readout
        + over_heads(head[2:3, :]) * inner
    )
    ssm_ref[...] = ssm
    gated = ssm * silu_value(gating[...])
    square_ref[0] = exact(jnp.ones((8, INNER), F32), gated * gated, (1, 1))
    feeding = jnp.exp(last - cum) * size
    fresh = dot(in_state, (over_heads(feeding) * inner).astype(BF), (0, 0))
    run[...] = over_heads(jnp.exp(last)) * run[...] + fresh


def ssm_block(seqs, step_pre, head, conv, io, gating, entry):
    total = conv.shape[0]
    blocks = total // BLOCK // seqs
    return call(
        lambda *refs: ssm_kernel(blocks, *refs),
        (total // BLOCK,),
        [
            tiled(8, BLOCK),
            full(head),
            tiled(LANES, BLOCK),
            tiled(2 * NS, BLOCK),
            tiled(INNER, BLOCK),
            pl.BlockSpec((1, NS, INNER), lambda i: (i // blocks, 0, 0)),
        ],
        [
            tiled(INNER, BLOCK),
            pl.BlockSpec((1, NS, INNER), lambda i: (i, 0, 0)),
            pl.BlockSpec((1, 8, BLOCK), lambda i: (i, 0, 0)),
        ],
        [
            shape((total, INNER)),
            shape((total // BLOCK, NS, INNER), BF),
            shape((total // BLOCK, 8, BLOCK)),
        ],
        [pltpu.VMEM((NS, INNER), F32)],
    )(step_pre, head, conv, io, gating, entry)


def states_back_kernel(blocks, step_pre, head, io, mixer, ssm, gating, mixer_root, along, gain, root, grad_ref, gating_ref, out_ref, run):
    i = pl.program_id(0)
    _, _, cum = block_steps(step_pre, head)
    gate = gating[...]
    sigmoid_part = jax.nn.sigmoid(gate)
    act = gate * sigmoid_part
    values = ssm[...]
    norm = values * act * mixer_root[...]
    gated_grad = mixer_root[...] * (mixer[...] * gain[...] - norm * along[...])
    grad = gated_grad * act
    grad_ref[...] = grad
    slope = sigmoid_part * (1.0 + gate * (1.0 - sigmoid_part))
    gating_ref[...] = (gated_grad * values * slope * root[...]).astype(BF)
    grown = (over_heads(jnp.exp(cum)) * grad).astype(BF)
    fresh = dot(io[:, NS:], grown, (0, 0))
    decay = over_heads(jnp.exp(cum[BLOCK - 1 :, :]))

    @pl.when(i % blocks == 0)
    def _():
        run[...] = fresh

    @pl.when(i % blocks != 0)
    def _():
        run[...] = decay * run[...] + fresh

    @pl.when(i % blocks == blocks - 1)
    def _():
        out_ref[0] = run[...].astype(BF)


def states_back(seqs, step_pre, head, io, mixer, ssm, gating, mixer_root, along, gain, root):
    total = ssm.shape[0]
    many = total // BLOCK
    blocks = many // seqs
    back = lambda width: pl.BlockSpec((BLOCK, width), lambda i: (many - 1 - i, 0))
    return call(
        lambda *refs: states_back_kernel(blocks, *refs),
        (many,),
        [back(8), full(head), back(2 * NS), back(INNER), back(INNER), back(INNER)]
        + [back(1), back(1), full(gain), back(1)],
        [
            back(INNER),
            back(INNER),
            pl.BlockSpec((1, NS, INNER), lambda i: (seqs - 1 - i // blocks, 0, 0)),
        ],
        [shape((total, INNER)), shape((total, INNER), BF), shape((seqs, NS, INNER), BF)],
        [pltpu.VMEM((NS, INNER), F32)],
    )(step_pre, head, io, mixer, ssm, gating, mixer_root, along, gain, root)


def ssm_back_kernel(blocks, side, step_pre, head, conv, io, grads, carried_ref, entry, key_value, root, conv_ref, parts_ref, step_ref, sums_ref, later):
    i = pl.program_id(0)

    @pl.when(i % blocks == 0)
    def _():
        later[...] = entry[0].astype(F32)

    @pl.when(i == 0)
    def _():
        sums_ref[...] = jnp.zeros_like(sums_ref)

    arg, size, cum = block_steps(step_pre, head)
    size_rows, cum_rows = as_rows(size), as_rows(cum)
    last = cum[BLOCK - 1 :, :]
    growth, to_end, decay = jnp.exp(cum), jnp.exp(last - cum), jnp.exp(last)
    feeding = to_end * size
    conv_sum = conv[:, :INNER]
    inner = silu_value(conv_sum)
    inner_low = inner.astype(BF)
    in_state, out_state = io[:, :NS], io[:, NS:]
    carried = carried_ref[0]
    after = later[...]
    after_low = after.astype(BF)
    grad = grads[...]
    grad_low = grad.astype(BF)
    pairing = dot(out_state, in_state, (1, 1))
    readout = dot(out_state, carried, (1, 0))
    spread = dot(in_state, after_low, (1, 0))
    grown = (over_heads(growth) * grad).astype(BF)
    feeding_wide = over_heads(feeding)
    fed_inner = (feeding_wide * inner).astype(BF)
    pairing_grad = jnp.zeros((BLOCK, BLOCK), F32)
    inner_parts, flows, step_rows = [], [], []
    for h in range(HEADS):
        at = slice(h * PM, (h + 1) * PM)
        fading = fading_of(cum, cum_rows, h)
        sized = size_rows[h : h + 1, :]
        mixing = (fading * pairing * sized).astype(BF)
        faded = dot(grad_low[:, at], inner_low[:, at], (1, 1)) * fading
        pairing_grad = pairing_grad + faded * sized
        stepwise = faded * pairing
        step_rows.append(jnp.sum(stepwise, axis=0, keepdims=True))
        flows.append(jnp.sum(stepwise * sized, axis=1, keepdims=True))
        inner_parts.append(dot(mixing, grad_low[:, at], (0, 0)))
    empty_row, empty_column = jnp.zeros((2, BLOCK), F32), jnp.zeros((BLOCK, 2), F32)
    step_rows = jnp.concatenate(step_rows + [empty_row], 0)
    flow = jnp.concatenate(flows + [empty_column], 1)
    pairing_low = pairing_grad.astype(BF)
    out_grad = dot(pairing_low, in_state, (1, 0)) + dot(grown, carried, (1, 1))
    in_grad = dot(pairing_low, out_state, (0, 0)) + dot(fed_inner, after_low, (1, 1))
    inner_grad = (
        jnp.concatenate(inner_parts, 1) + over_heads(head[2:3, :]) * grad + feeding_wide * spread
    )
    conv_ref[...] = inner_grad * silu_slope(conv_sum)
    for rank in range(RANKS):
        source = in_grad if rank < RANKS // 2 else out_grad
        at = (rank % 4) * SIDE
        own = jnp.where(side[0] == rank // 4, 1.0, 0.0)
        parts_ref[rank] = jnp.concatenate(
            [source[:, at : at + SIDE], key_value[:, at : at + SIDE] * own], 1
        ).astype(BF)
    feeding_grad = head_sums(spread * inner)
    fed = feeding_grad * feeding
    through = jnp.sum(after * carried.astype(F32), axis=0, keepdims=True)
    through = head_sums(jnp.broadcast_to(through, (8, INNER)))[:1]
    last_grad = jnp.sum(fed, axis=0, keepdims=True) + through * decay
    cum_grad = flow - as_columns(step_rows * size_rows) + head_sums(grad * readout) * growth - fed
    row, column = triangle()
    increment = exact(jnp.where(column >= row, 1.0, 0.0), cum_grad, (1, 0)) + last_grad
    rates = head[1:2, :]
    step_grad = as_columns(step_rows) + feeding_grad * to_end + increment * rates
    arg_grad = step_grad * jax.nn.sigmoid(arg)
    step_ref[...] = (arg_grad * root[...]).astype(BF)
    skip = jnp.broadcast_to(jnp.sum(grad * inner, axis=0, keepdims=True), (8, INNER))
    sums_ref[0:1, :] += jnp.sum(arg_grad, axis=0, keepdims=True)
    sums_ref[1:2, :] += jnp.sum(increment * size, axis=0, keepdims=True) * rates
    sums_ref[2:3, :] += head_sums(skip)[:1]
    later[...] = over_heads(decay) * after + dot(out_state, grown, (0, 0))


def ssm_back(side, seqs, step_pre, head, conv, io, grads, carried, entry, key_value, root):
    total = conv.shape[0]
    many = total // BLOCK
    blocks = many // seqs
    back = lambda width: pl.BlockSpec((BLOCK, width), lambda i, s: (many - 1 - i, 0))
    return call(
        lambda *refs: ssm_back_kernel(blocks, *refs),
        (many,),
        [back(8), full(head), back(LANES), back(2 * NS), back(INNER)]
        + [
            pl.BlockSpec((1, NS, INNER), lambda i, s: (many - 1 - i, 0, 0)),
            pl.BlockSpec((1, NS, INNER), lambda i, s: (seqs - 1 - i // blocks, 0, 0)),
            back(2 * HD),
            back(1),
        ],
        [
            back(INNER),
            pl.BlockSpec((RANKS, BLOCK, 2 * SIDE), lambda i, s: (0, many - 1 - i, 0)),
            back(8),
            pl.BlockSpec((8, 8), lambda i, s: (0, 0)),
        ],
        [
            shape((total, INNER)),
            shape((RANKS, total, 2 * SIDE), BF),
            shape((total, 8), BF),
            shape((8, 8)),
        ],
        [pltpu.VMEM((NS, INNER), F32)],
        1,
    )(side, step_pre, head, conv, io, grads, carried, entry, key_value, root)


def conv_back_kernel(tiles, inner, parts, conv, pre, edge, grad_ref, sums_ref, line):
    i = pl.program_id(0)
    got = jnp.sum(parts[...].astype(F32), axis=0)
    lane = lax.broadcasted_iota(jnp.int32, got.shape, 1)
    got = jnp.where(lane < SIDE, got * silu_slope(conv[:, INNER:]), got)
    grad = jnp.concatenate([inner[...], got], 1)
    grad_ref[...] = grad

    @pl.when(i % tiles == 0)
    def _():
        line[:EDGE] = edge[0]

    @pl.when(i % tiles != 0)
    def _():
        line[:EDGE] = line[TILE:]

    @pl.when(i == 0)
    def _():
        sums_ref[...] = jnp.zeros_like(sums_ref)

    line[EDGE:] = pre[...]
    for k in range(KC):
        before = line[EDGE - (KC - 1) + k : EDGE - (KC - 1) + k + TILE, :]
        sums_ref[k : k + 1, :] += jnp.sum(grad * before, axis=0, keepdims=True)
    sums_ref[KC : KC + 1, :] += jnp.sum(grad, axis=0, keepdims=True)


def conv_back(inner, parts, conv, pre, edge):
    total = conv.shape[0]
    tiles = total // TILE // edge.shape[0]
    return call(
        lambda *refs: conv_back_kernel(tiles, *refs),
        (total // TILE,),
        [
            tiled(INNER),
            pl.BlockSpec((RANKS, TILE, 2 * SIDE), lambda i: (0, i, 0)),
            tiled(LANES),
            tiled(LANES),
            pl.BlockSpec((1, EDGE, LANES), lambda i: (i // tiles, 0, 0)),
        ],
        [tiled(LANES), pl.BlockSpec((8, LANES), lambda i: (0, 0))],
        [shape((total, LANES)), shape((8, LANES))],
        [pltpu.VMEM((EDGE + TILE, LANES), F32)],
    )(inner, parts, conv, pre, edge)


def pre_back_kernel(tiles, grad, after, follow, taps, root, out_ref, line):
    i = pl.program_id(0)
    line[:TILE] = grad[...]

    @pl.when(i % tiles == tiles - 1)
    def _():
        line[TILE:] = follow[0]

    @pl.when(i % tiles != tiles - 1)
    def _():
        line[TILE:] = after[...]

    total = taps[KC - 1 : KC, :] * line[:TILE, :]
    for k in range(KC - 1):
        total = total + taps[k : k + 1, :] * line[KC - 1 - k : KC - 1 - k + TILE, :]
    out_ref[...] = (total * root[...]).astype(BF)


def pre_back(grad, follow, taps, root):
    total = grad.shape[0]
    tiles = total // TILE // follow.shape[0]
    last = total // EDGE - 1
    return call(
        lambda *refs: pre_back_kernel(tiles, *refs),
        (total // TILE,),
        [
            tiled(LANES),
            pl.BlockSpec((EDGE, LANES), lambda i: (jnp.minimum((i + 1) * (TILE // EDGE), last), 0)),
            pl.BlockSpec((1, EDGE, LANES), lambda i: (i // tiles, 0, 0)),
            full(taps),
            tiled(1),
        ],
        tiled(LANES),
        shape((total, LANES), BF),
        [pltpu.VMEM((TILE + EDGE, LANES), F32)],
    )(grad, grad, follow, taps, root)


def local(
    tokens,
    cotangent,
    norm_gain,
    gating_weight,
    inner_weight,
    state_weight,
    step_weight,
    conv_weight,
    conv_bias,
    mixer_gain,
    mixer_out,
    query_weight,
    key_weight,
    value_weight,
    output_weight,
    feed_gain,
    gate_matrix,
    lift_matrix,
    drop_matrix,
    step_bias,
    decay_log,
    skip_scale,
):
    sh, sl, ch = lax.axis_size("sh"), lax.axis_size("sl"), lax.axis_size("ch")
    world = sh * sl * ch * 4
    rows, width = tokens.shape
    drows = norm_gain.shape[0]
    my_sl, my_zl, my_core = (lax.axis_index(axis) for axis in TEAM)
    rank = (my_sl * 2 + my_zl) * 2 + my_core
    total = RANKS * rows
    count = 4 * rows
    whole = ch * count

    order = team_order()
    straight = jnp.arange(8, dtype=jnp.int32)
    tiles = [((z ^ my_zl) * 2 + (s ^ my_sl)) for s in (0, 1) for z in (0, 1)]
    scalars = jnp.stack([my_core, *tiles]).astype(jnp.int32)
    place = (lax.axis_index("ch") * count).astype(jnp.int32).reshape(1)
    side_index = my_sl.astype(jnp.int32).reshape(1)

    def scaled(weight, gain):
        return (weight.astype(F32) * gain.astype(F32)[:, None]).astype(BF)

    key_value = jnp.stack(
        [key_weight.reshape(drows, HK, 2, SIDE), value_weight.reshape(drows, HK, 2, SIDE)], 2
    ).reshape(drows, RANKS * SIDE)
    pack_in = jnp.concatenate(
        [
            by_rank(scaled(w, norm_gain))
            for w in (inner_weight, state_weight, key_value, gating_weight, query_weight)
        ],
        2,
    )
    own_tokens = shuffled(tokens, sh, sl, ch)
    own_cotangent = shuffled(cotangent, sh, sl, ch)
    mixed_in = ranks_exchange(pack_in)
    team_tokens = team_gather(own_tokens)
    w_inner = peers_gather(mixed_in[:, :LANES])
    w_gating = peers_gather(mixed_in[:, LANES:])

    conv_own, gain_own = conv_weight.shape[1], mixer_gain.shape[0]
    step_sent = jnp.broadcast_to(
        scaled(step_weight, norm_gain).T.reshape(1, sl, 1, 4, HEADS * drows),
        (sh, sl, ch, 4, HEADS * drows),
    ).reshape(world, HEADS * drows)
    shared = jnp.concatenate([conv_weight.reshape(-1), conv_bias, mixer_gain])
    small = lax.all_to_all(
        jnp.concatenate([jnp.broadcast_to(shared[None], (world, shared.shape[0])), step_sent], 1),
        WORLD,
        split_axis=0,
        concat_axis=0,
        tiled=True,
    )
    at = (KC + 1) * conv_own
    wide_conv = small[:, :at].reshape(world, KC + 1, conv_own)
    wide_conv = wide_conv.transpose(1, 0, 2).reshape(KC + 1, -1).astype(F32)
    wide_gain = small[:, at : at + gain_own].reshape(1, -1).astype(F32)
    own_step = small[:, at + gain_own :].reshape(sh, sl, ch, 4, HEADS, drows).swapaxes(1, 2)
    own_step = relative(relative(own_step, "sh", 0), "ch", 1)
    own_step = own_step.reshape(-1, HEADS, drows).swapaxes(0, 1).reshape(HEADS, width)
    own_step = jnp.pad(own_step, ((0, 8 - HEADS), (0, 0)))
    taps = jnp.concatenate(
        [
            lax.dynamic_slice_in_dim(wide_conv, rank * INNER, INNER, 1),
            lax.dynamic_slice_in_dim(wide_conv, DI + rank * SIDE, SIDE, 1),
            jnp.zeros((KC + 1, LANES - CONV), F32).at[KC - 1].set(1.0),
        ],
        1,
    )
    taps = jnp.pad(taps, ((0, 8 - KC - 1), (0, 0)))
    own_gain = lax.dynamic_slice_in_dim(wide_gain, rank * INNER, INNER, 1)
    head = jnp.stack([step_bias, -jnp.exp(decay_log), skip_scale])
    head = lax.dynamic_slice_in_dim(head, rank * HEADS, HEADS, 1)
    head = jnp.pad(head, ((0, 5), (0, 8 - HEADS)))

    ends = []
    for seq in range(sl):
        at_block = 2 * (1 - my_zl) + (seq ^ my_sl)
        halves = []
        for own, other in ((team_tokens[0], team_tokens[2]), (team_tokens[1], team_tokens[3])):
            own = lax.dynamic_index_in_dim(own[:, rows - EDGE :], at_block, 0, False)
            other = lax.dynamic_index_in_dim(other[:, rows - EDGE :], at_block, 0, False)
            halves.append(jnp.where(my_core == 1, own, other))
        ends.append(jnp.concatenate(halves, 1))
    halo = shifted(jnp.stack(ends), 1)
    if ch == 2:
        halo = jnp.flip(halo.reshape(sl, EDGE, sh, ch, -1), 3).reshape(sl, EDGE, width)

    pre, conv, side, step_pre, root, edge = project_inner(
        scalars, team_tokens, w_inner, halo, taps, own_step
    )
    sides = lax.all_gather(side, TEAM)
    gating, queries = project_gating(scalars, team_tokens, w_gating, root)
    io = sides[:, :, :SIDE].transpose(1, 0, 2).reshape(total, 2 * NS)
    key_value_rows = lax.dynamic_slice_in_dim(sides[:, :, SIDE:], my_sl * 4, 4, 0)
    key_value_rows = key_value_rows.transpose(1, 0, 2).reshape(sl, count, 2 * HD)
    if ch == 2:
        key_value_rows = paired(key_value_rows, swap(key_value_rows, "ch"), "ch", 1)
        key_value_rows = key_value_rows.reshape(sl, whole, 2 * HD)
    elif ch > 2:
        key_value_rows = lax.all_gather(key_value_rows, "ch", axis=1, tiled=True)
    leaving, piece_decay = states(sl, step_pre, head, conv, io)
    entry = entering(piece_decay[:, 0], leaving, False)
    attended, logs = attend(place, queries, key_value_rows)
    ssm, carried, square = ssm_block(sl, step_pre, head, conv, io, gating, entry)
    mixer_root = lax.rsqrt(team_sum(square[:, 0]) / DI + epsilon).reshape(total, 1)
    branch_rows = jnp.concatenate(
        [(ssm * silu_value(gating) * mixer_root * own_gain).astype(BF), attended.astype(BF)], 1
    )

    pack_rest = jnp.concatenate(
        [by_rank(mixer_out.T), by_rank(output_weight.T)]
        + [by_rank(scaled(w, feed_gain)) for w in (gate_matrix, lift_matrix)]
        + [by_rank(drop_matrix.T)],
        2,
    )
    mixed_rest = ranks_exchange(pack_rest)
    w_out = peers_gather(mixed_rest[:, :LANES])
    w_gate = peers_gather(mixed_rest[:, LANES : 2 * LANES])
    w_lift = peers_gather(mixed_rest[:, 2 * LANES : 3 * LANES])
    w_drop = peers_gather(mixed_rest[:, 3 * LANES :])
    team_cotangent = team_gather(own_cotangent)

    branch = team_scatter(back_dot(order, [(branch_rows, w_out)]))

    residual = own_tokens.astype(F32) + branch
    feed_root = inverse_root(residual)
    feed_rows = team_gather((residual * feed_root).astype(BF))
    active, gate_rows_grad, lift_rows_grad = feed_block(
        feed_rows, team_cotangent, w_gate, w_lift, w_drop
    )
    feed_grad = team_scatter(
        back_dot(straight, [(gate_rows_grad, w_gate), (lift_rows_grad, w_lift)])
    )
    residual_grad = own_cotangent.astype(F32) + norm_back(residual, feed_root, feed_grad)
    branch_grad = team_gather(residual_grad.astype(BF))
    drop_half = peers_half(straight, team_cotangent, active)
    gate_half = peers_half(straight, feed_rows, gate_rows_grad)
    lift_half = peers_half(straight, feed_rows, lift_rows_grad)
    active, drop_half, gate_half, lift_half, branch_grad = lax.optimization_barrier(
        (active, drop_half, gate_half, lift_half, branch_grad)
    )
    feed_back = ranks_return(
        [peers_sum(*drop_half), peers_sum(*gate_half), peers_sum(*lift_half)], drows
    ).astype(F32)
    drop_back = feed_back[:, :, :LANES]
    gate_back = feed_back[:, :, LANES : 2 * LANES]
    lift_back = feed_back[:, :, 2 * LANES :]
    layer_output = (residual + team_scatter(back_dot(straight, [(active, w_drop)]))).astype(BF)

    mixer_rows_grad, attn_grad, along, gain_part = rows_back(
        scalars, branch_grad, w_out, ssm, gating, mixer_root, own_gain
    )
    along = team_sum(along[:, 0]).reshape(total, 1) / DI
    query_grad, key_value_part = attend_back(
        place, queries, attn_grad, attended, logs, root, key_value_rows
    )
    if ch == 1:
        key_value_grad = key_value_part
    elif ch == 2:
        halves = key_value_part.reshape(sl, ch, count, 2 * HD)
        key_value_grad = added(
            kept(halves, "ch", 1), swap(given(halves, "ch", 1).astype(BF), "ch")
        )
    else:
        key_value_grad = lax.psum_scatter(
            key_value_part.astype(BF), "ch", scatter_dimension=1, tiled=True
        ).astype(F32)
    ssm_grad, gating_grad, leaving_back = states_back(
        sl, step_pre, head, io, mixer_rows_grad, ssm, gating, mixer_root, along, own_gain, root
    )
    entry_back = entering(piece_decay[:, 0], leaving_back, True)
    inner_conv_grad, parts, step_rows_grad, sums = ssm_back(
        side_index,
        sl,
        step_pre,
        head,
        conv,
        io,
        ssm_grad,
        carried,
        entry_back,
        key_value_grad.reshape(total, 2 * HD),
        root,
    )
    parts = lax.all_to_all(parts, TEAM, split_axis=0, concat_axis=0, tiled=True)
    gating_rows_grad = jnp.concatenate([gating_grad, query_grad], 1)
    gating_half = peers_half(order, team_tokens, gating_rows_grad)
    out_half = peers_half(order, branch_grad, branch_rows)
    conv_grad, conv_sums = conv_back(inner_conv_grad, parts, conv, pre, edge)
    follow = shifted(conv_grad.reshape(sl, count, LANES)[:, :EDGE], -1)
    inner_rows_grad = pre_back(conv_grad, follow, taps, root)
    step_halves = (own_step[:, : width // 2], own_step[:, width // 2 :])
    hidden_grad = team_scatter(
        back_dot(
            order,
            [
                (inner_rows_grad, w_inner),
                (gating_rows_grad, w_gating),
                (step_rows_grad, step_halves),
            ],
        )
    )
    inner_half = peers_half(order, team_tokens, inner_rows_grad)
    mixer_back = ranks_return(
        [peers_sum(*out_half), peers_sum(*gating_half), peers_sum(*inner_half)], drows
    ).astype(F32)
    out_back = mixer_back[:, :, :LANES]
    gating_back = mixer_back[:, :, LANES : 2 * LANES]
    inner_back = mixer_back[:, :, 2 * LANES :]
    token_values = own_tokens.astype(F32)
    token_root = inverse_root(token_values)
    tokens_grad = residual_grad + norm_back(token_values, token_root, hidden_grad / token_root)
    left, right, left_other, right_other = team_tokens
    step_back = jnp.concatenate(
        [
            grad_dot(order, left, left_other, step_rows_grad, F32),
            grad_dot(order, right, right_other, step_rows_grad, F32),
        ],
        0,
    )[:, :HEADS].T

    def placed(part, extent, at):
        base = jnp.zeros(part.shape[:-1] + (extent,), F32)
        return lax.dynamic_update_slice_in_dim(base, part, at, part.ndim - 1)

    conv_all = jnp.concatenate(
        [
            placed(conv_sums[: KC + 1, :INNER], DI, rank * INNER),
            placed(conv_sums[: KC + 1, INNER:CONV], 2 * NS, rank * SIDE),
        ],
        1,
    )
    gain_all = placed(gain_part[0], DI, rank * INNER)
    step_all = step_back.reshape(HEADS, -1, drows).swapaxes(0, 1)
    step_all = step_all.reshape(sh, ch, sl, 4, HEADS * drows)
    step_all = relative(relative(step_all, "sh", 0), "ch", 1).swapaxes(1, 2)
    per_head = jnp.concatenate(
        [placed(sums[at, :HEADS], HM, rank * HEADS) for at in range(3)]
    )
    sent = jnp.concatenate(
        [
            conv_all.reshape(KC + 1, world, conv_own).swapaxes(0, 1).reshape(world, -1),
            gain_all.reshape(world, -1),
            step_all.reshape(world, -1),
            jnp.broadcast_to(per_head[None], (world, 3 * HM)),
        ],
        1,
    )
    got_all = lax.all_to_all(sent, WORLD, split_axis=0, concat_axis=0, tiled=True)
    at = KC * conv_own + conv_own + gain_own
    step_core = got_all[:, at : at + HEADS * drows].reshape(sh, sl, ch, 4, HEADS, drows)
    step_core = jnp.sum(step_core, axis=(0, 2)).reshape(HM, drows).T
    got = jnp.sum(got_all, axis=0)
    at = 0
    conv_out = got[at : at + KC * conv_own].reshape(KC, conv_own)
    at += KC * conv_own
    conv_bias_out = got[at : at + conv_own]
    at += conv_own
    gain_out = got[at : at + gain_own]
    at += gain_own + HEADS * drows
    bias_out, decay_out, skip_out = (got[at + i * HM : at + (i + 1) * HM] for i in range(3))

    def against(weight, grad):
        return jnp.sum(weight.astype(F32) * grad, axis=1)

    inner_core = to_columns(inner_back[:, :, :INNER])
    state_core = to_columns(inner_back[:, :, INNER:CONV])
    key_value_core = to_columns(inner_back[:, :, CONV:]).reshape(drows, HK, 2, 2 * SIDE)
    key_core = key_value_core[:, :, 0].reshape(drows, HK * HD)
    value_core = key_value_core[:, :, 1].reshape(drows, HK * HD)
    gating_core = to_columns(gating_back[:, :, :INNER])
    query_core = to_columns(gating_back[:, :, INNER:])
    gate_core, lift_core = to_columns(gate_back), to_columns(lift_back)
    norm_out = (
        against(gating_weight, gating_core)
        + against(inner_weight, inner_core)
        + against(state_weight, state_core)
        + against(step_weight, step_core)
        + against(query_weight, query_core)
        + against(key_weight, key_core)
        + against(value_weight, value_core)
    )
    feed_out = against(gate_matrix, gate_core) + against(lift_matrix, lift_core)
    norm_scale = norm_gain.astype(F32)[:, None]
    feed_scale = feed_gain.astype(F32)[:, None]
    mixer_out_out = out_back[:, :, :INNER].transpose(0, 2, 1).reshape(DI, drows)
    output_out = out_back[:, :, INNER:].transpose(0, 2, 1).reshape(HA * HD, drows)
    drop_out = drop_back.transpose(0, 2, 1).reshape(-1, drows)
    return (
        unshuffled(layer_output, sh, sl, ch),
        unshuffled(tokens_grad, sh, sl, ch),
        norm_out,
        gating_core * norm_scale,
        inner_core * norm_scale,
        state_core * norm_scale,
        step_core * norm_scale,
        conv_out,
        conv_bias_out,
        gain_out,
        mixer_out_out,
        query_core * norm_scale,
        key_core * norm_scale,
        value_core * norm_scale,
        output_out,
        feed_out,
        gate_core * feed_scale,
        lift_core * feed_scale,
        drop_out,
        bias_out,
        decay_out,
        skip_out,
    )


def solution(mesh):
    seq, ctx = mesh.shape["seq"], mesh.shape["ctx"]
    fine = Mesh(mesh.devices.reshape(seq // 2, 2, ctx // 4, 2, 2), WORLD)
    lead, vector, tail = P(WORLD, None), P(WORLD), P(None, WORLD)
    in_specs = (
        lead,
        lead,
        vector,
        lead,
        lead,
        lead,
        lead,
        tail,
        vector,
        vector,
        tail,
        lead,
        lead,
        lead,
        tail,
        vector,
        lead,
        lead,
        tail,
        P(),
        P(),
        P(),
    )
    out_specs = (
        lead,
        lead,
        vector,
        lead,
        lead,
        lead,
        lead,
        tail,
        vector,
        vector,
        tail,
        lead,
        lead,
        lead,
        tail,
        vector,
        lead,
        lead,
        tail,
        P(),
        P(),
        P(),
    )
    return jax.shard_map(local, mesh=fine, in_specs=in_specs, out_specs=out_specs, check_vma=False)
```

time: 1220 us -> 1040 us (0.85)
  Pallas kernels: 0 us -> 176 us
  local copies, waits for them, and re-layouts: 324 us -> 152 us
  other arithmetic: 215 us -> 110 us
  matrix products: 97.9 us -> 0 us
  waiting for transfers between devices: 402 us -> 434 us
  starting transfers between devices: 150 us -> 136 us
    ppermute x80, waiting for transfers between devices: 235 us -> 414 us  [swap(): return lax.ppermute(value, axis, [(0, 1), (1, 0)])]
    pallas_call x0 -> x30, Pallas kernels: none -> 176 us  [the longest x14 41 us: grad_dot(): call(grad_dot_kernel, (half // tile,), [spec, spec, full(against)], pl.Bl...]
    unnamed x5 -> x1, waiting for transfers between devices: 126 us -> 0.02 us
    dot_general x39 -> x0, matrix products: 97.9 us -> none  [the longest x18 30.9 us: dots(): jnp.einsum(spec, *[o.astype(BF) for o in operands], preferred_element_typ...]
    unnamed x529 -> x403, local copies, waits for them, and re-layouts: 129 us -> 58.7 us
    select_n x43 -> x1, other arithmetic: 64.3 us -> 2.32 us  [paired(): jnp.where(bit == 0, jnp.stack([mine, theirs], dim), jnp.stack([theirs, mi...]
    convert_element_type x45 -> x12, local copies, waits for them, and re-layouts: 38.2 us -> 4.87 us  [the longest x4 2.95 us: team_scatter(): right_z = swap(right[1].astype(BF), 'zl')]
    dot_general x5 -> x0, local copies, waits for them, and re-layouts: 26.9 us -> none  [the longest x4 26.2 us: lead_dot(): lax.dot_general(operand, against, (((0,), (0,)), ((), ())), preferred_ele...]
  transfers between devices with their start and end apart: 100 -> 92, of which waited for: 43 -> 39; matrix products, arithmetic and copies ran while one was open for 46% -> 18% of each run, Pallas kernels for 0% -> 11%
where the time goes in v2:
time: 1040 us; the launch traced here: 1030 us
  waiting for transfers between devices  434 us (42%)
  Pallas kernels  176 us (17%)
  local copies, waits for them, and re-layouts  152 us (15%)
  starting transfers between devices  136 us (13%)
  other arithmetic  110 us (11%)
  between operations  17.5 us (2%)
    ppermute x80, waiting for transfers between devices, swap(): return lax.ppermute(value, axis, [(0, 1), (1, 0)])  414 us
    ppermute x80, starting transfers between devices, swap(): return lax.ppermute(value, axis, [(0, 1), (1, 0)])  95.4 us
    unnamed x403, local copies, waits for them, and re-layouts  58.7 us
    pallas_call x14, Pallas kernels, grad_dot(): call(grad_dot_kernel, (half // tile,), [spec, spec, full(against)], pl.Bl...  41 us
    pallas_call x4, Pallas kernels, back_dot(): call(lambda *refs: back_dot_kernel(len(terms), halves, *refs), (2 * halve...  37.2 us
    add x15, other arithmetic, added(): return mine.astype(F32) + theirs.astype(F32)  21.5 us
  transfers between devices with their start and end apart: 92, of which 39 were waited for; matrix products, arithmetic and copies ran while one was open for 18% of the time, Pallas kernels for 11%

profile of v2, /device:TPU:0, one launch (start us, length us, event | category | flops | bytes accessed | tf_op | source)
XLA Modules:
  0.0 1025.8 jit_solution(6052823201140919540)
XLA Ops:
  36.9 15.3 %collective-permute-done.3 = bf16[2,128,1024]{2,1,0:T(8,128)(2,1)S(1)} collective-permute-done((bf16[2,128,1024]{2,1,0:T(8,128)(2,1)S(1)}, bf16[2,128,1024]{2,1,0:T(8,128)(2,1)S(1)}, u32[]{:S(2)}, u32[]{:S(2)}) %collective-permute-start.3) | collective-permute-done | bytes 524320 | tf_op jit(solution)/shard_map/ppermute | solution.py:32
  67.0 20.9 %collective-permute-done.6 = bf16[512,512]{1,0:T(8,128)(2,1)} collective-permute-done((bf16[512,512]{1,0:T(8,128)(2,1)}, bf16[512,512]{1,0:T(8,128)(2,1)}, u32[]{:S(2)}, u32[]{:S(2)}) %collective-permute-start.6) | collective-permute-done | bytes 524320 | tf_op jit(solution)/shard_map/ppermute | solution.py:32
  100.7 14.2 %collective-permute-done.7.refs_6_.refs_4_ = bf16[1024,512]{1,0:T(8,128)(2,1)} collective-permute-done((bf16[1024,512]{1,0:T(8,128)(2,1)}, bf16[1024,512]{1,0:T(8,128)(2,1)}, u32[]{:S(2)}, u32[]{:S(2)}) %collective-permute-start.7) | collective-permute-done | bytes 1048608 | tf_op jit(solution)/shard_map/ppermute | solution.py:32
  114.9 10.4 %shard_map.381 = (f32[1024,512]{1,0:T(8,128)}, f32[1024,512]{1,0:T(8,128)}, bf16[1024,128]{1,0:T(8,128)(2,1)}, f32[1024,8]{1,0:T(8,128)S(1)}, f32[1024,1]{1,0:T(8,128)S(1)}, /*index=5*/f32[2,16,512]{2,1,0:T(8,128)S(1)}) custom-call(s32[5]{0:T(128)S(1)} %stack.177.refs_0_.scalars, bf16[4,128,1024]{2,1,0:T(8,128)(2,1)S(1)} %pad_maximum_fusion.2.refs_1_.l.own, ...), custom_call_target="tpu_custom_call" | custom-call | flops 1000000000 | bytes 1000000 | tf_op jit(solution)/shard_map/pallas_call | solution.py:305
  137.8 40.8 %collective-permute-done.9 = bf16[512,512]{1,0:T(8,128)(2,1)} collective-permute-done((bf16[512,512]{1,0:T(8,128)(2,1)}, bf16[512,512]{1,0:T(8,128)(2,1)}, u32[]{:S(2)}, u32[]{:S(2)}) %collective-permute-start.9) | collective-permute-done | bytes 524320 | tf_op jit(solution)/shard_map/ppermute | solution.py:32
  223.9 11.3 %shard_map.384 = (f32[1024,384]{1,0:T(8,128)S(1)}, bf16[8,256,384]{2,1,0:T(8,128)(2,1)S(1)}, f32[8,8,128]{2,1,0:T(8,128)S(1)}) custom-call(f32[1024,8]{1,0:T(8,128)S(1)} %copy-done.52, f32[8,8]{1,0:T(8,128)S(1)} %copy-done.79, f32[1024,512]{1,0:T(8,128)} %get-tuple-element.94.refs_2_.refs_3_, bf16[1024,512]{1,0:T(8,128)(2,1)S(1)} %copy-done.21, ...), custom_call_target="tpu_custom_call" | custom-call | flops 1000000000 | bytes 1000000 | tf_op jit(solution)/shard_map/pallas_call | solution.py:723
  238.6 14.7 %collective-permute-start.13 = (f32[8,128]{1,0:T(8,128)S(1)}, f32[8,128]{1,0:T(8,128)S(1)}, u32[]{:S(2)}, u32[]{:S(2)}) collective-permute-start(f32[8,128]{1,0:T(8,128)S(1)} %add.364), channel_id=1, source_target_pairs={{0,2},{2,0},{1,3},{3,1},{4,6},{6,4},{5,7},{7,5},{8,10},{10,8},{9,1... | collective-permute-start | bytes 12296 | tf_op jit(solution)/shard_map/ppermute | solution.py:32
  268.5 19.3 %collective-permute-done.15 = bf16[2,512,256]{1,0,2:T(2,128)(2,1)S(1)} collective-permute-done((bf16[2,512,256]{1,0,2:T(2,128)(2,1)}, bf16[2,512,256]{1,0,2:T(2,128)(2,1)S(1)}, u32[]{:S(2)}, u32[]{:S(2)}) %collective-permute-start.15) | collective-permute-done | bytes 524320 | tf_op jit(solution)/shard_map/ppermute | solution.py:32
  296.4 8.1 shard_map.386
  329.5 6.9 collective-permute-done.19
  338.2 13.1 %collective-permute-done.22 = bf16[2,128,1024]{2,1,0:T(8,128)(2,1)S(1)} collective-permute-done((bf16[2,128,1024]{2,1,0:T(8,128)(2,1)S(1)}, bf16[2,128,1024]{2,1,0:T(8,128)(2,1)S(1)}, u32[]{:S(2)}, u32[]{:S(2)}) %collective-permute-start.22) | collective-permute-done | bytes 524320 | tf_op jit(solution)/shard_map/ppermute | solution.py:32
  386.3 25.1 %collective-permute-done.38 = bf16[512,512]{1,0:T(8,128)(2,1)S(1)} collective-permute-done((bf16[512,512]{1,0:T(8,128)(2,1)S(1)}, bf16[512,512]{1,0:T(8,128)(2,1)S(1)}, u32[]{:S(2)}, u32[]{:S(2)}) %collective-permute-start.38) | collective-permute-done | bytes 524320 | tf_op jit(solution)/shard_map/ppermute | solution.py:32
  411.5 10.9 %collective-permute-done.40 = bf16[512,512]{1,0:T(8,128)(2,1)S(1)} collective-permute-done((bf16[512,512]{1,0:T(8,128)(2,1)S(1)}, bf16[512,512]{1,0:T(8,128)(2,1)S(1)}, u32[]{:S(2)}, u32[]{:S(2)}) %collective-permute-start.40) | collective-permute-done | bytes 524320 | tf_op jit(solution)/shard_map/ppermute | solution.py:32
  424.8 8.7 collective-permute-done.25
  435.9 12.6 %collective-permute-done.37.refs_9_.refs_4_ = bf16[1024,512]{1,0:T(8,128)(2,1)S(1)} collective-permute-done((bf16[1024,512]{1,0:T(8,128)(2,1)S(1)}, bf16[1024,512]{1,0:T(8,128)(2,1)S(1)}, u32[]{:S(2)}, u32[]{:S(2)}) %collective-permute-start.37) | collective-permute-done | bytes 1048608 | tf_op jit(solution)/shard_map/ppermute | solution.py:32
  448.5 22.5 %collective-permute-done.39.refs_11_.refs_8_ = bf16[1024,512]{1,0:T(8,128)(2,1)S(1)} collective-permute-done((bf16[1024,512]{1,0:T(8,128)(2,1)S(1)}, bf16[1024,512]{1,0:T(8,128)(2,1)S(1)}, u32[]{:S(2)}, u32[]{:S(2)}) %collective-permute-start.39) | collective-permute-done | bytes 1048608 | tf_op jit(solution)/shard_map/ppermute | solution.py:32
  471.0 21.2 %collective-permute-done.41.refs_13_.refs_4_ = bf16[1024,512]{1,0:T(8,128)(2,1)S(1)} collective-permute-done((bf16[1024,512]{1,0:T(8,128)(2,1)S(1)}, bf16[1024,512]{1,0:T(8,128)(2,1)S(1)}, u32[]{:S(2)}, u32[]{:S(2)}) %collective-permute-start.41) | collective-permute-done | bytes 1048608 | tf_op jit(solution)/shard_map/ppermute | solution.py:32
  494.5 11.8 %shard_map.387 = (bf16[1024,512]{1,0:T(8,128)(2,1)S(1)}, bf16[1024,512]{1,0:T(8,128)(2,1)S(1)}, bf16[1024,512]{1,0:T(8,128)(2,1)S(1)}) custom-call(bf16[4,128,1024]{2,1,0:T(8,128)(2,1)S(1)} %pad_maximum_fusion.8.refs_0_.own, bf16[4,128,1024]{2,1,0:T(8,128)(2,1)S(1)} %pad_maximum_fusion.9.refs_1_.own, bf16[4,128,1024]{2,1,0:T(8,128)(2,1)} %copy-done.34, ...), custom_call_target="tpu_custom_call" | custom-call | flops 1000000000 | bytes 1000000 | tf_op jit(solution)/shard_map/pallas_call | solution.py:521
  511.1 10.2 shard_map.394
  526.3 13.3 %collective-permute-done.46 = bf16[2,128,1024]{2,1,0:T(8,128)(2,1)S(1)} collective-permute-done((bf16[2,128,1024]{2,1,0:T(8,128)(2,1)S(1)}, bf16[2,128,1024]{2,1,0:T(8,128)(2,1)S(1)}, u32[]{:S(2)}, u32[]{:S(2)}) %collective-permute-start.46) | collective-permute-done | bytes 524320 | tf_op jit(solution)/shard_map/ppermute | solution.py:32
  597.6 22.5 %collective-permute-done.43 = bf16[1024,512]{1,0:T(8,128)(2,1)} collective-permute-done((bf16[1024,512]{1,0:T(8,128)(2,1)}, bf16[1024,512]{1,0:T(8,128)(2,1)}, u32[]{:S(2)}, u32[]{:S(2)}) %collective-permute-start.43) | collective-permute-done | bytes 1048608 | tf_op jit(solution)/shard_map/ppermute | solution.py:32
  620.1 18.2 %collective-permute-done.42 = bf16[1024,512]{1,0:T(8,128)(2,1)} collective-permute-done((bf16[1024,512]{1,0:T(8,128)(2,1)}, bf16[1024,512]{1,0:T(8,128)(2,1)}, u32[]{:S(2)}, u32[]{:S(2)}) %collective-permute-start.42) | collective-permute-done | bytes 1048608 | tf_op jit(solution)/shard_map/ppermute | solution.py:32
  661.6 9.6 shard_map.396
  689.8 19.5 %collective-permute-done.82 = bf16[512,512]{1,0:T(8,128)(2,1)} collective-permute-done((bf16[512,512]{1,0:T(8,128)(2,1)}, bf16[512,512]{1,0:T(8,128)(2,1)}, u32[]{:S(2)}, u32[]{:S(2)}) %collective-permute-start.82) | collective-permute-done | bytes 524320 | tf_op jit(solution)/shard_map/ppermute | solution.py:32
  710.5 10.0 collective-permute-done.83
  734.7 8.1 shard_map.397
  756.3 10.5 %collective-permute-done.66.refs_7_ = bf16[2,256,384]{2,1,0:T(8,128)(2,1)S(1)} collective-permute-done((bf16[2,256,384]{2,1,0:T(8,128)(2,1)S(1)}, bf16[2,256,384]{2,1,0:T(8,128)(2,1)S(1)}, u32[]{:S(2)}, u32[]{:S(2)}) %collective-permute-start.66) | collective-permute-done | bytes 393248 | tf_op jit(solution)/shard_map/ppermute | solution.py:154
  766.8 19.6 %shard_map.399 = (f32[1024,384]{1,0:T(8,128)S(1)}, bf16[8,1024,128]{2,1,0:T(8,128)(2,1)}, bf16[1024,8]{1,0:T(8,128)(2,1)S(1)}, f32[8,8]{1,0:T(8,128)S(1)}) custom-call(s32[1]{0:T(128)} %bitcast.90.refs_0_, f32[1024,8]{1,0:T(8,128)S(1)} %copy-done.54, f32[8,8]{1,0:T(8,128)S(1)} %copy-done.80, f32[1024,512]{1,0:T(8,128)} %get-tuple-element.94.refs_2_.refs_3_, ...), custom_call_target="tpu_custom_call" | custom-call | flops 1000000000 | bytes 1000000 | tf_op jit(solution)/shard_map/pallas_call | solution.py:883
  811.9 46.1 %collective-permute-done.58 = bf16[2,128,1024]{2,1,0:T(8,128)(2,1)S(1)} collective-permute-done((bf16[2,128,1024]{2,1,0:T(8,128)(2,1)S(1)}, bf16[2,128,1024]{2,1,0:T(8,128)(2,1)S(1)}, u32[]{:S(2)}, u32[]{:S(2)}) %collective-permute-start.58) | collective-permute-done | bytes 524320 | tf_op jit(solution)/shard_map/ppermute | solution.py:32
  899.1 12.3 %shard_map.402 = (f32[4,128,1024]{2,1,0:T(8,128)}, f32[4,128,1024]{2,1,0:T(8,128)}, bf16[4,128,1024]{2,1,0:T(8,128)(2,1)}, bf16[4,128,1024]{2,1,0:T(8,128)(2,1)}) custom-call(s32[8]{0:T(128)S(1)} %copy-done.81, bf16[1024,512]{1,0:T(8,128)(2,1)S(1)} %shard_map.401.refs_1_.refs_2_.against, bf16[1024,512]{1,0:T(8,128)(2,1)S(1)} %shard_map.401.refs_1_.refs_2_.against, ...), custom_call_target="tpu_custom_call" | custom-call | flops 1000000000 | bytes 1000000 | tf_op jit(solution)/shard_map/pallas_call | solution.py:434
  934.7 10.9 %collective-permute-done.79 = bf16[1024,512]{1,0:T(8,128)(2,1)} collective-permute-done((bf16[1024,512]{1,0:T(8,128)(2,1)}, bf16[1024,512]{1,0:T(8,128)(2,1)}, u32[]{:S(2)}, u32[]{:S(2)}) %collective-permute-start.79) | collective-permute-done | bytes 1048608 | tf_op jit(solution)/shard_map/ppermute | solution.py:32
  954.8 10.8 %collective-permute-done.73 = bf16[2,128,1024]{2,1,0:T(8,128)(2,1)S(1)} collective-permute-done((bf16[2,128,1024]{2,1,0:T(8,128)(2,1)S(1)}, bf16[2,128,1024]{2,1,0:T(8,128)(2,1)S(1)}, u32[]{:S(2)}, u32[]{:S(2)}) %collective-permute-start.73) | collective-permute-done | bytes 524320 | tf_op jit(solution)/shard_map/ppermute | solution.py:32
  (864 shorter events, 498.9 us)
Async XLA Ops:
  59.0 124.2 %all-gather.3.cloned.1.call-start = ((), (), s32[]{:S(2)}) async-start(), calls=%async_computation.7 | async-start | bytes 2359296 | tf_op jit(solution)/shard_map/all_gather | solution.py:1106
  130.8 78.5 %all-to-all-start.2 = ((bf16[8,64,2048]{2,1,0:T(8,128)(2,1)}), bf16[8,64,2048]{2,1,0:T(8,128)(2,1)}, u32[]{:S(2)}, u32[]{:S(2)}) async-start(bf16[8,64,2048]{2,1,0:T(8,128)(2,1)} %fusion.29), calls=%async_computation.2 | async-start | bytes 4194304 | tf_op jit(solution)/shard_map/all_to_all | solution.py:109
  135.4 43.3 %collective-permute-start.9 = (bf16[512,512]{1,0:T(8,128)(2,1)}, bf16[512,512]{1,0:T(8,128)(2,1)}, u32[]{:S(2)}, u32[]{:S(2)}) collective-permute-start(bf16[512,512]{1,0:T(8,128)(2,1)} %get-tuple-element.183), channel_id=1, source_target_pairs={{0,4},{4,0},{1,5},{5,1},{2,6},{6,2},{3,7},{7,3},{8,12},{12,8},{9,1... | collective-permute-start | bytes 1572872 | tf_op jit(solution)/shard_map/ppermute | solution.py:32
  212.3 41.1 %collective-permute-start.16 = (bf16[512,512]{1,0:T(8,128)(2,1)}, bf16[512,512]{1,0:T(8,128)(2,1)}, u32[]{:S(2)}, u32[]{:S(2)}) collective-permute-start(bf16[512,512]{1,0:T(8,128)(2,1)} %get-tuple-element.173), channel_id=1, source_target_pairs={{0,4},{4,0},{1,5},{5,1},{2,6},{6,2},{3,7},{7,3},{8,12},{12,8},{9,1... | collective-permute-start | bytes 1572872 | tf_op jit(solution)/shard_map/ppermute | solution.py:32
  255.6 40.7 %collective-permute-start.17 = (bf16[1024,512]{1,0:T(8,128)(2,1)}, bf16[1024,512]{1,0:T(8,128)(2,1)}, u32[]{:S(2)}, u32[]{:S(2)}) collective-permute-start(bf16[1024,512]{1,0:T(8,128)(2,1)} %pad_maximum_fusion.7.refs_3_.mine), channel_id=1, source_target_pairs={{0,16},{16,0},{1,17},{17,1},{2,18},{18,2},{3,19},{19,3},{4,20},{20... | collective-permute-start | bytes 3145736 | tf_op jit(solution)/shard_map/ppermute | solution.py:32
  326.6 49.5 %collective-permute-start.31 = (bf16[2,128,1024]{2,1,0:T(8,128)(2,1)}, bf16[2,128,1024]{2,1,0:T(8,128)(2,1)}, u32[]{:S(2)}, u32[]{:S(2)}) collective-permute-start(bf16[2,128,1024]{2,1,0:T(8,128)(2,1)} %pad_maximum_fusion.22), channel_id=1, source_target_pairs={{0,2},{2,0},{1,3},{3,1},{4,6},{6,4},{5,7},{7,5},{8,10},{10,8},{9,1... | collective-permute-start | bytes 1572872 | tf_op jit(solution)/shard_map/ppermute | solution.py:32
  373.2 62.1 %collective-permute-start.35 = (bf16[4,128,1024]{2,1,0:T(8,128)(2,1)S(1)}, bf16[4,128,1024]{2,1,0:T(8,128)(2,1)S(1)}, u32[]{:S(2)}, u32[]{:S(2)}) collective-permute-start(bf16[4,128,1024]{2,1,0:T(8,128)(2,1)S(1)} %pad_maximum_fusion.11.refs_5_.own), channel_id=1, source_target_pairs={{0,1},{1,0},{2,3},{3,2},{4,5},{5,4},{6,7},{7,6},{8,9},{9,8},{10,11... | collective-permute-start | bytes 3145736 | tf_op jit(solution)/shard_map/ppermute | solution.py:32
  382.9 39.5 %collective-permute-start.40 = (bf16[512,512]{1,0:T(8,128)(2,1)S(1)}, bf16[512,512]{1,0:T(8,128)(2,1)S(1)}, u32[]{:S(2)}, u32[]{:S(2)}) collective-permute-start(bf16[512,512]{1,0:T(8,128)(2,1)S(1)} %copy-done.139), channel_id=1, source_target_pairs={{0,4},{4,0},{1,5},{5,1},{2,6},{6,2},{3,7},{7,3},{8,12},{12,8},{9,1... | collective-permute-start | bytes 1572872 | tf_op jit(solution)/shard_map/ppermute | solution.py:32
  383.0 52.4 %collective-permute-start.34 = (bf16[4,128,1024]{2,1,0:T(8,128)(2,1)S(1)}, bf16[4,128,1024]{2,1,0:T(8,128)(2,1)S(1)}, u32[]{:S(2)}, u32[]{:S(2)}) collective-permute-start(bf16[4,128,1024]{2,1,0:T(8,128)(2,1)S(1)} %pad_maximum_fusion.10.refs_4_.own), channel_id=1, source_target_pairs={{0,1},{1,0},{2,3},{3,2},{4,5},{5,4},{6,7},{7,6},{8,9},{9,8},{10,11... | collective-permute-start | bytes 3145736 | tf_op jit(solution)/shard_map/ppermute | solution.py:32
  384.5 39.6 %collective-permute-start.27 = (bf16[2,128,1024]{2,1,0:T(8,128)(2,1)S(1)}, bf16[2,128,1024]{2,1,0:T(8,128)(2,1)S(1)}, u32[]{:S(2)}, u32[]{:S(2)}) collective-permute-start(bf16[2,128,1024]{2,1,0:T(8,128)(2,1)S(1)} %pad_maximum_fusion.21), channel_id=1, source_target_pairs={{0,8},{8,0},{1,9},{9,1},{2,10},{10,2},{3,11},{11,3},{4,12},{12,4},... | collective-permute-start | bytes 1572872 | tf_op jit(solution)/shard_map/ppermute | solution.py:32
  424.1 46.8 %collective-permute-start.39 = (bf16[1024,512]{1,0:T(8,128)(2,1)S(1)}, bf16[1024,512]{1,0:T(8,128)(2,1)S(1)}, u32[]{:S(2)}, u32[]{:S(2)}) collective-permute-start(bf16[1024,512]{1,0:T(8,128)(2,1)S(1)} %pad_maximum_fusion.13.refs_10_.refs_7_), channel_id=1, source_target_pairs={{0,16},{16,0},{1,17},{17,1},{2,18},{18,2},{3,19},{19,3},{4,20},{20... | collective-permute-start | bytes 3145736 | tf_op jit(solution)/shard_map/ppermute | solution.py:32
  433.6 58.6 %collective-permute-start.41 = (bf16[1024,512]{1,0:T(8,128)(2,1)S(1)}, bf16[1024,512]{1,0:T(8,128)(2,1)S(1)}, u32[]{:S(2)}, u32[]{:S(2)}) collective-permute-start(bf16[1024,512]{1,0:T(8,128)(2,1)S(1)} %pad_maximum_fusion.14.refs_12_.refs_3_), channel_id=1, source_target_pairs={{0,16},{16,0},{1,17},{17,1},{2,18},{18,2},{3,19},{19,3},{4,20},{20... | collective-permute-start | bytes 3145736 | tf_op jit(solution)/shard_map/ppermute | solution.py:32
  435.3 56.8 %collective-permute-start.29 = (bf16[4,128,1024]{2,1,0:T(8,128)(2,1)S(1)}, bf16[4,128,1024]{2,1,0:T(8,128)(2,1)S(1)}, u32[]{:S(2)}, u32[]{:S(2)}) collective-permute-start(bf16[4,128,1024]{2,1,0:T(8,128)(2,1)S(1)} %pad_maximum_fusion.9.refs_1_.own), channel_id=1, source_target_pairs={{0,1},{1,0},{2,3},{3,2},{4,5},{5,4},{6,7},{7,6},{8,9},{9,8},{10,11... | collective-permute-start | bytes 3145736 | tf_op jit(solution)/shard_map/ppermute | solution.py:32
  435.4 56.8 %collective-permute-start.28 = (bf16[4,128,1024]{2,1,0:T(8,128)(2,1)S(1)}, bf16[4,128,1024]{2,1,0:T(8,128)(2,1)S(1)}, u32[]{:S(2)}, u32[]{:S(2)}) collective-permute-start(bf16[4,128,1024]{2,1,0:T(8,128)(2,1)S(1)} %pad_maximum_fusion.8.refs_0_.own), channel_id=1, source_target_pairs={{0,1},{1,0},{2,3},{3,2},{4,5},{5,4},{6,7},{7,6},{8,9},{9,8},{10,11... | collective-permute-start | bytes 3145736 | tf_op jit(solution)/shard_map/ppermute | solution.py:32
  576.9 43.2 %collective-permute-start.43 = (bf16[1024,512]{1,0:T(8,128)(2,1)}, bf16[1024,512]{1,0:T(8,128)(2,1)}, u32[]{:S(2)}, u32[]{:S(2)}) collective-permute-start(bf16[1024,512]{1,0:T(8,128)(2,1)} %shard_map.391), channel_id=1, source_target_pairs={{0,16},{16,0},{1,17},{17,1},{2,18},{18,2},{3,19},{19,3},{4,20},{20... | collective-permute-start | bytes 3145736 | tf_op jit(solution)/shard_map/ppermute | solution.py:32
  580.4 57.9 %collective-permute-start.42 = (bf16[1024,512]{1,0:T(8,128)(2,1)}, bf16[1024,512]{1,0:T(8,128)(2,1)}, u32[]{:S(2)}, u32[]{:S(2)}) collective-permute-start(bf16[1024,512]{1,0:T(8,128)(2,1)} %shard_map.389), channel_id=1, source_target_pairs={{0,16},{16,0},{1,17},{17,1},{2,18},{18,2},{3,19},{19,3},{4,20},{20... | collective-permute-start | bytes 3145736 | tf_op jit(solution)/shard_map/ppermute | solution.py:32
  583.1 55.1 %collective-permute-start.56 = (bf16[4,128,1024]{2,1,0:T(8,128)(2,1)}, bf16[4,128,1024]{2,1,0:T(8,128)(2,1)}, u32[]{:S(2)}, u32[]{:S(2)}) collective-permute-start(bf16[4,128,1024]{2,1,0:T(8,128)(2,1)} %pad_maximum_fusion.17.r.own), channel_id=1, source_target_pairs={{0,1},{1,0},{2,3},{3,2},{4,5},{5,4},{6,7},{7,6},{8,9},{9,8},{10,11... | collective-permute-start | bytes 3145736 | tf_op jit(solution)/shard_map/ppermute | solution.py:32
  584.3 54.0 %collective-permute-start.55 = (bf16[4,128,1024]{2,1,0:T(8,128)(2,1)}, bf16[4,128,1024]{2,1,0:T(8,128)(2,1)}, u32[]{:S(2)}, u32[]{:S(2)}) collective-permute-start(bf16[4,128,1024]{2,1,0:T(8,128)(2,1)} %pad_maximum_fusion.16.l.own), channel_id=1, source_target_pairs={{0,1},{1,0},{2,3},{3,2},{4,5},{5,4},{6,7},{7,6},{8,9},{9,8},{10,11... | collective-permute-start | bytes 3145736 | tf_op jit(solution)/shard_map/ppermute | solution.py:32
  640.8 47.3 %collective-permute-start.81 = (bf16[512,512]{1,0:T(8,128)(2,1)}, bf16[512,512]{1,0:T(8,128)(2,1)}, u32[]{:S(2)}, u32[]{:S(2)}) collective-permute-start(bf16[512,512]{1,0:T(8,128)(2,1)} %slice.747), channel_id=1, source_target_pairs={{0,4},{4,0},{1,5},{5,1},{2,6},{6,2},{3,7},{7,3},{8,12},{12,8},{9,1... | collective-permute-start | bytes 1572872 | tf_op jit(solution)/shard_map/ppermute | solution.py:32
  645.6 63.7 %collective-permute-start.82 = (bf16[512,512]{1,0:T(8,128)(2,1)}, bf16[512,512]{1,0:T(8,128)(2,1)}, u32[]{:S(2)}, u32[]{:S(2)}) collective-permute-start(bf16[512,512]{1,0:T(8,128)(2,1)} %slice.746), channel_id=1, source_target_pairs={{0,4},{4,0},{1,5},{5,1},{2,6},{6,2},{3,7},{7,3},{8,12},{12,8},{9,1... | collective-permute-start | bytes 1572872 | tf_op jit(solution)/shard_map/ppermute | solution.py:32
  648.9 71.7 %collective-permute-start.83 = (bf16[512,512]{1,0:T(8,128)(2,1)}, bf16[512,512]{1,0:T(8,128)(2,1)}, u32[]{:S(2)}, u32[]{:S(2)}) collective-permute-start(bf16[512,512]{1,0:T(8,128)(2,1)} %slice.745), channel_id=1, source_target_pairs={{0,4},{4,0},{1,5},{5,1},{2,6},{6,2},{3,7},{7,3},{8,12},{12,8},{9,1... | collective-permute-start | bytes 1572872 | tf_op jit(solution)/shard_map/ppermute | solution.py:32
  655.2 143.5 %collective-permute-start.75 = (bf16[1024,512]{1,0:T(8,128)(2,1)}, bf16[1024,512]{1,0:T(8,128)(2,1)}, u32[]{:S(2)}, u32[]{:S(2)}) collective-permute-start(bf16[1024,512]{1,0:T(8,128)(2,1)} %shard_map.404), channel_id=1, source_target_pairs={{0,16},{16,0},{1,17},{17,1},{2,18},{18,2},{3,19},{19,3},{4,20},{20... | collective-permute-start | bytes 3145736 | tf_op jit(solution)/shard_map/ppermute | solution.py:32
  686.6 66.9 %collective-permute-start.67 = (bf16[2,512,256]{2,1,0:T(8,128)(2,1)}, bf16[2,512,256]{2,1,0:T(8,128)(2,1)}, u32[]{:S(2)}, u32[]{:S(2)}) collective-permute-start(bf16[2,512,256]{2,1,0:T(8,128)(2,1)} %fusion.28), channel_id=1, source_target_pairs={{0,4},{4,0},{1,5},{5,1},{2,6},{6,2},{3,7},{7,3},{8,12},{12,8},{9,1... | collective-permute-start | bytes 1572872 | tf_op jit(solution)/shard_map/ppermute | solution.py:32
  688.0 113.1 %collective-permute-start.57 = (bf16[4,128,1024]{2,1,0:T(8,128)(2,1)}, bf16[4,128,1024]{2,1,0:T(8,128)(2,1)}, u32[]{:S(2)}, u32[]{:S(2)}) collective-permute-start(bf16[4,128,1024]{2,1,0:T(8,128)(2,1)} %get-tuple-element.116), channel_id=1, source_target_pairs={{0,1},{1,0},{2,3},{3,2},{4,5},{5,4},{6,7},{7,6},{8,9},{9,8},{10,11... | collective-permute-start | bytes 3145736 | tf_op jit(solution)/shard_map/ppermute | solution.py:32
  709.3 95.2 %collective-permute-start.60 = (bf16[4,128,1024]{2,1,0:T(8,128)(2,1)}, bf16[4,128,1024]{2,1,0:T(8,128)(2,1)}, u32[]{:S(2)}, u32[]{:S(2)}) collective-permute-start(bf16[4,128,1024]{2,1,0:T(8,128)(2,1)} %get-tuple-element.118), channel_id=1, source_target_pairs={{0,1},{1,0},{2,3},{3,2},{4,5},{5,4},{6,7},{7,6},{8,9},{9,8},{10,11... | collective-permute-start | bytes 3145736 | tf_op jit(solution)/shard_map/ppermute | solution.py:32
  725.0 69.3 %all-to-all-start.6 = ((bf16[8,64,1536]{2,1,0:T(8,128)(2,1)}), bf16[8,64,1536]{2,1,0:T(8,128)(2,1)}, u32[]{:S(2)}, u32[]{:S(2)}) async-start(bf16[8,64,1536]{2,1,0:T(8,128)(2,1)} %pad_maximum_fusion.1), calls=%async_computation.6 | async-start | bytes 3145728 | tf_op jit(solution)/shard_map/all_to_all | solution.py:125
  753.5 53.8 %collective-permute-start.77 = (bf16[1024,512]{1,0:T(8,128)(2,1)}, bf16[1024,512]{1,0:T(8,128)(2,1)}, u32[]{:S(2)}, u32[]{:S(2)}) collective-permute-start(bf16[1024,512]{1,0:T(8,128)(2,1)} %shard_map.406), channel_id=1, source_target_pairs={{0,16},{16,0},{1,17},{17,1},{2,18},{18,2},{3,19},{19,3},{4,20},{20... | collective-permute-start | bytes 3145736 | tf_op jit(solution)/shard_map/ppermute | solution.py:32
  794.3 86.0 %all-to-all-start.3 = ((bf16[8,1024,128]{2,1,0:T(8,128)(2,1)}), bf16[8,1024,128]{2,1,0:T(8,128)(2,1)}, u32[]{:S(2)}, u32[]{:S(2)}) async-start(bf16[8,1024,128]{2,1,0:T(8,128)(2,1)} %get-tuple-element.132), calls=%async_computation.3 | async-start | bytes 4194304 | tf_op jit(solution)/shard_map/all_to_all | solution.py:1200
  801.1 61.7 %collective-permute-start.76 = (bf16[512,512]{1,0:T(8,128)(2,1)S(1)}, bf16[512,512]{1,0:T(8,128)(2,1)S(1)}, u32[]{:S(2)}, u32[]{:S(2)}) collective-permute-start(bf16[512,512]{1,0:T(8,128)(2,1)S(1)} %slice.750), channel_id=1, source_target_pairs={{0,4},{4,0},{1,5},{5,1},{2,6},{6,2},{3,7},{7,3},{8,12},{12,8},{9,1... | collective-permute-start | bytes 1572872 | tf_op jit(solution)/shard_map/ppermute | solution.py:32
  802.6 55.4 %collective-permute-start.58 = (bf16[2,128,1024]{2,1,0:T(8,128)(2,1)S(1)}, bf16[2,128,1024]{2,1,0:T(8,128)(2,1)S(1)}, u32[]{:S(2)}, u32[]{:S(2)}) collective-permute-start(bf16[2,128,1024]{2,1,0:T(8,128)(2,1)S(1)} %add_convert_fusion.3), channel_id=1, source_target_pairs={{0,2},{2,0},{1,3},{3,1},{4,6},{6,4},{5,7},{7,5},{8,10},{10,8},{9,1... | collective-permute-start | bytes 1572872 | tf_op jit(solution)/shard_map/ppermute | solution.py:32
  805.7 55.1 %collective-permute-start.61 = (bf16[2,128,1024]{2,1,0:T(8,128)(2,1)S(1)}, bf16[2,128,1024]{2,1,0:T(8,128)(2,1)S(1)}, u32[]{:S(2)}, u32[]{:S(2)}) collective-permute-start(bf16[2,128,1024]{2,1,0:T(8,128)(2,1)S(1)} %add_convert_fusion.2), channel_id=1, source_target_pairs={{0,8},{8,0},{1,9},{9,1},{2,10},{10,2},{3,11},{11,3},{4,12},{12,4},... | collective-permute-start | bytes 1572872 | tf_op jit(solution)/shard_map/ppermute | solution.py:32
  808.9 54.9 %collective-permute-start.78 = (bf16[512,512]{1,0:T(8,128)(2,1)S(1)}, bf16[512,512]{1,0:T(8,128)(2,1)S(1)}, u32[]{:S(2)}, u32[]{:S(2)}) collective-permute-start(bf16[512,512]{1,0:T(8,128)(2,1)S(1)} %slice.749), channel_id=1, source_target_pairs={{0,4},{4,0},{1,5},{5,1},{2,6},{6,2},{3,7},{7,3},{8,12},{12,8},{9,1... | collective-permute-start | bytes 1572872 | tf_op jit(solution)/shard_map/ppermute | solution.py:32
  (253 other events, 2916.2 us)
Sparse Core Ops, SparseCore 0:
  127.1 41.4 all-gather.2

commit v3 on v2

--- a/solution.py
+++ b/solution.py
@@ -96,13 +96,25 @@
     return jnp.where(lax.axis_index(axis_name) == 0, value, jnp.flip(value, dim))
 
 
-def peers_gather(part):
+def together(*values):
+    return lax.optimization_barrier(values)
+
+
+def along_ch(part):
     size = lax.axis_size("ch")
     if size == 2:
-        part = jnp.concatenate([part, swap(part, "ch")], 0)
-    elif size > 2:
-        part = lax.all_gather(part, "ch", axis=0, tiled=True)
-    return part, swap(part, "sh")
+        return jnp.concatenate([part, swap(part, "ch")], 0)
+    return lax.all_gather(part, "ch", axis=0, tiled=True)
+
+
+def peers_gather(parts):
+    out = []
+    ready = along_ch(parts[0])
+    for part in parts[1:]:
+        mine = ready
+        theirs, ready = together(swap(mine, "sh"), along_ch(part))
+        out.append((mine, theirs))
+    return out + [(ready, swap(ready, "sh"))]
 
 
 def ranks_exchange(pack):
@@ -110,12 +122,12 @@
     return mixed.reshape(-1, pack.shape[2])
 
 
-def peers_sum(mine, theirs):
-    part = added(mine, theirs)
-    if lax.axis_size("ch") == 2:
+def ch_part(part):
+    size = lax.axis_size("ch")
+    if size == 2:
         half = part.shape[0] // 2
         part = added(part[:half], swap(part[half:].astype(BF), "ch"))
-    elif lax.axis_size("ch") > 2:
+    elif size > 2:
         part = lax.psum_scatter(part.astype(BF), "ch", scatter_dimension=0, tiled=True)
     return part.astype(BF)
 
@@ -474,9 +486,9 @@
     )(order, own, other, against)
 
 
-def peers_half(order, gathered, against):
+def grad_halves(order, gathered, against):
     left, right, left_other, right_other = gathered
-    theirs = swap(grad_dot(order, right, right_other, against, BF), "sh")
+    theirs = grad_dot(order, right, right_other, against, BF)
     return grad_dot(order, left, left_other, against, F32), theirs
 
 
@@ -1049,8 +1061,12 @@
     own_cotangent = shuffled(cotangent, sh, sl, ch)
     mixed_in = ranks_exchange(pack_in)
     team_tokens = team_gather(own_tokens)
-    w_inner = peers_gather(mixed_in[:, :LANES])
-    w_gating = peers_gather(mixed_in[:, LANES:])
+    pack_rest = jnp.concatenate(
+        [by_rank(mixer_out.T), by_rank(output_weight.T)]
+        + [by_rank(scaled(w, feed_gain)) for w in (gate_matrix, lift_matrix)]
+        + [by_rank(drop_matrix.T)],
+        2,
+    )
 
     conv_own, gain_own = conv_weight.shape[1], mixer_gain.shape[0]
     step_sent = jnp.broadcast_to(
@@ -1058,12 +1074,19 @@
         (sh, sl, ch, 4, HEADS * drows),
     ).reshape(world, HEADS * drows)
     shared = jnp.concatenate([conv_weight.reshape(-1), conv_bias, mixer_gain])
-    small = lax.all_to_all(
-        jnp.concatenate([jnp.broadcast_to(shared[None], (world, shared.shape[0])), step_sent], 1),
-        WORLD,
-        split_axis=0,
-        concat_axis=0,
-        tiled=True,
+    small = jnp.concatenate(
+        [jnp.broadcast_to(shared[None], (world, shared.shape[0])), step_sent], 1
+    )
+    small, mixed_in = together(small, mixed_in)
+    small = lax.all_to_all(small, WORLD, split_axis=0, concat_axis=0, tiled=True)
+    pack_rest, small, team_tokens = together(pack_rest, small, team_tokens)
+    mixed_rest = ranks_exchange(pack_rest)
+    w_inner, w_gating, w_out, w_gate, w_lift, w_drop = peers_gather(
+        [
+            mixed_in[:, :LANES],
+            mixed_in[:, LANES:],
+            *(mixed_rest[:, at * LANES : (at + 1) * LANES] for at in range(4)),
+        ]
     )
     at = (KC + 1) * conv_own
     wide_conv = small[:, :at].reshape(world, KC + 1, conv_own)
@@ -1116,24 +1139,13 @@
     leaving, piece_decay = states(sl, step_pre, head, conv, io)
     entry = entering(piece_decay[:, 0], leaving, False)
     attended, logs = attend(place, queries, key_value_rows)
+    team_cotangent = team_gather(own_cotangent)
+    entry, *team_cotangent = together(entry, *team_cotangent)
     ssm, carried, square = ssm_block(sl, step_pre, head, conv, io, gating, entry)
     mixer_root = lax.rsqrt(team_sum(square[:, 0]) / DI + epsilon).reshape(total, 1)
     branch_rows = jnp.concatenate(
         [(ssm * silu_value(gating) * mixer_root * own_gain).astype(BF), attended.astype(BF)], 1
     )
-
-    pack_rest = jnp.concatenate(
-        [by_rank(mixer_out.T), by_rank(output_weight.T)]
-        + [by_rank(scaled(w, feed_gain)) for w in (gate_matrix, lift_matrix)]
-        + [by_rank(drop_matrix.T)],
-        2,
-    )
-    mixed_rest = ranks_exchange(pack_rest)
-    w_out = peers_gather(mixed_rest[:, :LANES])
-    w_gate = peers_gather(mixed_rest[:, LANES : 2 * LANES])
-    w_lift = peers_gather(mixed_rest[:, 2 * LANES : 3 * LANES])
-    w_drop = peers_gather(mixed_rest[:, 3 * LANES :])
-    team_cotangent = team_gather(own_cotangent)
 
     branch = team_scatter(back_dot(order, [(branch_rows, w_out)]))
 
@@ -1148,19 +1160,18 @@
     )
     residual_grad = own_cotangent.astype(F32) + norm_back(residual, feed_root, feed_grad)
     branch_grad = team_gather(residual_grad.astype(BF))
-    drop_half = peers_half(straight, team_cotangent, active)
-    gate_half = peers_half(straight, feed_rows, gate_rows_grad)
-    lift_half = peers_half(straight, feed_rows, lift_rows_grad)
-    active, drop_half, gate_half, lift_half, branch_grad = lax.optimization_barrier(
-        (active, drop_half, gate_half, lift_half, branch_grad)
-    )
-    feed_back = ranks_return(
-        [peers_sum(*drop_half), peers_sum(*gate_half), peers_sum(*lift_half)], drows
-    ).astype(F32)
-    drop_back = feed_back[:, :, :LANES]
-    gate_back = feed_back[:, :, LANES : 2 * LANES]
-    lift_back = feed_back[:, :, 2 * LANES :]
-    layer_output = (residual + team_scatter(back_dot(straight, [(active, w_drop)]))).astype(BF)
+    drop_mine, drop_theirs = grad_halves(straight, team_cotangent, active)
+    gate_mine, gate_theirs = grad_halves(straight, feed_rows, gate_rows_grad)
+    lift_mine, lift_theirs = grad_halves(straight, feed_rows, lift_rows_grad)
+    layer_parts = back_dot(straight, [(active, w_drop)])
+    drop_theirs = swap(drop_theirs, "sh")
+    branch_grad, layer_parts, drop_theirs, gate_theirs, lift_theirs = together(
+        branch_grad, layer_parts, drop_theirs, gate_theirs, lift_theirs
+    )
+    gate_theirs, drop_part = together(
+        swap(gate_theirs, "sh"), ch_part(added(drop_mine, drop_theirs))
+    )
+    layer_output = (residual + team_scatter(layer_parts)).astype(BF)
 
     mixer_rows_grad, attn_grad, along, gain_part = rows_back(
         scalars, branch_grad, w_out, ssm, gating, mixer_root, own_gain
@@ -1180,10 +1191,25 @@
         key_value_grad = lax.psum_scatter(
             key_value_part.astype(BF), "ch", scatter_dimension=1, tiled=True
         ).astype(F32)
+    out_mine, out_theirs = grad_halves(order, branch_grad, branch_rows)
+    along, gate_theirs, drop_part, out_theirs = together(
+        along, gate_theirs, drop_part, out_theirs
+    )
+    lift_theirs, gate_part = together(
+        swap(lift_theirs, "sh"), ch_part(added(gate_mine, gate_theirs))
+    )
     ssm_grad, gating_grad, leaving_back = states_back(
         sl, step_pre, head, io, mixer_rows_grad, ssm, gating, mixer_root, along, own_gain, root
     )
     entry_back = entering(piece_decay[:, 0], leaving_back, True)
+    gating_rows_grad = jnp.concatenate([gating_grad, query_grad], 1)
+    gating_mine, gating_theirs = grad_halves(order, team_tokens, gating_rows_grad)
+    ssm_grad, layer_output, lift_theirs, gate_part, gating_theirs = together(
+        ssm_grad, layer_output, lift_theirs, gate_part, gating_theirs
+    )
+    out_theirs, lift_part = together(
+        swap(out_theirs, "sh"), ch_part(added(lift_mine, lift_theirs))
+    )
     inner_conv_grad, parts, step_rows_grad, sums = ssm_back(
         side_index,
         sl,
@@ -1198,9 +1224,14 @@
         root,
     )
     parts = lax.all_to_all(parts, TEAM, split_axis=0, concat_axis=0, tiled=True)
-    gating_rows_grad = jnp.concatenate([gating_grad, query_grad], 1)
-    gating_half = peers_half(order, team_tokens, gating_rows_grad)
-    out_half = peers_half(order, branch_grad, branch_rows)
+    parts, out_theirs, lift_part = together(parts, out_theirs, lift_part)
+    gating_theirs, out_part = together(
+        swap(gating_theirs, "sh"), ch_part(added(out_mine, out_theirs))
+    )
+    feed_back = ranks_return([drop_part, gate_part, lift_part], drows).astype(F32)
+    drop_back = feed_back[:, :, :LANES]
+    gate_back = feed_back[:, :, LANES : 2 * LANES]
+    lift_back = feed_back[:, :, 2 * LANES :]
     conv_grad, conv_sums = conv_back(inner_conv_grad, parts, conv, pre, edge)
     follow = shifted(conv_grad.reshape(sl, count, LANES)[:, :EDGE], -1)
     inner_rows_grad = pre_back(conv_grad, follow, taps, root)
@@ -1215,10 +1246,12 @@
             ],
         )
     )
-    inner_half = peers_half(order, team_tokens, inner_rows_grad)
-    mixer_back = ranks_return(
-        [peers_sum(*out_half), peers_sum(*gating_half), peers_sum(*inner_half)], drows
-    ).astype(F32)
+    inner_mine, inner_theirs = grad_halves(order, team_tokens, inner_rows_grad)
+    inner_theirs, gating_part = together(
+        swap(inner_theirs, "sh"), ch_part(added(gating_mine, gating_theirs))
+    )
+    inner_part = ch_part(added(inner_mine, inner_theirs))
+    mixer_back = ranks_return([out_part, gating_part, inner_part], drows).astype(F32)
     out_back = mixer_back[:, :, :LANES]
     gating_back = mixer_back[:, :, LANES : 2 * LANES]
     inner_back = mixer_back[:, :, 2 * LANES :]

time: 1040 us -> 907 us (0.87)
  waiting for transfers between devices: 434 us -> 306 us
    ppermute x80, waiting for transfers between devices: 414 us -> 291 us  [swap(): return lax.ppermute(value, axis, [(0, 1), (1, 0)])]
    unnamed x403 -> x342, local copies, waits for them, and re-layouts: 58.7 us -> 51.3 us
  transfers between devices with their start and end apart: 92 -> 92, of which waited for: 39 -> 42; matrix products, arithmetic and copies ran while one was open for 18% -> 21% of each run, Pallas kernels for 11% -> 13%
where the time goes in v3:
time: 907 us; the launch traced here: 897 us
  waiting for transfers between devices  306 us (34%)
  Pallas kernels  176 us (19%)
  local copies, waits for them, and re-layouts  144 us (16%)
  starting transfers between devices  134 us (15%)
  other arithmetic  119 us (13%)
  between operations  17.2 us (2%)
    ppermute x80, waiting for transfers between devices, swap(): return lax.ppermute(value, axis, [(0, 1), (1, 0)])  291 us
    ppermute x80, starting transfers between devices, swap(): return lax.ppermute(value, axis, [(0, 1), (1, 0)])  95.3 us
    unnamed x342, local copies, waits for them, and re-layouts  51.3 us
    pallas_call x14, Pallas kernels, grad_dot(): call(grad_dot_kernel, (half // tile,), [spec, spec, full(against)], pl.Bl...  41 us
    pallas_call x4, Pallas kernels, back_dot(): call(lambda *refs: back_dot_kernel(len(terms), halves, *refs), (2 * halve...  37.4 us
    pallas_call x1, Pallas kernels, ssm_back(): call(lambda *refs: ssm_back_kernel(blocks, *refs), (many,), [back(8), ful...  19.6 us
  transfers between devices with their start and end apart: 92, of which 42 were waited for; matrix products, arithmetic and copies ran while one was open for 21% of the time, Pallas kernels for 13%

profile of v3, /device:TPU:0, one launch (start us, length us, event | category | flops | bytes accessed | tf_op | source)
XLA Modules:
  0.0 896.9 jit_solution(7086703039874801542)
XLA Ops:
  32.9 7.1 collective-permute-done
  43.9 9.9 %collective-permute-done.1 = bf16[2,128,1024]{2,1,0:T(8,128)(2,1)S(1)} collective-permute-done((bf16[2,128,1024]{2,1,0:T(8,128)(2,1)S(1)}, bf16[2,128,1024]{2,1,0:T(8,128)(2,1)S(1)}, u32[]{:S(2)}, u32[]{:S(2)}) %collective-permute-start.1) | collective-permute-done | bytes 524320 | tf_op jit(solution)/shard_map/ppermute | solution.py:32
  80.4 24.7 %collective-permute-done.6 = bf16[512,512]{1,0:T(8,128)(2,1)} collective-permute-done((bf16[512,512]{1,0:T(8,128)(2,1)}, bf16[512,512]{1,0:T(8,128)(2,1)}, u32[]{:S(2)}, u32[]{:S(2)}) %collective-permute-start.6) | collective-permute-done | bytes 524320 | tf_op jit(solution)/shard_map/ppermute | solution.py:32
  121.7 9.7 %collective-permute-done.7.refs_6_.refs_4_ = bf16[1024,512]{1,0:T(8,128)(2,1)} collective-permute-done((bf16[1024,512]{1,0:T(8,128)(2,1)}, bf16[1024,512]{1,0:T(8,128)(2,1)}, u32[]{:S(2)}, u32[]{:S(2)}) %collective-permute-start.7) | collective-permute-done | bytes 1048608 | tf_op jit(solution)/shard_map/ppermute | solution.py:32
  131.4 10.4 %shard_map.381 = (f32[1024,512]{1,0:T(8,128)}, f32[1024,512]{1,0:T(8,128)}, bf16[1024,128]{1,0:T(8,128)(2,1)}, f32[1024,8]{1,0:T(8,128)S(1)}, f32[1024,1]{1,0:T(8,128)S(1)}, /*index=5*/f32[2,16,512]{2,1,0:T(8,128)S(1)}) custom-call(s32[5]{0:T(128)S(1)} %stack.168.refs_0_.scalars, bf16[4,128,1024]{2,1,0:T(8,128)(2,1)S(1)} %pad_maximum_fusion.2.refs_1_.l.own, ...), custom_call_target="tpu_custom_call" | custom-call | flops 1000000000 | bytes 1000000 | tf_op jit(solution)/shard_map/pallas_call | solution.py:317
  153.6 8.2 collective-permute-done.13
  178.3 8.1 collective-permute-done.14
  212.1 6.7 shard_map.383
  230.2 11.6 %shard_map.384 = (f32[1024,384]{1,0:T(8,128)S(1)}, bf16[8,256,384]{2,1,0:T(8,128)(2,1)S(1)}, f32[8,8,128]{2,1,0:T(8,128)S(1)}) custom-call(f32[1024,8]{1,0:T(8,128)S(1)} %copy-done.52, f32[8,8]{1,0:T(8,128)S(1)} %pad.16.refs_1_.refs_2_, f32[1024,512]{1,0:T(8,128)} %get-tuple-element.148.refs_2_.refs_3_, bf16[1024,512]{1,0:T(8,128)(2,1)S(1)} %copy-done.22, ...), custom_call_target="tpu_custom_call" | custom-call | flops 1000000000 | bytes 1000000 | tf_op jit(solution)/shard_map/pallas_call | solution.py:735
  245.3 18.8 %collective-permute-start.20 = (f32[8,128]{1,0:T(8,128)S(1)}, f32[8,128]{1,0:T(8,128)S(1)}, u32[]{:S(2)}, u32[]{:S(2)}) collective-permute-start(f32[8,128]{1,0:T(8,128)S(1)} %add.362), channel_id=1, source_target_pairs={{0,2},{2,0},{1,3},{3,1},{4,6},{6,4},{5,7},{7,5},{8,10},{10,8},{9,1... | collective-permute-start | bytes 12296 | tf_op jit(solution)/shard_map/ppermute | solution.py:32
  277.1 20.1 %collective-permute-done.22 = bf16[2,512,256]{1,0,2:T(2,128)(2,1)S(1)} collective-permute-done((bf16[2,512,256]{1,0,2:T(2,128)(2,1)}, bf16[2,512,256]{1,0,2:T(2,128)(2,1)S(1)}, u32[]{:S(2)}, u32[]{:S(2)}) %collective-permute-start.22) | collective-permute-done | bytes 524320 | tf_op jit(solution)/shard_map/ppermute | solution.py:32
  307.6 8.1 shard_map.386
  326.8 7.2 collective-permute-done.29
  334.4 16.3 %collective-permute-done.26 = bf16[2,128,1024]{2,1,0:T(8,128)(2,1)S(1)} collective-permute-done((bf16[2,128,1024]{2,1,0:T(8,128)(2,1)S(1)}, bf16[2,128,1024]{2,1,0:T(8,128)(2,1)S(1)}, u32[]{:S(2)}, u32[]{:S(2)}) %collective-permute-start.26) | collective-permute-done | bytes 524320 | tf_op jit(solution)/shard_map/ppermute | solution.py:32
  375.5 7.6 collective-permute-done.33
  383.2 10.0 %collective-permute-done.40 = bf16[512,512]{1,0:T(8,128)(2,1)S(1)} collective-permute-done((bf16[512,512]{1,0:T(8,128)(2,1)S(1)}, bf16[512,512]{1,0:T(8,128)(2,1)S(1)}, u32[]{:S(2)}, u32[]{:S(2)}) %collective-permute-start.40) | collective-permute-done | bytes 524320 | tf_op jit(solution)/shard_map/ppermute | solution.py:32
  398.7 17.1 %collective-permute-done.41.refs_13_.refs_4_ = bf16[1024,512]{1,0:T(8,128)(2,1)S(1)} collective-permute-done((bf16[1024,512]{1,0:T(8,128)(2,1)S(1)}, bf16[1024,512]{1,0:T(8,128)(2,1)S(1)}, u32[]{:S(2)}, u32[]{:S(2)}) %collective-permute-start.41) | collective-permute-done | bytes 1048608 | tf_op jit(solution)/shard_map/ppermute | solution.py:32
  418.2 11.6 %shard_map.387 = (bf16[1024,512]{1,0:T(8,128)(2,1)S(1)}, bf16[1024,512]{1,0:T(8,128)(2,1)S(1)}, bf16[1024,512]{1,0:T(8,128)(2,1)S(1)}) custom-call(bf16[4,128,1024]{2,1,0:T(8,128)(2,1)S(1)} %pad_maximum_fusion.11.refs_0_.own, bf16[4,128,1024]{2,1,0:T(8,128)(2,1)S(1)} %pad_maximum_fusion.12.refs_1_.own, bf16[4,128,1024]{2,1,0:T(8,128)(2,1)} %copy-done.31, ...), custom_call_target="tpu_custom_call" | custom-call | flops 1000000000 | bytes 1000000 | tf_op jit(solution)/shard_map/pallas_call | solution.py:533
  430.8 10.4 %shard_map.388 = (f32[4,128,1024]{2,1,0:T(8,128)}, f32[4,128,1024]{2,1,0:T(8,128)}, bf16[4,128,1024]{2,1,0:T(8,128)(2,1)S(1)}, bf16[4,128,1024]{2,1,0:T(8,128)(2,1)S(1)}) custom-call(s32[8]{0:T(128)S(1)} %iota.17.refs_0_, bf16[1024,512]{1,0:T(8,128)(2,1)S(1)} %get-tuple-element.175.refs_1_.refs_2_.against, ...), custom_call_target="tpu_custom_call" | custom-call | flops 1000000000 | bytes 1000000 | tf_op jit(solution)/shard_map/pallas_call | solution.py:446
  446.4 13.1 %collective-permute-done.46 = bf16[2,128,1024]{2,1,0:T(8,128)(2,1)S(1)} collective-permute-done((bf16[2,128,1024]{2,1,0:T(8,128)(2,1)S(1)}, bf16[2,128,1024]{2,1,0:T(8,128)(2,1)S(1)}, u32[]{:S(2)}, u32[]{:S(2)}) %collective-permute-start.46) | collective-permute-done | bytes 524320 | tf_op jit(solution)/shard_map/ppermute | solution.py:32
  507.2 6.6 shard_map.389
  522.9 9.4 %shard_map.393 = (f32[1024,384]{1,0:T(8,128)}, bf16[1024,128]{1,0:T(8,128)(2,1)S(1)}, f32[4,8,256]{2,1,0:T(8,128)S(1)}, f32[1,384]{1,0:T(1,128)S(1)}) custom-call(s32[5]{0:T(128)S(1)} %stack.168.refs_0_.scalars, bf16[4,128,1024]{2,1,0:T(8,128)(2,1)} %pad_maximum_fusion.16.l.own, bf16[4,128,1024]{2,1,0:T(8,128)(2,1)} %pad_maximum_fusion.17.r.own, ...), custom_call_target="tpu_custom_call" | custom-call | flops 1000000000 | bytes 1000000 | tf_op jit(solution)/shard_map/pallas_call | solution.py:384
  551.8 27.6 %collective-permute-done.69 = bf16[2,512,256]{2,1,0:T(8,128)(2,1)S(1)} collective-permute-done((bf16[2,512,256]{2,1,0:T(8,128)(2,1)S(1)}, bf16[2,512,256]{2,1,0:T(8,128)(2,1)S(1)}, u32[]{:S(2)}, u32[]{:S(2)}) %collective-permute-start.69) | collective-permute-done | bytes 524320 | tf_op jit(solution)/shard_map/ppermute | solution.py:32
  580.8 9.2 %collective-permute-done.59 = bf16[512,512]{1,0:T(8,128)(2,1)S(1)} collective-permute-done((bf16[512,512]{1,0:T(8,128)(2,1)S(1)}, bf16[512,512]{1,0:T(8,128)(2,1)S(1)}, u32[]{:S(2)}, u32[]{:S(2)}) %collective-permute-start.59) | collective-permute-done | bytes 524320 | tf_op jit(solution)/shard_map/ppermute | solution.py:32
  601.2 8.1 shard_map.396
  625.1 10.1 %collective-permute-done.67 = bf16[512,512]{1,0:T(8,128)(2,1)} collective-permute-done((bf16[512,512]{1,0:T(8,128)(2,1)}, bf16[512,512]{1,0:T(8,128)(2,1)}, u32[]{:S(2)}, u32[]{:S(2)}) %collective-permute-start.67) | collective-permute-done | bytes 524320 | tf_op jit(solution)/shard_map/ppermute | solution.py:32
  641.7 19.6 %shard_map.400 = (f32[1024,384]{1,0:T(8,128)S(1)}, bf16[8,1024,128]{2,1,0:T(8,128)(2,1)}, bf16[1024,8]{1,0:T(8,128)(2,1)S(1)}, f32[8,8]{1,0:T(8,128)S(1)}) custom-call(s32[1]{0:T(128)} %bitcast.89.refs_0_, f32[1024,8]{1,0:T(8,128)S(1)} %copy-done.53, f32[8,8]{1,0:T(8,128)S(1)} %pad.16.refs_1_.refs_2_, f32[1024,512]{1,0:T(8,128)} %get-tuple-element.148.refs_2_.refs_3_, ...), custom_call_target="tpu_custom_call" | custom-call | flops 1000000000 | bytes 1000000 | tf_op jit(solution)/shard_map/pallas_call | solution.py:895
  713.4 8.1 collective-permute-done.71
  758.9 12.3 %shard_map.404 = (f32[4,128,1024]{2,1,0:T(8,128)}, f32[4,128,1024]{2,1,0:T(8,128)}, bf16[4,128,1024]{2,1,0:T(8,128)(2,1)}, bf16[4,128,1024]{2,1,0:T(8,128)(2,1)}) custom-call(s32[8]{0:T(128)S(1)} %copy-done.77, bf16[1024,512]{1,0:T(8,128)(2,1)S(1)} %shard_map.403.refs_1_.refs_2_.against, bf16[1024,512]{1,0:T(8,128)(2,1)S(1)} %shard_map.403.refs_1_.refs_2_.against, ...), custom_call_target="tpu_custom_call" | custom-call | flops 1000000000 | bytes 1000000 | tf_op jit(solution)/shard_map/pallas_call | solution.py:446
  797.2 10.5 %collective-permute-done.82 = bf16[512,512]{1,0:T(8,128)(2,1)} collective-permute-done((bf16[512,512]{1,0:T(8,128)(2,1)}, bf16[512,512]{1,0:T(8,128)(2,1)}, u32[]{:S(2)}, u32[]{:S(2)}) %collective-permute-start.82) | collective-permute-done | bytes 524320 | tf_op jit(solution)/shard_map/ppermute | solution.py:32
  818.3 7.7 collective-permute-done.77
  827.4 17.5 %collective-permute-done.74 = bf16[2,128,1024]{2,1,0:T(8,128)(2,1)S(1)} collective-permute-done((bf16[2,128,1024]{2,1,0:T(8,128)(2,1)S(1)}, bf16[2,128,1024]{2,1,0:T(8,128)(2,1)S(1)}, u32[]{:S(2)}, u32[]{:S(2)}) %collective-permute-start.74) | collective-permute-done | bytes 524320 | tf_op jit(solution)/shard_map/ppermute | solution.py:32
  (804 shorter events, 496.2 us)
Async XLA Ops:
  14.6 42.3 %all-to-all-start = ((bf16[8,64,1024]{2,1,0:T(8,128)(2,1)}), bf16[8,64,1024]{2,1,0:T(8,128)(2,1)}, u32[]{:S(2)}, u32[]{:S(2)}) async-start(bf16[8,64,1024]{2,1,0:T(8,128)(2,1)} %concatenate.119), calls=%async_computation | async-start | bytes 2097152 | tf_op jit(solution)/shard_map/all_to_all | solution.py:121
  66.5 38.5 %collective-permute-start.6 = (bf16[512,512]{1,0:T(8,128)(2,1)}, bf16[512,512]{1,0:T(8,128)(2,1)}, u32[]{:S(2)}, u32[]{:S(2)}) collective-permute-start(bf16[512,512]{1,0:T(8,128)(2,1)} %get-tuple-element.271), channel_id=1, source_target_pairs={{0,4},{4,0},{1,5},{5,1},{2,6},{6,2},{3,7},{7,3},{8,12},{12,8},{9,1... | collective-permute-start | bytes 1572872 | tf_op jit(solution)/shard_map/ppermute | solution.py:32
  69.2 50.2 %collective-permute-start.8 = (bf16[512,512]{1,0:T(8,128)(2,1)}, bf16[512,512]{1,0:T(8,128)(2,1)}, u32[]{:S(2)}, u32[]{:S(2)}) collective-permute-start(bf16[512,512]{1,0:T(8,128)(2,1)} %get-tuple-element.270), channel_id=1, source_target_pairs={{0,4},{4,0},{1,5},{5,1},{2,6},{6,2},{3,7},{7,3},{8,12},{12,8},{9,1... | collective-permute-start | bytes 1572872 | tf_op jit(solution)/shard_map/ppermute | solution.py:32
  74.4 97.1 %all-to-all-start.2 = ((bf16[8,64,2048]{2,1,0:T(8,128)(2,1)}), bf16[8,64,2048]{2,1,0:T(8,128)(2,1)}, u32[]{:S(2)}, u32[]{:S(2)}) async-start(bf16[8,64,2048]{2,1,0:T(8,128)(2,1)} %fusion.28), calls=%async_computation.2 | async-start | bytes 4194304 | tf_op jit(solution)/shard_map/all_to_all | solution.py:121
  78.8 119.4 %all-gather.3.cloned.1.call-start = ((), (), s32[]{:S(2)}) async-start(), calls=%async_computation.7 | async-start | bytes 2359296 | tf_op jit(solution)/shard_map/all_gather | solution.py:1129
  188.6 41.1 %collective-permute-start.17 = (bf16[4,128,1024]{2,1,0:T(8,128)(2,1)}, bf16[4,128,1024]{2,1,0:T(8,128)(2,1)}, u32[]{:S(2)}, u32[]{:S(2)}) collective-permute-start(bf16[4,128,1024]{2,1,0:T(8,128)(2,1)} %pad_maximum_fusion.7.refs_4_.own), channel_id=1, source_target_pairs={{0,1},{1,0},{2,3},{3,2},{4,5},{5,4},{6,7},{7,6},{8,9},{9,8},{10,11... | collective-permute-start | bytes 3145736 | tf_op jit(solution)/shard_map/ppermute | solution.py:32
  191.8 37.9 %collective-permute-start.18 = (bf16[4,128,1024]{2,1,0:T(8,128)(2,1)}, bf16[4,128,1024]{2,1,0:T(8,128)(2,1)}, u32[]{:S(2)}, u32[]{:S(2)}) collective-permute-start(bf16[4,128,1024]{2,1,0:T(8,128)(2,1)} %pad_maximum_fusion.8.refs_5_.own), channel_id=1, source_target_pairs={{0,1},{1,0},{2,3},{3,2},{4,5},{5,4},{6,7},{7,6},{8,9},{9,8},{10,11... | collective-permute-start | bytes 3145736 | tf_op jit(solution)/shard_map/ppermute | solution.py:32
  197.6 76.1 %collective-permute-start.23 = (bf16[1024,512]{1,0:T(8,128)(2,1)}, bf16[1024,512]{1,0:T(8,128)(2,1)}, u32[]{:S(2)}, u32[]{:S(2)}) collective-permute-start(bf16[1024,512]{1,0:T(8,128)(2,1)} %pad_maximum_fusion.6.refs_3_.mine), channel_id=1, source_target_pairs={{0,16},{16,0},{1,17},{17,1},{2,18},{18,2},{3,19},{19,3},{4,20},{20... | collective-permute-start | bytes 3145736 | tf_op jit(solution)/shard_map/ppermute | solution.py:32
  221.3 42.7 %collective-permute-start.24 = (bf16[512,512]{1,0:T(8,128)(2,1)}, bf16[512,512]{1,0:T(8,128)(2,1)}, u32[]{:S(2)}, u32[]{:S(2)}) collective-permute-start(bf16[512,512]{1,0:T(8,128)(2,1)} %get-tuple-element.262), channel_id=1, source_target_pairs={{0,4},{4,0},{1,5},{5,1},{2,6},{6,2},{3,7},{7,3},{8,12},{12,8},{9,1... | collective-permute-start | bytes 1572872 | tf_op jit(solution)/shard_map/ppermute | solution.py:32
  321.8 31.2 %collective-permute-start.38 = (bf16[512,512]{1,0:T(8,128)(2,1)S(1)}, bf16[512,512]{1,0:T(8,128)(2,1)S(1)}, u32[]{:S(2)}, u32[]{:S(2)}) collective-permute-start(bf16[512,512]{1,0:T(8,128)(2,1)S(1)} %copy-done.124), channel_id=1, source_target_pairs={{0,4},{4,0},{1,5},{5,1},{2,6},{6,2},{3,7},{7,3},{8,12},{12,8},{9,1... | collective-permute-start | bytes 1572872 | tf_op jit(solution)/shard_map/ppermute | solution.py:32
  321.8 32.2 %collective-permute-start.37 = (bf16[1024,512]{1,0:T(8,128)(2,1)S(1)}, bf16[1024,512]{1,0:T(8,128)(2,1)S(1)}, u32[]{:S(2)}, u32[]{:S(2)}) collective-permute-start(bf16[1024,512]{1,0:T(8,128)(2,1)S(1)} %copy-done.27), channel_id=1, source_target_pairs={{0,16},{16,0},{1,17},{17,1},{2,18},{18,2},{3,19},{19,3},{4,20},{20... | collective-permute-start | bytes 3145736 | tf_op jit(solution)/shard_map/ppermute | solution.py:32
  355.0 38.2 %collective-permute-start.39 = (bf16[1024,512]{1,0:T(8,128)(2,1)}, bf16[1024,512]{1,0:T(8,128)(2,1)}, u32[]{:S(2)}, u32[]{:S(2)}) collective-permute-start(bf16[1024,512]{1,0:T(8,128)(2,1)} %pad_maximum_fusion.13.refs_10_.refs_7_), channel_id=1, source_target_pairs={{0,16},{16,0},{1,17},{17,1},{2,18},{18,2},{3,19},{19,3},{4,20},{20... | collective-permute-start | bytes 3145736 | tf_op jit(solution)/shard_map/ppermute | solution.py:32
  494.0 28.8 %collective-permute-start.54 = (bf16[1024,512]{1,0:T(8,128)(2,1)}, bf16[1024,512]{1,0:T(8,128)(2,1)}, u32[]{:S(2)}, u32[]{:S(2)}) collective-permute-start(bf16[1024,512]{1,0:T(8,128)(2,1)} %shard_map.390), channel_id=1, source_target_pairs={{0,16},{16,0},{1,17},{17,1},{2,18},{18,2},{3,19},{19,3},{4,20},{20... | collective-permute-start | bytes 3145736 | tf_op jit(solution)/shard_map/ppermute | solution.py:32
  532.4 58.6 %collective-permute-start.58 = (bf16[1024,512]{1,0:T(8,128)(2,1)S(1)}, bf16[1024,512]{1,0:T(8,128)(2,1)S(1)}, u32[]{:S(2)}, u32[]{:S(2)}) collective-permute-start(bf16[1024,512]{1,0:T(8,128)(2,1)S(1)} %shard_map.391), channel_id=1, source_target_pairs={{0,16},{16,0},{1,17},{17,1},{2,18},{18,2},{3,19},{19,3},{4,20},{20... | collective-permute-start | bytes 3145736 | tf_op jit(solution)/shard_map/ppermute | solution.py:32
  534.2 58.8 %collective-permute-start.63 = (bf16[4,128,1024]{2,1,0:T(8,128)(2,1)}, bf16[4,128,1024]{2,1,0:T(8,128)(2,1)}, u32[]{:S(2)}, u32[]{:S(2)}) collective-permute-start(bf16[4,128,1024]{2,1,0:T(8,128)(2,1)} %get-tuple-element.201), channel_id=1, source_target_pairs={{0,1},{1,0},{2,3},{3,2},{4,5},{5,4},{6,7},{7,6},{8,9},{9,8},{10,11... | collective-permute-start | bytes 3145736 | tf_op jit(solution)/shard_map/ppermute | solution.py:32
  541.5 37.9 %collective-permute-start.69 = (bf16[2,512,256]{2,1,0:T(8,128)(2,1)S(1)}, bf16[2,512,256]{2,1,0:T(8,128)(2,1)S(1)}, u32[]{:S(2)}, u32[]{:S(2)}) collective-permute-start(bf16[2,512,256]{2,1,0:T(8,128)(2,1)S(1)} %fusion.27), channel_id=1, source_target_pairs={{0,4},{4,0},{1,5},{5,1},{2,6},{6,2},{3,7},{7,3},{8,12},{12,8},{9,1... | collective-permute-start | bytes 1572872 | tf_op jit(solution)/shard_map/ppermute | solution.py:32
  546.2 43.8 %collective-permute-start.59 = (bf16[512,512]{1,0:T(8,128)(2,1)S(1)}, bf16[512,512]{1,0:T(8,128)(2,1)S(1)}, u32[]{:S(2)}, u32[]{:S(2)}) collective-permute-start(bf16[512,512]{1,0:T(8,128)(2,1)S(1)} %slice.741), channel_id=1, source_target_pairs={{0,4},{4,0},{1,5},{5,1},{2,6},{6,2},{3,7},{7,3},{8,12},{12,8},{9,1... | collective-permute-start | bytes 1572872 | tf_op jit(solution)/shard_map/ppermute | solution.py:32
  547.7 48.2 %collective-permute-start.60 = (bf16[4,128,1024]{2,1,0:T(8,128)(2,1)}, bf16[4,128,1024]{2,1,0:T(8,128)(2,1)}, u32[]{:S(2)}, u32[]{:S(2)}) collective-permute-start(bf16[4,128,1024]{2,1,0:T(8,128)(2,1)} %get-tuple-element.199), channel_id=1, source_target_pairs={{0,1},{1,0},{2,3},{3,2},{4,5},{5,4},{6,7},{7,6},{8,9},{9,8},{10,11... | collective-permute-start | bytes 3145736 | tf_op jit(solution)/shard_map/ppermute | solution.py:32
  579.4 57.9 %collective-permute-start.66 = (bf16[1024,512]{1,0:T(8,128)(2,1)}, bf16[1024,512]{1,0:T(8,128)(2,1)}, u32[]{:S(2)}, u32[]{:S(2)}) collective-permute-start(bf16[1024,512]{1,0:T(8,128)(2,1)} %shard_map.392), channel_id=1, source_target_pairs={{0,16},{16,0},{1,17},{17,1},{2,18},{18,2},{3,19},{19,3},{4,20},{20... | collective-permute-start | bytes 3145736 | tf_op jit(solution)/shard_map/ppermute | solution.py:32
  599.5 35.7 %collective-permute-start.67 = (bf16[512,512]{1,0:T(8,128)(2,1)}, bf16[512,512]{1,0:T(8,128)(2,1)}, u32[]{:S(2)}, u32[]{:S(2)}) collective-permute-start(bf16[512,512]{1,0:T(8,128)(2,1)} %slice.740), channel_id=1, source_target_pairs={{0,4},{4,0},{1,5},{5,1},{2,6},{6,2},{3,7},{7,3},{8,12},{12,8},{9,1... | collective-permute-start | bytes 1572872 | tf_op jit(solution)/shard_map/ppermute | solution.py:32
  610.5 31.3 %collective-permute-start.68 = (bf16[2,256,384]{2,1,0:T(8,128)(2,1)S(1)}, bf16[2,256,384]{2,1,0:T(8,128)(2,1)S(1)}, u32[]{:S(2)}, u32[]{:S(2)}) collective-permute-start(bf16[2,256,384]{2,1,0:T(8,128)(2,1)S(1)} %get-tuple-element.213), channel_id=1, source_target_pairs={{4,0},{5,1},{6,2},{7,3},{12,8},{13,9},{14,10},{15,11},{20,16},{21,... | collective-permute-start | bytes 1179656 | tf_op jit(solution)/shard_map/ppermute | solution.py:166
  662.5 61.3 %all-to-all-start.3 = ((bf16[8,1024,128]{2,1,0:T(8,128)(2,1)}), bf16[8,1024,128]{2,1,0:T(8,128)(2,1)}, u32[]{:S(2)}, u32[]{:S(2)}) async-start(bf16[8,1024,128]{2,1,0:T(8,128)(2,1)} %get-tuple-element.216), calls=%async_computation.3 | async-start | bytes 4194304 | tf_op jit(solution)/shard_map/all_to_all | solution.py:1226
  681.5 42.3 %collective-permute-start.70 = (bf16[1024,512]{1,0:T(8,128)(2,1)}, bf16[1024,512]{1,0:T(8,128)(2,1)}, u32[]{:S(2)}, u32[]{:S(2)}) collective-permute-start(bf16[1024,512]{1,0:T(8,128)(2,1)} %shard_map.395), channel_id=1, source_target_pairs={{0,16},{16,0},{1,17},{17,1},{2,18},{18,2},{3,19},{19,3},{4,20},{20... | collective-permute-start | bytes 3145736 | tf_op jit(solution)/shard_map/ppermute | solution.py:32
  695.1 83.4 %collective-permute-start.79 = (bf16[1024,512]{1,0:T(8,128)(2,1)}, bf16[1024,512]{1,0:T(8,128)(2,1)}, u32[]{:S(2)}, u32[]{:S(2)}) collective-permute-start(bf16[1024,512]{1,0:T(8,128)(2,1)} %shard_map.399), channel_id=1, source_target_pairs={{0,16},{16,0},{1,17},{17,1},{2,18},{18,2},{3,19},{19,3},{4,20},{20... | collective-permute-start | bytes 3145736 | tf_op jit(solution)/shard_map/ppermute | solution.py:32
  734.5 41.9 %collective-permute-start.80 = (bf16[512,512]{1,0:T(8,128)(2,1)}, bf16[512,512]{1,0:T(8,128)(2,1)}, u32[]{:S(2)}, u32[]{:S(2)}) collective-permute-start(bf16[512,512]{1,0:T(8,128)(2,1)} %slice.738), channel_id=1, source_target_pairs={{0,4},{4,0},{1,5},{5,1},{2,6},{6,2},{3,7},{7,3},{8,12},{12,8},{9,1... | collective-permute-start | bytes 1572872 | tf_op jit(solution)/shard_map/ppermute | solution.py:32
  751.2 36.5 %all-to-all-start.5 = ((f32[32,1,1184]{2,1,0:T(1,128)}), f32[32,1,1184]{2,1,0:T(1,128)}, u32[]{:S(2)}, u32[]{:S(2)}) async-start(f32[32,1,1184]{2,1,0:T(1,128)} %copy.345), calls=%async_computation.5 | async-start | bytes 327680 | tf_op jit(solution)/shard_map/all_to_all | solution.py:1297
  771.3 37.9 %collective-permute-start.76 = (bf16[4,128,1024]{2,1,0:T(8,128)(2,1)}, bf16[4,128,1024]{2,1,0:T(8,128)(2,1)}, u32[]{:S(2)}, u32[]{:S(2)}) collective-permute-start(bf16[4,128,1024]{2,1,0:T(8,128)(2,1)} %get-tuple-element.229), channel_id=1, source_target_pairs={{0,1},{1,0},{2,3},{3,2},{4,5},{5,4},{6,7},{7,6},{8,9},{9,8},{10,11... | collective-permute-start | bytes 3145736 | tf_op jit(solution)/shard_map/ppermute | solution.py:32
  771.5 41.1 %collective-permute-start.73 = (bf16[4,128,1024]{2,1,0:T(8,128)(2,1)}, bf16[4,128,1024]{2,1,0:T(8,128)(2,1)}, u32[]{:S(2)}, u32[]{:S(2)}) collective-permute-start(bf16[4,128,1024]{2,1,0:T(8,128)(2,1)} %get-tuple-element.227), channel_id=1, source_target_pairs={{0,1},{1,0},{2,3},{3,2},{4,5},{5,4},{6,7},{7,6},{8,9},{9,8},{10,11... | collective-permute-start | bytes 3145736 | tf_op jit(solution)/shard_map/ppermute | solution.py:32
  786.1 28.3 %collective-permute-start.81 = (bf16[1024,512]{1,0:T(8,128)(2,1)S(1)}, bf16[1024,512]{1,0:T(8,128)(2,1)S(1)}, u32[]{:S(2)}, u32[]{:S(2)}) collective-permute-start(bf16[1024,512]{1,0:T(8,128)(2,1)S(1)} %shard_map.406), channel_id=1, source_target_pairs={{0,16},{16,0},{1,17},{17,1},{2,18},{18,2},{3,19},{19,3},{4,20},{20... | collective-permute-start | bytes 3145736 | tf_op jit(solution)/shard_map/ppermute | solution.py:32
  787.7 66.5 %all-to-all-start.6 = ((bf16[8,64,1536]{2,1,0:T(8,128)(2,1)}), bf16[8,64,1536]{2,1,0:T(8,128)(2,1)}, u32[]{:S(2)}, u32[]{:S(2)}) async-start(bf16[8,64,1536]{2,1,0:T(8,128)(2,1)} %pad_maximum_fusion.1), calls=%async_computation.6 | async-start | bytes 3145728 | tf_op jit(solution)/shard_map/all_to_all | solution.py:137
  813.8 31.1 %collective-permute-start.74 = (bf16[2,128,1024]{2,1,0:T(8,128)(2,1)S(1)}, bf16[2,128,1024]{2,1,0:T(8,128)(2,1)S(1)}, u32[]{:S(2)}, u32[]{:S(2)}) collective-permute-start(bf16[2,128,1024]{2,1,0:T(8,128)(2,1)S(1)} %add_convert_fusion.1), channel_id=1, source_target_pairs={{0,2},{2,0},{1,3},{3,1},{4,6},{6,4},{5,7},{7,5},{8,10},{10,8},{9,1... | collective-permute-start | bytes 1572872 | tf_op jit(solution)/shard_map/ppermute | solution.py:32
  814.8 33.1 %collective-permute-start.83 = (bf16[512,512]{1,0:T(8,128)(2,1)S(1)}, bf16[512,512]{1,0:T(8,128)(2,1)S(1)}, u32[]{:S(2)}, u32[]{:S(2)}) collective-permute-start(bf16[512,512]{1,0:T(8,128)(2,1)S(1)} %slice.736), channel_id=1, source_target_pairs={{0,4},{4,0},{1,5},{5,1},{2,6},{6,2},{3,7},{7,3},{8,12},{12,8},{9,1... | collective-permute-start | bytes 1572872 | tf_op jit(solution)/shard_map/ppermute | solution.py:32
  (223 other events, 2646.8 us)
Sparse Core Ops, SparseCore 0:
  144.2 28.7 all-gather.2

commit v4 on v3

--- a/solution.py
+++ b/solution.py
@@ -60,9 +60,7 @@
     return jnp.stack(blocks).astype(jnp.int32)
 
 
-def team_gather(rows):
-    half = rows.shape[1] // 2
-    left, right = rows[:, :half], rows[:, half:]
+def team_gather(left, right):
     left = jnp.stack([left, swap(left, "sl")])
     right = jnp.stack([right, swap(right, "zl")])
     left_z = swap(left, "zl")
@@ -72,16 +70,31 @@
     return left, right, swap(left, "core"), swap(right, "core")
 
 
-def team_scatter(parts):
+def scatter_core(parts):
     left, right, left_given, right_given = parts
     left_got, right_got = swap(left_given, "core"), swap(right_given, "core")
-    left_z = swap(added(left[2:], left_got[2:]).astype(BF), "zl")
-    right_x = swap(added(right[1::2], right_got[1::2]).astype(BF), "sl")
-    left = added(left[:2], left_got[:2]) + left_z.astype(F32)
-    right = added(right[0::2], right_got[0::2]) + right_x.astype(F32)
-    left_x = swap(left[1].astype(BF), "sl")
-    right_z = swap(right[1].astype(BF), "zl")
-    return jnp.concatenate([added(left[0], left_x), added(right[0], right_z)], 1)
+    return (
+        added(left[:2], left_got[:2]),
+        added(left[2:], left_got[2:]).astype(BF),
+        added(right[0::2], right_got[0::2]),
+        added(right[1::2], right_got[1::2]).astype(BF),
+    )
+
+
+def scatter_near(parts):
+    left, left_given, right, right_given = parts
+    left = left + swap(left_given, "zl").astype(F32)
+    right = right + swap(right_given, "sl").astype(F32)
+    return left[0], left[1].astype(BF), right[0], right[1].astype(BF)
+
+
+def scatter_last(parts):
+    left, left_given, right, right_given = parts
+    return left, swap(left_given, "sl"), right, swap(right_given, "zl")
+
+
+def team_scatter(parts):
+    return scatter_last(scatter_near(scatter_core(parts)))
 
 
 def team_sum(value):
@@ -146,16 +159,11 @@
     return pieces.transpose(1, 0, 2).reshape(pieces.shape[1], -1)
 
 
-def shuffled(rows, sh, sl, ch):
-    count, width = rows.shape
-    rows = rows.reshape(count, sh, sl, ch, -1).swapaxes(2, 3)
-    return relative(relative(rows, "sh", 1), "ch", 2).reshape(count, width)
-
-
-def unshuffled(rows, sh, sl, ch):
-    count, width = rows.shape
-    rows = relative(relative(rows.reshape(count, sh, ch, sl, -1), "sh", 1), "ch", 2)
-    return rows.swapaxes(2, 3).reshape(count, width)
+def column_blocks(sh, sl, ch):
+    place = lax.axis_index("sh")
+    if ch == 2:
+        place = place * 2 + lax.axis_index("ch")
+    return place.astype(jnp.int32).reshape(1)
 
 
 def shifted(value, steps):
@@ -224,7 +232,10 @@
 CONV = INNER + SIDE
 
 
-def call(kernel, grid, in_specs, out_specs, out_shape, scratch=(), scalars=0):
+COST = 0.4e9
+
+
+def call(cost, kernel, grid, in_specs, out_specs, out_shape, scratch=(), scalars=0):
     return pl.pallas_call(
         kernel,
         grid_spec=pltpu.PrefetchScalarGridSpec(
@@ -236,7 +247,7 @@
         ),
         out_shape=out_shape,
         compiler_params=pltpu.CompilerParams(vmem_limit_bytes=48 * 1024 * 1024),
-        cost_estimate=pl.CostEstimate(flops=10**9, bytes_accessed=10**6, transcendentals=0),
+        cost_estimate=pl.CostEstimate(flops=int(cost * COST), bytes_accessed=10**6, transcendentals=0),
     )
 
 
@@ -264,7 +275,7 @@
 
 
 def gathered_specs(gathered):
-    spec = pl.BlockSpec((1,) + gathered[0].shape[1:], lambda i, s: (s[1 + i], 0, 0))
+    spec = pl.BlockSpec((1, BLOCK, gathered[0].shape[2]), lambda i, s: (s[1 + i], 0, 0))
     return [spec] * 4
 
 
@@ -278,7 +289,172 @@
     return lax.rsqrt(jnp.mean(values * values, axis=-1, keepdims=True) + epsilon)
 
 
-def project_inner_kernel(tiles, scalars, l, r, lo, ro, mine, theirs, halo, taps, steps, pre_ref, conv_ref, side_ref, step_ref, root_ref, edge_ref, rows, line):
+def natural_blocks(dims):
+    sh, sl, ch, width = dims
+    block = width // (sh * sl * ch)
+    return [
+        (((a * sl + b) * ch + c) * block, ((a * ch + c) * sl + b) * block, block)
+        for a in range(sh)
+        for b in range(sl)
+        for c in range(ch)
+    ]
+
+
+def related(place, start, dims):
+    sh, _, ch, width = dims
+    unit = width // (sh * ch) if ch == 2 else width // sh
+    return pl.multiple_of(lax.bitwise_xor(place, start // unit) * unit + start % unit, 128)
+
+
+def related_blocks(dims):
+    sh, _, ch, width = dims
+    unit = width // (sh * ch) if ch == 2 else width // sh
+    return range(0, width, unit), unit
+
+
+def whole_blocks(width):
+    return pl.BlockSpec((BLOCK, width), lambda i, s: (0, 0))
+
+
+def shuffle_kernel(dims, place, rows, out_refs, scratch):
+    width = dims[3]
+    for natural, start, block in natural_blocks(dims):
+        scratch[:, start : start + block] = rows[:, natural : natural + block].astype(F32)
+    starts, unit = related_blocks(dims)
+    for start in starts:
+        at = related(place, start, dims)
+        out = out_refs[start // (width // 2)]
+        inside = start % (width // 2)
+        out[:, inside : inside + unit] = scratch[:, pl.ds(at, unit)].astype(BF)
+
+
+def arrive_kernel(dims, place, tokens, cotangent, tl, tr, whole, scratch):
+    half = dims[3] // 2
+    shuffle_kernel(dims, place[0], tokens, (tl, tr), scratch)
+    shuffle_kernel(dims, place[0], cotangent, (whole.at[:, :half], whole.at[:, half:]), scratch)
+
+
+def arrive(dims, place, tokens, cotangent):
+    width = dims[3]
+    half = shape((BLOCK, width // 2), BF)
+    return call(
+        2.0,
+        lambda *refs: arrive_kernel(dims, *refs),
+        (1,),
+        [whole_blocks(width)] * 2,
+        [whole_blocks(width // 2)] * 2 + [whole_blocks(width)],
+        [half] * 2 + [shape((BLOCK, width), BF)],
+        [pltpu.VMEM((BLOCK, width), F32)],
+        1,
+    )(place, tokens, cotangent)
+
+
+def leave_kernel(dims, added_to, place, rows, *refs):
+    out, scratch = refs[-2], refs[-1]
+    values = rows[...].astype(F32)
+    if added_to:
+        values = values + refs[0][...].astype(F32)
+    scratch[...] = values
+    sh, _, ch, width = dims
+    unit = related_blocks(dims)[1]
+    for natural, start, block in natural_blocks(dims):
+        at = pl.multiple_of(related(place[0], start // unit * unit, dims), 128)
+        if block % 128 == 0:
+            got = scratch[:, pl.ds(pl.multiple_of(at + start % unit, 128), block)]
+        else:
+            got = scratch[:, pl.ds(at, unit)][:, start % unit : start % unit + block]
+        out[:, natural : natural + block] = got.astype(out.dtype)
+
+
+def leave(dims, place, rows, ordered, dtype):
+    width = dims[3]
+    ins = [rows] if ordered is None else [rows, ordered]
+    return call(
+        1.5,
+        lambda *refs: leave_kernel(dims, ordered is not None, *refs),
+        (1,),
+        [whole_blocks(width)] * len(ins),
+        whole_blocks(width),
+        shape((BLOCK, width), dtype),
+        [pltpu.VMEM((BLOCK, width), F32)],
+        1,
+    )(place, *ins)
+
+
+def home_forward_kernel(dims, place, left, left_rest, right, right_rest, tl, tr, residual_ref, root_ref, l_ref, r_ref):
+    half = left.shape[1]
+    a = tl[...].astype(F32) + left[...] + left_rest[...].astype(F32)
+    b = tr[...].astype(F32) + right[...] + right_rest[...].astype(F32)
+    square = jnp.sum(a * a, axis=-1, keepdims=True) + jnp.sum(b * b, axis=-1, keepdims=True)
+    root = lax.rsqrt(square / (2 * half) + epsilon)
+    residual_ref[:, :half] = a
+    residual_ref[:, half:] = b
+    root_ref[...] = root
+    starts, unit = related_blocks(dims)
+    for start in starts:
+        out, inside = (l_ref, start) if start < half else (r_ref, start - half)
+        rows = residual_ref[:, pl.ds(related(place[0], start, dims), unit)]
+        out[:, inside : inside + unit] = (rows * root).astype(BF)
+
+
+def home_forward(dims, place, parts, tokens):
+    half = dims[3] // 2
+    return call(
+        1.4,
+        lambda *refs: home_forward_kernel(dims, *refs),
+        (1,),
+        [whole_blocks(half)] * 6,
+        [whole_blocks(2 * half), whole_blocks(1), whole_blocks(half), whole_blocks(half)],
+        [
+            shape((BLOCK, 2 * half)),
+            shape((BLOCK, 1)),
+            shape((BLOCK, half), BF),
+            shape((BLOCK, half), BF),
+        ],
+        (),
+        1,
+    )(place, *parts, *tokens)
+
+
+def home_back_kernel(dims, place, left, left_rest, right, right_rest, values, root, base, grad_ref, l_ref, r_ref, scratch):
+    half = left.shape[1]
+    width = 2 * half
+    scaled = root[...]
+    scratch[:, :half] = left[...] + left_rest[...].astype(F32)
+    scratch[:, half:] = right[...] + right_rest[...].astype(F32)
+    starts, unit = related_blocks(dims)
+    mean = jnp.zeros_like(scaled)
+    for start in starts:
+        norm = values[:, pl.ds(related(place[0], start, dims), unit)].astype(F32) * scaled
+        up = scratch[:, start : start + unit]
+        mean = mean + jnp.sum(up * norm, axis=-1, keepdims=True)
+    mean = mean / width
+    for start in starts:
+        at = related(place[0], start, dims)
+        norm = values[:, pl.ds(at, unit)].astype(F32) * scaled
+        up = scratch[:, start : start + unit]
+        grad_ref[:, pl.ds(at, unit)] = base[:, pl.ds(at, unit)].astype(F32) + scaled * (
+            up - norm * mean
+        )
+    l_ref[...] = grad_ref[:, :half].astype(BF)
+    r_ref[...] = grad_ref[:, half:].astype(BF)
+
+
+def home_back(dims, place, parts, values, root, base):
+    half = dims[3] // 2
+    return call(
+        1.4,
+        lambda *refs: home_back_kernel(dims, *refs),
+        (1,),
+        [whole_blocks(half)] * 4 + [whole_blocks(2 * half), whole_blocks(1), whole_blocks(2 * half)],
+        [whole_blocks(2 * half), whole_blocks(half), whole_blocks(half)],
+        [shape((BLOCK, 2 * half)), shape((BLOCK, half), BF), shape((BLOCK, half), BF)],
+        [pltpu.VMEM((BLOCK, 2 * half), F32)],
+        1,
+    )(place, *parts, values, root, base)
+
+
+def project_inner_kernel(tiles, scalars, l, r, lo, ro, mine, theirs, halo, taps, steps, pre_ref, conv_ref, side_ref, keys_ref, step_ref, root_ref, edge_ref, rows, line):
     i = pl.program_id(0)
     place_rows(scalars, (l, r, lo, ro), rows)
     values = rows[...]
@@ -304,17 +480,17 @@
     for k in range(KC):
         conv = conv + taps[k : k + 1, :] * line[EDGE - (KC - 1) + k : EDGE - (KC - 1) + k + TILE, :]
     conv_ref[...] = conv
-    last = conv[:, INNER:]
-    lane = lax.broadcasted_iota(jnp.int32, last.shape, 1)
-    side_ref[...] = jnp.where(lane < SIDE, silu_value(last), last).astype(BF)
+    side_ref[...] = silu_value(conv[:, INNER:CONV]).astype(BF)
+    keys_ref[...] = pre[:, CONV:].astype(BF)
 
 
 def project_inner(scalars, gathered, weight, halo, taps, steps):
     seqs = halo.shape[0]
-    total = 2 * 4 * gathered[0].shape[1]
+    total = 2 * 4 * BLOCK
     tiles = total // TILE // seqs
     width = 2 * gathered[0].shape[2]
     return call(
+        10.4,
         lambda *refs: project_inner_kernel(tiles, *refs),
         (total // TILE,),
         gathered_specs(gathered)
@@ -323,7 +499,8 @@
         [
             tiled(LANES),
             tiled(LANES),
-            tiled(2 * SIDE),
+            tiled(SIDE),
+            tiled(SIDE),
             tiled(8),
             tiled(1),
             pl.BlockSpec((1, EDGE, LANES), lambda i, s: (i // tiles, 0, 0)),
@@ -331,7 +508,8 @@
         [
             shape((total, LANES)),
             shape((total, LANES)),
-            shape((total, 2 * SIDE), BF),
+            shape((total, SIDE), BF),
+            shape((total, SIDE), BF),
             shape((total, 8)),
             shape((total, 1)),
             shape((seqs, EDGE, LANES)),
@@ -351,6 +529,7 @@
 def project_gating(scalars, gathered, weight, root):
     total, width = root.shape[0], 2 * gathered[0].shape[2]
     return call(
+        6.2,
         project_gating_kernel,
         (total // TILE,),
         gathered_specs(gathered) + [full(weight[0]), full(weight[1]), tiled(1)],
@@ -382,6 +561,7 @@
     total, width = root.shape[0], 2 * gathered[0].shape[2]
     tiles = total // TILE
     return call(
+        9.5,
         rows_back_kernel,
         (tiles,),
         gathered_specs(gathered)
@@ -444,6 +624,7 @@
     given_spec = pl.BlockSpec((2, BLOCK, half), lambda i, s: (jnp.minimum(i, halves - 1), 0, 0))
     blocks = total // BLOCK // 2
     return call(
+        3.0 + 3.0 * len(terms),
         lambda *refs: back_dot_kernel(len(terms), halves, *refs),
         (2 * halves,),
         specs,
@@ -470,73 +651,110 @@
     out[...] = product.astype(out.dtype)
 
 
-def grad_dot(order, own, other, against, dtype):
-    half = own.shape[2]
+def grad_dot(order, parts, against, dtype):
     total, width = against.shape
+    blocks = total // BLOCK // 2
     tile = 512
-    spec = pl.BlockSpec((own.shape[0], own.shape[1], tile), lambda i, s: (0, 0, i))
+    half = parts[0][3]
+    specs = [
+        pl.BlockSpec((blocks, BLOCK, tile), lambda i, s, at=at, off=off: (at, 0, i + off // tile))
+        for _, at, off, _ in parts
+    ]
     return call(
+        3.1,
         grad_dot_kernel,
         (half // tile,),
-        [spec, spec, full(against)],
+        [*specs, full(against)],
         pl.BlockSpec((tile, width), lambda i, s: (i, 0)),
         shape((half, width), dtype),
         [pltpu.VMEM((total, width), BF)],
         1,
-    )(order, own, other, against)
-
-
-def grad_halves(order, gathered, against):
+    )(order, *(array for array, _, _, _ in parts), against)
+
+
+def gathered_halves(gathered):
     left, right, left_other, right_other = gathered
-    theirs = grad_dot(order, right, right_other, against, BF)
-    return grad_dot(order, left, left_other, against, F32), theirs
-
-
-def feed_kernel(parts, l, r, lo, ro, cl, cr, clo, cro, gm, gt, lm, lt, dm, dt, active_ref, gate_ref, lift_ref):
-    i = pl.program_id(0)
-
-    def run(left, right, cleft, cright):
-        half = left.shape[2]
-
-        def product(a, b, mine, theirs):
-            return dot(a[...].reshape(TILE, half), mine[...], (1, 0)) + dot(
-                b[...].reshape(TILE, half), theirs[...], (1, 0)
-            )
-
-        gate = product(left, right, gm, gt)
-        lift = product(left, right, lm, lt)
-        grad = product(cleft, cright, dm, dt)
-        sigmoid_part = jax.nn.sigmoid(gate)
-        swish = gate * sigmoid_part
-        active_ref[...] = (swish * lift).astype(BF)
-        gate_ref[...] = (
-            grad * lift * sigmoid_part * (1.0 + gate * (1.0 - sigmoid_part))
-        ).astype(BF)
-        lift_ref[...] = (grad * swish).astype(BF)
-
-    @pl.when(i < parts)
-    def _():
-        run(l, r, cl, cr)
-
-    @pl.when(i >= parts)
-    def _():
-        run(lo, ro, clo, cro)
-
-
-def feed_block(rows, cotangent, gate, lift, drop):
-    blocks, count, half = rows[0].shape
-    total = 2 * blocks * count
-    parts = total // TILE // 2
-    own = pl.BlockSpec((2, count, half), lambda i: (jnp.minimum(i, parts - 1), 0, 0))
-    other = pl.BlockSpec((2, count, half), lambda i: (jnp.maximum(i - parts, 0), 0, 0))
+    half = left.shape[2]
+    return [(left, 0, 0, half), (left_other, 0, 0, half)], [
+        (right, 0, 0, half),
+        (right_other, 0, 0, half),
+    ]
+
+
+def straight_halves(rows):
+    total, width = rows.shape
+    rows = rows.reshape(total // BLOCK, BLOCK, width)
+    half = width // 2
+    return [(rows, 0, 0, half), (rows, 1, 0, half)], [(rows, 0, half, half), (rows, 1, half, half)]
+
+
+def grad_halves(order, halves, against):
+    theirs = grad_dot(order, halves[1], against, BF)
+    return grad_dot(order, halves[0], against, F32), theirs
+
+
+def feed_kernel(scalars, l, r, lo, ro, cotangent, gm, gt, lm, lt, dm, dt, active_ref, gate_ref, lift_ref, rows):
+    place_rows(scalars, (l, r, lo, ro), rows)
+    values = rows[...]
+    gate = halves_product(values, gm, gt)
+    lift = halves_product(values, lm, lt)
+    grad = halves_product(cotangent[...], dm, dt)
+    sigmoid_part = jax.nn.sigmoid(gate)
+    swish = gate * sigmoid_part
+    active_ref[...] = (swish * lift).astype(BF)
+    gate_ref[...] = (grad * lift * sigmoid_part * (1.0 + gate * (1.0 - sigmoid_part))).astype(BF)
+    lift_ref[...] = (grad * swish).astype(BF)
+
+
+def feed_block(scalars, gathered, cotangent, gate, lift, drop):
+    total, width = cotangent.shape
     weights = [*gate, *lift, *drop]
     return call(
-        lambda *refs: feed_kernel(parts, *refs),
-        (2 * parts,),
-        [own, own, other, other] * 2 + [full(w) for w in weights],
+        11.8,
+        feed_kernel,
+        (total // TILE,),
+        gathered_specs(gathered) + [tiled(width)] + [full(w) for w in weights],
         [tiled(LANES)] * 3,
         [shape((total, LANES), BF)] * 3,
-    )(*rows, *cotangent, *weights)
+        [pltpu.VMEM((TILE, width), BF)],
+        1,
+    )(scalars, *gathered, cotangent, *weights)
+
+
+def forth_dot_kernel(rows, mine, theirs, out):
+    half = mine.shape[0]
+    out[:, :half] = dot(rows[...], mine[...], (1, 1)).astype(BF)
+    out[:, half:] = dot(rows[...], theirs[...], (1, 1)).astype(BF)
+
+
+def forth_dot(rows, weights):
+    total, k = rows.shape
+    width = 2 * weights[0].shape[0]
+    return call(
+        4.2,
+        forth_dot_kernel,
+        (total // TILE,),
+        [tiled(k), full(weights[0]), full(weights[1])],
+        tiled(width),
+        shape((total, width), BF),
+    )(rows, *weights)
+
+
+def keys_kernel(seqs, parts, out):
+    for n in range(seqs):
+        out[n] = jnp.concatenate([parts[r][:, n * SIDE : (n + 1) * SIDE] for r in range(4)], 1)
+
+
+def keys_of(seqs, parts):
+    count = parts.shape[1]
+    return call(
+        1.7,
+        lambda *refs: keys_kernel(seqs, *refs),
+        (count // TILE,),
+        [pl.BlockSpec((4, TILE, seqs * SIDE), lambda i: (0, i, 0))],
+        pl.BlockSpec((seqs, TILE, 2 * HD), lambda i: (0, i, 0)),
+        shape((seqs, count, 2 * HD), BF),
+    )(parts)
 
 
 def scores_of(place, queries, keys):
@@ -569,6 +787,7 @@
     total = queries.shape[0]
     grid, rows = attend_specs(seqs, total)
     return call(
+        2.8,
         attend_kernel,
         grid,
         [rows(HD), pl.BlockSpec((1, whole, width), lambda n, i, s: (n, 0, 0))],
@@ -588,12 +807,21 @@
     scores_grad = (probs * (dot(grad, values, (1, 1)) - delta)).astype(BF)
     query_ref[...] = (dot(scores_grad, keys, (1, 0)) * (HD**-0.5 * root[...])).astype(BF)
 
-    @pl.when(pl.program_id(1) == 0)
+    @pl.when((pl.program_id(0) == 0) & (pl.program_id(1) == 0))
     def _():
         sum_ref[...] = jnp.zeros_like(sum_ref)
 
-    sum_ref[0, :, :HD] += dot(scores_grad, queries[...], (0, 0)) * HD**-0.5
-    sum_ref[0, :, HD:] += dot(probs.astype(BF), grad, (0, 0))
+    key_sum = dot(scores_grad, queries[...], (0, 0)) * HD**-0.5
+    value_sum = dot(probs.astype(BF), grad, (0, 0))
+    for n in range(sum_ref.shape[2] // SIDE):
+
+        @pl.when(pl.program_id(0) == n)
+        def _():
+            at = slice(n * SIDE, (n + 1) * SIDE)
+            sum_ref[0, :, at] += key_sum[:, :SIDE]
+            sum_ref[1, :, at] += key_sum[:, SIDE:]
+            sum_ref[2, :, at] += value_sum[:, :SIDE]
+            sum_ref[3, :, at] += value_sum[:, SIDE:]
 
 
 def attend_back(place, queries, grads, attended, logs, root, key_value):
@@ -602,11 +830,12 @@
     grid, rows = attend_specs(seqs, total)
     sums = pl.BlockSpec((1, whole, width), lambda n, i, s: (n, 0, 0))
     return call(
+        5,
         attend_back_kernel,
         grid,
         [rows(HD), rows(HD), rows(HD), rows(1), rows(1), sums],
-        [rows(HD), sums],
-        [shape((total, HD), BF), shape((seqs, whole, width))],
+        [rows(HD), pl.BlockSpec((4, whole, seqs * SIDE), lambda n, i, s: (0, 0, 0))],
+        [shape((total, HD), BF), shape((4, whole, seqs * SIDE))],
         (),
         1,
     )(place, queries, grads, attended, logs, root, key_value)
@@ -632,7 +861,7 @@
 
 
 def block_steps(step_pre, head):
-    arg = step_pre[...] + head[0:1, :]
+    arg = step_pre + head[0:1, :]
     size = jnp.maximum(arg, 0.0) + jnp.log1p(jnp.exp(-jnp.abs(arg)))
     row, column = triangle()
     cum = exact(jnp.where(row >= column, 1.0, 0.0), size * head[1:2, :], (1, 0))
@@ -649,44 +878,66 @@
     return exact(jnp.where(row == column, 1.0, 0.0), values, (1, 1))
 
 
-def states_kernel(blocks, step_pre, head, conv, io, out_ref, decay_ref, run):
+def joined(sides, first, n):
+    return jnp.concatenate(
+        [sides[r][:, n * SIDE : (n + 1) * SIDE] for r in range(first, first + 4)], 1
+    )
+
+
+def pair(seqs, width, back=0):
+    if back:
+        return pl.BlockSpec((seqs, BLOCK, width), lambda i, *s: (0, back - 1 - i, 0))
+    return pl.BlockSpec((seqs, BLOCK, width), lambda i, *s: (0, i, 0))
+
+
+def by_seq(seqs, *arrays):
+    return [a.reshape(*a.shape[:-2], seqs, -1, a.shape[-1]) for a in arrays]
+
+
+def states_kernel(seqs, blocks, step_pre, head, conv, sides, out_ref, decay_ref, run):
     i = pl.program_id(0)
-    _, size, cum = block_steps(step_pre, head)
-    last = cum[BLOCK - 1 :, :]
-    feeding = jnp.exp(last - cum) * size
-    inner = silu_value(conv[:, :INNER])
-    fresh = dot(io[:, :NS], (over_heads(feeding) * inner).astype(BF), (0, 0))
-    decay = over_heads(jnp.exp(last))
-
-    @pl.when(i % blocks == 0)
+
+    @pl.when(i == 0)
     def _():
-        run[...] = fresh
-        decay_ref[0] = decay
-
-    @pl.when(i % blocks != 0)
+        run[...] = jnp.zeros_like(run)
+        decay_ref[...] = jnp.ones_like(decay_ref)
+
+    for n in range(seqs):
+        _, size, cum = block_steps(step_pre[n], head)
+        last = cum[BLOCK - 1 :, :]
+        feeding = jnp.exp(last - cum) * size
+        inner = silu_value(conv[n, :, :INNER])
+        in_state = joined(sides, 0, n)
+        fresh = dot(in_state, (over_heads(feeding) * inner).astype(BF), (0, 0))
+        decay = over_heads(jnp.exp(last))
+        run[n] = decay * run[n] + fresh
+        decay_ref[n] = decay_ref[n] * decay
+
+    @pl.when(i == blocks - 1)
     def _():
-        run[...] = decay * run[...] + fresh
-        decay_ref[0] = decay_ref[0] * decay
-
-    @pl.when(i % blocks == blocks - 1)
-    def _():
-        out_ref[0] = run[...].astype(BF)
-
-
-def states(seqs, step_pre, head, conv, io):
-    total = conv.shape[0]
-    blocks = total // BLOCK // seqs
+        out_ref[...] = run[...].astype(BF)
+
+
+def states(seqs, step_pre, head, conv, sides):
+    step_pre, conv = by_seq(seqs, step_pre, conv)
+    blocks = conv.shape[1] // BLOCK
     return call(
-        lambda *refs: states_kernel(blocks, *refs),
-        (total // BLOCK,),
-        [tiled(8, BLOCK), full(head), tiled(LANES, BLOCK), tiled(2 * NS, BLOCK)],
-        [
-            pl.BlockSpec((1, NS, INNER), lambda i: (i // blocks, 0, 0)),
-            pl.BlockSpec((1, 1, INNER), lambda i: (i // blocks, 0, 0)),
+        4.5,
+        lambda *refs: states_kernel(seqs, blocks, *refs),
+        (blocks,),
+        [
+            pair(seqs, 8),
+            full(head),
+            pair(seqs, LANES),
+            pl.BlockSpec((4, BLOCK, seqs * SIDE), lambda i: (0, i, 0)),
+        ],
+        [
+            pl.BlockSpec((seqs, NS, INNER), lambda i: (0, 0, 0)),
+            pl.BlockSpec((seqs, 1, INNER), lambda i: (0, 0, 0)),
         ],
         [shape((seqs, NS, INNER), BF), shape((seqs, 1, INNER))],
-        [pltpu.VMEM((NS, INNER), F32)],
-    )(step_pre, head, conv, io)
+        [pltpu.VMEM((seqs, NS, INNER), F32)],
+    )(step_pre, head, conv, sides)
 
 
 def fading_of(cum, cum_rows, h):
@@ -695,142 +946,142 @@
     return jnp.where(row >= column, jnp.exp(jnp.minimum(span, 0.0)), 0.0)
 
 
-def ssm_kernel(blocks, step_pre, head, conv, io, gating, entry, ssm_ref, carried_ref, square_ref, run):
+def ssm_kernel(seqs, step_pre, head, conv, sides, gating, entry, ssm_ref, carried_ref, square_ref, run):
+    @pl.when(pl.program_id(0) == 0)
+    def _():
+        run[...] = entry[...].astype(F32)
+
+    for n in range(seqs):
+        _, size, cum = block_steps(step_pre[n], head)
+        size_rows, cum_rows = as_rows(size), as_rows(cum)
+        last = cum[BLOCK - 1 :, :]
+        inner = silu_value(conv[n, :, :INNER])
+        inner_low = inner.astype(BF)
+        in_state, out_state = joined(sides, 0, n), joined(sides, 4, n)
+        before = run[n]
+        carried = before.astype(BF)
+        carried_ref[n, 0] = carried
+        pairing = dot(out_state, in_state, (1, 1))
+        within = []
+        for h in range(HEADS):
+            mixing = fading_of(cum, cum_rows, h) * pairing * size_rows[h : h + 1, :]
+            within.append(dot(mixing.astype(BF), inner_low[:, h * PM : (h + 1) * PM], (1, 0)))
+        readout = dot(out_state, carried, (1, 0))
+        ssm = (
+            jnp.concatenate(within, 1)
+            + over_heads(jnp.exp(cum)) * readout
+            + over_heads(head[2:3, :]) * inner
+        )
+        ssm_ref[n] = ssm
+        gated = ssm * silu_value(gating[n])
+        square_ref[0, n] = exact(jnp.ones((8, INNER), F32), gated * gated, (1, 1))
+        feeding = jnp.exp(last - cum) * size
+        fresh = dot(in_state, (over_heads(feeding) * inner).astype(BF), (0, 0))
+        run[n] = over_heads(jnp.exp(last)) * before + fresh
+
+
+def ssm_block(seqs, step_pre, head, conv, sides, gating, entry):
+    total = conv.shape[0]
+    step_pre, conv, gating = by_seq(seqs, step_pre, conv, gating)
+    count = conv.shape[1]
+    blocks = count // BLOCK
+    ssm, carried, square = call(
+        11.2,
+        lambda *refs: ssm_kernel(seqs, *refs),
+        (blocks,),
+        [
+            pair(seqs, 8),
+            full(head),
+            pair(seqs, LANES),
+            pl.BlockSpec((RANKS, BLOCK, seqs * SIDE), lambda i: (0, i, 0)),
+            pair(seqs, INNER),
+            full(entry),
+        ],
+        [
+            pair(seqs, INNER),
+            pl.BlockSpec((seqs, 1, NS, INNER), lambda i: (0, i, 0, 0)),
+            pl.BlockSpec((1, seqs, 8, BLOCK), lambda i: (i, 0, 0, 0)),
+        ],
+        [
+            shape((seqs, count, INNER)),
+            shape((seqs, blocks, NS, INNER), BF),
+            shape((blocks, seqs, 8, BLOCK)),
+        ],
+        [pltpu.VMEM((seqs, NS, INNER), F32)],
+    )(step_pre, head, conv, sides, gating, entry)
+    square = square[:, :, 0].swapaxes(0, 1).reshape(total // BLOCK, BLOCK)
+    return ssm.reshape(total, INNER), carried, square
+
+
+def states_back_kernel(seqs, blocks, step_pre, head, sides, mixer, ssm, gating, mixer_root, along, gain, root, grad_ref, gating_ref, out_ref, run):
     i = pl.program_id(0)
-
-    @pl.when(i % blocks == 0)
-    def _():
-        run[...] = entry[0].astype(F32)
-
-    _, size, cum = block_steps(step_pre, head)
-    size_rows, cum_rows = as_rows(size), as_rows(cum)
-    last = cum[BLOCK - 1 :, :]
-    inner = silu_value(conv[:, :INNER])
-    inner_low = inner.astype(BF)
-    in_state, out_state = io[:, :NS], io[:, NS:]
-    carried = run[...].astype(BF)
-    carried_ref[0] = carried
-    pairing = dot(out_state, in_state, (1, 1))
-    within = []
-    for h in range(HEADS):
-        mixing = fading_of(cum, cum_rows, h) * pairing * size_rows[h : h + 1, :]
-        within.append(dot(mixing.astype(BF), inner_low[:, h * PM : (h + 1) * PM], (1, 0)))
-    readout = dot(out_state, carried, (1, 0))
-    ssm = (
-        jnp.concatenate(within, 1)
-        + over_heads(jnp.exp(cum)) * readout
-        + over_heads(head[2:3, :]) * inner
-    )
-    ssm_ref[...] = ssm
-    gated = ssm * silu_value(gating[...])
-    square_ref[0] = exact(jnp.ones((8, INNER), F32), gated * gated, (1, 1))
-    feeding = jnp.exp(last - cum) * size
-    fresh = dot(in_state, (over_heads(feeding) * inner).astype(BF), (0, 0))
-    run[...] = over_heads(jnp.exp(last)) * run[...] + fresh
-
-
-def ssm_block(seqs, step_pre, head, conv, io, gating, entry):
-    total = conv.shape[0]
-    blocks = total // BLOCK // seqs
-    return call(
-        lambda *refs: ssm_kernel(blocks, *refs),
-        (total // BLOCK,),
-        [
-            tiled(8, BLOCK),
-            full(head),
-            tiled(LANES, BLOCK),
-            tiled(2 * NS, BLOCK),
-            tiled(INNER, BLOCK),
-            pl.BlockSpec((1, NS, INNER), lambda i: (i // blocks, 0, 0)),
-        ],
-        [
-            tiled(INNER, BLOCK),
-            pl.BlockSpec((1, NS, INNER), lambda i: (i, 0, 0)),
-            pl.BlockSpec((1, 8, BLOCK), lambda i: (i, 0, 0)),
-        ],
-        [
-            shape((total, INNER)),
-            shape((total // BLOCK, NS, INNER), BF),
-            shape((total // BLOCK, 8, BLOCK)),
-        ],
-        [pltpu.VMEM((NS, INNER), F32)],
-    )(step_pre, head, conv, io, gating, entry)
-
-
-def states_back_kernel(blocks, step_pre, head, io, mixer, ssm, gating, mixer_root, along, gain, root, grad_ref, gating_ref, out_ref, run):
-    i = pl.program_id(0)
-    _, _, cum = block_steps(step_pre, head)
-    gate = gating[...]
-    sigmoid_part = jax.nn.sigmoid(gate)
-    act = gate * sigmoid_part
-    values = ssm[...]
-    norm = values * act * mixer_root[...]
-    gated_grad = mixer_root[...] * (mixer[...] * gain[...] - norm * along[...])
-    grad = gated_grad * act
-    grad_ref[...] = grad
-    slope = sigmoid_part * (1.0 + gate * (1.0 - sigmoid_part))
-    gating_ref[...] = (gated_grad * values * slope * root[...]).astype(BF)
-    grown = (over_heads(jnp.exp(cum)) * grad).astype(BF)
-    fresh = dot(io[:, NS:], grown, (0, 0))
-    decay = over_heads(jnp.exp(cum[BLOCK - 1 :, :]))
-
-    @pl.when(i % blocks == 0)
-    def _():
-        run[...] = fresh
-
-    @pl.when(i % blocks != 0)
-    def _():
-        run[...] = decay * run[...] + fresh
-
-    @pl.when(i % blocks == blocks - 1)
-    def _():
-        out_ref[0] = run[...].astype(BF)
-
-
-def states_back(seqs, step_pre, head, io, mixer, ssm, gating, mixer_root, along, gain, root):
-    total = ssm.shape[0]
-    many = total // BLOCK
-    blocks = many // seqs
-    back = lambda width: pl.BlockSpec((BLOCK, width), lambda i: (many - 1 - i, 0))
-    return call(
-        lambda *refs: states_back_kernel(blocks, *refs),
-        (many,),
-        [back(8), full(head), back(2 * NS), back(INNER), back(INNER), back(INNER)]
-        + [back(1), back(1), full(gain), back(1)],
-        [
-            back(INNER),
-            back(INNER),
-            pl.BlockSpec((1, NS, INNER), lambda i: (seqs - 1 - i // blocks, 0, 0)),
-        ],
-        [shape((total, INNER)), shape((total, INNER), BF), shape((seqs, NS, INNER), BF)],
-        [pltpu.VMEM((NS, INNER), F32)],
-    )(step_pre, head, io, mixer, ssm, gating, mixer_root, along, gain, root)
-
-
-def ssm_back_kernel(blocks, side, step_pre, head, conv, io, grads, carried_ref, entry, key_value, root, conv_ref, parts_ref, step_ref, sums_ref, later):
-    i = pl.program_id(0)
-
-    @pl.when(i % blocks == 0)
-    def _():
-        later[...] = entry[0].astype(F32)
 
     @pl.when(i == 0)
     def _():
-        sums_ref[...] = jnp.zeros_like(sums_ref)
-
-    arg, size, cum = block_steps(step_pre, head)
+        run[...] = jnp.zeros_like(run)
+
+    for n in range(seqs):
+        _, _, cum = block_steps(step_pre[n], head)
+        gate = gating[n]
+        sigmoid_part = jax.nn.sigmoid(gate)
+        act = gate * sigmoid_part
+        values = ssm[n]
+        scaled = mixer_root[n]
+        norm = values * act * scaled
+        gated_grad = scaled * (mixer[n] * gain[...] - norm * along[n])
+        grad = gated_grad * act
+        grad_ref[n] = grad
+        slope = sigmoid_part * (1.0 + gate * (1.0 - sigmoid_part))
+        gating_ref[n] = (gated_grad * values * slope * root[n]).astype(BF)
+        grown = (over_heads(jnp.exp(cum)) * grad).astype(BF)
+        fresh = dot(joined(sides, 0, n), grown, (0, 0))
+        run[n] = over_heads(jnp.exp(cum[BLOCK - 1 :, :])) * run[n] + fresh
+
+    @pl.when(i == blocks - 1)
+    def _():
+        out_ref[...] = run[...].astype(BF)
+
+
+def states_back(seqs, step_pre, head, sides, mixer, ssm, gating, mixer_root, along, gain, root):
+    total = ssm.shape[0]
+    step_pre, mixer, ssm, gating, mixer_root, along, root = by_seq(
+        seqs, step_pre, mixer, ssm, gating, mixer_root, along, root
+    )
+    count = ssm.shape[1]
+    blocks = count // BLOCK
+    back = lambda width: pair(seqs, width, blocks)
+    grad, gating_grad, leaving = call(
+        6.6,
+        lambda *refs: states_back_kernel(seqs, blocks, *refs),
+        (blocks,),
+        [back(8), full(head)]
+        + [pl.BlockSpec((4, BLOCK, seqs * SIDE), lambda i: (1, blocks - 1 - i, 0))]
+        + [back(INNER), back(INNER), back(INNER), back(1), back(1), full(gain), back(1)],
+        [back(INNER), back(INNER), pl.BlockSpec((seqs, NS, INNER), lambda i: (0, 0, 0))],
+        [
+            shape((seqs, count, INNER)),
+            shape((seqs, count, INNER), BF),
+            shape((seqs, NS, INNER), BF),
+        ],
+        [pltpu.VMEM((seqs, NS, INNER), F32)],
+    )(step_pre, head, sides, mixer, ssm, gating, mixer_root, along, gain, root)
+    return grad.reshape(total, INNER), gating_grad.reshape(total, INNER), leaving
+
+
+def ssm_back_one(n, step_pre, head, conv, sides, grads, carried_ref, root, conv_ref, step_ref, sums_ref, later):
+    arg, size, cum = block_steps(step_pre[n], head)
     size_rows, cum_rows = as_rows(size), as_rows(cum)
     last = cum[BLOCK - 1 :, :]
     growth, to_end, decay = jnp.exp(cum), jnp.exp(last - cum), jnp.exp(last)
     feeding = to_end * size
-    conv_sum = conv[:, :INNER]
+    conv_sum = conv[n, :, :INNER]
     inner = silu_value(conv_sum)
     inner_low = inner.astype(BF)
-    in_state, out_state = io[:, :NS], io[:, NS:]
-    carried = carried_ref[0]
-    after = later[...]
+    in_state, out_state = joined(sides, 0, n), joined(sides, 4, n)
+    carried = carried_ref[n, 0]
+    after = later[n]
     after_low = after.astype(BF)
-    grad = grads[...]
+    grad = grads[n]
     grad_low = grad.astype(BF)
     pairing = dot(out_state, in_state, (1, 1))
     readout = dot(out_state, carried, (1, 0))
@@ -860,14 +1111,7 @@
     inner_grad = (
         jnp.concatenate(inner_parts, 1) + over_heads(head[2:3, :]) * grad + feeding_wide * spread
     )
-    conv_ref[...] = inner_grad * silu_slope(conv_sum)
-    for rank in range(RANKS):
-        source = in_grad if rank < RANKS // 2 else out_grad
-        at = (rank % 4) * SIDE
-        own = jnp.where(side[0] == rank // 4, 1.0, 0.0)
-        parts_ref[rank] = jnp.concatenate(
-            [source[:, at : at + SIDE], key_value[:, at : at + SIDE] * own], 1
-        ).astype(BF)
+    conv_ref[n] = inner_grad * silu_slope(conv_sum)
     feeding_grad = head_sums(spread * inner)
     fed = feeding_grad * feeding
     through = jnp.sum(after * carried.astype(F32), axis=0, keepdims=True)
@@ -879,51 +1123,79 @@
     rates = head[1:2, :]
     step_grad = as_columns(step_rows) + feeding_grad * to_end + increment * rates
     arg_grad = step_grad * jax.nn.sigmoid(arg)
-    step_ref[...] = (arg_grad * root[...]).astype(BF)
+    step_ref[n] = (arg_grad * root[n]).astype(BF)
     skip = jnp.broadcast_to(jnp.sum(grad * inner, axis=0, keepdims=True), (8, INNER))
     sums_ref[0:1, :] += jnp.sum(arg_grad, axis=0, keepdims=True)
     sums_ref[1:2, :] += jnp.sum(increment * size, axis=0, keepdims=True) * rates
     sums_ref[2:3, :] += head_sums(skip)[:1]
-    later[...] = over_heads(decay) * after + dot(out_state, grown, (0, 0))
-
-
-def ssm_back(side, seqs, step_pre, head, conv, io, grads, carried, entry, key_value, root):
+    later[n] = over_heads(decay) * after + dot(out_state, grown, (0, 0))
+    return in_grad, out_grad
+
+
+def ssm_back_kernel(seqs, step_pre, head, conv, sides, grads, carried, entry, root, conv_ref, parts_ref, step_ref, sums_ref, later):
+    @pl.when(pl.program_id(0) == 0)
+    def _():
+        later[...] = entry[...].astype(F32)
+        sums_ref[...] = jnp.zeros_like(sums_ref)
+
+    grad_pairs = [
+        ssm_back_one(
+            n, step_pre, head, conv, sides, grads, carried, root, conv_ref, step_ref, sums_ref, later
+        )
+        for n in range(seqs)
+    ]
+    for rank in range(RANKS):
+        at = (rank % 4) * SIDE
+        parts_ref[rank] = jnp.concatenate(
+            [grad[rank // 4][:, at : at + SIDE] for grad in grad_pairs], 1
+        ).astype(BF)
+
+
+def ssm_back(seqs, step_pre, head, conv, sides, grads, carried, entry, root):
     total = conv.shape[0]
-    many = total // BLOCK
-    blocks = many // seqs
-    back = lambda width: pl.BlockSpec((BLOCK, width), lambda i, s: (many - 1 - i, 0))
-    return call(
-        lambda *refs: ssm_back_kernel(blocks, *refs),
-        (many,),
-        [back(8), full(head), back(LANES), back(2 * NS), back(INNER)]
-        + [
-            pl.BlockSpec((1, NS, INNER), lambda i, s: (many - 1 - i, 0, 0)),
-            pl.BlockSpec((1, NS, INNER), lambda i, s: (seqs - 1 - i // blocks, 0, 0)),
-            back(2 * HD),
+    step_pre, conv, grads, root = by_seq(seqs, step_pre, conv, grads, root)
+    count = conv.shape[1]
+    blocks = count // BLOCK
+    back = lambda width: pair(seqs, width, blocks)
+    conv_grad, parts, step_rows, sums = call(
+        19,
+        lambda *refs: ssm_back_kernel(seqs, *refs),
+        (blocks,),
+        [
+            back(8),
+            full(head),
+            back(LANES),
+            pl.BlockSpec((RANKS, BLOCK, seqs * SIDE), lambda i: (0, blocks - 1 - i, 0)),
+            back(INNER),
+            pl.BlockSpec((seqs, 1, NS, INNER), lambda i: (0, blocks - 1 - i, 0, 0)),
+            full(entry),
             back(1),
         ],
         [
             back(INNER),
-            pl.BlockSpec((RANKS, BLOCK, 2 * SIDE), lambda i, s: (0, many - 1 - i, 0)),
+            pl.BlockSpec((RANKS, BLOCK, seqs * SIDE), lambda i: (0, blocks - 1 - i, 0)),
             back(8),
-            pl.BlockSpec((8, 8), lambda i, s: (0, 0)),
-        ],
-        [
-            shape((total, INNER)),
-            shape((RANKS, total, 2 * SIDE), BF),
-            shape((total, 8), BF),
+            pl.BlockSpec((8, 8), lambda i: (0, 0)),
+        ],
+        [
+            shape((seqs, count, INNER)),
+            shape((RANKS, count, seqs * SIDE), BF),
+            shape((seqs, count, 8), BF),
             shape((8, 8)),
         ],
-        [pltpu.VMEM((NS, INNER), F32)],
-        1,
-    )(side, step_pre, head, conv, io, grads, carried, entry, key_value, root)
-
-
-def conv_back_kernel(tiles, inner, parts, conv, pre, edge, grad_ref, sums_ref, line):
+        [pltpu.VMEM((seqs, NS, INNER), F32)],
+    )(step_pre, head, conv, sides, grads, carried, entry, root)
+    return conv_grad.reshape(total, INNER), parts, step_rows.reshape(total, 8), sums
+
+
+def conv_back_kernel(tiles, inner, parts, keys, conv, pre, edge, grad_ref, sums_ref, line):
     i = pl.program_id(0)
+    first = i < tiles
     got = jnp.sum(parts[...].astype(F32), axis=0)
-    lane = lax.broadcasted_iota(jnp.int32, got.shape, 1)
-    got = jnp.where(lane < SIDE, got * silu_slope(conv[:, INNER:]), got)
+    got = jnp.where(first, got[:, :SIDE], got[:, SIDE:]) * silu_slope(conv[:, INNER:CONV])
+    keys_got = keys[...]
+    keys_got = jnp.where(first, keys_got[:, :SIDE], keys_got[:, SIDE:])
+    got = jnp.concatenate([got, keys_got], 1)
     grad = jnp.concatenate([inner[...], got], 1)
     grad_ref[...] = grad
 
@@ -946,15 +1218,17 @@
     sums_ref[KC : KC + 1, :] += jnp.sum(grad, axis=0, keepdims=True)
 
 
-def conv_back(inner, parts, conv, pre, edge):
+def conv_back(inner, parts, keys, conv, pre, edge):
     total = conv.shape[0]
     tiles = total // TILE // edge.shape[0]
     return call(
+        4.8,
         lambda *refs: conv_back_kernel(tiles, *refs),
         (total // TILE,),
         [
             tiled(INNER),
-            pl.BlockSpec((RANKS, TILE, 2 * SIDE), lambda i: (0, i, 0)),
+            pl.BlockSpec((RANKS, TILE, 2 * SIDE), lambda i: (0, i % tiles, 0)),
+            pl.BlockSpec((TILE, 2 * SIDE), lambda i: (i % tiles, 0)),
             tiled(LANES),
             tiled(LANES),
             pl.BlockSpec((1, EDGE, LANES), lambda i: (i // tiles, 0, 0)),
@@ -962,7 +1236,7 @@
         [tiled(LANES), pl.BlockSpec((8, LANES), lambda i: (0, 0))],
         [shape((total, LANES)), shape((8, LANES))],
         [pltpu.VMEM((EDGE + TILE, LANES), F32)],
-    )(inner, parts, conv, pre, edge)
+    )(inner, parts, keys, conv, pre, edge)
 
 
 def pre_back_kernel(tiles, grad, after, follow, taps, root, out_ref, line):
@@ -988,6 +1262,7 @@
     tiles = total // TILE // follow.shape[0]
     last = total // EDGE - 1
     return call(
+        1.4,
         lambda *refs: pre_back_kernel(tiles, *refs),
         (total // TILE,),
         [
@@ -1042,7 +1317,9 @@
     tiles = [((z ^ my_zl) * 2 + (s ^ my_sl)) for s in (0, 1) for z in (0, 1)]
     scalars = jnp.stack([my_core, *tiles]).astype(jnp.int32)
     place = (lax.axis_index("ch") * count).astype(jnp.int32).reshape(1)
-    side_index = my_sl.astype(jnp.int32).reshape(1)
+    dims = (sh, sl, ch, width)
+    home = column_blocks(sh, sl, ch)
+    nowhere = jnp.zeros_like(home)
 
     def scaled(weight, gain):
         return (weight.astype(F32) * gain.astype(F32)[:, None]).astype(BF)
@@ -1057,17 +1334,6 @@
         ],
         2,
     )
-    own_tokens = shuffled(tokens, sh, sl, ch)
-    own_cotangent = shuffled(cotangent, sh, sl, ch)
-    mixed_in = ranks_exchange(pack_in)
-    team_tokens = team_gather(own_tokens)
-    pack_rest = jnp.concatenate(
-        [by_rank(mixer_out.T), by_rank(output_weight.T)]
-        + [by_rank(scaled(w, feed_gain)) for w in (gate_matrix, lift_matrix)]
-        + [by_rank(drop_matrix.T)],
-        2,
-    )
-
     conv_own, gain_own = conv_weight.shape[1], mixer_gain.shape[0]
     step_sent = jnp.broadcast_to(
         scaled(step_weight, norm_gain).T.reshape(1, sl, 1, 4, HEADS * drows),
@@ -1077,17 +1343,49 @@
     small = jnp.concatenate(
         [jnp.broadcast_to(shared[None], (world, shared.shape[0])), step_sent], 1
     )
-    small, mixed_in = together(small, mixed_in)
-    small = lax.all_to_all(small, WORLD, split_axis=0, concat_axis=0, tiled=True)
-    pack_rest, small, team_tokens = together(pack_rest, small, team_tokens)
-    mixed_rest = ranks_exchange(pack_rest)
-    w_inner, w_gating, w_out, w_gate, w_lift, w_drop = peers_gather(
-        [
-            mixed_in[:, :LANES],
-            mixed_in[:, LANES:],
-            *(mixed_rest[:, at * LANES : (at + 1) * LANES] for at in range(4)),
-        ]
-    )
+    with jax.named_scope("small_exchange"):
+        small = lax.all_to_all(small, WORLD, split_axis=0, concat_axis=0, tiled=True)
+    small, pack_in = together(small, pack_in)
+    with jax.named_scope("weights_in"):
+        mixed_in = ranks_exchange(pack_in)
+    *own_tokens, own_cotangent = arrive(dims, home, tokens, cotangent)
+    with jax.named_scope("tokens_gather"):
+        before = jnp.stack([part[rows - EDGE :] for part in own_tokens])
+        before = shifted(before, 1)
+        if ch == 2:
+            before = jnp.flip(before.reshape(2, EDGE, sh // 2, ch, -1), 3)
+            before = before.reshape(2, EDGE, width // 2)
+        team_tokens = list(
+            team_gather(*(jnp.concatenate([own_tokens[h], before[h]], 0) for h in range(2)))
+        )
+    ends = []
+    for seq in range(sl):
+        at_block = 2 * (1 - my_zl) + (seq ^ my_sl)
+        halves = []
+        for own, other in ((team_tokens[0], team_tokens[2]), (team_tokens[1], team_tokens[3])):
+            own = lax.dynamic_index_in_dim(own[:, rows:], at_block, 0, False)
+            other = lax.dynamic_index_in_dim(other[:, rows:], at_block, 0, False)
+            halves.append(jnp.where(my_core == 1, own, other))
+        ends.append(jnp.concatenate(halves, 1))
+    halo = jnp.stack(ends)
+    with jax.named_scope("weights_first"):
+        ready = along_ch(mixed_in[:, :LANES])
+    pack_rest = jnp.concatenate(
+        [by_rank(mixer_out.T), by_rank(output_weight.T)]
+        + [by_rank(scaled(w, feed_gain)) for w in (gate_matrix, lift_matrix)]
+        + [by_rank(drop_matrix.T)],
+        2,
+    )
+    pack_rest, sent_cotangent, *team_tokens = together(pack_rest, own_cotangent, *team_tokens)
+    with jax.named_scope("weights_rest"):
+        mixed_rest = ranks_exchange(pack_rest)
+    team_cotangent = lax.all_gather(sent_cotangent, TEAM, axis=0, tiled=True)
+    with jax.named_scope("weights_inner"):
+        theirs, gating_ready, mixed_rest = together(
+            swap(ready, "sh"), along_ch(mixed_in[:, LANES:]), mixed_rest
+        )
+    w_inner = (ready, theirs)
+
     at = (KC + 1) * conv_own
     wide_conv = small[:, :at].reshape(world, KC + 1, conv_own)
     wide_conv = wide_conv.transpose(1, 0, 2).reshape(KC + 1, -1).astype(F32)
@@ -1110,159 +1408,201 @@
     head = lax.dynamic_slice_in_dim(head, rank * HEADS, HEADS, 1)
     head = jnp.pad(head, ((0, 5), (0, 8 - HEADS)))
 
-    ends = []
-    for seq in range(sl):
-        at_block = 2 * (1 - my_zl) + (seq ^ my_sl)
-        halves = []
-        for own, other in ((team_tokens[0], team_tokens[2]), (team_tokens[1], team_tokens[3])):
-            own = lax.dynamic_index_in_dim(own[:, rows - EDGE :], at_block, 0, False)
-            other = lax.dynamic_index_in_dim(other[:, rows - EDGE :], at_block, 0, False)
-            halves.append(jnp.where(my_core == 1, own, other))
-        ends.append(jnp.concatenate(halves, 1))
-    halo = shifted(jnp.stack(ends), 1)
-    if ch == 2:
-        halo = jnp.flip(halo.reshape(sl, EDGE, sh, ch, -1), 3).reshape(sl, EDGE, width)
-
-    pre, conv, side, step_pre, root, edge = project_inner(
+    pre, conv, side, own_keys, step_pre, root, edge = project_inner(
         scalars, team_tokens, w_inner, halo, taps, own_step
     )
-    sides = lax.all_gather(side, TEAM)
+    def packed(values):
+        return values.reshape(sl, count, SIDE).swapaxes(0, 1).reshape(count, sl * SIDE)
+
+    sides = lax.all_gather(packed(side), TEAM)
+    with jax.named_scope("keys_exchange"):
+        own_keys = packed(own_keys)[None]
+        if ch == 2:
+            own_keys = paired(own_keys[0], swap(own_keys[0], "ch"), "ch", 0)
+        elif ch > 2:
+            own_keys = lax.all_gather(own_keys[0], "ch")
+        own_keys = paired(own_keys, swap(own_keys, "zl"), "zl", 0)
+        own_keys = paired(own_keys, swap(own_keys, "core"), "core", 1)
+        key_value_rows = keys_of(sl, own_keys.reshape(4, whole, sl * SIDE))
+    with jax.named_scope("weights_gating"):
+        theirs, out_ready = together(
+            swap(gating_ready, "sh"), along_ch(mixed_rest[:, :LANES])
+        )
+    w_gating = (gating_ready, theirs)
     gating, queries = project_gating(scalars, team_tokens, w_gating, root)
-    io = sides[:, :, :SIDE].transpose(1, 0, 2).reshape(total, 2 * NS)
-    key_value_rows = lax.dynamic_slice_in_dim(sides[:, :, SIDE:], my_sl * 4, 4, 0)
-    key_value_rows = key_value_rows.transpose(1, 0, 2).reshape(sl, count, 2 * HD)
-    if ch == 2:
-        key_value_rows = paired(key_value_rows, swap(key_value_rows, "ch"), "ch", 1)
-        key_value_rows = key_value_rows.reshape(sl, whole, 2 * HD)
-    elif ch > 2:
-        key_value_rows = lax.all_gather(key_value_rows, "ch", axis=1, tiled=True)
-    leaving, piece_decay = states(sl, step_pre, head, conv, io)
-    entry = entering(piece_decay[:, 0], leaving, False)
+    rest = [mixed_rest[:, at * LANES : (at + 1) * LANES] for at in range(1, 4)]
+    with jax.named_scope("weights_out"):
+        theirs, gate_ready = together(swap(out_ready, "sh"), along_ch(rest[0]))
+    w_out = (out_ready, theirs)
+    leaving, piece_decay = states(sl, step_pre, head, conv, sides)
+    with jax.named_scope("state_exchange"):
+        entry = entering(piece_decay[:, 0], leaving, False)
+    entry, gate_ready = together(entry, gate_ready)
+    with jax.named_scope("weights_gate"):
+        theirs, lift_ready = together(swap(gate_ready, "sh"), along_ch(rest[1]))
+    w_gate = (gate_ready, theirs)
     attended, logs = attend(place, queries, key_value_rows)
-    team_cotangent = team_gather(own_cotangent)
-    entry, *team_cotangent = together(entry, *team_cotangent)
-    ssm, carried, square = ssm_block(sl, step_pre, head, conv, io, gating, entry)
-    mixer_root = lax.rsqrt(team_sum(square[:, 0]) / DI + epsilon).reshape(total, 1)
+    ssm, carried, square = ssm_block(sl, step_pre, head, conv, sides, gating, entry)
+    with jax.named_scope("square_sum"):
+        square = team_sum(square)
+    mixer_root = lax.rsqrt(square / DI + epsilon).reshape(total, 1)
     branch_rows = jnp.concatenate(
         [(ssm * silu_value(gating) * mixer_root * own_gain).astype(BF), attended.astype(BF)], 1
     )
-
-    branch = team_scatter(back_dot(order, [(branch_rows, w_out)]))
-
-    residual = own_tokens.astype(F32) + branch
-    feed_root = inverse_root(residual)
-    feed_rows = team_gather((residual * feed_root).astype(BF))
+    branch_rows, lift_ready = together(branch_rows, lift_ready)
+    with jax.named_scope("weights_lift"):
+        theirs, drop_ready = together(swap(lift_ready, "sh"), along_ch(rest[2]))
+    w_lift = (lift_ready, theirs)
+    branch_parts = back_dot(order, [(branch_rows, w_out)])
+    with jax.named_scope("branch_scatter"):
+        branch = team_scatter(branch_parts)
+    branch = list(branch)
+    drop_ready, branch[0] = together(drop_ready, branch[0])
+    with jax.named_scope("weights_drop"):
+        w_drop = (drop_ready, swap(drop_ready, "sh"))
+    residual, feed_root, *feed_halves = home_forward(dims, nowhere, branch, own_tokens)
+    with jax.named_scope("feed_gather"):
+        feed_rows = team_gather(*feed_halves)
     active, gate_rows_grad, lift_rows_grad = feed_block(
-        feed_rows, team_cotangent, w_gate, w_lift, w_drop
-    )
-    feed_grad = team_scatter(
-        back_dot(straight, [(gate_rows_grad, w_gate), (lift_rows_grad, w_lift)])
-    )
-    residual_grad = own_cotangent.astype(F32) + norm_back(residual, feed_root, feed_grad)
-    branch_grad = team_gather(residual_grad.astype(BF))
-    drop_mine, drop_theirs = grad_halves(straight, team_cotangent, active)
-    gate_mine, gate_theirs = grad_halves(straight, feed_rows, gate_rows_grad)
-    lift_mine, lift_theirs = grad_halves(straight, feed_rows, lift_rows_grad)
-    layer_parts = back_dot(straight, [(active, w_drop)])
-    drop_theirs = swap(drop_theirs, "sh")
-    branch_grad, layer_parts, drop_theirs, gate_theirs, lift_theirs = together(
-        branch_grad, layer_parts, drop_theirs, gate_theirs, lift_theirs
-    )
-    gate_theirs, drop_part = together(
-        swap(gate_theirs, "sh"), ch_part(added(drop_mine, drop_theirs))
-    )
-    layer_output = (residual + team_scatter(layer_parts)).astype(BF)
+        scalars, feed_rows, team_cotangent, w_gate, w_lift, w_drop
+    )
+    feed_parts = back_dot(order, [(gate_rows_grad, w_gate), (lift_rows_grad, w_lift)])
+    with jax.named_scope("feed_scatter"):
+        feed_grad = team_scatter(feed_parts)
+    gate_mine, gate_theirs = grad_halves(order, gathered_halves(feed_rows), gate_rows_grad)
+    with jax.named_scope("gate_back"):
+        gate_theirs = swap(gate_theirs, "sh")
+    feed_grad = list(feed_grad)
+    feed_grad[0], gate_theirs, active = together(feed_grad[0], gate_theirs, active)
+    lift_mine, lift_theirs = grad_halves(order, gathered_halves(feed_rows), lift_rows_grad)
+    straight = jnp.arange(8, dtype=jnp.int32)
+    drop_mine, drop_theirs = grad_halves(straight, straight_halves(team_cotangent), active)
+    layer_part = forth_dot(active, w_drop)
+    with jax.named_scope("lift_back"):
+        lift_theirs, gate_part = together(
+            swap(lift_theirs, "sh"), ch_part(added(gate_mine, gate_theirs))
+        )
+    residual_grad, *branch_halves = home_back(
+        dims, nowhere, feed_grad, residual, feed_root, own_cotangent
+    )
+    with jax.named_scope("branch_gather"):
+        branch_grad = team_gather(*branch_halves)
+    layer_part, *branch_grad = together(layer_part, *branch_grad)
+    layer_part = lax.psum_scatter(layer_part, TEAM, scatter_dimension=0, tiled=True)
 
     mixer_rows_grad, attn_grad, along, gain_part = rows_back(
         scalars, branch_grad, w_out, ssm, gating, mixer_root, own_gain
     )
-    along = team_sum(along[:, 0]).reshape(total, 1) / DI
-    query_grad, key_value_part = attend_back(
+    mixer_rows_grad, lift_theirs, gate_part = together(mixer_rows_grad, lift_theirs, gate_part)
+    with jax.named_scope("drop_back"):
+        drop_theirs, lift_part = together(
+            swap(drop_theirs, "sh"), ch_part(added(lift_mine, lift_theirs))
+        )
+    with jax.named_scope("along_sum"):
+        along = team_sum(along[:, 0]).reshape(total, 1) / DI
+    query_grad, key_parts = attend_back(
         place, queries, attn_grad, attended, logs, root, key_value_rows
     )
-    if ch == 1:
-        key_value_grad = key_value_part
-    elif ch == 2:
-        halves = key_value_part.reshape(sl, ch, count, 2 * HD)
-        key_value_grad = added(
-            kept(halves, "ch", 1), swap(given(halves, "ch", 1).astype(BF), "ch")
+    with jax.named_scope("keys_back"):
+        key_parts = lax.all_to_all(
+            key_parts.astype(BF), ("zl", "core"), split_axis=0, concat_axis=0, tiled=True
         )
-    else:
-        key_value_grad = lax.psum_scatter(
-            key_value_part.astype(BF), "ch", scatter_dimension=1, tiled=True
-        ).astype(F32)
-    out_mine, out_theirs = grad_halves(order, branch_grad, branch_rows)
-    along, gate_theirs, drop_part, out_theirs = together(
-        along, gate_theirs, drop_part, out_theirs
-    )
-    lift_theirs, gate_part = together(
-        swap(lift_theirs, "sh"), ch_part(added(gate_mine, gate_theirs))
-    )
+        key_parts = jnp.sum(key_parts.astype(F32), axis=0).reshape(ch, count, sl * SIDE)
+        if ch == 1:
+            key_grad = key_parts[0]
+        elif ch == 2:
+            key_grad = added(
+                kept(key_parts, "ch", 0), swap(given(key_parts, "ch", 0).astype(BF), "ch")
+            )
+        else:
+            key_grad = lax.psum_scatter(
+                key_parts.astype(BF), "ch", scatter_dimension=0, tiled=False
+            ).astype(F32)
+    out_mine, out_theirs = grad_halves(order, gathered_halves(branch_grad), branch_rows)
+    along, drop_theirs, lift_part, out_theirs = together(
+        along, drop_theirs, lift_part, out_theirs
+    )
+    with jax.named_scope("out_back"):
+        out_theirs, drop_part = together(
+            swap(out_theirs, "sh"), ch_part(added(drop_mine, drop_theirs))
+        )
     ssm_grad, gating_grad, leaving_back = states_back(
-        sl, step_pre, head, io, mixer_rows_grad, ssm, gating, mixer_root, along, own_gain, root
-    )
-    entry_back = entering(piece_decay[:, 0], leaving_back, True)
+        sl, step_pre, head, sides, mixer_rows_grad, ssm, gating, mixer_root, along, own_gain, root
+    )
+    with jax.named_scope("state_back"):
+        entry_back = entering(piece_decay[:, 0], leaving_back, True)
     gating_rows_grad = jnp.concatenate([gating_grad, query_grad], 1)
-    gating_mine, gating_theirs = grad_halves(order, team_tokens, gating_rows_grad)
-    ssm_grad, layer_output, lift_theirs, gate_part, gating_theirs = together(
-        ssm_grad, layer_output, lift_theirs, gate_part, gating_theirs
-    )
-    out_theirs, lift_part = together(
-        swap(out_theirs, "sh"), ch_part(added(lift_mine, lift_theirs))
-    )
+    gating_mine, gating_theirs = grad_halves(order, gathered_halves(team_tokens), gating_rows_grad)
+    entry_back, out_theirs, drop_part = together(entry_back, out_theirs, drop_part)
     inner_conv_grad, parts, step_rows_grad, sums = ssm_back(
-        side_index,
-        sl,
-        step_pre,
-        head,
-        conv,
-        io,
-        ssm_grad,
-        carried,
-        entry_back,
-        key_value_grad.reshape(total, 2 * HD),
-        root,
-    )
-    parts = lax.all_to_all(parts, TEAM, split_axis=0, concat_axis=0, tiled=True)
-    parts, out_theirs, lift_part = together(parts, out_theirs, lift_part)
-    gating_theirs, out_part = together(
-        swap(gating_theirs, "sh"), ch_part(added(out_mine, out_theirs))
-    )
-    feed_back = ranks_return([drop_part, gate_part, lift_part], drows).astype(F32)
-    drop_back = feed_back[:, :, :LANES]
-    gate_back = feed_back[:, :, LANES : 2 * LANES]
-    lift_back = feed_back[:, :, 2 * LANES :]
-    conv_grad, conv_sums = conv_back(inner_conv_grad, parts, conv, pre, edge)
-    follow = shifted(conv_grad.reshape(sl, count, LANES)[:, :EDGE], -1)
+        sl, step_pre, head, conv, sides, ssm_grad, carried, entry_back, root
+    )
+    parts, key_grad = together(parts, key_grad)
+    with jax.named_scope("parts_exchange"):
+        parts = lax.all_to_all(parts, TEAM, split_axis=0, concat_axis=0, tiled=True)
+    parts, drop_part = together(parts, drop_part)
+    with jax.named_scope("first_return"):
+        first_back = ranks_return([gate_part, lift_part, drop_part], drows)
+    with jax.named_scope("gating_back"):
+        gating_theirs, out_part = together(
+            swap(gating_theirs, "sh"), ch_part(added(out_mine, out_theirs))
+        )
+    conv_grad, conv_sums = conv_back(inner_conv_grad, parts, key_grad, conv, pre, edge)
+    with jax.named_scope("follow"):
+        follow = shifted(conv_grad.reshape(sl, count, LANES)[:, :EDGE], -1)
     inner_rows_grad = pre_back(conv_grad, follow, taps, root)
+    inner_rows_grad, gating_theirs, out_part = together(inner_rows_grad, gating_theirs, out_part)
+    inner_theirs = grad_dot(order, gathered_halves(team_tokens)[1], inner_rows_grad, BF)
+    inner_mine = grad_dot(order, gathered_halves(team_tokens)[0], inner_rows_grad, F32)
+    half = width // 2
     step_halves = (own_step[:, : width // 2], own_step[:, width // 2 :])
-    hidden_grad = team_scatter(
-        back_dot(
-            order,
-            [
-                (inner_rows_grad, w_inner),
-                (gating_rows_grad, w_gating),
-                (step_rows_grad, step_halves),
-            ],
-        )
-    )
-    inner_mine, inner_theirs = grad_halves(order, team_tokens, inner_rows_grad)
-    inner_theirs, gating_part = together(
-        swap(inner_theirs, "sh"), ch_part(added(gating_mine, gating_theirs))
-    )
-    inner_part = ch_part(added(inner_mine, inner_theirs))
-    mixer_back = ranks_return([out_part, gating_part, inner_part], drows).astype(F32)
-    out_back = mixer_back[:, :, :LANES]
-    gating_back = mixer_back[:, :, LANES : 2 * LANES]
-    inner_back = mixer_back[:, :, 2 * LANES :]
-    token_values = own_tokens.astype(F32)
-    token_root = inverse_root(token_values)
-    tokens_grad = residual_grad + norm_back(token_values, token_root, hidden_grad / token_root)
-    left, right, left_other, right_other = team_tokens
+    hidden_parts = back_dot(
+        order,
+        [
+            (inner_rows_grad, w_inner),
+            (gating_rows_grad, w_gating),
+            (step_rows_grad, step_halves),
+        ],
+    )
+    with jax.named_scope("inner_back"):
+        inner_theirs = swap(inner_theirs, "sh")
+    with jax.named_scope("hidden_scatter"):
+        hidden_parts = scatter_core(hidden_parts)
+    with jax.named_scope("gating_part"):
+        gating_part = ch_part(added(gating_mine, gating_theirs))
+    inner_theirs, gating_part, first_back, *hidden_parts = together(
+        inner_theirs, gating_part, first_back, *hidden_parts
+    )
+    with jax.named_scope("hidden_scatter"):
+        hidden_parts = scatter_near(hidden_parts)
+    with jax.named_scope("inner_part"):
+        inner_part = ch_part(added(inner_mine, inner_theirs))
+    inner_part, *hidden_parts = together(inner_part, *hidden_parts)
+    with jax.named_scope("third_return"):
+        third_back = ranks_return([out_part, gating_part, inner_part], drows).astype(F32)
+    with jax.named_scope("hidden_scatter"):
+        hidden_parts = scatter_last(hidden_parts)
+    first_back = first_back.astype(F32)
+    gate_back = first_back[:, :, :LANES]
+    lift_back = first_back[:, :, LANES : 2 * LANES]
+    drop_back = first_back[:, :, 2 * LANES : 3 * LANES]
+    out_back = third_back[:, :, :LANES]
+    gating_back = third_back[:, :, LANES : 2 * LANES]
+    inner_back = third_back[:, :, 2 * LANES :]
+    token_values = jnp.concatenate(own_tokens, 1)
+    token_root = inverse_root(token_values.astype(F32))
+    hidden_parts = [part.astype(F32) / token_root for part in hidden_parts]
+    half = width // 2
+    tokens_grad, _, _ = home_back(
+        dims, nowhere, hidden_parts, token_values, token_root, residual_grad
+    )
+    tokens_out = leave(dims, home, tokens_grad, None, F32)
+    layer_output = leave(dims, home, residual, layer_part, BF)
+    token_left, token_right = gathered_halves(team_tokens)
     step_back = jnp.concatenate(
         [
-            grad_dot(order, left, left_other, step_rows_grad, F32),
-            grad_dot(order, right, right_other, step_rows_grad, F32),
+            grad_dot(order, token_left, step_rows_grad, F32),
+            grad_dot(order, token_right, step_rows_grad, F32),
         ],
         0,
     )[:, :HEADS].T
@@ -1335,8 +1675,8 @@
     output_out = out_back[:, :, INNER:].transpose(0, 2, 1).reshape(HA * HD, drows)
     drop_out = drop_back.transpose(0, 2, 1).reshape(-1, drows)
     return (
-        unshuffled(layer_output, sh, sl, ch),
-        unshuffled(tokens_grad, sh, sl, ch),
+        layer_output,
+        tokens_out,
         norm_out,
         gating_core * norm_scale,
         inner_core * norm_scale,

time: 907 us -> 843 us (0.929)
  local copies, waits for them, and re-layouts: 144 us -> 94.5 us
  other arithmetic: 119 us -> 76.6 us
  starting transfers between devices: 134 us -> 159 us
    reshape x14 -> x4, local copies, waits for them, and re-layouts: 14.4 us -> 1.62 us  [the longest x1 1.02 us: local(): mixer_root = lax.rsqrt(square / DI + epsilon).reshape(total, 1)]
    ppermute x4, waiting for transfers between devices: 6.69 us -> 18.5 us  [shifted(): lax.ppermute(value, 'ch', [(at, at + steps) for at in range(leading, last)])]
    ppermute x80 -> x70, starting transfers between devices: 95.3 us -> 107 us  [swap(): return lax.ppermute(value, axis, [(0, 1), (1, 0)])]
    concatenate x7 -> x3, local copies, waits for them, and re-layouts: 10 us -> 0.06 us  [the longest x1 0.05 us: local(): token_values = jnp.concatenate(own_tokens, 1)]
    unnamed x342 -> x340, local copies, waits for them, and re-layouts: 51.3 us -> 44.4 us
    ppermute x80 -> x70, waiting for transfers between devices: 291 us -> 288 us  [swap(): return lax.ppermute(value, axis, [(0, 1), (1, 0)])]
    pallas_call x30 -> x37, Pallas kernels: 176 us -> 179 us  [the longest x14 42.3 us: grad_dot(): call(3.1, grad_dot_kernel, (half // tile,), [*specs, full(against)], pl.B...]
  transfers between devices with their start and end apart: 92 -> 85, of which waited for: 42 -> 34; matrix products, arithmetic and copies ran while one was open for 21% -> 14% of each run, Pallas kernels for 13% -> 17%
where the time goes in v4:
time: 843 us; the launch traced here: 832 us
  waiting for transfers between devices  306 us (36%)
  Pallas kernels  179 us (21%)
  starting transfers between devices  159 us (19%)
  local copies, waits for them, and re-layouts  94.5 us (11%)
  other arithmetic  76.6 us (9%)
  between operations  17.2 us (2%)
    ppermute x70, waiting for transfers between devices, swap(): return lax.ppermute(value, axis, [(0, 1), (1, 0)])  288 us
    ppermute x70, starting transfers between devices, swap(): return lax.ppermute(value, axis, [(0, 1), (1, 0)])  107 us
    unnamed x340, local copies, waits for them, and re-layouts  44.4 us
    pallas_call x14, Pallas kernels, grad_dot(): call(3.1, grad_dot_kernel, (half // tile,), [*specs, full(against)], pl.B...  42.3 us
    pallas_call x3, Pallas kernels, back_dot(): call(3.0 + 3.0 * len(terms), lambda *refs: back_dot_kernel(len(terms), ha...  30.9 us
    ppermute x4, waiting for transfers between devices, shifted(): lax.ppermute(value, 'ch', [(at, at + steps) for at in range(leading, last)])  18.5 us
    pallas_call x1, Pallas kernels, ssm_back(): call(19, lambda *refs: ssm_back_kernel(seqs, *refs), (blocks,), [back(8),...  18.4 us
  transfers between devices with their start and end apart: 85, of which 34 were waited for; matrix products, arithmetic and copies ran while one was open for 14% of the time, Pallas kernels for 17%

profile of v4, /device:TPU:0, one launch (start us, length us, event | category | flops | bytes accessed | tf_op | source)
XLA Modules:
  0.0 832.1 jit_solution(1376416029575108551)
XLA Ops:
  10.5 6.1 collective-permute-start
  41.0 21.1 %collective-permute-done.2 = bf16[2,144,1024]{2,1,0:T(8,128)(2,1)S(1)} collective-permute-done((bf16[2,144,1024]{2,1,0:T(8,128)(2,1)S(1)}, bf16[2,144,1024]{2,1,0:T(8,128)(2,1)S(1)}, u32[]{:S(2)}, u32[]{:S(2)}) %collective-permute-start.2) | collective-permute-done | bytes 589856 | tf_op jit(solution)/shard_map/tokens_gather/ppermute | solution.py:32
  83.7 24.4 %collective-permute-done.7 = bf16[512,512]{1,0:T(8,128)(2,1)S(1)} collective-permute-done((bf16[512,512]{1,0:T(8,128)(2,1)S(1)}, bf16[512,512]{1,0:T(8,128)(2,1)S(1)}, u32[]{:S(2)}, u32[]{:S(2)}) %collective-permute-start.7) | collective-permute-done | bytes 524320 | tf_op jit(solution)/shard_map/weights_first/ppermute | solution.py:32
  117.9 23.0 %collective-permute-done.9 = bf16[512,512]{1,0:T(8,128)(2,1)S(1)} collective-permute-done((bf16[512,512]{1,0:T(8,128)(2,1)}, bf16[512,512]{1,0:T(8,128)(2,1)S(1)}, u32[]{:S(2)}, u32[]{:S(2)}) %collective-permute-start.9) | collective-permute-done | bytes 524320 | tf_op jit(solution)/shard_map/weights_inner/ppermute | solution.py:32
  142.0 10.4 %shard_map.382 = (f32[1024,512]{1,0:T(8,128)}, f32[1024,512]{1,0:T(8,128)}, bf16[1024,64]{1,0:T(8,128)(2,1)S(1)}, bf16[1024,64]{1,0:T(8,128)(2,1)S(1)}, f32[1024...) custom-call(s32[5]{0:T(128)S(1)} %copy-done.69, ...), custom_call_target="tpu_custom_call" | custom-call | flops 4160000000 | bytes 1000000 | tf_op jit(solution)/shard_map/pallas_call | solution.py:492
  166.2 44.9 %collective-permute-done.18 = bf16[512,128]{0,1:T(8,128)(2,1)S(1)} collective-permute-done((bf16[512,128]{0,1:T(8,128)(2,1)S(1)}, bf16[512,128]{0,1:T(8,128)(2,1)S(1)}, u32[]{:S(2)}, u32[]{:S(2)}) %collective-permute-start.18) | collective-permute-done | bytes 131104 | tf_op jit(solution)/shard_map/keys_exchange/ppermute | solution.py:32
  216.3 26.4 %collective-permute-done.19 = bf16[2,512,128]{1,2,0:T(8,128)(2,1)S(1)} collective-permute-done((bf16[2,512,128]{1,2,0:T(8,128)(2,1)S(1)}, bf16[2,512,128]{1,2,0:T(8,128)(2,1)S(1)}, u32[]{:S(2)}, u32[]{:S(2)}) %collective-permute-start.19) | collective-permute-done | bytes 262176 | tf_op jit(solution)/shard_map/keys_exchange/ppermute | solution.py:32
  258.9 6.6 shard_map.383
  265.5 10.8 %shard_map.385 = (f32[2,512,384]{2,1,0:T(8,128)S(1)}, bf16[2,4,256,384]{3,2,1,0:T(8,128)(2,1)S(1)}, f32[4,2,8,128]{3,2,1,0:T(8,128)S(1)}) custom-call(f32[2,512,8]{2,1,0:T(8,128)S(1)} %bitcast.324, f32[8,8]{1,0:T(8,128)S(1)} %pad.16.refs_1_, f32[2,512,512]{2,1,0:T(8,128)} %bitcast.304, bf16[8,512,128]{2,1,0:T(8,128)(2,1)S(1)} %copy-done.72, ...), custom_call_target="tpu_custom_call" | custom-call | flops 4480000000 | bytes 1000000 | tf_op jit(solution)/shard_map/pallas_call | solution.py:988
  284.0 7.4 collective-permute-start.16
  303.5 7.7 shard_map.387
  315.6 9.9 %collective-permute-start.26 = (bf16[2,128,1024]{2,1,0:T(8,128)(2,1)S(1)}, bf16[2,128,1024]{2,1,0:T(8,128)(2,1)S(1)}, u32[]{:S(2)}, u32[]{:S(2)}) collective-permute-start(bf16[2,128,1024]{2,1,0:T(8,128)(2,1)S(1)} %add_convert_fusion.5), channel_id=1, source_target_pairs={{0,2},{2,0},{1,3},{3,1},{4,6},{6,4},{5,7},{7,5},{8,10},{10,8},{9,1... | collective-permute-start | bytes 1572872 | tf_op jit(solution)/shard_map/branch_scatter/ppermute | solution.py:32
  325.5 14.0 %collective-permute-done.24 = bf16[512,512]{1,0:T(8,128)(2,1)S(1)} collective-permute-done((bf16[512,512]{1,0:T(8,128)(2,1)S(1)}, bf16[512,512]{1,0:T(8,128)(2,1)S(1)}, u32[]{:S(2)}, u32[]{:S(2)}) %collective-permute-start.24) | collective-permute-done | bytes 524320 | tf_op jit(solution)/shard_map/weights_lift/ppermute | solution.py:32
  342.6 12.1 %collective-permute-done.29 = bf16[2,128,1024]{2,1,0:T(8,128)(2,1)S(1)} collective-permute-done((bf16[2,128,1024]{2,1,0:T(8,128)(2,1)S(1)}, bf16[2,128,1024]{2,1,0:T(8,128)(2,1)S(1)}, u32[]{:S(2)}, u32[]{:S(2)}) %collective-permute-start.29) | collective-permute-done | bytes 524320 | tf_op jit(solution)/shard_map/branch_scatter/ppermute | solution.py:32
  377.2 6.1 collective-permute-done.32
  385.2 9.1 %collective-permute-done.37.dt.theirs = bf16[1024,512]{1,0:T(8,128)(2,1)} collective-permute-done((bf16[1024,512]{1,0:T(8,128)(2,1)S(1)}, bf16[1024,512]{1,0:T(8,128)(2,1)}, u32[]{:S(2)}, u32[]{:S(2)}) %collective-permute-start.37) | collective-permute-done | bytes 1048608 | tf_op jit(solution)/shard_map/weights_drop/ppermute | solution.py:32
  394.3 12.0 %shard_map.389 = (bf16[1024,512]{1,0:T(8,128)(2,1)S(1)}, bf16[1024,512]{1,0:T(8,128)(2,1)S(1)}, bf16[1024,512]{1,0:T(8,128)(2,1)S(1)}) custom-call(s32[5]{0:T(128)S(1)} %copy-done.70, bf16[4,128,1024]{2,1,0:T(8,128)(2,1)S(1)} %pad_maximum_fusion.11.l.own, bf16[4,128,1024]{2,1,0:T(8,128)(2,1)} %pad_maximum_fusion.12.r.own, ...), custom_call_target="tpu_custom_call" | custom-call | flops 4720000000 | bytes 1000000 | tf_op jit(solution)/shard_map/pallas_call | solution.py:712
  407.3 11.2 %shard_map.390 = (f32[4,128,1024]{2,1,0:T(8,128)}, f32[4,128,1024]{2,1,0:T(8,128)}, bf16[4,128,1024]{2,1,0:T(8,128)(2,1)S(1)}, bf16[4,128,1024]{2,1,0:T(8,128)(2,1)S(1)}) custom-call(s32[8]{0:T(128)S(1)} %stack.240.refs_0_.scalars, bf16[1024,512]{1,0:T(8,128)(2,1)S(1)} %get-tuple-element.206.refs_1_.refs_2_.against, ...), custom_call_target="tpu_custom_call" | custom-call | flops 3600000000 | bytes 1000000 | tf_op jit(solution)/shard_map/pallas_call | solution.py:626
  429.6 7.0 collective-permute-done.39
  445.0 6.7 collective-permute-done.40
  508.4 9.4 %shard_map.395 = (f32[1024,384]{1,0:T(8,128)}, bf16[1024,128]{1,0:T(8,128)(2,1)S(1)}, f32[4,8,256]{2,1,0:T(8,128)S(1)}, f32[1,384]{1,0:T(1,128)S(1)}) custom-call(s32[5]{0:T(128)S(1)} %copy-done.70, bf16[4,128,1024]{2,1,0:T(8,128)(2,1)} %pad_maximum_fusion.13.l.own, bf16[4,128,1024]{2,1,0:T(8,128)(2,1)} %pad_maximum_fusion.14.r.own, ...), custom_call_target="tpu_custom_call" | custom-call | flops 3800000000 | bytes 1000000 | tf_op jit(solution)/shard_map/pallas_call | solution.py:563
  524.5 6.4 shard_map.404
  564.4 5.6 shard_map.401
  577.9 14.5 %collective-permute-done.58.refs_6_ = bf16[2,256,384]{2,1,0:T(8,128)(2,1)S(1)} collective-permute-done((bf16[2,256,384]{2,1,0:T(8,128)(2,1)S(1)}, bf16[2,256,384]{2,1,0:T(8,128)(2,1)S(1)}, u32[]{:S(2)}, u32[]{:S(2)}) %collective-permute-start.58) | collective-permute-done | bytes 393248 | tf_op jit(solution)/shard_map/state_back/ppermute | solution.py:174
  596.3 18.4 %shard_map.403 = (f32[2,512,384]{2,1,0:T(8,128)S(1)}, bf16[8,512,128]{2,1,0:T(8,128)(2,1)S(1)}, bf16[2,512,8]{2,1,0:T(8,128)(2,1)S(1)}, f32[8,8]{1,0:T(8,128)S(1)}) custom-call(f32[2,512,8]{2,1,0:T(8,128)S(1)} %bitcast.326, f32[8,8]{1,0:T(8,128)S(1)} %pad.16.refs_1_, f32[2,512,512]{2,1,0:T(8,128)} %bitcast.305, bf16[8,512,128]{2,1,0:T(8,128)(2,1)S(1)} %copy-done.74, ...), custom_call_target="tpu_custom_call" | custom-call | flops 7600000000 | bytes 1000000 | tf_op jit(solution)/shard_map/pallas_call | solution.py:1160
  618.3 10.2 %all-to-all-start.4 = ((bf16[8,512,128]{2,1,0:T(8,128)(2,1)}), bf16[8,512,128]{2,1,0:T(8,128)(2,1)}, u32[]{:S(2)}, u32[]{:S(2)}) async-start(bf16[8,512,128]{2,1,0:T(8,128)(2,1)} %copy-done.43), calls=%async_computation.5 | async-start | bytes 2097152 | tf_op jit(solution)/shard_map/parts_exchange/all_to_all | solution.py:1542
  680.0 12.0 %shard_map.412 = (f32[4,128,1024]{2,1,0:T(8,128)}, f32[4,128,1024]{2,1,0:T(8,128)}, bf16[4,128,1024]{2,1,0:T(8,128)(2,1)}, bf16[4,128,1024]{2,1,0:T(8,128)(2,1)}) custom-call(s32[8]{0:T(128)S(1)} %stack.240.refs_0_.scalars, bf16[1024,512]{1,0:T(8,128)(2,1)S(1)} %shard_map.406.against.refs_1_.refs_2_, ...), custom_call_target="tpu_custom_call" | custom-call | flops 4800000000 | bytes 1000000 | tf_op jit(solution)/shard_map/pallas_call | solution.py:626
  702.8 17.4 %collective-permute-done.66 = bf16[512,512]{1,0:T(8,128)(2,1)S(1)} collective-permute-done((bf16[512,512]{1,0:T(8,128)(2,1)S(1)}, bf16[512,512]{1,0:T(8,128)(2,1)S(1)}, u32[]{:S(2)}, u32[]{:S(2)}) %collective-permute-start.66) | collective-permute-done | bytes 524320 | tf_op jit(solution)/shard_map/gating_part/ppermute | solution.py:32
  727.8 7.0 collective-permute-start.70
  755.6 11.0 %collective-permute-done.71 = bf16[2,128,1024]{2,1,0:T(8,128)(2,1)S(1)} collective-permute-done((bf16[2,128,1024]{2,1,0:T(8,128)(2,1)S(1)}, bf16[2,128,1024]{2,1,0:T(8,128)(2,1)S(1)}, u32[]{:S(2)}, u32[]{:S(2)}) %collective-permute-start.71) | collective-permute-done | bytes 524320 | tf_op jit(solution)/shard_map/hidden_scatter/ppermute | solution.py:32
  766.8 9.6 %collective-permute-done.69 = bf16[512,512]{1,0:T(8,128)(2,1)S(1)} collective-permute-done((bf16[512,512]{1,0:T(8,128)(2,1)S(1)}, bf16[512,512]{1,0:T(8,128)(2,1)S(1)}, u32[]{:S(2)}, u32[]{:S(2)}) %collective-permute-start.69) | collective-permute-done | bytes 524320 | tf_op jit(solution)/shard_map/inner_part/ppermute | solution.py:32
  797.1 10.9 %collective-permute-done.73 = bf16[128,1024]{1,0:T(8,128)(2,1)S(1)} collective-permute-done((bf16[128,1024]{1,0:T(8,128)(2,1)S(1)}, bf16[128,1024]{1,0:T(8,128)(2,1)S(1)}, u32[]{:S(2)}, u32[]{:S(2)}) %collective-permute-start.73) | collective-permute-done | bytes 262176 | tf_op jit(solution)/shard_map/hidden_scatter/ppermute | solution.py:32
  (760 shorter events, 405.6 us)
Async XLA Ops:
  31.3 37.5 %all-to-all-start.1 = ((bf16[8,64,1024]{2,1,0:T(8,128)(2,1)}), bf16[8,64,1024]{2,1,0:T(8,128)(2,1)S(1)}, u32[]{:S(2)}, u32[]{:S(2)}) async-start(bf16[8,64,1024]{2,1,0:T(8,128)(2,1)} %concatenate.138), calls=%async_computation.1 | async-start | bytes 2097152 | tf_op jit(solution)/shard_map/weights_in/all_to_all | solution.py:134
  68.8 73.1 %all-to-all-start.2 = ((bf16[8,64,2048]{2,1,0:T(8,128)(2,1)}), bf16[8,64,2048]{2,1,0:T(8,128)(2,1)}, u32[]{:S(2)}, u32[]{:S(2)}) async-start(bf16[8,64,2048]{2,1,0:T(8,128)(2,1)} %copy-done.105), calls=%async_computation.2 | async-start | bytes 4194304 | tf_op jit(solution)/shard_map/weights_rest/all_to_all | solution.py:134
  73.3 171.1 %all-gather.3.cloned.1.call-start = ((), (), s32[]{:S(2)}) async-start(), calls=%async_computation.9 | async-start | bytes 1179648 | tf_op jit(solution)/shard_map/all_gather | solution.py:1417
  80.5 27.6 %collective-permute-start.7 = (bf16[512,512]{1,0:T(8,128)(2,1)S(1)}, bf16[512,512]{1,0:T(8,128)(2,1)S(1)}, u32[]{:S(2)}, u32[]{:S(2)}) collective-permute-start(bf16[512,512]{1,0:T(8,128)(2,1)S(1)} %get-tuple-element.313), channel_id=1, source_target_pairs={{0,4},{4,0},{1,5},{5,1},{2,6},{6,2},{3,7},{7,3},{8,12},{12,8},{9,1... | collective-permute-start | bytes 1572872 | tf_op jit(solution)/shard_map/weights_first/ppermute | solution.py:32
  108.2 33.8 %collective-permute-start.8 = (bf16[1024,512]{1,0:T(8,128)(2,1)S(1)}, bf16[1024,512]{1,0:T(8,128)(2,1)}, u32[]{:S(2)}, u32[]{:S(2)}) collective-permute-start(bf16[1024,512]{1,0:T(8,128)(2,1)S(1)} %pad_maximum_fusion.4.refs_5_.refs_3_), channel_id=1, source_target_pairs={{0,16},{16,0},{1,17},{17,1},{2,18},{18,2},{3,19},{19,3},{4,20},{20... | collective-permute-start | bytes 3145736 | tf_op jit(solution)/shard_map/weights_inner/ppermute | solution.py:32
  155.5 229.7 %all-gather.5.cloned.1.call-start = ((), (), s32[]{:S(2)}) async-start(), calls=%async_computation.10 | async-start | bytes 4718592 | tf_op jit(solution)/shard_map/all_gather | solution.py:1382
  155.6 57.2 %collective-permute-start.10 = (bf16[1024,512]{1,0:T(8,128)(2,1)}, bf16[1024,512]{1,0:T(8,128)(2,1)}, u32[]{:S(2)}, u32[]{:S(2)}) collective-permute-start(bf16[1024,512]{1,0:T(8,128)(2,1)} %pad_maximum_fusion.5.mine.refs_7_), channel_id=1, source_target_pairs={{0,16},{16,0},{1,17},{17,1},{2,18},{18,2},{3,19},{19,3},{4,20},{20... | collective-permute-start | bytes 3145736 | tf_op jit(solution)/shard_map/weights_gating/ppermute | solution.py:32
  159.0 52.2 %collective-permute-start.11 = (bf16[512,512]{1,0:T(8,128)(2,1)S(1)}, bf16[512,512]{1,0:T(8,128)(2,1)S(1)}, u32[]{:S(2)}, u32[]{:S(2)}) collective-permute-start(bf16[512,512]{1,0:T(8,128)(2,1)S(1)} %get-tuple-element.307), channel_id=1, source_target_pairs={{0,4},{4,0},{1,5},{5,1},{2,6},{6,2},{3,7},{7,3},{8,12},{12,8},{9,1... | collective-permute-start | bytes 1572872 | tf_op jit(solution)/shard_map/weights_gating/ppermute | solution.py:32
  159.3 51.8 %collective-permute-start.18 = (bf16[512,128]{0,1:T(8,128)(2,1)S(1)}, bf16[512,128]{0,1:T(8,128)(2,1)S(1)}, u32[]{:S(2)}, u32[]{:S(2)}) collective-permute-start(bf16[512,128]{0,1:T(8,128)(2,1)S(1)} %bitcast.344), channel_id=1, source_target_pairs={{0,4},{4,0},{1,5},{5,1},{2,6},{6,2},{3,7},{7,3},{8,12},{12,8},{9,1... | collective-permute-start | bytes 393224 | tf_op jit(solution)/shard_map/keys_exchange/ppermute | solution.py:32
  163.2 91.1 %collective-permute-start.14 = (bf16[512,512]{1,0:T(8,128)(2,1)}, bf16[512,512]{1,0:T(8,128)(2,1)}, u32[]{:S(2)}, u32[]{:S(2)}) collective-permute-start(bf16[512,512]{1,0:T(8,128)(2,1)} %get-tuple-element.306), channel_id=1, source_target_pairs={{0,4},{4,0},{1,5},{5,1},{2,6},{6,2},{3,7},{7,3},{8,12},{12,8},{9,1... | collective-permute-start | bytes 1572872 | tf_op jit(solution)/shard_map/weights_out/ppermute | solution.py:32
  163.3 93.3 %collective-permute-start.22 = (bf16[512,512]{1,0:T(8,128)(2,1)}, bf16[512,512]{1,0:T(8,128)(2,1)}, u32[]{:S(2)}, u32[]{:S(2)}) collective-permute-start(bf16[512,512]{1,0:T(8,128)(2,1)} %get-tuple-element.305), channel_id=1, source_target_pairs={{0,4},{4,0},{1,5},{5,1},{2,6},{6,2},{3,7},{7,3},{8,12},{12,8},{9,1... | collective-permute-start | bytes 1572872 | tf_op jit(solution)/shard_map/weights_gate/ppermute | solution.py:32
  211.1 31.6 %collective-permute-start.19 = (bf16[2,512,128]{1,2,0:T(8,128)(2,1)S(1)}, bf16[2,512,128]{1,2,0:T(8,128)(2,1)S(1)}, u32[]{:S(2)}, u32[]{:S(2)}) collective-permute-start(bf16[2,512,128]{1,2,0:T(8,128)(2,1)S(1)} %maximum_select_fusion.4), channel_id=1, source_target_pairs={{0,2},{2,0},{1,3},{3,1},{4,6},{6,4},{5,7},{7,5},{8,10},{10,8},{9,1... | collective-permute-start | bytes 786440 | tf_op jit(solution)/shard_map/keys_exchange/ppermute | solution.py:32
  212.8 52.7 %collective-permute-start.13 = (bf16[1024,512]{1,0:T(8,128)(2,1)}, bf16[1024,512]{1,0:T(8,128)(2,1)}, u32[]{:S(2)}, u32[]{:S(2)}) collective-permute-start(bf16[1024,512]{1,0:T(8,128)(2,1)} %pad_maximum_fusion.6.refs_3_.mine), channel_id=1, source_target_pairs={{0,16},{16,0},{1,17},{17,1},{2,18},{18,2},{3,19},{19,3},{4,20},{20... | collective-permute-start | bytes 3145736 | tf_op jit(solution)/shard_map/weights_out/ppermute | solution.py:32
  243.6 35.9 %collective-permute-start.20 = (bf16[2,2,512,128]{2,3,1,0:T(8,128)(2,1)}, bf16[2,2,512,128]{2,3,1,0:T(8,128)(2,1)}, u32[]{:S(2)}, u32[]{:S(2)}) collective-permute-start(bf16[2,2,512,128]{2,3,1,0:T(8,128)(2,1)} %maximum_select_fusion.2), channel_id=1, source_target_pairs={{0,1},{1,0},{2,3},{3,2},{4,5},{5,4},{6,7},{7,6},{8,9},{9,8},{10,11... | collective-permute-start | bytes 1572872 | tf_op jit(solution)/shard_map/keys_exchange/ppermute | solution.py:32
  311.3 28.3 %collective-permute-start.23 = (bf16[1024,512]{1,0:T(8,128)(2,1)S(1)}, bf16[1024,512]{1,0:T(8,128)(2,1)S(1)}, u32[]{:S(2)}, u32[]{:S(2)}) collective-permute-start(bf16[1024,512]{1,0:T(8,128)(2,1)S(1)} %copy-done.129), channel_id=1, source_target_pairs={{0,16},{16,0},{1,17},{17,1},{2,18},{18,2},{3,19},{19,3},{4,20},{20... | collective-permute-start | bytes 3145736 | tf_op jit(solution)/shard_map/weights_lift/ppermute | solution.py:32
  312.9 26.7 %collective-permute-start.28 = (bf16[4,128,1024]{2,1,0:T(8,128)(2,1)S(1)}, bf16[4,128,1024]{2,1,0:T(8,128)(2,1)S(1)}, u32[]{:S(2)}, u32[]{:S(2)}) collective-permute-start(bf16[4,128,1024]{2,1,0:T(8,128)(2,1)S(1)} %get-tuple-element.198), channel_id=1, source_target_pairs={{0,1},{1,0},{2,3},{3,2},{4,5},{5,4},{6,7},{7,6},{8,9},{9,8},{10,11... | collective-permute-start | bytes 3145736 | tf_op jit(solution)/shard_map/branch_scatter/ppermute | solution.py:32
  468.2 40.2 %collective-permute-start.51 = (bf16[1024,512]{1,0:T(8,128)(2,1)}, bf16[1024,512]{1,0:T(8,128)(2,1)}, u32[]{:S(2)}, u32[]{:S(2)}) collective-permute-start(bf16[1024,512]{1,0:T(8,128)(2,1)} %shard_map.396), channel_id=1, source_target_pairs={{0,16},{16,0},{1,17},{17,1},{2,18},{18,2},{3,19},{19,3},{4,20},{20... | collective-permute-start | bytes 3145736 | tf_op jit(solution)/shard_map/lift_back/ppermute | solution.py:32
  474.9 33.5 %collective-permute-start.49 = (bf16[4,128,1024]{2,1,0:T(8,128)(2,1)}, bf16[4,128,1024]{2,1,0:T(8,128)(2,1)}, u32[]{:S(2)}, u32[]{:S(2)}) collective-permute-start(bf16[4,128,1024]{2,1,0:T(8,128)(2,1)} %pad_maximum_fusion.13.l.own), channel_id=1, source_target_pairs={{0,1},{1,0},{2,3},{3,2},{4,5},{5,4},{6,7},{7,6},{8,9},{9,8},{10,11... | collective-permute-start | bytes 3145736 | tf_op jit(solution)/shard_map/branch_gather/ppermute | solution.py:32
  476.0 32.3 %collective-permute-start.50 = (bf16[4,128,1024]{2,1,0:T(8,128)(2,1)}, bf16[4,128,1024]{2,1,0:T(8,128)(2,1)}, u32[]{:S(2)}, u32[]{:S(2)}) collective-permute-start(bf16[4,128,1024]{2,1,0:T(8,128)(2,1)} %pad_maximum_fusion.14.r.own), channel_id=1, source_target_pairs={{0,1},{1,0},{2,3},{3,2},{4,5},{5,4},{6,7},{7,6},{8,9},{9,8},{10,11... | collective-permute-start | bytes 3145736 | tf_op jit(solution)/shard_map/branch_gather/ppermute | solution.py:32
  479.0 27.0 %collective-permute-start.52 = (bf16[512,512]{1,0:T(8,128)(2,1)}, bf16[512,512]{1,0:T(8,128)(2,1)}, u32[]{:S(2)}, u32[]{:S(2)}) collective-permute-start(bf16[512,512]{1,0:T(8,128)(2,1)} %slice.625), channel_id=1, source_target_pairs={{0,4},{4,0},{1,5},{5,1},{2,6},{6,2},{3,7},{7,3},{8,12},{12,8},{9,1... | collective-permute-start | bytes 1572872 | tf_op jit(solution)/shard_map/lift_back/ppermute | solution.py:32
  492.1 57.4 %collective-permute-start.56 = (bf16[1024,512]{1,0:T(8,128)(2,1)}, bf16[1024,512]{1,0:T(8,128)(2,1)}, u32[]{:S(2)}, u32[]{:S(2)}) collective-permute-start(bf16[1024,512]{1,0:T(8,128)(2,1)} %shard_map.398), channel_id=1, source_target_pairs={{0,16},{16,0},{1,17},{17,1},{2,18},{18,2},{3,19},{19,3},{4,20},{20... | collective-permute-start | bytes 3145736 | tf_op jit(solution)/shard_map/drop_back/ppermute | solution.py:32
  539.4 53.0 %all-to-all-start.3 = ((bf16[4,1024,128]{2,1,0:T(8,128)(2,1)}), bf16[4,1024,128]{2,1,0:T(8,128)(2,1)}, u32[]{:S(2)}, u32[]{:S(2)}) async-start(bf16[4,1024,128]{2,1,0:T(8,128)(2,1)} %convert_element_type.360), calls=%async_computation.4 | async-start | bytes 2097152 | tf_op jit(solution)/shard_map/keys_back/all_to_all | solution.py:1507
  543.8 267.1 %reduce-scatter.2.cloned.1.call-start = ((), (), s32[]{:S(2)}) async-start(), calls=%async_computation.11 | async-start | bytes 4718592 | tf_op jit(solution)/shard_map/reduce_scatter | solution.py:1491
  549.5 28.4 %collective-permute-start.59 = (bf16[1024,512]{1,0:T(8,128)(2,1)}, bf16[1024,512]{1,0:T(8,128)(2,1)}, u32[]{:S(2)}, u32[]{:S(2)}) collective-permute-start(bf16[1024,512]{1,0:T(8,128)(2,1)} %shard_map.400), channel_id=1, source_target_pairs={{0,16},{16,0},{1,17},{17,1},{2,18},{18,2},{3,19},{19,3},{4,20},{20... | collective-permute-start | bytes 3145736 | tf_op jit(solution)/shard_map/out_back/ppermute | solution.py:32
  618.3 38.3 %all-to-all-start.4 = ((bf16[8,512,128]{2,1,0:T(8,128)(2,1)}), bf16[8,512,128]{2,1,0:T(8,128)(2,1)}, u32[]{:S(2)}, u32[]{:S(2)}) async-start(bf16[8,512,128]{2,1,0:T(8,128)(2,1)} %copy-done.43), calls=%async_computation.5 | async-start | bytes 2097152 | tf_op jit(solution)/shard_map/parts_exchange/all_to_all | solution.py:1542
  632.8 41.7 %collective-permute-start.63 = (bf16[1024,512]{1,0:T(8,128)(2,1)}, bf16[1024,512]{1,0:T(8,128)(2,1)}, u32[]{:S(2)}, u32[]{:S(2)}) collective-permute-start(bf16[1024,512]{1,0:T(8,128)(2,1)} %shard_map.407), channel_id=1, source_target_pairs={{0,16},{16,0},{1,17},{17,1},{2,18},{18,2},{3,19},{19,3},{4,20},{20... | collective-permute-start | bytes 3145736 | tf_op jit(solution)/shard_map/gating_back/ppermute | solution.py:32
  640.4 32.1 %collective-permute-start.64 = (bf16[512,512]{1,0:T(8,128)(2,1)}, bf16[512,512]{1,0:T(8,128)(2,1)}, u32[]{:S(2)}, u32[]{:S(2)}) collective-permute-start(bf16[512,512]{1,0:T(8,128)(2,1)} %slice.622), channel_id=1, source_target_pairs={{0,4},{4,0},{1,5},{5,1},{2,6},{6,2},{3,7},{7,3},{8,12},{12,8},{9,1... | collective-permute-start | bytes 1572872 | tf_op jit(solution)/shard_map/gating_back/ppermute | solution.py:32
  659.2 68.5 %all-to-all-start.5 = ((bf16[8,64,1536]{2,1,0:T(8,128)(2,1)}), bf16[8,64,1536]{2,1,0:T(8,128)(2,1)}, u32[]{:S(2)}, u32[]{:S(2)}) async-start(bf16[8,64,1536]{2,1,0:T(8,128)(2,1)} %pad_maximum_fusion), calls=%async_computation.6 | async-start | bytes 3145728 | tf_op jit(solution)/shard_map/first_return/all_to_all | solution.py:150
  692.0 29.2 %collective-permute-start.67 = (bf16[4,128,1024]{2,1,0:T(8,128)(2,1)}, bf16[4,128,1024]{2,1,0:T(8,128)(2,1)}, u32[]{:S(2)}, u32[]{:S(2)}) collective-permute-start(bf16[4,128,1024]{2,1,0:T(8,128)(2,1)} %get-tuple-element.265), channel_id=1, source_target_pairs={{0,1},{1,0},{2,3},{3,2},{4,5},{5,4},{6,7},{7,6},{8,9},{9,8},{10,11... | collective-permute-start | bytes 3145736 | tf_op jit(solution)/shard_map/hidden_scatter/ppermute | solution.py:32
  693.8 30.3 %collective-permute-start.68 = (bf16[4,128,1024]{2,1,0:T(8,128)(2,1)}, bf16[4,128,1024]{2,1,0:T(8,128)(2,1)S(1)}, u32[]{:S(2)}, u32[]{:S(2)}) collective-permute-start(bf16[4,128,1024]{2,1,0:T(8,128)(2,1)} %get-tuple-element.267), channel_id=1, source_target_pairs={{0,1},{1,0},{2,3},{3,2},{4,5},{5,4},{6,7},{7,6},{8,9},{9,8},{10,11... | collective-permute-start | bytes 3145736 | tf_op jit(solution)/shard_map/hidden_scatter/ppermute | solution.py:32
  742.4 35.5 %all-to-all-start.7 = ((f32[32,1,1184]{2,1,0:T(1,128)}), f32[32,1,1184]{2,1,0:T(1,128)}, u32[]{:S(2)}, u32[]{:S(2)}) async-start(f32[32,1,1184]{2,1,0:T(1,128)} %copy.264), calls=%async_computation.8 | async-start | bytes 327680 | tf_op jit(solution)/shard_map/all_to_all | solution.py:1637
  777.9 35.0 %all-to-all-start.6 = ((bf16[8,64,1536]{2,1,0:T(8,128)(2,1)}), bf16[8,64,1536]{2,1,0:T(8,128)(2,1)}, u32[]{:S(2)}, u32[]{:S(2)}) async-start(bf16[8,64,1536]{2,1,0:T(8,128)(2,1)} %pad_maximum_fusion.1), calls=%async_computation.7 | async-start | bytes 3145728 | tf_op jit(solution)/shard_map/third_return/all_to_all | solution.py:150
  (216 other events, 2240.3 us)
Sparse Core Ops, SparseCore 0:
  155.7 21.1 all-gather.2
  179.0 64.8 all-gather.4
  554.9 66.7 reduce-scatter.1

commit v5 on v4

--- a/solution.py
+++ b/solution.py
@@ -230,9 +230,6 @@
 HEADS = HM // RANKS
 SIDE = 2 * NS // RANKS
 CONV = INNER + SIDE
-
-
-COST = 0.4e9
 
 
 def call(cost, kernel, grid, in_specs, out_specs, out_shape, scratch=(), scalars=0):
@@ -247,7 +244,7 @@
         ),
         out_shape=out_shape,
         compiler_params=pltpu.CompilerParams(vmem_limit_bytes=48 * 1024 * 1024),
-        cost_estimate=pl.CostEstimate(flops=int(cost * COST), bytes_accessed=10**6, transcendentals=0),
+        cost_estimate=pl.CostEstimate(flops=int(cost * 10**9), bytes_accessed=10**6, transcendentals=0),
     )
 
 
@@ -338,7 +335,7 @@
     width = dims[3]
     half = shape((BLOCK, width // 2), BF)
     return call(
-        2.0,
+        2,
         lambda *refs: arrive_kernel(dims, *refs),
         (1,),
         [whole_blocks(width)] * 2,
@@ -443,7 +440,7 @@
 def home_back(dims, place, parts, values, root, base):
     half = dims[3] // 2
     return call(
-        1.4,
+        1.6,
         lambda *refs: home_back_kernel(dims, *refs),
         (1,),
         [whole_blocks(half)] * 4 + [whole_blocks(2 * half), whole_blocks(1), whole_blocks(2 * half)],
@@ -561,7 +558,7 @@
     total, width = root.shape[0], 2 * gathered[0].shape[2]
     tiles = total // TILE
     return call(
-        9.5,
+        9.1,
         rows_back_kernel,
         (tiles,),
         gathered_specs(gathered)
@@ -624,7 +621,7 @@
     given_spec = pl.BlockSpec((2, BLOCK, half), lambda i, s: (jnp.minimum(i, halves - 1), 0, 0))
     blocks = total // BLOCK // 2
     return call(
-        3.0 + 3.0 * len(terms),
+        3 + 3 * len(terms),
         lambda *refs: back_dot_kernel(len(terms), halves, *refs),
         (2 * halves,),
         specs,
@@ -688,6 +685,59 @@
     return [(rows, 0, 0, half), (rows, 1, 0, half)], [(rows, 0, half, half), (rows, 1, half, half)]
 
 
+def feed_grads_kernel(order, l, r, lo, ro, cotangent, active, gate, lift, *refs):
+    mine, theirs, (gate_rows, lift_rows) = refs[:3], refs[3:6], refs[6:]
+    i = pl.program_id(0)
+
+    @pl.when(i == 0)
+    def _():
+        for k in range(8):
+            start = pl.multiple_of(order[k] * BLOCK, BLOCK)
+            gate_rows[k * BLOCK : (k + 1) * BLOCK] = gate[pl.ds(start, BLOCK), :]
+            lift_rows[k * BLOCK : (k + 1) * BLOCK] = lift[pl.ds(start, BLOCK), :]
+
+    def run(own, other, out):
+        tile = own.shape[2]
+        rows = own.shape[0] * own.shape[1]
+        own, other = own[...].reshape(rows, tile), other[...].reshape(rows, tile)
+        for at, against in ((0, gate_rows), (1, lift_rows)):
+            product = dot(own, against[:rows], (0, 0)) + dot(other, against[rows:], (0, 0))
+            out[at][...] = product.astype(BF)
+        out[2][...] = dot(cotangent[...], active[...], (0, 0)).astype(BF)
+
+    @pl.when(i < pl.num_programs(0) // 2)
+    def _():
+        run(r, ro, theirs)
+
+    @pl.when(i >= pl.num_programs(0) // 2)
+    def _():
+        run(l, lo, mine)
+
+
+def feed_grads(order, gathered, cotangent, active, gate, lift):
+    total, width = cotangent.shape
+    tile = 512
+    tiles = width // tile
+    half = tiles // 2
+    dims = gathered[0].shape[:2] + (tile,)
+    right = pl.BlockSpec(dims, lambda i, s: (0, 0, jnp.minimum(i, half - 1)))
+    left = pl.BlockSpec(dims, lambda i, s: (0, 0, jnp.maximum(i - half, 0)))
+    return call(
+        13,
+        feed_grads_kernel,
+        (tiles,),
+        [left, right, left, right, pl.BlockSpec((total, tile), lambda i, s: (0, (i + half) % tiles))]
+        + [full(x) for x in (active, gate, lift)],
+        [
+            *[pl.BlockSpec((tile, LANES), lambda i, s: (jnp.maximum(i - half, 0), 0))] * 3,
+            *[pl.BlockSpec((tile, LANES), lambda i, s: (jnp.minimum(i, half - 1), 0))] * 3,
+        ],
+        [shape((width // 2, LANES), BF)] * 6,
+        [pltpu.VMEM((total, LANES), BF)] * 2,
+        1,
+    )(order, *gathered, cotangent, active, gate, lift)
+
+
 def grad_halves(order, halves, against):
     theirs = grad_dot(order, halves[1], against, BF)
     return grad_dot(order, halves[0], against, F32), theirs
@@ -731,7 +781,7 @@
     total, k = rows.shape
     width = 2 * weights[0].shape[0]
     return call(
-        4.2,
+        4.4,
         forth_dot_kernel,
         (total // TILE,),
         [tiled(k), full(weights[0]), full(weights[1])],
@@ -830,7 +880,7 @@
     grid, rows = attend_specs(seqs, total)
     sums = pl.BlockSpec((1, whole, width), lambda n, i, s: (n, 0, 0))
     return call(
-        5,
+        6.4,
         attend_back_kernel,
         grid,
         [rows(HD), rows(HD), rows(HD), rows(1), rows(1), sums],
@@ -922,7 +972,7 @@
     step_pre, conv = by_seq(seqs, step_pre, conv)
     blocks = conv.shape[1] // BLOCK
     return call(
-        4.5,
+        4.2,
         lambda *refs: states_kernel(seqs, blocks, *refs),
         (blocks,),
         [
@@ -986,7 +1036,7 @@
     count = conv.shape[1]
     blocks = count // BLOCK
     ssm, carried, square = call(
-        11.2,
+        10.8,
         lambda *refs: ssm_kernel(seqs, *refs),
         (blocks,),
         [
@@ -1051,7 +1101,7 @@
     blocks = count // BLOCK
     back = lambda width: pair(seqs, width, blocks)
     grad, gating_grad, leaving = call(
-        6.6,
+        5.7,
         lambda *refs: states_back_kernel(seqs, blocks, *refs),
         (blocks,),
         [back(8), full(head)]
@@ -1158,7 +1208,7 @@
     blocks = count // BLOCK
     back = lambda width: pair(seqs, width, blocks)
     conv_grad, parts, step_rows, sums = call(
-        19,
+        18.8,
         lambda *refs: ssm_back_kernel(seqs, *refs),
         (blocks,),
         [
@@ -1350,40 +1400,41 @@
         mixed_in = ranks_exchange(pack_in)
     *own_tokens, own_cotangent = arrive(dims, home, tokens, cotangent)
     with jax.named_scope("tokens_gather"):
-        before = jnp.stack([part[rows - EDGE :] for part in own_tokens])
-        before = shifted(before, 1)
-        if ch == 2:
-            before = jnp.flip(before.reshape(2, EDGE, sh // 2, ch, -1), 3)
-            before = before.reshape(2, EDGE, width // 2)
-        team_tokens = list(
-            team_gather(*(jnp.concatenate([own_tokens[h], before[h]], 0) for h in range(2)))
-        )
+        team_tokens = list(team_gather(*own_tokens))
+    last = 4
     ends = []
     for seq in range(sl):
         at_block = 2 * (1 - my_zl) + (seq ^ my_sl)
         halves = []
         for own, other in ((team_tokens[0], team_tokens[2]), (team_tokens[1], team_tokens[3])):
-            own = lax.dynamic_index_in_dim(own[:, rows:], at_block, 0, False)
-            other = lax.dynamic_index_in_dim(other[:, rows:], at_block, 0, False)
+            own = lax.dynamic_index_in_dim(own[:, rows - last :], at_block, 0, False)
+            other = lax.dynamic_index_in_dim(other[:, rows - last :], at_block, 0, False)
             halves.append(jnp.where(my_core == 1, own, other))
         ends.append(jnp.concatenate(halves, 1))
     halo = jnp.stack(ends)
     with jax.named_scope("weights_first"):
-        ready = along_ch(mixed_in[:, :LANES])
+        if ch == 2:
+            first = mixed_in[:, :LANES]
+            got = swap(jnp.concatenate([first, halo.reshape(-1, LANES)], 0), "ch")
+            ready = jnp.concatenate([first, got[: first.shape[0]]], 0)
+            halo = got[first.shape[0] :].reshape(sl, last, sh, ch, -1)
+            halo = jnp.flip(halo, 3).reshape(sl, last, width)
+            halo = jnp.where(lax.axis_index("ch") == 0, jnp.zeros_like(halo), halo)
+        else:
+            ready = along_ch(mixed_in[:, :LANES])
+            halo = shifted(halo, 1)
+        halo = jnp.pad(halo, ((0, 0), (EDGE - last, 0), (0, 0)))
     pack_rest = jnp.concatenate(
         [by_rank(mixer_out.T), by_rank(output_weight.T)]
         + [by_rank(scaled(w, feed_gain)) for w in (gate_matrix, lift_matrix)]
         + [by_rank(drop_matrix.T)],
         2,
     )
-    pack_rest, sent_cotangent, *team_tokens = together(pack_rest, own_cotangent, *team_tokens)
+    pack_rest, *team_tokens = together(pack_rest, *team_tokens)
     with jax.named_scope("weights_rest"):
         mixed_rest = ranks_exchange(pack_rest)
-    team_cotangent = lax.all_gather(sent_cotangent, TEAM, axis=0, tiled=True)
     with jax.named_scope("weights_inner"):
-        theirs, gating_ready, mixed_rest = together(
-            swap(ready, "sh"), along_ch(mixed_in[:, LANES:]), mixed_rest
-        )
+        theirs, gating_ready = together(swap(ready, "sh"), along_ch(mixed_in[:, LANES:]))
     w_inner = (ready, theirs)
 
     at = (KC + 1) * conv_own
@@ -1415,6 +1466,8 @@
         return values.reshape(sl, count, SIDE).swapaxes(0, 1).reshape(count, sl * SIDE)
 
     sides = lax.all_gather(packed(side), TEAM)
+    sent_cotangent, sides = together(own_cotangent, sides)
+    team_cotangent = lax.all_gather(sent_cotangent, TEAM, axis=0, tiled=True)
     with jax.named_scope("keys_exchange"):
         own_keys = packed(own_keys)[None]
         if ch == 2:
@@ -1430,17 +1483,16 @@
         )
     w_gating = (gating_ready, theirs)
     gating, queries = project_gating(scalars, team_tokens, w_gating, root)
-    rest = [mixed_rest[:, at * LANES : (at + 1) * LANES] for at in range(1, 4)]
     with jax.named_scope("weights_out"):
-        theirs, gate_ready = together(swap(out_ready, "sh"), along_ch(rest[0]))
-    w_out = (out_ready, theirs)
+        w_out = (out_ready, swap(out_ready, "sh"))
+    sides, gating = together(sides, gating)
     leaving, piece_decay = states(sl, step_pre, head, conv, sides)
     with jax.named_scope("state_exchange"):
         entry = entering(piece_decay[:, 0], leaving, False)
-    entry, gate_ready = together(entry, gate_ready)
-    with jax.named_scope("weights_gate"):
-        theirs, lift_ready = together(swap(gate_ready, "sh"), along_ch(rest[1]))
-    w_gate = (gate_ready, theirs)
+    entry, mixed_rest = together(entry, mixed_rest)
+    rest = [mixed_rest[:, at * LANES : (at + 1) * LANES] for at in range(1, 4)]
+    with jax.named_scope("weights_gate_first"):
+        gate_ready = along_ch(rest[0])
     attended, logs = attend(place, queries, key_value_rows)
     ssm, carried, square = ssm_block(sl, step_pre, head, conv, sides, gating, entry)
     with jax.named_scope("square_sum"):
@@ -1449,13 +1501,19 @@
     branch_rows = jnp.concatenate(
         [(ssm * silu_value(gating) * mixer_root * own_gain).astype(BF), attended.astype(BF)], 1
     )
-    branch_rows, lift_ready = together(branch_rows, lift_ready)
+    branch_rows, gate_ready, rest[1] = together(branch_rows, gate_ready, rest[1])
+    with jax.named_scope("weights_gate"):
+        theirs, lift_ready = together(swap(gate_ready, "sh"), along_ch(rest[1]))
+    w_gate = (gate_ready, theirs)
+    branch_parts = back_dot(order, [(branch_rows, w_out)])
+    with jax.named_scope("branch_scatter"):
+        branch = scatter_core(branch_parts)
+    lift_ready, rest[2], *branch = together(lift_ready, rest[2], *branch)
     with jax.named_scope("weights_lift"):
         theirs, drop_ready = together(swap(lift_ready, "sh"), along_ch(rest[2]))
     w_lift = (lift_ready, theirs)
-    branch_parts = back_dot(order, [(branch_rows, w_out)])
     with jax.named_scope("branch_scatter"):
-        branch = team_scatter(branch_parts)
+        branch = scatter_last(scatter_near(branch))
     branch = list(branch)
     drop_ready, branch[0] = together(drop_ready, branch[0])
     with jax.named_scope("weights_drop"):
@@ -1469,19 +1527,17 @@
     feed_parts = back_dot(order, [(gate_rows_grad, w_gate), (lift_rows_grad, w_lift)])
     with jax.named_scope("feed_scatter"):
         feed_grad = team_scatter(feed_parts)
-    gate_mine, gate_theirs = grad_halves(order, gathered_halves(feed_rows), gate_rows_grad)
+    feed_back = feed_grads(
+        order, feed_rows, team_cotangent, active, gate_rows_grad, lift_rows_grad
+    )
+    mine, given_parts = feed_back[:3], feed_back[3:]
     with jax.named_scope("gate_back"):
-        gate_theirs = swap(gate_theirs, "sh")
+        gate_got = swap(given_parts[0], "sh")
     feed_grad = list(feed_grad)
-    feed_grad[0], gate_theirs, active = together(feed_grad[0], gate_theirs, active)
-    lift_mine, lift_theirs = grad_halves(order, gathered_halves(feed_rows), lift_rows_grad)
-    straight = jnp.arange(8, dtype=jnp.int32)
-    drop_mine, drop_theirs = grad_halves(straight, straight_halves(team_cotangent), active)
+    feed_grad[0], active, gate_got = together(feed_grad[0], active, gate_got)
     layer_part = forth_dot(active, w_drop)
     with jax.named_scope("lift_back"):
-        lift_theirs, gate_part = together(
-            swap(lift_theirs, "sh"), ch_part(added(gate_mine, gate_theirs))
-        )
+        lift_got, gate_part = together(swap(given_parts[1], "sh"), ch_part(added(mine[0], gate_got)))
     residual_grad, *branch_halves = home_back(
         dims, nowhere, feed_grad, residual, feed_root, own_cotangent
     )
@@ -1493,11 +1549,9 @@
     mixer_rows_grad, attn_grad, along, gain_part = rows_back(
         scalars, branch_grad, w_out, ssm, gating, mixer_root, own_gain
     )
-    mixer_rows_grad, lift_theirs, gate_part = together(mixer_rows_grad, lift_theirs, gate_part)
+    mixer_rows_grad, lift_got, gate_part = together(mixer_rows_grad, lift_got, gate_part)
     with jax.named_scope("drop_back"):
-        drop_theirs, lift_part = together(
-            swap(drop_theirs, "sh"), ch_part(added(lift_mine, lift_theirs))
-        )
+        drop_got, lift_part = together(swap(given_parts[2], "sh"), ch_part(added(mine[1], lift_got)))
     with jax.named_scope("along_sum"):
         along = team_sum(along[:, 0]).reshape(total, 1) / DI
     query_grad, key_parts = attend_back(
@@ -1519,12 +1573,10 @@
                 key_parts.astype(BF), "ch", scatter_dimension=0, tiled=False
             ).astype(F32)
     out_mine, out_theirs = grad_halves(order, gathered_halves(branch_grad), branch_rows)
-    along, drop_theirs, lift_part, out_theirs = together(
-        along, drop_theirs, lift_part, out_theirs
-    )
+    along, drop_got, lift_part, out_theirs = together(along, drop_got, lift_part, out_theirs)
     with jax.named_scope("out_back"):
         out_theirs, drop_part = together(
-            swap(out_theirs, "sh"), ch_part(added(drop_mine, drop_theirs))
+            swap(out_theirs, "sh"), ch_part(added(mine[2], drop_got))
         )
     ssm_grad, gating_grad, leaving_back = states_back(
         sl, step_pre, head, sides, mixer_rows_grad, ssm, gating, mixer_root, along, own_gain, root
@@ -1534,15 +1586,14 @@
     gating_rows_grad = jnp.concatenate([gating_grad, query_grad], 1)
     gating_mine, gating_theirs = grad_halves(order, gathered_halves(team_tokens), gating_rows_grad)
     entry_back, out_theirs, drop_part = together(entry_back, out_theirs, drop_part)
+    with jax.named_scope("first_return"):
+        first_back = ranks_return([gate_part, lift_part, drop_part], drows)
     inner_conv_grad, parts, step_rows_grad, sums = ssm_back(
         sl, step_pre, head, conv, sides, ssm_grad, carried, entry_back, root
     )
-    parts, key_grad = together(parts, key_grad)
+    parts, key_grad, first_back = together(parts, key_grad, first_back)
     with jax.named_scope("parts_exchange"):
         parts = lax.all_to_all(parts, TEAM, split_axis=0, concat_axis=0, tiled=True)
-    parts, drop_part = together(parts, drop_part)
-    with jax.named_scope("first_return"):
-        first_back = ranks_return([gate_part, lift_part, drop_part], drows)
     with jax.named_scope("gating_back"):
         gating_theirs, out_part = together(
             swap(gating_theirs, "sh"), ch_part(added(out_mine, out_theirs))
@@ -1554,6 +1605,7 @@
     inner_rows_grad, gating_theirs, out_part = together(inner_rows_grad, gating_theirs, out_part)
     inner_theirs = grad_dot(order, gathered_halves(team_tokens)[1], inner_rows_grad, BF)
     inner_mine = grad_dot(order, gathered_halves(team_tokens)[0], inner_rows_grad, F32)
+    inner_rows_grad, inner_theirs = together(inner_rows_grad, inner_theirs)
     half = width // 2
     step_halves = (own_step[:, : width // 2], own_step[:, width // 2 :])
     hidden_parts = back_dot(
@@ -1566,29 +1618,24 @@
     )
     with jax.named_scope("inner_back"):
         inner_theirs = swap(inner_theirs, "sh")
-    with jax.named_scope("hidden_scatter"):
-        hidden_parts = scatter_core(hidden_parts)
+    with jax.named_scope("second_return"):
+        second_back = ranks_return([out_part], drows)
+    inner_theirs, second_back, *hidden_parts = together(inner_theirs, second_back, *hidden_parts)
     with jax.named_scope("gating_part"):
         gating_part = ch_part(added(gating_mine, gating_theirs))
-    inner_theirs, gating_part, first_back, *hidden_parts = together(
-        inner_theirs, gating_part, first_back, *hidden_parts
-    )
     with jax.named_scope("hidden_scatter"):
-        hidden_parts = scatter_near(hidden_parts)
+        hidden_parts = team_scatter(hidden_parts)
     with jax.named_scope("inner_part"):
         inner_part = ch_part(added(inner_mine, inner_theirs))
-    inner_part, *hidden_parts = together(inner_part, *hidden_parts)
     with jax.named_scope("third_return"):
-        third_back = ranks_return([out_part, gating_part, inner_part], drows).astype(F32)
-    with jax.named_scope("hidden_scatter"):
-        hidden_parts = scatter_last(hidden_parts)
+        third_back = ranks_return([gating_part, inner_part], drows).astype(F32)
     first_back = first_back.astype(F32)
     gate_back = first_back[:, :, :LANES]
     lift_back = first_back[:, :, LANES : 2 * LANES]
     drop_back = first_back[:, :, 2 * LANES : 3 * LANES]
-    out_back = third_back[:, :, :LANES]
-    gating_back = third_back[:, :, LANES : 2 * LANES]
-    inner_back = third_back[:, :, 2 * LANES :]
+    out_back = second_back.astype(F32)
+    gating_back = third_back[:, :, :LANES]
+    inner_back = third_back[:, :, LANES:]
     token_values = jnp.concatenate(own_tokens, 1)
     token_root = inverse_root(token_values.astype(F32))
     hidden_parts = [part.astype(F32) / token_root for part in hidden_parts]

time: 843 us -> 795 us (0.943)
  starting transfers between devices: 159 us -> 130 us
  waiting for transfers between devices: 306 us -> 285 us
  local copies, waits for them, and re-layouts: 94.5 us -> 111 us
  Pallas kernels: 179 us -> 165 us
    ppermute x70, waiting for transfers between devices: 288 us -> 249 us  [swap(): return lax.ppermute(value, axis, [(0, 1), (1, 0)])]
    ppermute x70, starting transfers between devices: 107 us -> 81 us  [swap(): return lax.ppermute(value, axis, [(0, 1), (1, 0)])]
    pallas_call x14 -> x8, Pallas kernels: 42.3 us -> 21.8 us  [grad_dot(): call(3.1, grad_dot_kernel, (half // tile,), [*specs, full(against)], pl.B...]
    unnamed x340 -> x398, local copies, waits for them, and re-layouts: 44.4 us -> 63.9 us
    all_to_all x2 -> x3, waiting for transfers between devices: 0.01 us -> 11 us  [ranks_return(): return lax.all_to_all(pack, TEAM, split_axis=0, concat_axis=0, tiled=True)]
    all_to_all x2 -> x3, starting transfers between devices: 8.87 us -> 19.2 us  [ranks_return(): return lax.all_to_all(pack, TEAM, split_axis=0, concat_axis=0, tiled=True)]
    ppermute x4 -> x3, starting transfers between devices: 12.5 us -> 3.99 us  [shifted(): lax.ppermute(value, 'ch', [(at, at + steps) for at in range(leading, last)])]
    pallas_call x13 -> x14, Pallas kernels: 95.4 us -> 103 us  [the longest x3 28.9 us: back_dot(): call(3 + 3 * len(terms), lambda *refs: back_dot_kernel(len(terms), halves...]
  transfers between devices with their start and end apart: 85 -> 85, of which waited for: 34 -> 33; matrix products, arithmetic and copies ran while one was open for 14% -> 15% of each run, Pallas kernels for 17% -> 17%
where the time goes in v5:
time: 795 us; the launch traced here: 784 us
  waiting for transfers between devices  285 us (36%)
  Pallas kernels  165 us (21%)
  starting transfers between devices  130 us (16%)
  local copies, waits for them, and re-layouts  111 us (14%)
  other arithmetic  76.8 us (10%)
  between operations  17 us (2%)
    ppermute x70, waiting for transfers between devices, swap(): return lax.ppermute(value, axis, [(0, 1), (1, 0)])  249 us
    ppermute x70, starting transfers between devices, swap(): return lax.ppermute(value, axis, [(0, 1), (1, 0)])  81 us
    unnamed x398, local copies, waits for them, and re-layouts  63.9 us
    pallas_call x3, Pallas kernels, back_dot(): call(3 + 3 * len(terms), lambda *refs: back_dot_kernel(len(terms), halves...  28.9 us
    pallas_call x8, Pallas kernels, grad_dot(): call(3.1, grad_dot_kernel, (half // tile,), [*specs, full(against)], pl.B...  21.8 us
    pallas_call x1, Pallas kernels, ssm_back(): call(18.8, lambda *refs: ssm_back_kernel(seqs, *refs), (blocks,), [back(8...  19.2 us
    all_to_all x3, starting transfers between devices, ranks_return(): return lax.all_to_all(pack, TEAM, split_axis=0, concat_axis=0, tiled=True)  19.2 us
  transfers between devices with their start and end apart: 85, of which 33 were waited for; matrix products, arithmetic and copies ran while one was open for 15% of the time, Pallas kernels for 17%

profile of v5, /device:TPU:0, one launch (start us, length us, event | category | flops | bytes accessed | tf_op | source)
XLA Modules:
  0.0 784.0 jit_solution(9921343907519727720)
XLA Ops:
  67.4 14.0 %collective-permute-done.6 = bf16[544,512]{1,0:T(8,128)(2,1)} collective-permute-done((bf16[544,512]{1,0:T(8,128)(2,1)}, bf16[544,512]{1,0:T(8,128)(2,1)}, u32[]{:S(2)}, u32[]{:S(2)}) %collective-permute-start.6) | collective-permute-done | bytes 557088 | tf_op jit(solution)/shard_map/weights_first/ppermute | solution.py:32
  86.1 25.0 %collective-permute-done.8 = bf16[512,512]{1,0:T(8,128)(2,1)S(1)} collective-permute-done((bf16[512,512]{1,0:T(8,128)(2,1)}, bf16[512,512]{1,0:T(8,128)(2,1)S(1)}, u32[]{:S(2)}, u32[]{:S(2)}) %collective-permute-start.8) | collective-permute-done | bytes 524320 | tf_op jit(solution)/shard_map/weights_inner/ppermute | solution.py:32
  118.2 10.2 %shard_map.382 = (f32[1024,512]{1,0:T(8,128)}, f32[1024,512]{1,0:T(8,128)}, bf16[1024,64]{1,0:T(8,128)(2,1)S(1)}, bf16[1024,64]{1,0:T(8,128)(2,1)S(1)}, f32[1024...) custom-call(s32[5]{0:T(128)S(1)} %copy-done.69, ...), custom_call_target="tpu_custom_call" | custom-call | flops 10400000000 | bytes 1000000 | tf_op jit(solution)/shard_map/pallas_call | solution.py:489
  140.4 6.9 collective-permute-done.15
  151.0 13.2 %collective-permute-done.16 = bf16[2,512,128]{1,2,0:T(8,128)(2,1)} collective-permute-done((bf16[2,512,128]{1,2,0:T(8,128)(2,1)}, bf16[2,512,128]{1,2,0:T(8,128)(2,1)}, u32[]{:S(2)}, u32[]{:S(2)}) %collective-permute-start.16) | collective-permute-done | bytes 262176 | tf_op jit(solution)/shard_map/keys_exchange/ppermute | solution.py:32
  169.8 5.9 shard_map.383
  194.6 10.7 %shard_map.385 = (f32[2,512,384]{2,1,0:T(8,128)S(1)}, bf16[2,4,256,384]{3,2,1,0:T(8,128)(2,1)S(1)}, f32[4,2,8,128]{3,2,1,0:T(8,128)S(1)}) custom-call(f32[2,512,8]{2,1,0:T(8,128)S(1)} %bitcast.320, f32[8,8]{1,0:T(8,128)S(1)} %pad.21.refs_1_, f32[2,512,512]{2,1,0:T(8,128)} %bitcast.315, bf16[8,512,128]{2,1,0:T(8,128)(2,1)S(1)} %copy-done.73, ...), custom_call_target="tpu_custom_call" | custom-call | flops 10800000000 | bytes 1000000 | tf_op jit(solution)/shard_map/pallas_call | solution.py:1038
  208.4 8.0 %collective-permute-start.13 = (f32[8,128]{1,0:T(8,128)S(1)}, f32[8,128]{1,0:T(8,128)S(1)}, u32[]{:S(2)}, u32[]{:S(2)}) collective-permute-start(f32[8,128]{1,0:T(8,128)S(1)} %add.294), channel_id=1, source_target_pairs={{0,2},{2,0},{1,3},{3,1},{4,6},{6,4},{5,7},{7,5},{8,10},{10,8},{9,1... | collective-permute-start | bytes 12296 | tf_op jit(solution)/shard_map/square_sum/ppermute | solution.py:32
  229.1 22.4 %collective-permute-done.18 = bf16[512,512]{1,0:T(8,128)(2,1)S(1)} collective-permute-done((bf16[512,512]{1,0:T(8,128)(2,1)S(1)}, bf16[512,512]{1,0:T(8,128)(2,1)S(1)}, u32[]{:S(2)}, u32[]{:S(2)}) %collective-permute-start.18) | collective-permute-done | bytes 524320 | tf_op jit(solution)/shard_map/weights_gate_first/ppermute | solution.py:32
  251.9 6.2 shard_map.387
  262.0 22.0 %collective-permute-done.20 = bf16[512,512]{1,0:T(8,128)(2,1)S(1)} collective-permute-done((bf16[512,512]{1,0:T(8,128)(2,1)S(1)}, bf16[512,512]{1,0:T(8,128)(2,1)S(1)}, u32[]{:S(2)}, u32[]{:S(2)}) %collective-permute-start.20) | collective-permute-done | bytes 524320 | tf_op jit(solution)/shard_map/weights_gate/ppermute | solution.py:32
  291.1 9.6 %collective-permute-done.28 = bf16[2,128,1024]{2,1,0:T(8,128)(2,1)S(1)} collective-permute-done((bf16[2,128,1024]{2,1,0:T(8,128)(2,1)S(1)}, bf16[2,128,1024]{2,1,0:T(8,128)(2,1)S(1)}, u32[]{:S(2)}, u32[]{:S(2)}) %collective-permute-start.28) | collective-permute-done | bytes 524320 | tf_op jit(solution)/shard_map/branch_scatter/ppermute | solution.py:32
  301.0 11.9 %collective-permute-done.26 = bf16[2,128,1024]{2,1,0:T(8,128)(2,1)S(1)} collective-permute-done((bf16[2,128,1024]{2,1,0:T(8,128)(2,1)S(1)}, bf16[2,128,1024]{2,1,0:T(8,128)(2,1)S(1)}, u32[]{:S(2)}, u32[]{:S(2)}) %collective-permute-start.26) | collective-permute-done | bytes 524320 | tf_op jit(solution)/shard_map/branch_scatter/ppermute | solution.py:32
  331.7 5.9 collective-permute-done.33
  339.5 10.1 %collective-permute-done.36.dt.theirs = bf16[1024,512]{1,0:T(8,128)(2,1)S(1)} collective-permute-done((bf16[1024,512]{1,0:T(8,128)(2,1)S(1)}, bf16[1024,512]{1,0:T(8,128)(2,1)S(1)}, u32[]{:S(2)}, u32[]{:S(2)}) %collective-permute-start.36) | collective-permute-done | bytes 1048608 | tf_op jit(solution)/shard_map/weights_drop/ppermute | solution.py:32
  354.1 11.9 %shard_map.389 = (bf16[1024,512]{1,0:T(8,128)(2,1)S(1)}, bf16[1024,512]{1,0:T(8,128)(2,1)S(1)}, bf16[1024,512]{1,0:T(8,128)(2,1)S(1)}) custom-call(s32[5]{0:T(128)S(1)} %copy-done.70, bf16[4,128,1024]{2,1,0:T(8,128)(2,1)S(1)} %copy-done.27, bf16[4,128,1024]{2,1,0:T(8,128)(2,1)S(1)} %copy-done.25, bf16[4,128,1024]{2,1,0:T(8,128)(2,1)} %collective-permute-done.34.lo, ...), custom_call_target="tpu_custom_call" | custom-call | flops 11800000512 | bytes 1000000 | tf_op jit(solution)/shard_map/pallas_call | solution.py:762
  367.9 10.7 %shard_map.390 = (f32[4,128,1024]{2,1,0:T(8,128)}, f32[4,128,1024]{2,1,0:T(8,128)}, bf16[4,128,1024]{2,1,0:T(8,128)(2,1)S(1)}, bf16[4,128,1024]{2,1,0:T(8,128)(2,1)S(1)}) custom-call(s32[8]{0:T(128)S(1)} %stack.228.refs_0_.order.scalars, bf16[1024,512]{1,0:T(8,128)(2,1)S(1)} %get-tuple-element.221.refs_1_.refs_2_.gate, ...), custom_call_target="tpu_custom_call" | custom-call | flops 8999999488 | bytes 1000000 | tf_op jit(solution)/shard_map/pallas_call | solution.py:623
  384.7 12.3 %shard_map.391 = (bf16[1024,512]{1,0:T(8,128)(2,1)S(1)}, bf16[1024,512]{1,0:T(8,128)(2,1)S(1)}, bf16[1024,512]{1,0:T(8,128)(2,1)S(1)}, bf16[1024,512]{1,0:T(8,12...) custom-call(s32[8]{0:T(128)S(1)} %stack.228.refs_0_.order.scalars, ...), custom_call_target="tpu_custom_call" | custom-call | flops 12999999488 | bytes 1000000 | tf_op jit(solution)/shard_map/pallas_call | solution.py:725
  402.6 11.3 %collective-permute-done.38 = bf16[2,128,1024]{2,1,0:T(8,128)(2,1)S(1)} collective-permute-done((bf16[2,128,1024]{2,1,0:T(8,128)(2,1)S(1)}, bf16[2,128,1024]{2,1,0:T(8,128)(2,1)S(1)}, u32[]{:S(2)}, u32[]{:S(2)}) %collective-permute-start.38) | collective-permute-done | bytes 524320 | tf_op jit(solution)/shard_map/feed_scatter/ppermute | solution.py:32
  414.8 7.2 collective-permute-done.39
  461.3 15.1 %collective-permute-done.51 = bf16[512,512]{1,0:T(8,128)(2,1)} collective-permute-done((bf16[512,512]{1,0:T(8,128)(2,1)}, bf16[512,512]{1,0:T(8,128)(2,1)}, u32[]{:S(2)}, u32[]{:S(2)}) %collective-permute-start.51) | collective-permute-done | bytes 524320 | tf_op jit(solution)/shard_map/lift_back/ppermute | solution.py:32
  478.8 9.0 %shard_map.395 = (f32[1024,384]{1,0:T(8,128)}, bf16[1024,128]{1,0:T(8,128)(2,1)S(1)}, f32[4,8,256]{2,1,0:T(8,128)S(1)}, f32[1,384]{1,0:T(1,128)S(1)}) custom-call(s32[5]{0:T(128)S(1)} %copy-done.71, bf16[4,128,1024]{2,1,0:T(8,128)(2,1)} %pad_maximum_fusion.12.l.own, bf16[4,128,1024]{2,1,0:T(8,128)(2,1)} %pad_maximum_fusion.13.r.own, ...), custom_call_target="tpu_custom_call" | custom-call | flops 9100000256 | bytes 1000000 | tf_op jit(solution)/shard_map/pallas_call | solution.py:560
  490.7 6.4 shard_map.399
  531.5 5.6 shard_map.397
  548.6 11.9 %collective-permute-done.57.refs_6_ = bf16[2,256,384]{2,1,0:T(8,128)(2,1)S(1)} collective-permute-done((bf16[2,256,384]{2,1,0:T(8,128)(2,1)S(1)}, bf16[2,256,384]{2,1,0:T(8,128)(2,1)S(1)}, u32[]{:S(2)}, u32[]{:S(2)}) %collective-permute-start.57) | collective-permute-done | bytes 393248 | tf_op jit(solution)/shard_map/state_back/ppermute | solution.py:174
  561.8 11.5 %all-to-all-start.4 = ((bf16[8,64,1536]{2,1,0:T(8,128)(2,1)}), bf16[8,64,1536]{2,1,0:T(8,128)(2,1)}, u32[]{:S(2)}, u32[]{:S(2)}) async-start(bf16[8,64,1536]{2,1,0:T(8,128)(2,1)} %pad_maximum_fusion), calls=%async_computation.5 | async-start | bytes 3145728 | tf_op jit(solution)/shard_map/first_return/all_to_all | solution.py:150
  581.8 19.2 %shard_map.398 = (f32[2,512,384]{2,1,0:T(8,128)S(1)}, bf16[8,512,128]{2,1,0:T(8,128)(2,1)}, bf16[2,512,8]{2,1,0:T(8,128)(2,1)S(1)}, f32[8,8]{1,0:T(8,128)S(1)}) custom-call(f32[2,512,8]{2,1,0:T(8,128)S(1)} %bitcast.322, f32[8,8]{1,0:T(8,128)S(1)} %copy-done.53, f32[2,512,512]{2,1,0:T(8,128)} %bitcast.316, bf16[8,512,128]{2,1,0:T(8,128)(2,1)S(1)} %copy-done.75, ...), custom_call_target="tpu_custom_call" | custom-call | flops 18800001024 | bytes 1000000 | tf_op jit(solution)/shard_map/pallas_call | solution.py:1210
  608.5 10.4 %all-to-all-done.4 = bf16[8,64,1536]{2,1,0:T(8,128)(2,1)} async-done(((bf16[8,64,1536]{2,1,0:T(8,128)(2,1)}), bf16[8,64,1536]{2,1,0:T(8,128)(2,1)}, u32[]{:S(2)}, u32[]{:S(2)}) %all-to-all-start.4) | async-done | bytes 1572896 | tf_op jit(solution)/shard_map/first_return/all_to_all | solution.py:150
  632.0 5.9 all-to-all-done.5.refs_1_
  675.2 12.1 %shard_map.405 = (f32[4,128,1024]{2,1,0:T(8,128)}, f32[4,128,1024]{2,1,0:T(8,128)}, bf16[4,128,1024]{2,1,0:T(8,128)(2,1)S(1)}, bf16[4,128,1024]{2,1,0:T(8,128)(2,1)}) custom-call(s32[8]{0:T(128)S(1)} %copy-done.68, bf16[1024,512]{1,0:T(8,128)(2,1)S(1)} %copy-done.35, bf16[1024,512]{1,0:T(8,128)(2,1)S(1)} %copy-done.35, ...), custom_call_target="tpu_custom_call" | custom-call | flops 12000000000 | bytes 1000000 | tf_op jit(solution)/shard_map/pallas_call | solution.py:623
  703.6 20.8 %collective-permute-done.72 = bf16[512,512]{1,0:T(8,128)(2,1)S(1)} collective-permute-done((bf16[512,512]{1,0:T(8,128)(2,1)S(1)}, bf16[512,512]{1,0:T(8,128)(2,1)S(1)}, u32[]{:S(2)}, u32[]{:S(2)}) %collective-permute-start.72) | collective-permute-done | bytes 524320 | tf_op jit(solution)/shard_map/inner_part/ppermute | solution.py:32
  736.1 19.4 %collective-permute-done.69 = bf16[2,128,1024]{2,1,0:T(8,128)(2,1)S(1)} collective-permute-done((bf16[2,128,1024]{2,1,0:T(8,128)(2,1)S(1)}, bf16[2,128,1024]{2,1,0:T(8,128)(2,1)S(1)}, u32[]{:S(2)}, u32[]{:S(2)}) %collective-permute-start.69) | collective-permute-done | bytes 524320 | tf_op jit(solution)/shard_map/hidden_scatter/ppermute | solution.py:32
  (809 shorter events, 384.3 us)
Async XLA Ops:
  55.4 26.0 %collective-permute-start.6 = (bf16[544,512]{1,0:T(8,128)(2,1)}, bf16[544,512]{1,0:T(8,128)(2,1)}, u32[]{:S(2)}, u32[]{:S(2)}) collective-permute-start(bf16[544,512]{1,0:T(8,128)(2,1)} %pad_maximum_fusion.16), channel_id=1, source_target_pairs={{0,4},{4,0},{1,5},{5,1},{2,6},{6,2},{3,7},{7,3},{8,12},{12,8},{9,1... | collective-permute-start | bytes 1671176 | tf_op jit(solution)/shard_map/weights_first/ppermute | solution.py:32
  62.6 73.1 %all-to-all-start.2 = ((bf16[8,64,2048]{2,1,0:T(8,128)(2,1)}), bf16[8,64,2048]{2,1,0:T(8,128)(2,1)}, u32[]{:S(2)}, u32[]{:S(2)}) async-start(bf16[8,64,2048]{2,1,0:T(8,128)(2,1)} %fusion.14), calls=%async_computation.2 | async-start | bytes 4194304 | tf_op jit(solution)/shard_map/weights_rest/all_to_all | solution.py:134
  66.9 99.2 %all-gather.3.cloned.1.call-start = ((), (), s32[]{:S(2)}) async-start(), calls=%async_computation.10 | async-start | bytes 1179648 | tf_op jit(solution)/shard_map/all_gather | solution.py:1468
  83.6 30.8 %collective-permute-start.7 = (bf16[1024,512]{1,0:T(8,128)(2,1)}, bf16[1024,512]{1,0:T(8,128)(2,1)}, u32[]{:S(2)}, u32[]{:S(2)}) collective-permute-start(bf16[1024,512]{1,0:T(8,128)(2,1)} %pad_maximum_fusion.3.refs_5_.refs_3_), channel_id=1, source_target_pairs={{0,16},{16,0},{1,17},{17,1},{2,18},{18,2},{3,19},{19,3},{4,20},{20... | collective-permute-start | bytes 3145736 | tf_op jit(solution)/shard_map/weights_inner/ppermute | solution.py:32
  85.1 26.1 %collective-permute-start.8 = (bf16[512,512]{1,0:T(8,128)(2,1)}, bf16[512,512]{1,0:T(8,128)(2,1)S(1)}, u32[]{:S(2)}, u32[]{:S(2)}) collective-permute-start(bf16[512,512]{1,0:T(8,128)(2,1)} %get-tuple-element.324), channel_id=1, source_target_pairs={{0,4},{4,0},{1,5},{5,1},{2,6},{6,2},{3,7},{7,3},{8,12},{12,8},{9,1... | collective-permute-start | bytes 1572872 | tf_op jit(solution)/shard_map/weights_inner/ppermute | solution.py:32
  132.6 219.0 %all-gather.5.cloned.1.call-start = ((), (), s32[]{:S(2)}) async-start(), calls=%async_computation.11 | async-start | bytes 4718592 | tf_op jit(solution)/shard_map/all_gather | solution.py:1470
  132.7 35.9 %collective-permute-start.9 = (bf16[1024,512]{1,0:T(8,128)(2,1)}, bf16[1024,512]{1,0:T(8,128)(2,1)}, u32[]{:S(2)}, u32[]{:S(2)}) collective-permute-start(bf16[1024,512]{1,0:T(8,128)(2,1)} %pad_maximum_fusion.4.mine.refs_7_), channel_id=1, source_target_pairs={{0,16},{16,0},{1,17},{17,1},{2,18},{18,2},{3,19},{19,3},{4,20},{20... | collective-permute-start | bytes 3145736 | tf_op jit(solution)/shard_map/weights_gating/ppermute | solution.py:32
  137.5 28.7 %collective-permute-start.10 = (bf16[512,512]{1,0:T(8,128)(2,1)}, bf16[512,512]{1,0:T(8,128)(2,1)}, u32[]{:S(2)}, u32[]{:S(2)}) collective-permute-start(bf16[512,512]{1,0:T(8,128)(2,1)} %slice.443), channel_id=1, source_target_pairs={{0,4},{4,0},{1,5},{5,1},{2,6},{6,2},{3,7},{7,3},{8,12},{12,8},{9,1... | collective-permute-start | bytes 1572872 | tf_op jit(solution)/shard_map/weights_gating/ppermute | solution.py:32
  220.5 31.4 %collective-permute-start.21 = (bf16[1024,512]{1,0:T(8,128)(2,1)S(1)}, bf16[1024,512]{1,0:T(8,128)(2,1)S(1)}, u32[]{:S(2)}, u32[]{:S(2)}) collective-permute-start(bf16[1024,512]{1,0:T(8,128)(2,1)S(1)} %copy-done.14), channel_id=1, source_target_pairs={{0,16},{16,0},{1,17},{17,1},{2,18},{18,2},{3,19},{19,3},{4,20},{20... | collective-permute-start | bytes 3145736 | tf_op jit(solution)/shard_map/weights_out/ppermute | solution.py:32
  224.9 26.5 %collective-permute-start.18 = (bf16[512,512]{1,0:T(8,128)(2,1)S(1)}, bf16[512,512]{1,0:T(8,128)(2,1)S(1)}, u32[]{:S(2)}, u32[]{:S(2)}) collective-permute-start(bf16[512,512]{1,0:T(8,128)(2,1)S(1)} %get-tuple-element.319), channel_id=1, source_target_pairs={{0,4},{4,0},{1,5},{5,1},{2,6},{6,2},{3,7},{7,3},{8,12},{12,8},{9,1... | collective-permute-start | bytes 1572872 | tf_op jit(solution)/shard_map/weights_gate_first/ppermute | solution.py:32
  251.5 32.6 %collective-permute-start.19 = (bf16[1024,512]{1,0:T(8,128)(2,1)S(1)}, bf16[1024,512]{1,0:T(8,128)(2,1)S(1)}, u32[]{:S(2)}, u32[]{:S(2)}) collective-permute-start(bf16[1024,512]{1,0:T(8,128)(2,1)S(1)} %pad_maximum_fusion.7.gm.refs_3_), channel_id=1, source_target_pairs={{0,16},{16,0},{1,17},{17,1},{2,18},{18,2},{3,19},{19,3},{4,20},{20... | collective-permute-start | bytes 3145736 | tf_op jit(solution)/shard_map/weights_gate/ppermute | solution.py:32
  258.0 26.1 %collective-permute-start.23 = (bf16[4,128,1024]{2,1,0:T(8,128)(2,1)S(1)}, bf16[4,128,1024]{2,1,0:T(8,128)(2,1)S(1)}, u32[]{:S(2)}, u32[]{:S(2)}) collective-permute-start(bf16[4,128,1024]{2,1,0:T(8,128)(2,1)S(1)} %get-tuple-element.205), channel_id=1, source_target_pairs={{0,1},{1,0},{2,3},{3,2},{4,5},{5,4},{6,7},{7,6},{8,9},{9,8},{10,11... | collective-permute-start | bytes 3145736 | tf_op jit(solution)/shard_map/branch_scatter/ppermute | solution.py:32
  258.1 27.0 %collective-permute-start.22 = (bf16[4,128,1024]{2,1,0:T(8,128)(2,1)S(1)}, bf16[4,128,1024]{2,1,0:T(8,128)(2,1)S(1)}, u32[]{:S(2)}, u32[]{:S(2)}) collective-permute-start(bf16[4,128,1024]{2,1,0:T(8,128)(2,1)S(1)} %get-tuple-element.203), channel_id=1, source_target_pairs={{0,1},{1,0},{2,3},{3,2},{4,5},{5,4},{6,7},{7,6},{8,9},{9,8},{10,11... | collective-permute-start | bytes 3145736 | tf_op jit(solution)/shard_map/branch_scatter/ppermute | solution.py:32
  286.9 26.1 %collective-permute-start.26 = (bf16[2,128,1024]{2,1,0:T(8,128)(2,1)S(1)}, bf16[2,128,1024]{2,1,0:T(8,128)(2,1)S(1)}, u32[]{:S(2)}, u32[]{:S(2)}) collective-permute-start(bf16[2,128,1024]{2,1,0:T(8,128)(2,1)S(1)} %get-tuple-element.210), channel_id=1, source_target_pairs={{0,2},{2,0},{1,3},{3,1},{4,6},{6,4},{5,7},{7,5},{8,10},{10,8},{9,1... | collective-permute-start | bytes 1572872 | tf_op jit(solution)/shard_map/branch_scatter/ppermute | solution.py:32
  286.9 27.9 %collective-permute-start.25 = (bf16[512,512]{1,0:T(8,128)(2,1)S(1)}, bf16[512,512]{1,0:T(8,128)(2,1)S(1)}, u32[]{:S(2)}, u32[]{:S(2)}) collective-permute-start(bf16[512,512]{1,0:T(8,128)(2,1)S(1)} %get-tuple-element.207), channel_id=1, source_target_pairs={{0,4},{4,0},{1,5},{5,1},{2,6},{6,2},{3,7},{7,3},{8,12},{12,8},{9,1... | collective-permute-start | bytes 1572872 | tf_op jit(solution)/shard_map/weights_lift/ppermute | solution.py:32
  436.3 42.5 %collective-permute-start.50 = (bf16[1024,512]{1,0:T(8,128)(2,1)}, bf16[1024,512]{1,0:T(8,128)(2,1)}, u32[]{:S(2)}, u32[]{:S(2)}) collective-permute-start(bf16[1024,512]{1,0:T(8,128)(2,1)} %copy-done.79), channel_id=1, source_target_pairs={{0,16},{16,0},{1,17},{17,1},{2,18},{18,2},{3,19},{19,3},{4,20},{20... | collective-permute-start | bytes 3145736 | tf_op jit(solution)/shard_map/lift_back/ppermute | solution.py:32
  445.6 33.2 %collective-permute-start.49 = (bf16[4,128,1024]{2,1,0:T(8,128)(2,1)}, bf16[4,128,1024]{2,1,0:T(8,128)(2,1)}, u32[]{:S(2)}, u32[]{:S(2)}) collective-permute-start(bf16[4,128,1024]{2,1,0:T(8,128)(2,1)} %pad_maximum_fusion.13.r.own), channel_id=1, source_target_pairs={{0,1},{1,0},{2,3},{3,2},{4,5},{5,4},{6,7},{7,6},{8,9},{9,8},{10,11... | collective-permute-start | bytes 3145736 | tf_op jit(solution)/shard_map/branch_gather/ppermute | solution.py:32
  447.8 31.0 %collective-permute-start.48 = (bf16[4,128,1024]{2,1,0:T(8,128)(2,1)}, bf16[4,128,1024]{2,1,0:T(8,128)(2,1)}, u32[]{:S(2)}, u32[]{:S(2)}) collective-permute-start(bf16[4,128,1024]{2,1,0:T(8,128)(2,1)} %pad_maximum_fusion.12.l.own), channel_id=1, source_target_pairs={{0,1},{1,0},{2,3},{3,2},{4,5},{5,4},{6,7},{7,6},{8,9},{9,8},{10,11... | collective-permute-start | bytes 3145736 | tf_op jit(solution)/shard_map/branch_gather/ppermute | solution.py:32
  450.1 26.3 %collective-permute-start.51 = (bf16[512,512]{1,0:T(8,128)(2,1)}, bf16[512,512]{1,0:T(8,128)(2,1)}, u32[]{:S(2)}, u32[]{:S(2)}) collective-permute-start(bf16[512,512]{1,0:T(8,128)(2,1)} %slice.599), channel_id=1, source_target_pairs={{0,4},{4,0},{1,5},{5,1},{2,6},{6,2},{3,7},{7,3},{8,12},{12,8},{9,1... | collective-permute-start | bytes 1572872 | tf_op jit(solution)/shard_map/lift_back/ppermute | solution.py:32
  451.5 66.1 %collective-permute-start.55 = (bf16[1024,512]{1,0:T(8,128)(2,1)}, bf16[1024,512]{1,0:T(8,128)(2,1)}, u32[]{:S(2)}, u32[]{:S(2)}) collective-permute-start(bf16[1024,512]{1,0:T(8,128)(2,1)} %get-tuple-element.247), channel_id=1, source_target_pairs={{0,16},{16,0},{1,17},{17,1},{2,18},{18,2},{3,19},{19,3},{4,20},{20... | collective-permute-start | bytes 3145736 | tf_op jit(solution)/shard_map/drop_back/ppermute | solution.py:32
  509.6 52.2 %all-to-all-start.3 = ((bf16[4,1024,128]{2,1,0:T(8,128)(2,1)}), bf16[4,1024,128]{2,1,0:T(8,128)(2,1)}, u32[]{:S(2)}, u32[]{:S(2)}) async-start(bf16[4,1024,128]{2,1,0:T(8,128)(2,1)} %convert_element_type.377), calls=%async_computation.4 | async-start | bytes 2097152 | tf_op jit(solution)/shard_map/keys_back/all_to_all | solution.py:1561
  513.9 247.3 %reduce-scatter.2.cloned.1.call-start = ((), (), s32[]{:S(2)}) async-start(), calls=%async_computation.12 | async-start | bytes 4718592 | tf_op jit(solution)/shard_map/reduce_scatter | solution.py:1547
  546.5 79.3 %collective-permute-start.62 = (bf16[1024,512]{1,0:T(8,128)(2,1)}, bf16[1024,512]{1,0:T(8,128)(2,1)}, u32[]{:S(2)}, u32[]{:S(2)}) collective-permute-start(bf16[1024,512]{1,0:T(8,128)(2,1)} %shard_map.402), channel_id=1, source_target_pairs={{0,16},{16,0},{1,17},{17,1},{2,18},{18,2},{3,19},{19,3},{4,20},{20... | collective-permute-start | bytes 3145736 | tf_op jit(solution)/shard_map/gating_back/ppermute | solution.py:32
  561.8 57.2 %all-to-all-start.4 = ((bf16[8,64,1536]{2,1,0:T(8,128)(2,1)}), bf16[8,64,1536]{2,1,0:T(8,128)(2,1)}, u32[]{:S(2)}, u32[]{:S(2)}) async-start(bf16[8,64,1536]{2,1,0:T(8,128)(2,1)} %pad_maximum_fusion), calls=%async_computation.5 | async-start | bytes 3145728 | tf_op jit(solution)/shard_map/first_return/all_to_all | solution.py:150
  576.2 31.4 %collective-permute-start.60 = (bf16[512,128]{1,0:T(8,128)(2,1)}, bf16[512,128]{1,0:T(8,128)(2,1)}, u32[]{:S(2)}, u32[]{:S(2)}) collective-permute-start(bf16[512,128]{1,0:T(8,128)(2,1)} %fusion.31), channel_id=1, source_target_pairs={{0,4},{4,0},{1,5},{5,1},{2,6},{6,2},{3,7},{7,3},{8,12},{12,8},{9,1... | collective-permute-start | bytes 393224 | tf_op jit(solution)/shard_map/keys_back/ppermute | solution.py:32
  579.0 44.6 %collective-permute-start.63 = (bf16[512,512]{1,0:T(8,128)(2,1)}, bf16[512,512]{1,0:T(8,128)(2,1)}, u32[]{:S(2)}, u32[]{:S(2)}) collective-permute-start(bf16[512,512]{1,0:T(8,128)(2,1)} %slice.596), channel_id=1, source_target_pairs={{0,4},{4,0},{1,5},{5,1},{2,6},{6,2},{3,7},{7,3},{8,12},{12,8},{9,1... | collective-permute-start | bytes 1572872 | tf_op jit(solution)/shard_map/gating_back/ppermute | solution.py:32
  662.4 32.1 %collective-permute-start.71 = (bf16[512,512]{1,0:T(8,128)(2,1)}, bf16[512,512]{1,0:T(8,128)(2,1)}, u32[]{:S(2)}, u32[]{:S(2)}) collective-permute-start(bf16[512,512]{1,0:T(8,128)(2,1)} %slice.595), channel_id=1, source_target_pairs={{0,4},{4,0},{1,5},{5,1},{2,6},{6,2},{3,7},{7,3},{8,12},{12,8},{9,1... | collective-permute-start | bytes 1572872 | tf_op jit(solution)/shard_map/gating_part/ppermute | solution.py:32
  696.1 33.3 %collective-permute-start.68 = (bf16[4,128,1024]{2,1,0:T(8,128)(2,1)}, bf16[4,128,1024]{2,1,0:T(8,128)(2,1)}, u32[]{:S(2)}, u32[]{:S(2)}) collective-permute-start(bf16[4,128,1024]{2,1,0:T(8,128)(2,1)} %get-tuple-element.292), channel_id=1, source_target_pairs={{0,1},{1,0},{2,3},{3,2},{4,5},{5,4},{6,7},{7,6},{8,9},{9,8},{10,11... | collective-permute-start | bytes 3145736 | tf_op jit(solution)/shard_map/hidden_scatter/ppermute | solution.py:32
  698.3 26.1 %collective-permute-start.72 = (bf16[512,512]{1,0:T(8,128)(2,1)S(1)}, bf16[512,512]{1,0:T(8,128)(2,1)S(1)}, u32[]{:S(2)}, u32[]{:S(2)}) collective-permute-start(bf16[512,512]{1,0:T(8,128)(2,1)S(1)} %slice.594), channel_id=1, source_target_pairs={{0,4},{4,0},{1,5},{5,1},{2,6},{6,2},{3,7},{7,3},{8,12},{12,8},{9,1... | collective-permute-start | bytes 1572872 | tf_op jit(solution)/shard_map/inner_part/ppermute | solution.py:32
  701.8 31.2 %collective-permute-start.66 = (bf16[2,128,1024]{2,1,0:T(8,128)(2,1)S(1)}, bf16[2,128,1024]{2,1,0:T(8,128)(2,1)}, u32[]{:S(2)}, u32[]{:S(2)}) collective-permute-start(bf16[2,128,1024]{2,1,0:T(8,128)(2,1)S(1)} %add_convert_fusion.1), channel_id=1, source_target_pairs={{0,2},{2,0},{1,3},{3,1},{4,6},{6,4},{5,7},{7,5},{8,10},{10,8},{9,1... | collective-permute-start | bytes 1572872 | tf_op jit(solution)/shard_map/hidden_scatter/ppermute | solution.py:32
  725.8 44.4 %all-to-all-start.7 = ((bf16[8,64,1024]{2,1,0:T(8,128)(2,1)}), bf16[8,64,1024]{2,1,0:T(8,128)(2,1)S(1)}, u32[]{:S(2)}, u32[]{:S(2)}) async-start(bf16[8,64,1024]{2,1,0:T(8,128)(2,1)} %pad_maximum_fusion.15), calls=%async_computation.8 | async-start | bytes 2097152 | tf_op jit(solution)/shard_map/third_return/all_to_all | solution.py:150
  735.5 27.7 %collective-permute-start.67 = (bf16[128,1024]{1,0:T(8,128)(2,1)S(1)}, bf16[128,1024]{1,0:T(8,128)(2,1)}, u32[]{:S(2)}, u32[]{:S(2)}) collective-permute-start(bf16[128,1024]{1,0:T(8,128)(2,1)S(1)} %fusion.26), channel_id=1, source_target_pairs={{0,8},{8,0},{1,9},{9,1},{2,10},{10,2},{3,11},{11,3},{4,12},{12,4},... | collective-permute-start | bytes 786440 | tf_op jit(solution)/shard_map/hidden_scatter/ppermute | solution.py:32
  (245 other events, 2835.2 us)
Sparse Core Ops, SparseCore 0:
  132.8 17.9 all-gather.2
  208.5 48.5 all-gather.4
  517.0 96.2 reduce-scatter.1

commit v6 on v5

--- a/solution.py
+++ b/solution.py
@@ -1574,6 +1574,8 @@
             ).astype(F32)
     out_mine, out_theirs = grad_halves(order, gathered_halves(branch_grad), branch_rows)
     along, drop_got, lift_part, out_theirs = together(along, drop_got, lift_part, out_theirs)
+    with jax.named_scope("first_return"):
+        first_back = ranks_return([gate_part, lift_part], drows)
     with jax.named_scope("out_back"):
         out_theirs, drop_part = together(
             swap(out_theirs, "sh"), ch_part(added(mine[2], drop_got))
@@ -1586,8 +1588,6 @@
     gating_rows_grad = jnp.concatenate([gating_grad, query_grad], 1)
     gating_mine, gating_theirs = grad_halves(order, gathered_halves(team_tokens), gating_rows_grad)
     entry_back, out_theirs, drop_part = together(entry_back, out_theirs, drop_part)
-    with jax.named_scope("first_return"):
-        first_back = ranks_return([gate_part, lift_part, drop_part], drows)
     inner_conv_grad, parts, step_rows_grad, sums = ssm_back(
         sl, step_pre, head, conv, sides, ssm_grad, carried, entry_back, root
     )
@@ -1619,7 +1619,7 @@
     with jax.named_scope("inner_back"):
         inner_theirs = swap(inner_theirs, "sh")
     with jax.named_scope("second_return"):
-        second_back = ranks_return([out_part], drows)
+        second_back = ranks_return([out_part, drop_part], drows)
     inner_theirs, second_back, *hidden_parts = together(inner_theirs, second_back, *hidden_parts)
     with jax.named_scope("gating_part"):
         gating_part = ch_part(added(gating_mine, gating_theirs))
@@ -1629,11 +1629,9 @@
         inner_part = ch_part(added(inner_mine, inner_theirs))
     with jax.named_scope("third_return"):
         third_back = ranks_return([gating_part, inner_part], drows).astype(F32)
-    first_back = first_back.astype(F32)
-    gate_back = first_back[:, :, :LANES]
-    lift_back = first_back[:, :, LANES : 2 * LANES]
-    drop_back = first_back[:, :, 2 * LANES : 3 * LANES]
-    out_back = second_back.astype(F32)
+    first_back, second_back = first_back.astype(F32), second_back.astype(F32)
+    gate_back, lift_back = first_back[:, :, :LANES], first_back[:, :, LANES:]
+    out_back, drop_back = second_back[:, :, :LANES], second_back[:, :, LANES:]
     gating_back = third_back[:, :, :LANES]
     inner_back = third_back[:, :, LANES:]
     token_values = jnp.concatenate(own_tokens, 1)

time: 795 us -> 790 us (level)
    ppermute x3, waiting for transfers between devices: 14.2 us -> 2.44 us  [shifted(): lax.ppermute(value, 'ch', [(at, at + steps) for at in range(leading, last)])]
    unnamed x398 -> x393, local copies, waits for them, and re-layouts: 63.9 us -> 63.4 us
  transfers between devices with their start and end apart: 85 -> 85, of which waited for: 33 -> 32; matrix products, arithmetic and copies ran while one was open for 15% -> 16% of each run, Pallas kernels for 17% -> 17%
where the time goes in v6:
time: 790 us; the launch traced here: 779 us
  waiting for transfers between devices  282 us (36%)
  Pallas kernels  166 us (21%)
  starting transfers between devices  126 us (16%)
  local copies, waits for them, and re-layouts  109 us (14%)
  other arithmetic  79.1 us (10%)
  between operations  17 us (2%)
    ppermute x70, waiting for transfers between devices, swap(): return lax.ppermute(value, axis, [(0, 1), (1, 0)])  256 us
    ppermute x70, starting transfers between devices, swap(): return lax.ppermute(value, axis, [(0, 1), (1, 0)])  81.3 us
    unnamed x393, local copies, waits for them, and re-layouts  63.4 us
    pallas_call x3, Pallas kernels, back_dot(): call(3 + 3 * len(terms), lambda *refs: back_dot_kernel(len(terms), halves...  29.2 us
    pallas_call x8, Pallas kernels, grad_dot(): call(3.1, grad_dot_kernel, (half // tile,), [*specs, full(against)], pl.B...  21.8 us
    pallas_call x1, Pallas kernels, ssm_back(): call(18.8, lambda *refs: ssm_back_kernel(seqs, *refs), (blocks,), [back(8...  19.4 us
  transfers between devices with their start and end apart: 85, of which 32 were waited for; matrix products, arithmetic and copies ran while one was open for 16% of the time, Pallas kernels for 17%

profile of v6, /device:TPU:0, one launch (start us, length us, event | category | flops | bytes accessed | tf_op | source)
XLA Modules:
  0.0 779.2 jit_solution(17477838195357622095)
XLA Ops:
  67.4 14.0 %collective-permute-done.6 = bf16[544,512]{1,0:T(8,128)(2,1)} collective-permute-done((bf16[544,512]{1,0:T(8,128)(2,1)}, bf16[544,512]{1,0:T(8,128)(2,1)}, u32[]{:S(2)}, u32[]{:S(2)}) %collective-permute-start.6) | collective-permute-done | bytes 557088 | tf_op jit(solution)/shard_map/weights_first/ppermute | solution.py:32
  86.0 25.0 %collective-permute-done.8 = bf16[512,512]{1,0:T(8,128)(2,1)S(1)} collective-permute-done((bf16[512,512]{1,0:T(8,128)(2,1)}, bf16[512,512]{1,0:T(8,128)(2,1)S(1)}, u32[]{:S(2)}, u32[]{:S(2)}) %collective-permute-start.8) | collective-permute-done | bytes 524320 | tf_op jit(solution)/shard_map/weights_inner/ppermute | solution.py:32
  118.2 10.3 %shard_map.382 = (f32[1024,512]{1,0:T(8,128)}, f32[1024,512]{1,0:T(8,128)}, bf16[1024,64]{1,0:T(8,128)(2,1)S(1)}, bf16[1024,64]{1,0:T(8,128)(2,1)S(1)}, f32[1024...) custom-call(s32[5]{0:T(128)S(1)} %copy-done.70, ...), custom_call_target="tpu_custom_call" | custom-call | flops 10400000000 | bytes 1000000 | tf_op jit(solution)/shard_map/pallas_call | solution.py:489
  140.5 7.0 collective-permute-done.15
  151.1 13.1 %collective-permute-done.16 = bf16[2,512,128]{1,2,0:T(8,128)(2,1)} collective-permute-done((bf16[2,512,128]{1,2,0:T(8,128)(2,1)}, bf16[2,512,128]{1,2,0:T(8,128)(2,1)}, u32[]{:S(2)}, u32[]{:S(2)}) %collective-permute-start.16) | collective-permute-done | bytes 262176 | tf_op jit(solution)/shard_map/keys_exchange/ppermute | solution.py:32
  169.9 6.0 shard_map.383
  194.7 10.7 %shard_map.385 = (f32[2,512,384]{2,1,0:T(8,128)S(1)}, bf16[2,4,256,384]{3,2,1,0:T(8,128)(2,1)S(1)}, f32[4,2,8,128]{3,2,1,0:T(8,128)S(1)}) custom-call(f32[2,512,8]{2,1,0:T(8,128)S(1)} %bitcast.320, f32[8,8]{1,0:T(8,128)S(1)} %pad.21.refs_1_, f32[2,512,512]{2,1,0:T(8,128)} %bitcast.315, bf16[8,512,128]{2,1,0:T(8,128)(2,1)S(1)} %copy-done.74, ...), custom_call_target="tpu_custom_call" | custom-call | flops 10800000000 | bytes 1000000 | tf_op jit(solution)/shard_map/pallas_call | solution.py:1038
  208.5 8.0 %collective-permute-start.13 = (f32[8,128]{1,0:T(8,128)S(1)}, f32[8,128]{1,0:T(8,128)S(1)}, u32[]{:S(2)}, u32[]{:S(2)}) collective-permute-start(f32[8,128]{1,0:T(8,128)S(1)} %add.294), channel_id=1, source_target_pairs={{0,2},{2,0},{1,3},{3,1},{4,6},{6,4},{5,7},{7,5},{8,10},{10,8},{9,1... | collective-permute-start | bytes 12296 | tf_op jit(solution)/shard_map/square_sum/ppermute | solution.py:32
  229.1 22.3 %collective-permute-done.18 = bf16[512,512]{1,0:T(8,128)(2,1)S(1)} collective-permute-done((bf16[512,512]{1,0:T(8,128)(2,1)S(1)}, bf16[512,512]{1,0:T(8,128)(2,1)S(1)}, u32[]{:S(2)}, u32[]{:S(2)}) %collective-permute-start.18) | collective-permute-done | bytes 524320 | tf_op jit(solution)/shard_map/weights_gate_first/ppermute | solution.py:32
  251.9 6.2 shard_map.387
  262.1 22.0 %collective-permute-done.20 = bf16[512,512]{1,0:T(8,128)(2,1)S(1)} collective-permute-done((bf16[512,512]{1,0:T(8,128)(2,1)S(1)}, bf16[512,512]{1,0:T(8,128)(2,1)S(1)}, u32[]{:S(2)}, u32[]{:S(2)}) %collective-permute-start.20) | collective-permute-done | bytes 524320 | tf_op jit(solution)/shard_map/weights_gate/ppermute | solution.py:32
  291.2 9.6 %collective-permute-done.28 = bf16[2,128,1024]{2,1,0:T(8,128)(2,1)S(1)} collective-permute-done((bf16[2,128,1024]{2,1,0:T(8,128)(2,1)S(1)}, bf16[2,128,1024]{2,1,0:T(8,128)(2,1)S(1)}, u32[]{:S(2)}, u32[]{:S(2)}) %collective-permute-start.28) | collective-permute-done | bytes 524320 | tf_op jit(solution)/shard_map/branch_scatter/ppermute | solution.py:32
  301.1 11.9 %collective-permute-done.26 = bf16[2,128,1024]{2,1,0:T(8,128)(2,1)S(1)} collective-permute-done((bf16[2,128,1024]{2,1,0:T(8,128)(2,1)S(1)}, bf16[2,128,1024]{2,1,0:T(8,128)(2,1)S(1)}, u32[]{:S(2)}, u32[]{:S(2)}) %collective-permute-start.26) | collective-permute-done | bytes 524320 | tf_op jit(solution)/shard_map/branch_scatter/ppermute | solution.py:32
  331.8 5.9 collective-permute-done.33
  339.6 10.1 %collective-permute-done.36.dt.theirs = bf16[1024,512]{1,0:T(8,128)(2,1)S(1)} collective-permute-done((bf16[1024,512]{1,0:T(8,128)(2,1)S(1)}, bf16[1024,512]{1,0:T(8,128)(2,1)S(1)}, u32[]{:S(2)}, u32[]{:S(2)}) %collective-permute-start.36) | collective-permute-done | bytes 1048608 | tf_op jit(solution)/shard_map/weights_drop/ppermute | solution.py:32
  354.3 11.9 %shard_map.389 = (bf16[1024,512]{1,0:T(8,128)(2,1)S(1)}, bf16[1024,512]{1,0:T(8,128)(2,1)S(1)}, bf16[1024,512]{1,0:T(8,128)(2,1)S(1)}) custom-call(s32[5]{0:T(128)S(1)} %copy-done.71, bf16[4,128,1024]{2,1,0:T(8,128)(2,1)S(1)} %copy-done.27, bf16[4,128,1024]{2,1,0:T(8,128)(2,1)S(1)} %copy-done.25, bf16[4,128,1024]{2,1,0:T(8,128)(2,1)} %collective-permute-done.34.lo, ...), custom_call_target="tpu_custom_call" | custom-call | flops 11800000512 | bytes 1000000 | tf_op jit(solution)/shard_map/pallas_call | solution.py:762
  368.1 10.6 %shard_map.390 = (f32[4,128,1024]{2,1,0:T(8,128)}, f32[4,128,1024]{2,1,0:T(8,128)}, bf16[4,128,1024]{2,1,0:T(8,128)(2,1)S(1)}, bf16[4,128,1024]{2,1,0:T(8,128)(2,1)S(1)}) custom-call(s32[8]{0:T(128)S(1)} %stack.228.refs_0_.order.scalars, bf16[1024,512]{1,0:T(8,128)(2,1)S(1)} %get-tuple-element.221.refs_1_.refs_2_.gate, ...), custom_call_target="tpu_custom_call" | custom-call | flops 8999999488 | bytes 1000000 | tf_op jit(solution)/shard_map/pallas_call | solution.py:623
  384.8 12.2 %shard_map.391 = (bf16[1024,512]{1,0:T(8,128)(2,1)S(1)}, bf16[1024,512]{1,0:T(8,128)(2,1)S(1)}, bf16[1024,512]{1,0:T(8,128)(2,1)S(1)}, bf16[1024,512]{1,0:T(8,12...) custom-call(s32[8]{0:T(128)S(1)} %stack.228.refs_0_.order.scalars, ...), custom_call_target="tpu_custom_call" | custom-call | flops 12999999488 | bytes 1000000 | tf_op jit(solution)/shard_map/pallas_call | solution.py:725
  402.7 11.3 %collective-permute-done.38 = bf16[2,128,1024]{2,1,0:T(8,128)(2,1)S(1)} collective-permute-done((bf16[2,128,1024]{2,1,0:T(8,128)(2,1)S(1)}, bf16[2,128,1024]{2,1,0:T(8,128)(2,1)S(1)}, u32[]{:S(2)}, u32[]{:S(2)}) %collective-permute-start.38) | collective-permute-done | bytes 524320 | tf_op jit(solution)/shard_map/feed_scatter/ppermute | solution.py:32
  414.9 7.2 collective-permute-done.39
  461.3 15.3 %collective-permute-done.51 = bf16[512,512]{1,0:T(8,128)(2,1)} collective-permute-done((bf16[512,512]{1,0:T(8,128)(2,1)}, bf16[512,512]{1,0:T(8,128)(2,1)}, u32[]{:S(2)}, u32[]{:S(2)}) %collective-permute-start.51) | collective-permute-done | bytes 524320 | tf_op jit(solution)/shard_map/lift_back/ppermute | solution.py:32
  478.9 9.0 %shard_map.395 = (f32[1024,384]{1,0:T(8,128)}, bf16[1024,128]{1,0:T(8,128)(2,1)S(1)}, f32[4,8,256]{2,1,0:T(8,128)S(1)}, f32[1,384]{1,0:T(1,128)S(1)}) custom-call(s32[5]{0:T(128)S(1)} %copy-done.72, bf16[4,128,1024]{2,1,0:T(8,128)(2,1)} %pad_maximum_fusion.11.l.own, bf16[4,128,1024]{2,1,0:T(8,128)(2,1)} %pad_maximum_fusion.12.r.own, ...), custom_call_target="tpu_custom_call" | custom-call | flops 9100000256 | bytes 1000000 | tf_op jit(solution)/shard_map/pallas_call | solution.py:560
  490.8 6.4 shard_map.399
  531.5 6.3 shard_map.397
  551.1 6.6 all-to-all-start.4
  566.1 19.4 %shard_map.398 = (f32[2,512,384]{2,1,0:T(8,128)S(1)}, bf16[8,512,128]{2,1,0:T(8,128)(2,1)}, bf16[2,512,8]{2,1,0:T(8,128)(2,1)S(1)}, f32[8,8]{1,0:T(8,128)S(1)}) custom-call(f32[2,512,8]{2,1,0:T(8,128)S(1)} %bitcast.322, f32[8,8]{1,0:T(8,128)S(1)} %copy-done.54, f32[2,512,512]{2,1,0:T(8,128)} %bitcast.316, bf16[8,512,128]{2,1,0:T(8,128)(2,1)S(1)} %copy-done.76, ...), custom_call_target="tpu_custom_call" | custom-call | flops 18800001024 | bytes 1000000 | tf_op jit(solution)/shard_map/pallas_call | solution.py:1210
  592.9 5.9 all-to-all-done.4
  611.1 13.5 %all-to-all-done.5.refs_1_ = bf16[8,512,128]{2,1,0:T(8,128)(2,1)S(1)} async-done(((bf16[8,512,128]{2,1,0:T(8,128)(2,1)}), bf16[8,512,128]{2,1,0:T(8,128)(2,1)S(1)}, u32[]{:S(2)}, u32[]{:S(2)}) %all-to-all-start.5) | async-done | bytes 1048608 | tf_op jit(solution)/shard_map/parts_exchange/all_to_all | solution.py:1596
  663.3 12.4 %shard_map.405 = (f32[4,128,1024]{2,1,0:T(8,128)}, f32[4,128,1024]{2,1,0:T(8,128)}, bf16[4,128,1024]{2,1,0:T(8,128)(2,1)S(1)}, bf16[4,128,1024]{2,1,0:T(8,128)(2,1)}) custom-call(s32[8]{0:T(128)S(1)} %copy-done.69, bf16[1024,512]{1,0:T(8,128)(2,1)S(1)} %copy-done.35, bf16[1024,512]{1,0:T(8,128)(2,1)S(1)} %copy-done.35, ...), custom_call_target="tpu_custom_call" | custom-call | flops 12000000000 | bytes 1000000 | tf_op jit(solution)/shard_map/pallas_call | solution.py:623
  681.9 5.9 collective-permute-done.64
  698.1 20.1 %collective-permute-done.72 = bf16[512,512]{1,0:T(8,128)(2,1)S(1)} collective-permute-done((bf16[512,512]{1,0:T(8,128)(2,1)S(1)}, bf16[512,512]{1,0:T(8,128)(2,1)S(1)}, u32[]{:S(2)}, u32[]{:S(2)}) %collective-permute-start.72) | collective-permute-done | bytes 524320 | tf_op jit(solution)/shard_map/inner_part/ppermute | solution.py:32
  729.5 20.3 %collective-permute-done.69 = bf16[2,128,1024]{2,1,0:T(8,128)(2,1)S(1)} collective-permute-done((bf16[2,128,1024]{2,1,0:T(8,128)(2,1)S(1)}, bf16[2,128,1024]{2,1,0:T(8,128)(2,1)S(1)}, u32[]{:S(2)}, u32[]{:S(2)}) %collective-permute-start.69) | collective-permute-done | bytes 524320 | tf_op jit(solution)/shard_map/hidden_scatter/ppermute | solution.py:32
  (805 shorter events, 385.5 us)
Async XLA Ops:
  62.6 73.1 %all-to-all-start.2 = ((bf16[8,64,2048]{2,1,0:T(8,128)(2,1)}), bf16[8,64,2048]{2,1,0:T(8,128)(2,1)}, u32[]{:S(2)}, u32[]{:S(2)}) async-start(bf16[8,64,2048]{2,1,0:T(8,128)(2,1)} %fusion.14), calls=%async_computation.2 | async-start | bytes 4194304 | tf_op jit(solution)/shard_map/weights_rest/all_to_all | solution.py:134
  66.9 99.2 %all-gather.3.cloned.1.call-start = ((), (), s32[]{:S(2)}) async-start(), calls=%async_computation.10 | async-start | bytes 1179648 | tf_op jit(solution)/shard_map/all_gather | solution.py:1468
  83.5 30.9 %collective-permute-start.7 = (bf16[1024,512]{1,0:T(8,128)(2,1)}, bf16[1024,512]{1,0:T(8,128)(2,1)}, u32[]{:S(2)}, u32[]{:S(2)}) collective-permute-start(bf16[1024,512]{1,0:T(8,128)(2,1)} %pad_maximum_fusion.2.refs_5_.refs_3_), channel_id=1, source_target_pairs={{0,16},{16,0},{1,17},{17,1},{2,18},{18,2},{3,19},{19,3},{4,20},{20... | collective-permute-start | bytes 3145736 | tf_op jit(solution)/shard_map/weights_inner/ppermute | solution.py:32
  132.7 219.2 %all-gather.5.cloned.1.call-start = ((), (), s32[]{:S(2)}) async-start(), calls=%async_computation.11 | async-start | bytes 4718592 | tf_op jit(solution)/shard_map/all_gather | solution.py:1470
  132.7 35.9 %collective-permute-start.9 = (bf16[1024,512]{1,0:T(8,128)(2,1)}, bf16[1024,512]{1,0:T(8,128)(2,1)}, u32[]{:S(2)}, u32[]{:S(2)}) collective-permute-start(bf16[1024,512]{1,0:T(8,128)(2,1)} %pad_maximum_fusion.3.mine.refs_7_), channel_id=1, source_target_pairs={{0,16},{16,0},{1,17},{17,1},{2,18},{18,2},{3,19},{19,3},{4,20},{20... | collective-permute-start | bytes 3145736 | tf_op jit(solution)/shard_map/weights_gating/ppermute | solution.py:32
  137.6 28.6 %collective-permute-start.10 = (bf16[512,512]{1,0:T(8,128)(2,1)}, bf16[512,512]{1,0:T(8,128)(2,1)}, u32[]{:S(2)}, u32[]{:S(2)}) collective-permute-start(bf16[512,512]{1,0:T(8,128)(2,1)} %slice.446), channel_id=1, source_target_pairs={{0,4},{4,0},{1,5},{5,1},{2,6},{6,2},{3,7},{7,3},{8,12},{12,8},{9,1... | collective-permute-start | bytes 1572872 | tf_op jit(solution)/shard_map/weights_gating/ppermute | solution.py:32
  220.6 31.3 %collective-permute-start.21 = (bf16[1024,512]{1,0:T(8,128)(2,1)S(1)}, bf16[1024,512]{1,0:T(8,128)(2,1)S(1)}, u32[]{:S(2)}, u32[]{:S(2)}) collective-permute-start(bf16[1024,512]{1,0:T(8,128)(2,1)S(1)} %copy-done.14), channel_id=1, source_target_pairs={{0,16},{16,0},{1,17},{17,1},{2,18},{18,2},{3,19},{19,3},{4,20},{20... | collective-permute-start | bytes 3145736 | tf_op jit(solution)/shard_map/weights_out/ppermute | solution.py:32
  225.0 26.5 %collective-permute-start.18 = (bf16[512,512]{1,0:T(8,128)(2,1)S(1)}, bf16[512,512]{1,0:T(8,128)(2,1)S(1)}, u32[]{:S(2)}, u32[]{:S(2)}) collective-permute-start(bf16[512,512]{1,0:T(8,128)(2,1)S(1)} %get-tuple-element.318), channel_id=1, source_target_pairs={{0,4},{4,0},{1,5},{5,1},{2,6},{6,2},{3,7},{7,3},{8,12},{12,8},{9,1... | collective-permute-start | bytes 1572872 | tf_op jit(solution)/shard_map/weights_gate_first/ppermute | solution.py:32
  251.6 32.7 %collective-permute-start.19 = (bf16[1024,512]{1,0:T(8,128)(2,1)S(1)}, bf16[1024,512]{1,0:T(8,128)(2,1)S(1)}, u32[]{:S(2)}, u32[]{:S(2)}) collective-permute-start(bf16[1024,512]{1,0:T(8,128)(2,1)S(1)} %pad_maximum_fusion.6.gm.refs_3_), channel_id=1, source_target_pairs={{0,16},{16,0},{1,17},{17,1},{2,18},{18,2},{3,19},{19,3},{4,20},{20... | collective-permute-start | bytes 3145736 | tf_op jit(solution)/shard_map/weights_gate/ppermute | solution.py:32
  258.2 26.1 %collective-permute-start.23 = (bf16[4,128,1024]{2,1,0:T(8,128)(2,1)S(1)}, bf16[4,128,1024]{2,1,0:T(8,128)(2,1)S(1)}, u32[]{:S(2)}, u32[]{:S(2)}) collective-permute-start(bf16[4,128,1024]{2,1,0:T(8,128)(2,1)S(1)} %get-tuple-element.205), channel_id=1, source_target_pairs={{0,1},{1,0},{2,3},{3,2},{4,5},{5,4},{6,7},{7,6},{8,9},{9,8},{10,11... | collective-permute-start | bytes 3145736 | tf_op jit(solution)/shard_map/branch_scatter/ppermute | solution.py:32
  258.2 27.0 %collective-permute-start.22 = (bf16[4,128,1024]{2,1,0:T(8,128)(2,1)S(1)}, bf16[4,128,1024]{2,1,0:T(8,128)(2,1)S(1)}, u32[]{:S(2)}, u32[]{:S(2)}) collective-permute-start(bf16[4,128,1024]{2,1,0:T(8,128)(2,1)S(1)} %get-tuple-element.203), channel_id=1, source_target_pairs={{0,1},{1,0},{2,3},{3,2},{4,5},{5,4},{6,7},{7,6},{8,9},{9,8},{10,11... | collective-permute-start | bytes 3145736 | tf_op jit(solution)/shard_map/branch_scatter/ppermute | solution.py:32
  287.0 27.9 %collective-permute-start.25 = (bf16[512,512]{1,0:T(8,128)(2,1)S(1)}, bf16[512,512]{1,0:T(8,128)(2,1)S(1)}, u32[]{:S(2)}, u32[]{:S(2)}) collective-permute-start(bf16[512,512]{1,0:T(8,128)(2,1)S(1)} %get-tuple-element.207), channel_id=1, source_target_pairs={{0,4},{4,0},{1,5},{5,1},{2,6},{6,2},{3,7},{7,3},{8,12},{12,8},{9,1... | collective-permute-start | bytes 1572872 | tf_op jit(solution)/shard_map/weights_lift/ppermute | solution.py:32
  436.4 42.5 %collective-permute-start.50 = (bf16[1024,512]{1,0:T(8,128)(2,1)}, bf16[1024,512]{1,0:T(8,128)(2,1)}, u32[]{:S(2)}, u32[]{:S(2)}) collective-permute-start(bf16[1024,512]{1,0:T(8,128)(2,1)} %copy-done.80), channel_id=1, source_target_pairs={{0,16},{16,0},{1,17},{17,1},{2,18},{18,2},{3,19},{19,3},{4,20},{20... | collective-permute-start | bytes 3145736 | tf_op jit(solution)/shard_map/lift_back/ppermute | solution.py:32
  445.7 33.2 %collective-permute-start.49 = (bf16[4,128,1024]{2,1,0:T(8,128)(2,1)}, bf16[4,128,1024]{2,1,0:T(8,128)(2,1)}, u32[]{:S(2)}, u32[]{:S(2)}) collective-permute-start(bf16[4,128,1024]{2,1,0:T(8,128)(2,1)} %pad_maximum_fusion.12.r.own), channel_id=1, source_target_pairs={{0,1},{1,0},{2,3},{3,2},{4,5},{5,4},{6,7},{7,6},{8,9},{9,8},{10,11... | collective-permute-start | bytes 3145736 | tf_op jit(solution)/shard_map/branch_gather/ppermute | solution.py:32
  448.0 31.0 %collective-permute-start.48 = (bf16[4,128,1024]{2,1,0:T(8,128)(2,1)}, bf16[4,128,1024]{2,1,0:T(8,128)(2,1)}, u32[]{:S(2)}, u32[]{:S(2)}) collective-permute-start(bf16[4,128,1024]{2,1,0:T(8,128)(2,1)} %pad_maximum_fusion.11.l.own), channel_id=1, source_target_pairs={{0,1},{1,0},{2,3},{3,2},{4,5},{5,4},{6,7},{7,6},{8,9},{9,8},{10,11... | collective-permute-start | bytes 3145736 | tf_op jit(solution)/shard_map/branch_gather/ppermute | solution.py:32
  450.2 26.3 %collective-permute-start.51 = (bf16[512,512]{1,0:T(8,128)(2,1)}, bf16[512,512]{1,0:T(8,128)(2,1)}, u32[]{:S(2)}, u32[]{:S(2)}) collective-permute-start(bf16[512,512]{1,0:T(8,128)(2,1)} %slice.602), channel_id=1, source_target_pairs={{0,4},{4,0},{1,5},{5,1},{2,6},{6,2},{3,7},{7,3},{8,12},{12,8},{9,1... | collective-permute-start | bytes 1572872 | tf_op jit(solution)/shard_map/lift_back/ppermute | solution.py:32
  451.6 66.1 %collective-permute-start.55 = (bf16[1024,512]{1,0:T(8,128)(2,1)}, bf16[1024,512]{1,0:T(8,128)(2,1)}, u32[]{:S(2)}, u32[]{:S(2)}) collective-permute-start(bf16[1024,512]{1,0:T(8,128)(2,1)} %get-tuple-element.247), channel_id=1, source_target_pairs={{0,16},{16,0},{1,17},{17,1},{2,18},{18,2},{3,19},{19,3},{4,20},{20... | collective-permute-start | bytes 3145736 | tf_op jit(solution)/shard_map/drop_back/ppermute | solution.py:32
  509.7 41.4 %all-to-all-start.3 = ((bf16[4,1024,128]{2,1,0:T(8,128)(2,1)}), bf16[4,1024,128]{2,1,0:T(8,128)(2,1)}, u32[]{:S(2)}, u32[]{:S(2)}) async-start(bf16[4,1024,128]{2,1,0:T(8,128)(2,1)} %convert_element_type.377), calls=%async_computation.4 | async-start | bytes 2097152 | tf_op jit(solution)/shard_map/keys_back/all_to_all | solution.py:1561
  514.0 247.7 %reduce-scatter.2.cloned.1.call-start = ((), (), s32[]{:S(2)}) async-start(), calls=%async_computation.12 | async-start | bytes 4718592 | tf_op jit(solution)/shard_map/reduce_scatter | solution.py:1547
  521.5 27.6 %collective-permute-start.59 = (bf16[512,512]{1,0:T(8,128)(2,1)}, bf16[512,512]{1,0:T(8,128)(2,1)}, u32[]{:S(2)}, u32[]{:S(2)}) collective-permute-start(bf16[512,512]{1,0:T(8,128)(2,1)} %slice.600), channel_id=1, source_target_pairs={{0,4},{4,0},{1,5},{5,1},{2,6},{6,2},{3,7},{7,3},{8,12},{12,8},{9,1... | collective-permute-start | bytes 1572872 | tf_op jit(solution)/shard_map/out_back/ppermute | solution.py:32
  523.1 39.5 %collective-permute-start.58 = (bf16[1024,512]{1,0:T(8,128)(2,1)}, bf16[1024,512]{1,0:T(8,128)(2,1)}, u32[]{:S(2)}, u32[]{:S(2)}) collective-permute-start(bf16[1024,512]{1,0:T(8,128)(2,1)} %shard_map.396), channel_id=1, source_target_pairs={{0,16},{16,0},{1,17},{17,1},{2,18},{18,2},{3,19},{19,3},{4,20},{20... | collective-permute-start | bytes 3145736 | tf_op jit(solution)/shard_map/out_back/ppermute | solution.py:32
  543.6 62.2 %collective-permute-start.62 = (bf16[1024,512]{1,0:T(8,128)(2,1)}, bf16[1024,512]{1,0:T(8,128)(2,1)}, u32[]{:S(2)}, u32[]{:S(2)}) collective-permute-start(bf16[1024,512]{1,0:T(8,128)(2,1)} %shard_map.402), channel_id=1, source_target_pairs={{0,16},{16,0},{1,17},{17,1},{2,18},{18,2},{3,19},{19,3},{4,20},{20... | collective-permute-start | bytes 3145736 | tf_op jit(solution)/shard_map/gating_back/ppermute | solution.py:32
  551.1 47.7 %all-to-all-start.4 = ((bf16[8,64,1024]{2,1,0:T(8,128)(2,1)}), bf16[8,64,1024]{2,1,0:T(8,128)(2,1)}, u32[]{:S(2)}, u32[]{:S(2)}) async-start(bf16[8,64,1024]{2,1,0:T(8,128)(2,1)} %pad_maximum_fusion.13), calls=%async_computation.5 | async-start | bytes 2097152 | tf_op jit(solution)/shard_map/first_return/all_to_all | solution.py:150
  560.6 31.4 %collective-permute-start.60 = (bf16[512,128]{1,0:T(8,128)(2,1)}, bf16[512,128]{1,0:T(8,128)(2,1)}, u32[]{:S(2)}, u32[]{:S(2)}) collective-permute-start(bf16[512,128]{1,0:T(8,128)(2,1)} %fusion.31), channel_id=1, source_target_pairs={{0,4},{4,0},{1,5},{5,1},{2,6},{6,2},{3,7},{7,3},{8,12},{12,8},{9,1... | collective-permute-start | bytes 393224 | tf_op jit(solution)/shard_map/keys_back/ppermute | solution.py:32
  565.1 38.4 %collective-permute-start.63 = (bf16[512,512]{1,0:T(8,128)(2,1)}, bf16[512,512]{1,0:T(8,128)(2,1)}, u32[]{:S(2)}, u32[]{:S(2)}) collective-permute-start(bf16[512,512]{1,0:T(8,128)(2,1)} %slice.599), channel_id=1, source_target_pairs={{0,4},{4,0},{1,5},{5,1},{2,6},{6,2},{3,7},{7,3},{8,12},{12,8},{9,1... | collective-permute-start | bytes 1572872 | tf_op jit(solution)/shard_map/gating_back/ppermute | solution.py:32
  649.2 39.2 %collective-permute-start.71 = (bf16[512,512]{1,0:T(8,128)(2,1)}, bf16[512,512]{1,0:T(8,128)(2,1)}, u32[]{:S(2)}, u32[]{:S(2)}) collective-permute-start(bf16[512,512]{1,0:T(8,128)(2,1)} %slice.598), channel_id=1, source_target_pairs={{0,4},{4,0},{1,5},{5,1},{2,6},{6,2},{3,7},{7,3},{8,12},{12,8},{9,1... | collective-permute-start | bytes 1572872 | tf_op jit(solution)/shard_map/gating_part/ppermute | solution.py:32
  653.1 34.7 %all-to-all-start.6 = ((bf16[8,64,1024]{2,1,0:T(8,128)(2,1)}), bf16[8,64,1024]{2,1,0:T(8,128)(2,1)}, u32[]{:S(2)}, u32[]{:S(2)}) async-start(bf16[8,64,1024]{2,1,0:T(8,128)(2,1)} %pad_maximum_fusion.15), calls=%async_computation.7 | async-start | bytes 2097152 | tf_op jit(solution)/shard_map/second_return/all_to_all | solution.py:150
  689.9 33.9 %collective-permute-start.68 = (bf16[4,128,1024]{2,1,0:T(8,128)(2,1)}, bf16[4,128,1024]{2,1,0:T(8,128)(2,1)}, u32[]{:S(2)}, u32[]{:S(2)}) collective-permute-start(bf16[4,128,1024]{2,1,0:T(8,128)(2,1)} %get-tuple-element.292), channel_id=1, source_target_pairs={{0,1},{1,0},{2,3},{3,2},{4,5},{5,4},{6,7},{7,6},{8,9},{9,8},{10,11... | collective-permute-start | bytes 3145736 | tf_op jit(solution)/shard_map/hidden_scatter/ppermute | solution.py:32
  692.1 26.2 %collective-permute-start.72 = (bf16[512,512]{1,0:T(8,128)(2,1)S(1)}, bf16[512,512]{1,0:T(8,128)(2,1)S(1)}, u32[]{:S(2)}, u32[]{:S(2)}) collective-permute-start(bf16[512,512]{1,0:T(8,128)(2,1)S(1)} %slice.597), channel_id=1, source_target_pairs={{0,4},{4,0},{1,5},{5,1},{2,6},{6,2},{3,7},{7,3},{8,12},{12,8},{9,1... | collective-permute-start | bytes 1572872 | tf_op jit(solution)/shard_map/inner_part/ppermute | solution.py:32
  696.5 31.0 %collective-permute-start.66 = (bf16[2,128,1024]{2,1,0:T(8,128)(2,1)}, bf16[2,128,1024]{2,1,0:T(8,128)(2,1)}, u32[]{:S(2)}, u32[]{:S(2)}) collective-permute-start(bf16[2,128,1024]{2,1,0:T(8,128)(2,1)} %add_convert_fusion.1), channel_id=1, source_target_pairs={{0,2},{2,0},{1,3},{3,1},{4,6},{6,4},{5,7},{7,5},{8,10},{10,8},{9,1... | collective-permute-start | bytes 1572872 | tf_op jit(solution)/shard_map/hidden_scatter/ppermute | solution.py:32
  719.6 44.6 %all-to-all-start.7 = ((bf16[8,64,1024]{2,1,0:T(8,128)(2,1)}), bf16[8,64,1024]{2,1,0:T(8,128)(2,1)}, u32[]{:S(2)}, u32[]{:S(2)}) async-start(bf16[8,64,1024]{2,1,0:T(8,128)(2,1)} %pad_maximum_fusion.16), calls=%async_computation.8 | async-start | bytes 2097152 | tf_op jit(solution)/shard_map/third_return/all_to_all | solution.py:150
  729.0 26.2 %collective-permute-start.67 = (bf16[128,1024]{1,0:T(8,128)(2,1)S(1)}, bf16[128,1024]{1,0:T(8,128)(2,1)S(1)}, u32[]{:S(2)}, u32[]{:S(2)}) collective-permute-start(bf16[128,1024]{1,0:T(8,128)(2,1)S(1)} %fusion.26), channel_id=1, source_target_pairs={{0,8},{8,0},{1,9},{9,1},{2,10},{10,2},{3,11},{11,3},{4,12},{12,4},... | collective-permute-start | bytes 786440 | tf_op jit(solution)/shard_map/hidden_scatter/ppermute | solution.py:32
  (242 other events, 2802.1 us)
Sparse Core Ops, SparseCore 0:
  132.8 18.1 all-gather.2
  208.6 48.4 all-gather.4
  517.1 103.7 reduce-scatter.1
